TPU v7x, 32 devices: a whole 2x2x4 slice. The times are simulated.
32 devices in a mesh: pipe: 2 (over core), dp: 16 (over z, y, x).
Axes of the slice: x: 2, y: 2, z: 4, core: 2. Of those that a mesh axis runs over, the one named last changes fastest.
Arguments:
- clips_in: bfloat16 [3, 6272, 2048], P(None, 'dp'), may hold values from -6 to 6
- cotangent: bfloat16 [3, 6272, 2048], P(None, 'dp'), may hold values from -6 to 6
- segment_ids: int32 [3, 16, 8], P(None, 'dp'), may hold values from 0 to 1, as said below
- w_in: float32 [2, 2048, 512], P('pipe', None, 'dp'), may hold values from -0.125 to 0.125
- w_squeeze: float32 [2, 512, 128], P('pipe', 'dp'), may hold values from -0.25 to 0.25
- w_near: float32 [2, 1152, 512], P('pipe', None, 'dp'), may hold values from -0.1875 to 0.1875
- w_far: float32 [2, 1152, 512], P('pipe', None, 'dp'), may hold values from -0.1875 to 0.1875
- w_mid: float32 [2, 4608, 512], P('pipe', None, 'dp'), may hold values from -0.09375 to 0.09375
- w_out: float32 [2, 512, 2048], P('pipe', None, 'dp'), may hold values from -0.25 to 0.25
- gain_mid: float32 [2, 2, 512], P('pipe', None, 'dp'), may hold values from 0.5 to 1.5
- bias_mid: float32 [2, 2, 512], P('pipe', None, 'dp'), may hold values from -0.5 to 0.5
- gain_out: float32 [2, 2048], P('pipe', 'dp'), may hold values from 0.5 to 1.5
- bias_out: float32 [2, 2048], P('pipe', 'dp'), may hold values from -0.5 to 0.5
Outputs:
- activations: bfloat16 [2, 3, 6272, 2048], P('pipe', None, 'dp')
- input_grads: bfloat16 [2, 3, 6272, 2048], P('pipe', None, 'dp')
- grad_w_in: float32 [2, 2048, 512], P('pipe', None, 'dp')
- grad_w_squeeze: float32 [2, 512, 128], P('pipe', 'dp')
- grad_w_near: float32 [2, 1152, 512], P('pipe', None, 'dp')
- grad_w_far: float32 [2, 1152, 512], P('pipe', None, 'dp')
- grad_w_mid: float32 [2, 4608, 512], P('pipe', None, 'dp')
- grad_w_out: float32 [2, 512, 2048], P('pipe', None, 'dp')
- grad_gain_mid: float32 [2, 2, 512], P('pipe', None, 'dp')
- grad_bias_mid: float32 [2, 2, 512], P('pipe', None, 'dp')
- grad_gain_out: float32 [2, 2048], P('pipe', 'dp')
- grad_bias_out: float32 [2, 2048], P('pipe', 'dp')
Inputs may be any that keep to these rules, and one draw needn't show every extreme that they name: `segment_ids`: in every clip slot the ids are 0 on the first video's segments and 1 on the second's; each video has one segment or more.
All inputs are finite; a program needn't handle non-finite values.
Results may differ from a plain program's by a relative error of at most 0.023.
Values may be sent and summed in bfloat16 or wider, within the bound.
No kernel may reach another device: no remote copies, remote signals or barrier semaphores. Data moves between devices by JAX's collectives and lax.ppermute only.
A program may use at most 256 MiB of HBM per device.

v0:
```python
import jax
import jax.numpy as jnp
from jax import lax
from jax.sharding import PartitionSpec as P

SEG = 8
SIDE = 7


epsilon = 1e-05


def passed_along(value, axis, steps):
    count = lax.axis_size(axis)
    initial, last = (max(0, -steps), min(count, count - steps))
    return lax.ppermute(value, axis, [(source, source + steps) for source in range(initial, last)])


def patches(field_in, spread):
    channels = field_in.shape[-1]
    frames = field_in.reshape(-1, SIDE, SIDE, channels)
    padded = jnp.pad(frames, ((0, 0), (spread, spread), (spread, spread), (0, 0)))
    pieces = []
    for row_tap in range(3):
        for col_tap in range(3):
            pieces.append(
                padded[
                    :,
                    row_tap * spread : row_tap * spread + SIDE,
                    col_tap * spread : col_tap * spread + SIDE,
                    :,
                ]
            )
    return jnp.concatenate(pieces, axis=-1).reshape(field_in.shape[0], 9 * channels)


def unpatch(gradient, spread, channels):
    zeros_in = jnp.zeros((gradient.shape[0], channels), jnp.float32)
    outputs, pull_back = jax.vjp(lambda field_in: patches(field_in, spread), zeros_in)
    return pull_back(gradient)[0]


def boundary(segment_ids):
    same_video = (segment_ids[..., 1:] == segment_ids[..., :-1]).astype(jnp.float32)
    closing = jnp.zeros(segment_ids.shape[:-1] + (1,), jnp.float32)
    return jnp.concatenate([same_video, closing], axis=-1)


def difference(field_in, row_mask):
    frames = field_in.reshape(row_mask.shape[0], SEG, SIDE * SIDE, field_in.shape[-1])
    shifted = jnp.concatenate([frames[:, 1:], jnp.zeros_like(frames[:, :1])], axis=1)
    return (row_mask[:, :, None, None] * (shifted - frames)).reshape(field_in.shape)


def difference_back(gradient, row_mask):
    frames = (
        gradient.reshape(row_mask.shape[0], SEG, SIDE * SIDE, gradient.shape[-1])
        * row_mask[:, :, None, None]
    )
    earlier = jnp.concatenate([jnp.zeros_like(frames[:, :1]), frames[:, :-1]], axis=1)
    return (earlier - frames).reshape(gradient.shape)


def silu_slope(values):
    sigmoid_v = jax.nn.sigmoid(values)
    return sigmoid_v * (1.0 + values * (1.0 - sigmoid_v))


def product(left_side, right_side):
    return jnp.dot(left_side, right_side, preferred_element_type=jnp.float32)


def against(left_side, right_side):
    return lax.dot_general(
        left_side, right_side, (((1,), (1,)), ((), ())), preferred_element_type=jnp.float32
    )


def across(left_side, right_side):
    return lax.dot_general(
        left_side, right_side, (((0,), (0,)), ((), ())), preferred_element_type=jnp.float32
    )


def norm_forward(values, gain_vec, bias_vec, row_total):
    centre_mean = lax.psum(jnp.sum(values, axis=0), "dp") / row_total
    centre = values - centre_mean
    spread = lax.psum(jnp.sum(centre * centre, axis=0), "dp") / row_total
    inv_scale = lax.rsqrt(spread + epsilon)
    normal = centre * inv_scale
    return (normal, inv_scale, normal * gain_vec + bias_vec)


def norm_backward(grad_out, normal, inv_scale, gain_vec, row_total):
    bias_sum, gain_sum = lax.psum(
        (jnp.sum(grad_out, axis=0), jnp.sum(grad_out * normal, axis=0)), "dp"
    )
    grad_in = inv_scale * gain_vec * (grad_out - (bias_sum + normal * gain_sum) / row_total)
    return (grad_in, gain_sum, bias_sum)


def make_settle(totals, is_valid):

    def settle(position, term):
        if totals is None:
            return is_valid * term
        return totals[position] + is_valid * term

    return settle


def forward(source, row_mask, weights, row_total):
    w_in, w_squeeze, w_near, w_far, w_mid, w_out, gain_mid, bias_mid, gain_out, bias_out = weights
    first_act = product(source, w_in)
    normal_one, scale_one, pre_one = norm_forward(
        first_act, gain_mid[0].astype(jnp.float32), bias_mid[0].astype(jnp.float32), row_total
    )
    hidden = jax.nn.silu(pre_one)
    differences = difference(hidden, row_mask).astype(jnp.bfloat16)
    squeezed = product(differences, w_squeeze).astype(jnp.bfloat16)
    logits = product(patches(squeezed, 1), w_near) + product(patches(squeezed, 2), w_far)
    opening = jax.nn.sigmoid(logits)
    mixed_act = (hidden * (0.5 + opening)).astype(jnp.bfloat16)
    second_act = product(patches(mixed_act, 1), w_mid)
    normal_two, scale_two, pre_two = norm_forward(
        second_act, gain_mid[1].astype(jnp.float32), bias_mid[1].astype(jnp.float32), row_total
    )
    middle = jax.nn.silu(pre_two).astype(jnp.bfloat16)
    third_act = product(middle, w_out)
    normal_three, scale_three, pre_three = norm_forward(
        third_act, gain_out.astype(jnp.float32), bias_out.astype(jnp.float32), row_total
    )
    summed = source.astype(jnp.float32) + pre_three
    stored = (
        source,
        normal_one,
        scale_one,
        differences,
        squeezed,
        opening,
        mixed_act,
        normal_two,
        scale_two,
        middle,
        normal_three,
        scale_three,
        summed,
    )
    return (jax.nn.silu(summed).astype(jnp.bfloat16), stored)


def backward(stored, grad_result, row_mask, weights, row_total, settle):
    w_in, w_squeeze, w_near, w_far, w_mid, w_out, gain_mid, bias_mid, gain_out, bias_out = weights
    (
        source,
        normal_one,
        scale_one,
        differences,
        squeezed,
        opening,
        mixed_act,
        normal_two,
        scale_two,
        middle,
        normal_three,
        scale_three,
        summed,
    ) = stored
    gain_one = gain_mid[0].astype(jnp.float32)
    bias_one = bias_mid[0].astype(jnp.float32)
    gain_two = gain_mid[1].astype(jnp.float32)
    bias_two = bias_mid[1].astype(jnp.float32)
    gain_three = gain_out.astype(jnp.float32)
    grad_summed = grad_result.astype(jnp.float32) * silu_slope(summed)
    grad_third, gain_grad_three, bias_grad_three = norm_backward(
        grad_summed, normal_three, scale_three, gain_three, row_total
    )
    grad_third = grad_third.astype(jnp.bfloat16)
    grad_w_out = settle(5, across(middle, grad_third))
    grad_middle = against(grad_third, w_out)
    grad_pre_two = grad_middle * silu_slope(normal_two * gain_two + bias_two)
    grad_second, gain_grad_two, bias_grad_two = norm_backward(
        grad_pre_two, normal_two, scale_two, gain_two, row_total
    )
    grad_second = grad_second.astype(jnp.bfloat16)
    grad_w_mid = settle(4, across(patches(mixed_act, 1), grad_second))
    grad_mixed = unpatch(against(grad_second, w_mid), 1, mixed_act.shape[1])
    pre_one = normal_one * gain_one + bias_one
    hidden = jax.nn.silu(pre_one)
    grad_logits = (grad_mixed * hidden * opening * (1.0 - opening)).astype(jnp.bfloat16)
    grad_w_near = settle(2, across(patches(squeezed, 1), grad_logits))
    grad_w_far = settle(3, across(patches(squeezed, 2), grad_logits))
    width_red = squeezed.shape[1]
    grad_squeezed = (
        unpatch(against(grad_logits, w_near), 1, width_red)
        + unpatch(against(grad_logits, w_far), 2, width_red)
    ).astype(jnp.bfloat16)
    grad_w_squeeze = settle(1, across(differences, grad_squeezed))
    grad_hidden = grad_mixed * (0.5 + opening) + difference_back(
        against(grad_squeezed, w_squeeze), row_mask
    )
    grad_pre_one = grad_hidden * silu_slope(pre_one)
    grad_first, gain_grad_one, bias_grad_one = norm_backward(
        grad_pre_one, normal_one, scale_one, gain_one, row_total
    )
    grad_first = grad_first.astype(jnp.bfloat16)
    grad_w_in = settle(0, across(source, grad_first))
    grad_inputs = (against(grad_first, w_in) + grad_summed).astype(jnp.bfloat16)
    weight_terms = (grad_w_in, grad_w_squeeze, grad_w_near, grad_w_far, grad_w_mid, grad_w_out)
    norm_terms = (
        jnp.stack([gain_grad_one, gain_grad_two]),
        jnp.stack([bias_grad_one, bias_grad_two]),
        gain_grad_three,
        bias_grad_three,
    )
    return (grad_inputs, weight_terms, norm_terms)


def local(
    clips_in,
    cotangent,
    segment_ids,
    w_in,
    w_squeeze,
    w_near,
    w_far,
    w_mid,
    w_out,
    gain_mid,
    bias_mid,
    gain_out,
    bias_out,
):
    lowered = (
        w_in[0].astype(jnp.bfloat16),
        w_squeeze[0].astype(jnp.bfloat16),
        w_near[0].astype(jnp.bfloat16),
        w_far[0].astype(jnp.bfloat16),
        w_mid[0].astype(jnp.bfloat16),
        w_out[0].astype(jnp.bfloat16),
        gain_mid[0].astype(jnp.bfloat16),
        bias_mid[0].astype(jnp.bfloat16),
        gain_out[0].astype(jnp.bfloat16),
        bias_out[0].astype(jnp.bfloat16),
    )
    weights = (
        lax.all_gather(lowered[0], "dp", axis=1, tiled=True),
        lax.all_gather(lowered[1], "dp", axis=0, tiled=True),
        lax.all_gather(lowered[2], "dp", axis=1, tiled=True),
        lax.all_gather(lowered[3], "dp", axis=1, tiled=True),
        lax.all_gather(lowered[4], "dp", axis=1, tiled=True),
        lax.all_gather(lowered[5], "dp", axis=1, tiled=True),
        lax.all_gather(lowered[6], "dp", axis=1, tiled=True),
        lax.all_gather(lowered[7], "dp", axis=1, tiled=True),
        lax.all_gather(lowered[8], "dp", axis=0, tiled=True),
        lax.all_gather(lowered[9], "dp", axis=0, tiled=True),
    )
    section_first = lax.axis_index("pipe") == 0
    row_total = float(clips_in.shape[1] * lax.axis_size("dp"))
    boundaries = boundary(segment_ids)
    batches = clips_in.shape[0]
    steps_total = batches + 1
    outputs_fwd, retained = ([], [])
    incoming = jnp.zeros_like(clips_in[0])
    for step_index in range(steps_total):
        if step_index > 0:
            incoming = passed_along(outputs_fwd[-1], "pipe", 1)
        early_batch = min(step_index, batches - 1)
        late_batch = max(step_index - 1, 0)
        source = jnp.where(section_first, clips_in[early_batch], incoming)
        row_mask = jnp.where(section_first, boundaries[early_batch], boundaries[late_batch])
        result, stored = forward(source, row_mask, weights, row_total)
        outputs_fwd.append(result)
        retained.append(stored)
    norm_sums = None
    sums_full = None
    grads_back = []
    for step_index in range(steps_total):
        if step_index > 0:
            incoming = passed_along(grads_back[-1], "pipe", -1)
        else:
            incoming = jnp.zeros_like(clips_in[0])
        early_batch = max(step_index - 1, 0)
        late_batch = min(step_index, batches - 1)
        grad_result = jnp.where(section_first, incoming, cotangent[late_batch])
        row_mask = jnp.where(section_first, boundaries[early_batch], boundaries[late_batch])
        stored = jax.tree.map(
            lambda early_leaf, late_leaf: jnp.where(section_first, early_leaf, late_leaf),
            retained[max(step_index - 1, 0)],
            retained[min(step_index + 1, steps_total - 1)],
        )
        is_valid = jnp.where(section_first, step_index >= 1, step_index <= batches - 1).astype(
            jnp.float32
        )
        settle = make_settle(sums_full, is_valid)
        grad_inputs, weight_terms, norm_terms = backward(
            stored, grad_result, row_mask, weights, row_total, settle
        )
        grads_back.append(grad_inputs)
        norm_terms = tuple((is_valid * norm_term for norm_term in norm_terms))
        norm_sums = (
            norm_terms if norm_sums is None else jax.tree.map(jnp.add, norm_sums, norm_terms)
        )
        sums_full = weight_terms
    shares = (
        lax.psum_scatter(sums_full[0], "dp", scatter_dimension=1, tiled=True),
        lax.psum_scatter(sums_full[1], "dp", scatter_dimension=0, tiled=True),
        lax.psum_scatter(sums_full[2], "dp", scatter_dimension=1, tiled=True),
        lax.psum_scatter(sums_full[3], "dp", scatter_dimension=1, tiled=True),
        lax.psum_scatter(sums_full[4], "dp", scatter_dimension=1, tiled=True),
        lax.psum_scatter(sums_full[5], "dp", scatter_dimension=1, tiled=True),
    )
    dp_index = lax.axis_index("dp")
    mid_piece = gain_mid.shape[2]
    out_piece = gain_out.shape[1]
    grad_gain_mid = lax.dynamic_slice_in_dim(norm_sums[0], dp_index * mid_piece, mid_piece, 1)[None]
    grad_bias_mid = lax.dynamic_slice_in_dim(norm_sums[1], dp_index * mid_piece, mid_piece, 1)[None]
    grad_gain_out = lax.dynamic_slice_in_dim(norm_sums[2], dp_index * out_piece, out_piece, 0)[None]
    grad_bias_out = lax.dynamic_slice_in_dim(norm_sums[3], dp_index * out_piece, out_piece, 0)[None]
    activations = jnp.stack(
        [
            jnp.where(section_first, outputs_fwd[micro_batch], outputs_fwd[micro_batch + 1])
            for micro_batch in range(batches)
        ]
    )[None]
    input_grads = jnp.stack(
        [
            jnp.where(section_first, grads_back[micro_batch + 1], grads_back[micro_batch])
            for micro_batch in range(batches)
        ]
    )[None]
    return (
        activations,
        input_grads,
        shares[0][None],
        shares[1][None],
        shares[2][None],
        shares[3][None],
        shares[4][None],
        shares[5][None],
        grad_gain_mid,
        grad_bias_mid,
        grad_gain_out,
        grad_bias_out,
    )


def solution(mesh):
    return jax.shard_map(
        local,
        mesh=mesh,
        in_specs=(
            P(None, "dp", None),
            P(None, "dp", None),
            P(None, "dp", None),
            P("pipe", None, "dp"),
            P("pipe", "dp", None),
            P("pipe", None, "dp"),
            P("pipe", None, "dp"),
            P("pipe", None, "dp"),
            P("pipe", None, "dp"),
            P("pipe", None, "dp"),
            P("pipe", None, "dp"),
            P("pipe", "dp"),
            P("pipe", "dp"),
        ),
        out_specs=(
            P("pipe", None, "dp", None),
            P("pipe", None, "dp", None),
            P("pipe", None, "dp"),
            P("pipe", "dp", None),
            P("pipe", None, "dp"),
            P("pipe", None, "dp"),
            P("pipe", None, "dp"),
            P("pipe", None, "dp"),
            P("pipe", None, "dp"),
            P("pipe", None, "dp"),
            P("pipe", "dp"),
            P("pipe", "dp"),
        ),
        check_vma=False,
    )
```

profile of v0, /device:TPU:0, one launch (start us, length us, event | category | flops | bytes accessed | tf_op | source)
XLA Modules:
  0.0 3147.0 jit_solution(11911988340369102083)
XLA Ops:
  16.6 44.3 %all-gather.1 = bf16[1,2,512]{1,0,2:T(2,128)(2,1)S(1)} all-gather(bf16[1,2,32]{1,0,2:T(2,128)(2,1)S(1)} %copy.53), channel_id=3, replica_groups=mesh['pipe'=2,'dp'=16] {'dp'}, dimensions={2}, use_global_device_ids=true | all-gather | bytes 2176 | tf_op jit(solution)/shard_map/all_gather | solution.py:253
  63.8 37.0 %all-gather.2 = bf16[1,2,512]{1,0,2:T(2,128)(2,1)S(1)} all-gather(bf16[1,2,32]{1,0,2:T(2,128)(2,1)S(1)} %copy.54), channel_id=4, replica_groups=mesh['pipe'=2,'dp'=16] {'dp'}, dimensions={2}, use_global_device_ids=true | all-gather | bytes 2176 | tf_op jit(solution)/shard_map/all_gather | solution.py:254
  104.2 38.5 %all-gather.3 = bf16[1,512,128]{2,1,0:T(8,128)(2,1)S(1)} all-gather(bf16[1,32,128]{2,1,0:T(8,128)(2,1)S(1)} %convert_element_type.366), channel_id=5, replica_groups=mesh['pipe'=2,'dp'=16] {'dp'}, dimensions={1}, use_global_device_ids=true | all-gather | bytes 139264 | tf_op jit(solution)/shard_map/all_gather | solution.py:248
  142.8 35.3 %all-gather.8 = bf16[1,2048]{1,0:T(2,128)(2,1)S(1)} all-gather(bf16[1,128]{1,0:T(2,128)(2,1)S(1)} %convert_element_type.379), channel_id=10, replica_groups=mesh['pipe'=2,'dp'=16] {'dp'}, dimensions={1}, use_global_device_ids=true | all-gather | bytes 4352 | tf_op jit(solution)/shard_map/all_gather | solution.py:255
  178.1 37.3 %all-gather.9 = bf16[1,2048]{1,0:T(2,128)(2,1)S(1)} all-gather(bf16[1,128]{1,0:T(2,128)(2,1)S(1)} %convert_element_type.382), channel_id=11, replica_groups=mesh['pipe'=2,'dp'=16] {'dp'}, dimensions={1}, use_global_device_ids=true | all-gather | bytes 4352 | tf_op jit(solution)/shard_map/all_gather | solution.py:256
  218.6 37.5 %psum.336 = f32[512]{0:T(512)S(1)} all-reduce(f32[512]{0:T(512)S(1)} %get-tuple-element.453), channel_id=1, replica_groups=mesh['pipe'=2,'dp'=16] {'dp'}, use_global_device_ids=true, to_apply=%region_1.2 | all-reduce | flops 512 | bytes 4096 | tf_op jit(solution)/shard_map/psum | solution.py:86
  256.2 38.9 %psum.337 = f32[512]{0:T(512)S(1)} all-reduce(f32[512]{0:T(512)S(1)} %multiply_reduce_fusion.23), channel_id=1, replica_groups=mesh['pipe'=2,'dp'=16] {'dp'}, use_global_device_ids=true, to_apply=%region_3.4 | all-reduce | flops 512 | bytes 4096 | tf_op jit(solution)/shard_map/psum | solution.py:88
  340.7 37.2 %psum.338 = f32[512]{0:T(512)S(1)} all-reduce(f32[512]{0:T(512)S(1)} %get-tuple-element.457), channel_id=1, replica_groups=mesh['pipe'=2,'dp'=16] {'dp'}, use_global_device_ids=true, to_apply=%region_5.6 | all-reduce | flops 512 | bytes 4096 | tf_op jit(solution)/shard_map/psum | solution.py:86
  378.0 37.9 %psum.339 = f32[512]{0:T(512)S(1)} all-reduce(f32[512]{0:T(512)S(1)} %multiply_reduce_fusion.22), channel_id=1, replica_groups=mesh['pipe'=2,'dp'=16] {'dp'}, use_global_device_ids=true, to_apply=%region_7.8 | all-reduce | flops 512 | bytes 4096 | tf_op jit(solution)/shard_map/psum | solution.py:88
  419.0 37.7 %psum.340 = f32[2048]{0:T(1024)S(1)} all-reduce(f32[2048]{0:T(1024)S(1)} %get-tuple-element.459), channel_id=1, replica_groups=mesh['pipe'=2,'dp'=16] {'dp'}, use_global_device_ids=true, to_apply=%region_9.10 | all-reduce | flops 2048 | bytes 16384 | tf_op jit(solution)/shard_map/psum | solution.py:86
  457.1 38.4 %psum.341 = f32[2048]{0:T(1024)S(1)} all-reduce(f32[2048]{0:T(1024)S(1)} %multiply_reduce_fusion.7), channel_id=1, replica_groups=mesh['pipe'=2,'dp'=16] {'dp'}, use_global_device_ids=true, to_apply=%region_11.12 | all-reduce | flops 2048 | bytes 16384 | tf_op jit(solution)/shard_map/psum | solution.py:88
  506.6 37.2 %psum.342 = f32[512]{0:T(512)S(1)} all-reduce(f32[512]{0:T(512)S(1)} %get-tuple-element.461), channel_id=1, replica_groups=mesh['pipe'=2,'dp'=16] {'dp'}, use_global_device_ids=true, to_apply=%region_13.14 | all-reduce | flops 512 | bytes 4096 | tf_op jit(solution)/shard_map/psum | solution.py:86
  545.0 37.9 %psum.343 = f32[512]{0:T(512)S(1)} all-reduce(f32[512]{0:T(512)S(1)} %multiply_reduce_fusion.21), channel_id=1, replica_groups=mesh['pipe'=2,'dp'=16] {'dp'}, use_global_device_ids=true, to_apply=%region_15.16 | all-reduce | flops 512 | bytes 4096 | tf_op jit(solution)/shard_map/psum | solution.py:88
  701.0 37.2 %psum.344 = f32[512]{0:T(512)S(1)} all-reduce(f32[512]{0:T(512)S(1)} %get-tuple-element.464), channel_id=1, replica_groups=mesh['pipe'=2,'dp'=16] {'dp'}, use_global_device_ids=true, to_apply=%region_17.18 | all-reduce | flops 512 | bytes 4096 | tf_op jit(solution)/shard_map/psum | solution.py:86
  739.4 37.9 %psum.345 = f32[512]{0:T(512)S(1)} all-reduce(f32[512]{0:T(512)S(1)} %multiply_reduce_fusion.20), channel_id=1, replica_groups=mesh['pipe'=2,'dp'=16] {'dp'}, use_global_device_ids=true, to_apply=%region_19.20 | all-reduce | flops 512 | bytes 4096 | tf_op jit(solution)/shard_map/psum | solution.py:88
  782.6 37.7 %psum.346 = f32[2048]{0:T(1024)S(1)} all-reduce(f32[2048]{0:T(1024)S(1)} %get-tuple-element.466), channel_id=1, replica_groups=mesh['pipe'=2,'dp'=16] {'dp'}, use_global_device_ids=true, to_apply=%region_21.22 | all-reduce | flops 2048 | bytes 16384 | tf_op jit(solution)/shard_map/psum | solution.py:86
  822.6 38.8 %psum.347 = f32[2048]{0:T(1024)S(1)} all-reduce(f32[2048]{0:T(1024)S(1)} %multiply_reduce_fusion.6), channel_id=1, replica_groups=mesh['pipe'=2,'dp'=16] {'dp'}, use_global_device_ids=true, to_apply=%region_23.24 | all-reduce | flops 2048 | bytes 16384 | tf_op jit(solution)/shard_map/psum | solution.py:88
  876.1 37.2 %psum.348 = f32[512]{0:T(512)S(1)} all-reduce(f32[512]{0:T(512)S(1)} %get-tuple-element.468), channel_id=1, replica_groups=mesh['pipe'=2,'dp'=16] {'dp'}, use_global_device_ids=true, to_apply=%region_25.26 | all-reduce | flops 512 | bytes 4096 | tf_op jit(solution)/shard_map/psum | solution.py:86
  914.6 37.9 %psum.349 = f32[512]{0:T(512)S(1)} all-reduce(f32[512]{0:T(512)S(1)} %multiply_reduce_fusion.19), channel_id=1, replica_groups=mesh['pipe'=2,'dp'=16] {'dp'}, use_global_device_ids=true, to_apply=%region_27.28 | all-reduce | flops 512 | bytes 4096 | tf_op jit(solution)/shard_map/psum | solution.py:88
  1070.7 37.2 %psum.350 = f32[512]{0:T(512)S(1)} all-reduce(f32[512]{0:T(512)S(1)} %get-tuple-element.471), channel_id=1, replica_groups=mesh['pipe'=2,'dp'=16] {'dp'}, use_global_device_ids=true, to_apply=%region_29.30 | all-reduce | flops 512 | bytes 4096 | tf_op jit(solution)/shard_map/psum | solution.py:86
  1109.1 38.2 %psum.351 = f32[512]{0:T(512)S(1)} all-reduce(f32[512]{0:T(512)S(1)} %multiply_reduce_fusion.18), channel_id=1, replica_groups=mesh['pipe'=2,'dp'=16] {'dp'}, use_global_device_ids=true, to_apply=%region_31.32 | all-reduce | flops 512 | bytes 4096 | tf_op jit(solution)/shard_map/psum | solution.py:88
  1152.0 37.7 %psum.352 = f32[2048]{0:T(1024)S(1)} all-reduce(f32[2048]{0:T(1024)S(1)} %get-tuple-element.473), channel_id=1, replica_groups=mesh['pipe'=2,'dp'=16] {'dp'}, use_global_device_ids=true, to_apply=%region_33.34 | all-reduce | flops 2048 | bytes 16384 | tf_op jit(solution)/shard_map/psum | solution.py:86
  1191.9 38.5 %psum.353 = f32[2048]{0:T(1024)S(1)} all-reduce(f32[2048]{0:T(1024)S(1)} %multiply_reduce_fusion.5), channel_id=1, replica_groups=mesh['pipe'=2,'dp'=16] {'dp'}, use_global_device_ids=true, to_apply=%region_35.36 | all-reduce | flops 2048 | bytes 16384 | tf_op jit(solution)/shard_map/psum | solution.py:88
  1253.3 72.2 %all-reduce.152 = (f32[512]{0:T(512)}, f32[2048]{0:T(1024)}, f32[2048]{0:T(1024)}) all-reduce(f32[512]{0:T(512)S(1)} %get-tuple-element.475, f32[2048]{0:T(1024)} %get-tuple-element.19, f32[2048]{0:T(1024)S(1)} %get-tuple-element.18), channel_id=1, replica_groups=mesh['pipe'=2,'dp'=16] {'dp'}, use_global_device_ids=true, to_apply=%region_37.38 | all-reduce | flops 4608 | bytes 36864 | tf_op jit(solution)/shard_map/psum | solution.py:86
  1335.0 37.8 %all-reduce.151 = (f32[512]{0:T(512)}, f32[512]{0:T(512)S(1)}, f32[512]{0:T(512)}) all-reduce(f32[512]{0:T(512)} %multiply_reduce_fusion.17, f32[512]{0:T(512)} %get-tuple-element.35, f32[512]{0:T(512)} %get-tuple-element.34), channel_id=1, replica_groups=mesh['pipe'=2,'dp'=16] {'dp'}, use_global_device_ids=true, to_apply=%region_39.40 | all-reduce | flops 1536 | bytes 12288 | tf_op jit(solution)/shard_map/psum | solution.py:88
  1383.7 8.9 reshape.640
  1543.0 39.6 %all-reduce.150 = (f32[512]{0:T(512)}, f32[512]{0:T(512)S(1)}, f32[512]{0:T(512)S(1)}) all-reduce(f32[512]{0:T(512)S(1)} %get-tuple-element.479, f32[512]{0:T(512)S(1)} %get-tuple-element.33, f32[512]{0:T(512)S(1)} %get-tuple-element.32), channel_id=1, replica_groups=mesh['pipe'=2,'dp'=16] {'dp'}, use_global_device_ids=true, to_apply=%region_41.42 | all-reduce | flops 1536 | bytes 12288 | tf_op jit(solution)/shard_map/psum | solution.py:86
  1738.3 71.9 %all-reduce.149 = (f32[512]{0:T(512)S(1)}, f32[2048]{0:T(1024)S(1)}, f32[2048]{0:T(1024)S(1)}) all-reduce(f32[512]{0:T(512)S(1)} %multiply_reduce_fusion.16, f32[2048]{0:T(1024)S(1)} %get-tuple-element.17, f32[2048]{0:T(1024)S(1)} %get-tuple-element.16), channel_id=1, replica_groups=mesh['pipe'=2,'dp'=16] {'dp'}, use_global_device_ids=true, to_apply=%region_43.44 | all-reduce | flops 4608 | bytes 36864 | tf_op jit(solution)/shard_map/psum | solution.py:88
  1821.5 72.1 %all-reduce.148 = (f32[2048]{0:T(1024)S(1)}, f32[512]{0:T(512)S(1)}, f32[512]{0:T(512)S(1)}) all-reduce(f32[2048]{0:T(1024)S(1)} %get-tuple-element.481, f32[512]{0:T(512)S(1)} %get-tuple-element.31, f32[512]{0:T(512)S(1)} %get-tuple-element.30), channel_id=1, replica_groups=mesh['pipe'=2,'dp'=16] {'dp'}, use_global_device_ids=true, to_apply=%region_45.46 | all-reduce | flops 3072 | bytes 24576 | tf_op jit(solution)/shard_map/psum | solution.py:86
  1896.0 7.4 fusion.4
  1903.5 8.9 reshape.645
  1947.9 71.7 %all-reduce.147 = (f32[2048]{0:T(1024)S(1)}, f32[512]{0:T(512)S(1)}, f32[512]{0:T(512)S(1)}) all-reduce(f32[2048]{0:T(1024)S(1)} %multiply_reduce_fusion.4, f32[512]{0:T(512)S(1)} %get-tuple-element.29, f32[512]{0:T(512)S(1)} %get-tuple-element.28), channel_id=1, replica_groups=mesh['pipe'=2,'dp'=16] {'dp'}, use_global_device_ids=true, to_apply=%region_47.48 | all-reduce | flops 3072 | bytes 24576 | tf_op jit(solution)/shard_map/psum | solution.py:88
  2042.5 71.7 %all-reduce.146 = (f32[2048]{0:T(1024)S(1)}, f32[2048]{0:T(1024)S(1)}) all-reduce(f32[2048]{0:T(1024)S(1)} %get-tuple-element.15, f32[2048]{0:T(1024)S(1)} %get-tuple-element.14), channel_id=1, replica_groups=mesh['pipe'=2,'dp'=16] {'dp'}, use_global_device_ids=true, to_apply=%region_75.76 | all-reduce | flops 4096 | bytes 32768 | tf_op jit(solution)/shard_map/psum | solution.py:95
  2119.9 36.6 %all-reduce.145 = (f32[512]{0:T(512)S(1)}, f32[512]{0:T(512)S(1)}) all-reduce(f32[512]{0:T(512)S(1)} %get-tuple-element.27, f32[512]{0:T(512)S(1)} %get-tuple-element.26), channel_id=1, replica_groups=mesh['pipe'=2,'dp'=16] {'dp'}, use_global_device_ids=true, to_apply=%region_79.80 | all-reduce | flops 1024 | bytes 8192 | tf_op jit(solution)/shard_map/psum | solution.py:95
  2157.5 7.4 fusion.2
  2164.8 9.0 reshape.650
  2201.2 38.5 %all-reduce.144 = (f32[512]{0:T(512)S(1)}, f32[512]{0:T(512)S(1)}) all-reduce(f32[512]{0:T(512)S(1)} %get-tuple-element.25, f32[512]{0:T(512)S(1)} %get-tuple-element.24), channel_id=1, replica_groups=mesh['pipe'=2,'dp'=16] {'dp'}, use_global_device_ids=true, to_apply=%region_83.84 | all-reduce | flops 1024 | bytes 8192 | tf_op jit(solution)/shard_map/psum | solution.py:95
  2273.3 71.7 %all-reduce.143 = (f32[2048]{0:T(1024)S(1)}, f32[2048]{0:T(1024)S(1)}) all-reduce(f32[2048]{0:T(1024)S(1)} %get-tuple-element.13, f32[2048]{0:T(1024)S(1)} %get-tuple-element.12), channel_id=1, replica_groups=mesh['pipe'=2,'dp'=16] {'dp'}, use_global_device_ids=true, to_apply=%region_87.88 | all-reduce | flops 4096 | bytes 32768 | tf_op jit(solution)/shard_map/psum | solution.py:95
  2350.7 37.0 %all-reduce.142 = (f32[512]{0:T(512)S(1)}, f32[512]{0:T(512)S(1)}) all-reduce(f32[512]{0:T(512)S(1)} %get-tuple-element.23, f32[512]{0:T(512)S(1)} %get-tuple-element.22), channel_id=1, replica_groups=mesh['pipe'=2,'dp'=16] {'dp'}, use_global_device_ids=true, to_apply=%region_91.92 | all-reduce | flops 1024 | bytes 8192 | tf_op jit(solution)/shard_map/psum | solution.py:95
  2395.9 8.9 reshape.655
  2513.3 38.7 %all-reduce.141 = (f32[512]{0:T(512)S(1)}, f32[512]{0:T(512)S(1)}) all-reduce(f32[512]{0:T(512)S(1)} %get-tuple-element.21, f32[512]{0:T(512)S(1)} %get-tuple-element.20), channel_id=1, replica_groups=mesh['pipe'=2,'dp'=16] {'dp'}, use_global_device_ids=true, to_apply=%region_95.96 | all-reduce | flops 1024 | bytes 8192 | tf_op jit(solution)/shard_map/psum | solution.py:95
  2554.3 8.3 multiply_add_fusion.2
  2640.6 7.4 fusion.228
  2653.1 11.2 multiply_add_fusion
  2682.3 84.9 %reduce-scatter.11.cloned.1.call-done = f32[1152,32]{0,1:T(8,128)} async-done(((f32[1152,512]{0,1:T(8,128)}), f32[1152,32]{0,1:T(8,128)}) %reduce-scatter.11.cloned.1.call-update) | async-done | bytes 147472 | tf_op jit(solution)/shard_map/reduce_scatter | solution.py:308
  2767.2 97.3 %reduce-scatter.17.cloned.1.call-done = f32[512,128]{1,0:T(8,128)} async-done(((f32[512,2048]{1,0:T(8,128)}), f32[512,128]{1,0:T(8,128)}) %reduce-scatter.17.cloned.1.call-update) | async-done | bytes 262160 | tf_op jit(solution)/shard_map/reduce_scatter | solution.py:311
  2864.5 97.6 %reduce-scatter.7.cloned.1.call-done = f32[2048,32]{0,1:T(8,128)} async-done(((f32[2048,512]{0,1:T(8,128)}), f32[2048,32]{0,1:T(8,128)}) %reduce-scatter.7.cloned.1.call-update) | async-done | bytes 262160 | tf_op jit(solution)/shard_map/reduce_scatter | solution.py:306
  2962.1 178.2 %reduce-scatter.15.cloned.1.call-done = f32[4608,32]{0,1:T(8,128)} async-done(((f32[4608,512]{0,1:T(8,128)}), f32[4608,32]{0,1:T(8,128)}) %reduce-scatter.15.cloned.1.call-update) | async-done | bytes 589840 | tf_op jit(solution)/shard_map/reduce_scatter | solution.py:310
  (1431 shorter events, 1060.1 us)
Async XLA Ops:
  7.2 96.4 %copy-start.338 = (s32[3,1,8]{2,1,0:T(1,128)S(1)}, s32[3,1,8]{2,1,0:T(1,128)}, u32[]{:S(2)}) copy-start(s32[3,1,8]{2,1,0:T(1,128)} %param.15) | copy-start | bytes 292
  7.2 97.0 %copy-start.284 = (f32[1,32,128]{2,1,0:T(8,128)S(1)}, f32[1,32,128]{2,1,0:T(8,128)}, u32[]{:S(2)}) copy-start(f32[1,32,128]{2,1,0:T(8,128)} %param.17) | copy-start | bytes 49156
  7.2 135.5 %copy-start.352 = (f32[1,128]{1,0:T(1,128)S(1)}, f32[1,128]{1,0:T(1,128)}, u32[]{:S(2)}) copy-start(f32[1,128]{1,0:T(1,128)} %param.24) | copy-start | bytes 1540
  7.2 170.8 %copy-start.353 = (f32[1,128]{1,0:T(1,128)S(1)}, f32[1,128]{1,0:T(1,128)}, u32[]{:S(2)}) copy-start(f32[1,128]{1,0:T(1,128)} %param.25) | copy-start | bytes 1540
  7.2 208.2 %all-gather.16.cloned.1.call-start = ((), (), s32[]{:S(2)}) async-start(), calls=%async_computation.12 | async-start | bytes 2228224 | tf_op jit(solution)/shard_map/all_gather | solution.py:247
  8.9 300.1 %all-gather.18.cloned.1.call-start = ((), (), s32[]{:S(2)}) async-start(), calls=%async_computation.13 | async-start | bytes 1253376 | tf_op jit(solution)/shard_map/all_gather | solution.py:249
  10.5 300.8 %all-gather.20.cloned.1.call-start = ((), (), s32[]{:S(2)}) async-start(), calls=%async_computation.14 | async-start | bytes 1253376 | tf_op jit(solution)/shard_map/all_gather | solution.py:250
  12.2 322.9 %all-gather.22.cloned.1.call-start = ((), (), s32[]{:S(2)}) async-start(), calls=%async_computation.15 | async-start | bytes 5013504 | tf_op jit(solution)/shard_map/all_gather | solution.py:251
  14.1 401.9 %all-gather.24.cloned.1.call-start = ((), (), s32[]{:S(2)}) async-start(), calls=%async_computation.16 | async-start | bytes 2228224 | tf_op jit(solution)/shard_map/all_gather | solution.py:252
  15.8 2666.6 %reduce-scatter.9.cloned.1.call-start = ((), (), s32[]{:S(2)}) async-start(), calls=%async_computation.7 | async-start | bytes 278528 | tf_op jit(solution)/shard_map/reduce_scatter | solution.py:307
  63.7 1083.6 %copy-start.248 = (f32[512]{0:T(512)}, f32[512]{0:T(512)S(1)}, u32[]{:S(2)}) copy-start(f32[512]{0:T(512)S(1)} %get-tuple-element.36) | copy-start | bytes 6148
  103.6 674.3 %copy-start.295 = (f32[512]{0:T(512)}, f32[512]{0:T(512)S(1)}, u32[]{:S(2)}) copy-start(f32[512]{0:T(512)S(1)} %get-tuple-element.38) | copy-start | bytes 6148
  103.6 2079.2 %copy-start.213 = (f32[512]{0:T(512)}, f32[512]{0:T(512)S(1)}, u32[]{:S(2)}) copy-start(f32[512]{0:T(512)S(1)} %get-tuple-element.39) | copy-start | bytes 6148
  104.2 192.3 %copy-start.339 = (f32[8]{0:T(128)}, f32[8]{0:T(128)S(1)}, u32[]{:S(2)}) copy-start(f32[8]{0:T(128)S(1)} %get-tuple-element.452) | copy-start | bytes 100
  178.0 2088.5 %copy-start.139 = (f32[1,2048]{1,0:T(1,128)}, f32[1,2048]{1,0:T(1,128)S(1)}, u32[]{:S(2)}) copy-start(f32[1,2048]{1,0:T(1,128)S(1)} %convert_element_type.447) | copy-start | bytes 24580
  215.4 2051.2 %copy-start.179 = (f32[1,2048]{1,0:T(1,128)}, f32[1,2048]{1,0:T(1,128)S(1)}, u32[]{:S(2)}) copy-start(f32[1,2048]{1,0:T(1,128)S(1)} %convert_element_type.448) | copy-start | bytes 24580
  218.6 78.2 %copy-start.50 = (f32[392,512]{1,0:T(8,128)}, f32[392,512]{1,0:T(8,128)S(1)}, u32[]{:S(2)}) copy-start(f32[392,512]{1,0:T(8,128)S(1)} %get-tuple-element.454) | copy-start | bytes 2408452
  256.1 1145.4 %copy-start.221 = (f32[512]{0:T(512)}, f32[512]{0:T(512)S(1)}, u32[]{:S(2)}) copy-start(f32[512]{0:T(512)S(1)} %broadcast_multiply_fusion.11) | copy-start | bytes 6148
  416.0 361.4 %copy-start.253 = (f32[512]{0:T(512)}, f32[512]{0:T(512)S(1)}, u32[]{:S(2)}) copy-start(f32[512]{0:T(512)S(1)} %psum.339) | copy-start | bytes 6148
  498.4 4.6 collective-permute-start
  543.8 857.7 %copy-start.223 = (f32[512]{0:T(512)}, f32[512]{0:T(512)S(1)}, u32[]{:S(2)}) copy-start(f32[512]{0:T(512)S(1)} %broadcast_multiply_fusion.9) | copy-start | bytes 6148
  867.6 4.7 collective-permute-start.1
  876.1 82.1 %copy-start.346 = (f32[8]{0:T(128)S(1)}, f32[8]{0:T(128)}, u32[]{:S(2)}) copy-start(f32[8]{0:T(128)} %get-tuple-element.448) | copy-start | bytes 100
  1064.3 83.0 %copy-start.296 = (f32[512]{0:T(512)S(1)}, f32[512]{0:T(512)}, u32[]{:S(2)}) copy-start(f32[512]{0:T(512)} %copy-done.295) | copy-start | bytes 6148
  1231.0 583.6 %copy-start.216 = (f32[2048]{0:T(1024)}, f32[2048]{0:T(1024)S(1)}, u32[]{:S(2)}) copy-start(f32[2048]{0:T(1024)S(1)} %get-tuple-element.434) | copy-start | bytes 24580
  1237.4 11.9 collective-permute-start.2
  1326.2 856.6 %copy-start.228 = (f32[512]{0:T(512)}, f32[512]{0:T(512)S(1)}, u32[]{:S(2)}) copy-start(f32[512]{0:T(512)S(1)} %broadcast_multiply_fusion.5) | copy-start | bytes 6148
  1589.1 143.2 %collective-permute-start.3 = (bf16[392,2048]{1,0:T(8,128)(2,1)}, bf16[392,2048]{1,0:T(8,128)(2,1)}, u32[]{:S(2)}, u32[]{:S(2)}) collective-permute-start(bf16[392,2048]{1,0:T(8,128)(2,1)} %add_convert_fusion.3), channel_id=1, source_target_pairs={{16,0},{17,1},{18,2},{19,3},{20,4},{21,5},{22,6},{23,7},{24,8},{25... | collective-permute-start | bytes 4816904 | tf_op jit(solution)/shard_map/ppermute | solution.py:16
  1732.1 86.1 %copy-start.241 = (f32[512]{0:T(512)}, f32[512]{0:T(512)S(1)}, u32[]{:S(2)}) copy-start(f32[512]{0:T(512)S(1)} %broadcast_multiply_fusion.4) | copy-start | bytes 6148
  1732.2 78.0 %copy-start.254 = (f32[512]{0:T(512)S(1)}, f32[512]{0:T(512)}, u32[]{:S(2)}) copy-start(f32[512]{0:T(512)} %copy-done.253) | copy-start | bytes 6148
  1732.2 78.0 %copy-start.269 = (f32[512]{0:T(512)S(1)}, f32[512]{0:T(512)}, u32[]{:S(2)}) copy-start(f32[512]{0:T(512)} %copy-done.268) | copy-start | bytes 6148
  1732.2 78.0 %copy-start.271 = (f32[512]{0:T(512)S(1)}, f32[512]{0:T(512)}, u32[]{:S(2)}) copy-start(f32[512]{0:T(512)} %copy-done.270) | copy-start | bytes 6148
  1732.2 78.6 %copy-start.236 = (f32[512]{0:T(512)S(1)}, f32[512]{0:T(512)}, u32[]{:S(2)}) copy-start(f32[512]{0:T(512)} %copy-done.235) | copy-start | bytes 6148
  1732.2 78.6 %copy-start.257 = (f32[512]{0:T(512)S(1)}, f32[512]{0:T(512)}, u32[]{:S(2)}) copy-start(f32[512]{0:T(512)} %copy-done.255) | copy-start | bytes 6148
  1732.2 78.6 %copy-start.261 = (f32[512]{0:T(512)S(1)}, f32[512]{0:T(512)}, u32[]{:S(2)}) copy-start(f32[512]{0:T(512)} %copy-done.259) | copy-start | bytes 6148
  1732.3 78.6 %copy-start.266 = (f32[512]{0:T(512)S(1)}, f32[512]{0:T(512)}, u32[]{:S(2)}) copy-start(f32[512]{0:T(512)} %copy-done.265) | copy-start | bytes 6148
  1732.3 78.6 %copy-start.278 = (f32[512]{0:T(512)S(1)}, f32[512]{0:T(512)}, u32[]{:S(2)}) copy-start(f32[512]{0:T(512)} %copy-done.276) | copy-start | bytes 6148
  1732.3 78.6 %copy-start.282 = (f32[512]{0:T(512)S(1)}, f32[512]{0:T(512)}, u32[]{:S(2)}) copy-start(f32[512]{0:T(512)} %copy-done.280) | copy-start | bytes 6148
  1819.4 128.2 %copy-start.5 = (f32[392,2048]{1,0:T(8,128)}, f32[392,2048]{1,0:T(8,128)S(1)}, u32[]{:S(2)}) copy-start(f32[392,2048]{1,0:T(8,128)S(1)} %get-tuple-element.482) | copy-start | bytes 9633796
  1944.2 400.8 %copy-start.211 = (f32[2048]{0:T(1024)}, f32[2048]{0:T(1024)S(1)}, u32[]{:S(2)}) copy-start(f32[2048]{0:T(1024)S(1)} %broadcast_multiply_fusion) | copy-start | bytes 24580
  2027.1 10.0 collective-permute-start.4
  2245.4 21.2 collective-permute-start.5
  2266.6 78.4 %copy-start.247 = (f32[2048]{0:T(1024)S(1)}, f32[2048]{0:T(1024)}, u32[]{:S(2)}) copy-start(f32[2048]{0:T(1024)} %get-tuple-element.429) | copy-start | bytes 24580
  2430.7 251.6 %reduce-scatter.13.cloned.1.call-start = ((), (), s32[]{:S(2)}) async-start(), calls=%async_computation.9 | async-start | bytes 2506752 | tf_op jit(solution)/shard_map/reduce_scatter | solution.py:309
  2436.1 331.1 %reduce-scatter.11.cloned.1.call-start = ((), (), s32[]{:S(2)}) async-start(), calls=%async_computation.8 | async-start | bytes 2506752 | tf_op jit(solution)/shard_map/reduce_scatter | solution.py:308
  2482.4 382.1 %reduce-scatter.17.cloned.1.call-start = ((), (), s32[]{:S(2)}) async-start(), calls=%async_computation.11 | async-start | bytes 4456448 | tf_op jit(solution)/shard_map/reduce_scatter | solution.py:311
  2493.2 468.9 %reduce-scatter.7.cloned.1.call-start = ((), (), s32[]{:S(2)}) async-start(), calls=%async_computation.6 | async-start | bytes 4456448 | tf_op jit(solution)/shard_map/reduce_scatter | solution.py:306
  2562.7 577.6 %reduce-scatter.15.cloned.1.call-start = ((), (), s32[]{:S(2)}) async-start(), calls=%async_computation.10 | async-start | bytes 10027008 | tf_op jit(solution)/shard_map/reduce_scatter | solution.py:310
  (323 other events, 3301.7 us)
Sparse Core Ops, SparseCore 0:
  11.4 66.1 all-gather.15
  80.9 54.9 all-gather.17
  139.3 55.3 all-gather.19
  197.3 80.3 all-gather.21
  280.9 62.8 all-gather.23
  2430.9 73.9 reduce-scatter.8
  2511.1 123.8 reduce-scatter.12
  2640.4 126.7 reduce-scatter.10
  2770.2 94.2 reduce-scatter.16
  2867.3 94.7 reduce-scatter.6
  2969.3 170.9 reduce-scatter.14
where the time goes:
time: 3170 us; the launch traced here: 3150 us
  blocking collectives  1530 us (48%)
  local copies, waits for them, and re-layouts  719 us (23%)
  waiting for transfers between devices  461 us (15%)
  matrix products  222 us (7%)
  other arithmetic  181 us (6%)
    psum x12, blocking collectives, norm_forward(): spread = lax.psum(jnp.sum(centre * centre, axis=0), 'dp') / row_total  526 us
    psum x12, blocking collectives, norm_forward(): centre_mean = lax.psum(jnp.sum(values, axis=0), 'dp') / row_total  520 us
    psum x6, blocking collectives, norm_backward(): lax.psum((jnp.sum(grad_out, axis=0), jnp.sum(grad_out * normal, axis=0)),...  294 us
    concatenate x216, local copies, waits for them, and re-layouts, patches(): jnp.concatenate(pieces, axis=-1).reshape(field_in.shape[0], 9 * channels)  273 us
    unnamed x889, local copies, waits for them, and re-layouts  235 us
    reduce_scatter x1, waiting for transfers between devices, local(): lax.psum_scatter(sums_full[4], 'dp', scatter_dimension=1, tiled=True)  178 us
    reduce_scatter x1, waiting for transfers between devices, local(): lax.psum_scatter(sums_full[0], 'dp', scatter_dimension=1, tiled=True)  97.6 us
    reduce_scatter x1, waiting for transfers between devices, local(): lax.psum_scatter(sums_full[5], 'dp', scatter_dimension=1, tiled=True)  97.3 us
  transfers between devices with their start and end apart: 17, of which 6 were waited for; matrix products, arithmetic and copies ran while one was open for 14% of the time, Pallas kernels for 0%

commit v1 on v0

v1 whole, which is shorter than its diff:
```python
import functools

import jax
import jax.numpy as jnp
from jax import lax
from jax.experimental import pallas as pl
from jax.experimental.pallas import tpu as pltpu
from jax.sharding import PartitionSpec as P

SEG = 8
SIDE = 7
PIX = SIDE * SIDE
HALF = SEG // 2
STRIDE = HALF + 1
LINE = 16
ROWS = PIX * LINE
EPS = 1e-05
F32 = jnp.float32
BF16 = jnp.bfloat16
VMEM_BYTES = 40 * 1024 * 1024


def dot(left, right):
    return lax.dot_general(left, right, (((1,), (0,)), ((), ())), preferred_element_type=F32)


def dot_nt(left, right):
    return lax.dot_general(left, right, (((1,), (1,)), ((), ())), preferred_element_type=F32)


def dot_tn(left, right):
    return lax.dot_general(left, right, (((0,), (0,)), ((), ())), preferred_element_type=F32)


def sigmoid(v):
    return 0.5 * jnp.tanh(0.5 * v) + 0.5


def line_of(width):
    return lax.broadcasted_iota(jnp.int32, (LINE, width), 0)


def own_lines(width):
    r = line_of(width)
    inside = (r < 4) | ((r >= 5) & (r < 9)) | ((r >= 10) & (r < 14))
    return inside.astype(F32)


def per_line(values):
    width = values.shape[1]
    r = line_of(width)
    return jnp.where(r < 5, values[0:1], jnp.where(r < 10, values[1:2], values[2:3]))


def per_batch(lines, count):
    r = line_of(lines.shape[1])
    pieces = []
    for b in range(3):
        keep = (r >= 5 * b) & (r < 5 * b + count)
        pieces.append(jnp.sum(jnp.where(keep, lines, 0.0), axis=0, keepdims=True))
    return pieces


def flat(v):
    return v.reshape(-1, v.shape[-1])


def chunks(body, init=0):
    return lax.fori_loop(0, SIDE, body, init)


def ref_stats(a_ref, first, width):
    lanes = pl.ds(first, width)

    def add(i, s):
        return s + jnp.sum(a_ref[pl.ds(i * SIDE, SIDE), :, lanes], axis=0)

    sums = per_batch(chunks(add, jnp.zeros((LINE, width), F32)), HALF)
    means = [s / (HALF * PIX) for s in sums]
    mean_lines = per_line(jnp.concatenate(means, axis=0))

    def add_sq(i, s):
        d = a_ref[pl.ds(i * SIDE, SIDE), :, lanes] - mean_lines[None]
        return s + jnp.sum(d * d, axis=0)

    sq = per_batch(chunks(add_sq, jnp.zeros((LINE, width), F32)), HALF)
    zero = jnp.zeros((1, width), F32)
    return jnp.concatenate(means + [zero] + sq + [zero], axis=0)


def pack(st):
    cut = st.shape[1] * 3 // 4
    rest = [
        jnp.concatenate([st[r : r + 1, cut:] for r in rows], axis=1)
        for rows in ((0, 1, 2), (4, 5, 6))
    ]
    return jnp.concatenate([st[0:3, :cut], st[4:7, :cut]] + rest, axis=0)


def unpack(p, group):
    third = p.shape[1] // 3
    row = p[6 + group : 7 + group]
    rest = jnp.concatenate([row[:, third * k : third * (k + 1)] for k in range(3)], axis=0)
    return jnp.concatenate([p[3 * group : 3 * group + 3], rest], axis=1)


def spread(st, out_ref):
    packed = pack(st)
    for k in range(out_ref.shape[0]):
        out_ref[k] = packed


def merge_norm(gs, rows_each):
    count = sum(g.shape[0] for g in gs)
    total = sum(jnp.sum(g[...], axis=0) for g in gs)
    mean = total / count
    off = 0.0
    for g in gs:
        d = g[...] - mean[None]
        off = off + jnp.sum(d * d, axis=0)
    var = (unpack(total, 1) + rows_each * unpack(off, 0)) / (rows_each * count)
    return eight(unpack(mean, 0), var)


def merge_sums(gs, rows_each):
    total = sum(jnp.sum(g[...], axis=0) for g in gs)
    return eight(unpack(total, 0), unpack(total, 1))


def eight(first, second):
    zero = jnp.zeros((1, first.shape[1]), F32)
    return jnp.concatenate([first, zero, second, zero], axis=0)


def merge_wide(merge, place, g, g_other, out_ref):
    core = place[0]
    rows_each = float(2 * HALF * PIX)
    half = out_ref.shape[1] // 2
    out_ref[:, pl.ds(pl.multiple_of(core * half, half), half)] = merge([g], rows_each)
    out_ref[:, pl.ds(pl.multiple_of((1 - core) * half, half), half)] = merge([g_other], rows_each)


def split_wide(place, st, keep_ref, send_ref):
    core = place[0]
    half = st.shape[1] // 2
    keep_ref[...] = st[:, pl.ds(pl.multiple_of(core * half, half), half)]
    send_ref[...] = st[:, pl.ds(pl.multiple_of((1 - core) * half, half), half)]


def pair_kernel(norm, keep, recv, out_ref):
    a, b = keep[...], recv[...]
    if norm:
        d = a[0:3] - b[0:3]
        mean = 0.5 * (a[0:3] + b[0:3])
        st = eight(mean, a[4:7] + b[4:7] + (HALF * PIX / 2.0) * d * d)
    else:
        st = a + b
    spread(st, out_ref)


OWN_ROWS = float(HALF * PIX)


def gains_kernel(wt, place, *rest):
    refs, (gb_ref, gbo_ref, buf, sems) = rest[: wt.count], rest[wt.count :]
    wait_all(wt.copies("gain", place, refs, buf, sems))
    i = lax.broadcasted_iota(jnp.int32, (128, 512), 0)
    j = lax.broadcasted_iota(jnp.int32, (128, 512), 1)
    mid = jnp.zeros((16, 512), F32)
    for k in range(16):
        g = buf[k // 4, k // 2 % 2, k % 2, 0]
        hot = jnp.where((i < 32) & (j == 32 * k + i), 1.0, 0.0).astype(BF16)
        mid = mid + dot(g, hot)
        gbo_ref[:, 128 * k : 128 * k + 128] = g[4:12].astype(F32)
    gb_ref[...] = mid[0:8]


def wait_all(copies):
    for c in copies:
        c.wait()


class Weights:
    def __init__(self, kind, segments):
        self.kind, self.segments = kind, segments

    @property
    def count(self):
        return 2 if self.kind == "whole" else 8

    def sems(self, name):
        return len(self.segments[name]) * (2 if self.kind == "whole" else 4)

    def copies(self, name, place, refs, buf, sems):
        core, y, x = place[0], place[1], place[2]
        found = []
        for part, start, at, width in self.segments[name]:
            for side in range(2):
                c = core if side == 0 else 1 - core
                if self.kind == "whole":
                    pairs = [(refs[side], (ALL, ALL, ALL))]
                elif part == "P":
                    pairs = [(refs[4 * side], (ALL, y, ALL)), (refs[4 * side + 1], (ALL, 1 - y, ALL))]
                else:
                    pairs = [(refs[4 * side + 2], (ALL, ALL, x)), (refs[4 * side + 3], (ALL, ALL, 1 - x))]
                for ref, where in pairs:
                    source = ref.at[..., pl.ds(start, width)]
                    if isinstance(at, tuple):
                        target = buf.at[where + (c, at[0])]
                    else:
                        target = buf.at[where + (c, ALL, pl.ds(at, width))]
                    found.append(pltpu.make_async_copy(source, target, sems.at[len(found)]))
        for copy in found:
            copy.start()
        return found


ALL = slice(None)


def first_matmul(x_ref, w_buf, a_ref, stb_ref):
    for j in range(2):
        w = w_buf[2 * j : 2 * j + 2].reshape(256, 2048)
        a_ref[:, :, pl.ds(256 * j, 256)] = dot_nt(flat(x_ref[...]), w).reshape(PIX, LINE, 256)
    spread(ref_stats(a_ref, 0, 512), stb_ref)


def permute_kernel(core_ref, x_ref, out_ref):
    core = core_ref[0]
    i = lax.broadcasted_iota(jnp.int32, (ROWS, SEG * PIX), 0)
    j = lax.broadcasted_iota(jnp.int32, (ROWS, SEG * PIX), 1)
    pixel, line = i >> 4, i & 15
    hots = []
    for b in range(3):
        t = line - 5 * b
        target = (HALF * core + t) * PIX + pixel
        hots.append(jnp.where((t >= 0) & (t < HALF) & (j == target), 1.0, 0.0).astype(BF16))
    for k in range(4):
        lanes = pl.ds(512 * k, 512)
        total = dot(hots[0], x_ref[0, :, lanes])
        total = total + dot(hots[1], x_ref[1, :, lanes])
        total = total + dot(hots[2], x_ref[2, :, lanes])
        out_ref[:, :, lanes] = total.astype(BF16).reshape(PIX, LINE, 512)


def restore_kernel(place, early_ref, late_ref, early_in, late_in, out_ref, buf, sems):
    core = place[0]

    def fetch(mine, received):
        copies = [
            pltpu.make_async_copy(mine, buf.at[core], sems.at[0]),
            pltpu.make_async_copy(received, buf.at[1 - core], sems.at[1]),
        ]
        for c in copies:
            c.start()
        for c in copies:
            c.wait()

    @pl.when(core == 0)
    def _():
        fetch(early_ref, early_in)

    @pl.when(core == 1)
    def _():
        fetch(late_ref, late_in)

    def hot(first, count, side, b):
        j = lax.broadcasted_iota(jnp.int32, (count, ROWS), 0) + first
        i = lax.broadcasted_iota(jnp.int32, (count, ROWS), 1)
        seg = jnp.zeros_like(j)
        for k in range(1, SEG):
            seg = seg + jnp.where(j >= PIX * k, 1, 0)
        t = seg - HALF * side
        target = (j - PIX * seg) * LINE + 5 * b + t
        return jnp.where((t >= 0) & (t < HALF) & (i == target), 1.0, 0.0).astype(BF16)

    for b in range(3):
        lower, upper = hot(0, 208, 0, b), hot(192, 200, 1, b)
        for k in range(4):
            lanes = pl.ds(512 * k, 512)
            low = dot(lower, flat(buf[0, :, :, lanes])).astype(BF16)
            high = dot(upper, flat(buf[1, :, :, lanes])).astype(BF16)
            out_ref[b, 0:192, lanes] = low[:192]
            out_ref[b, 192:208, lanes] = low[192:] + high[:16]
            out_ref[b, 208:392, lanes] = high[16:]


def first_kernel(wt, place, x_ref, *rest):
    refs, (a_ref, st_ref, w_buf, sems) = rest[: wt.count], rest[wt.count :]
    copies = wt.copies("in", place, refs, w_buf, sems)
    wait_all(copies)
    first_matmul(x_ref, w_buf, a_ref, st_ref)


def tap_ranges(shift):
    return max(0, -shift), min(SIDE, SIDE - shift)


def build_patches(sq, patch):
    patch[...] = jnp.zeros(patch.shape, BF16)
    sq4 = sq.reshape(SIDE, SIDE, LINE, 128)
    for k in (1, 2):
        for tap in range(9):
            dy, dx = k * (tap // 3 - 1), k * (tap % 3 - 1)
            (y0, y1), (x0, x1) = tap_ranges(dy), tap_ranges(dx)
            col = ((k - 1) * 9 + tap) * 128
            patch[y0:y1, x0:x1, :, col : col + 128] = sq4[y0 + dy : y1 + dy, x0 + dx : x1 + dx]


def clear_border(pad):
    zero_row = jnp.zeros((9, LINE, 512), BF16)
    pad[0] = zero_row
    pad[8] = zero_row
    for y in range(1, 8):
        pad[y, 0] = jnp.zeros((LINE, 512), BF16)
        pad[y, 8] = jnp.zeros((LINE, 512), BF16)


def middle_kernel(wt, place, a_in, a_other, g, g_other, gb_ref, msk_ref, *rest):
    refs = rest[: wt.count]
    (
        a_ref, diff_ref, sq_ref, op_ref, mix_ref, second_ref, st_ref, mv_ref,
        sq_buf, nf_buf, mid_buf, hid, patch, sq_sems, nf_sems, mid_sems,
    ) = rest[wt.count :]
    core = place[0]
    sq_copies = wt.copies("sq", place, refs, sq_buf, sq_sems)
    nf_copies = wt.copies("nf", place, refs, nf_buf, nf_sems)
    mid_copies = wt.copies("mid", place, refs, mid_buf, mid_sems)
    clear_border(mix_ref)
    mv_ref[...] = merge_norm([g, g_other], OWN_ROWS)
    r = line_of(512)
    halo = ((r == 4) | (r == 9) | (r == 14)) & (core == 0)
    mean = per_line(mv_ref[0:3])
    scale = lax.rsqrt(per_line(mv_ref[4:7]) + EPS) * gb_ref[0:1]
    shift = gb_ref[1:2]
    m = msk_ref[:, 0:1]

    def hidden_chunk(i, _):
        rows = pl.ds(i * SIDE, SIDE)
        a = jnp.where(halo[None], pltpu.roll(a_other[rows], 4, 1), a_in[rows])
        a_ref[rows] = a
        n1 = (a - mean[None]) * scale[None] + shift[None]
        h = n1 * sigmoid(n1)
        hid[rows] = h
        diff_ref[rows] = (m[None] * (pltpu.roll(h, LINE - 1, 1) - h)).astype(BF16)
        return 0

    chunks(hidden_chunk)
    wait_all(sq_copies)
    sq = dot(flat(diff_ref[...]), sq_buf[...].reshape(512, 128)).astype(BF16)
    sq_ref[...] = sq.reshape(PIX, LINE, 128)
    build_patches(sq, patch)
    wait_all(nf_copies)
    for j in range(2):
        lanes = pl.ds(256 * j, 256)
        w = nf_buf[2 * j : 2 * j + 2].reshape(256, 2304)
        logits = dot_nt(patch[...].reshape(ROWS, 2304), w).reshape(PIX, LINE, 256)
        opening = sigmoid(logits)
        op_ref[:, :, lanes] = opening.astype(BF16)
        mixed = (hid[:, :, lanes] * (0.5 + opening)).astype(BF16)
        mix_ref[1:8, 1:8, :, lanes] = mixed.reshape(SIDE, SIDE, LINE, 256)
    wait_all(mid_copies)

    second_ref[...] = jnp.zeros(second_ref.shape, F32)

    def tap_step(tap, _):
        ty, tx = tap // 3, tap % 3
        v = mix_ref[pl.ds(ty, SIDE), pl.ds(tx, SIDE)].reshape(ROWS, 512)
        w = mid_buf[..., pl.ds(pl.multiple_of(tap * 512, 512), 512)].reshape(512, 512)
        second_ref[...] += dot_nt(v, w).reshape(PIX, LINE, 512)
        return 0

    lax.fori_loop(0, 9, tap_step, 0)
    spread(ref_stats(second_ref, 0, 512), st_ref)


def wide_kernel(wt, place, second, g, g_other, gb_ref, *rest):
    refs = rest[: wt.count]
    mid_ref, third_ref, keep_ref, send_ref, mv_ref, buf, st_ref, sems = rest[wt.count :]
    copies = wt.copies("out", place, refs, buf, sems)
    mv_ref[...] = merge_norm([g, g_other], OWN_ROWS)
    mean = per_line(mv_ref[0:3])
    scale = lax.rsqrt(per_line(mv_ref[4:7]) + EPS) * gb_ref[2:3]
    shift = gb_ref[3:4]

    def chunk(i, _):
        rows = pl.ds(i * SIDE, SIDE)
        n2 = (second[rows] - mean[None]) * scale[None] + shift[None]
        mid_ref[rows] = (n2 * sigmoid(n2)).astype(BF16)
        return 0

    chunks(chunk)
    wait_all(copies)

    def tile(j, _):
        w = buf[j].reshape(512, 512)
        lanes = pl.ds(pl.multiple_of(512 * j, 512), 512)
        third_ref[:, :, lanes] = dot_nt(flat(mid_ref[...]), w).reshape(PIX, LINE, 512)
        st_ref[:, lanes] = ref_stats(third_ref, pl.multiple_of(512 * j, 512), 512)
        return 0

    lax.fori_loop(0, 4, tile, 0)
    split_wide(place, st_ref, keep_ref, send_ref)


def finish(third, x_ref, mv_ref, gb_ref, each):
    own = own_lines(512)

    def tile(j, _):
        lanes = pl.ds(pl.multiple_of(512 * j, 512), 512)
        mean = per_line(mv_ref[0:3, lanes])
        inv = lax.rsqrt(per_line(mv_ref[4:7, lanes]) + EPS)
        gain, bias = gb_ref[0:1, lanes], gb_ref[1:2, lanes]

        def chunk(i, carry):
            rows = pl.ds(i * SIDE, SIDE)
            xhat = (third[rows, :, lanes] - mean[None]) * inv[None]
            z = x_ref[rows, :, lanes].astype(F32) + xhat * gain[None] + bias[None]
            sg = sigmoid(z)
            return each(rows, lanes, xhat, z, sg, own, carry)

        zero = jnp.zeros((LINE, 512), F32)
        s1, s2 = chunks(chunk, (zero, zero))
        each(None, lanes, None, None, None, None, (s1, s2))
        return 0

    lax.fori_loop(0, 4, tile, 0)


def sums_of(dh, dg):
    zero = jnp.zeros((1, dh.shape[1]), F32)
    return jnp.concatenate(per_batch(dh, STRIDE) + [zero] + per_batch(dg, STRIDE) + [zero], axis=0)


def turn_kernel(wt, place, third, x_ref, g, g_other, gb_ref, *rest):
    refs = rest[: wt.count]
    act_ref, xhat_ref, slope_ref, a_ref, st_ref, mv_ref, w_buf, sems = rest[wt.count :]
    copies = wt.copies("in", place, refs, w_buf, sems)
    merge_wide(merge_norm, place, g, g_other, mv_ref)

    def each(rows, lanes, xhat, z, sg, own, carry):
        if rows is None:
            return carry
        act_ref[rows, :, lanes] = (z * sg * own[None]).astype(BF16)
        xhat_ref[rows, :, lanes] = xhat.astype(BF16)
        slope_ref[rows, :, lanes] = (sg * (1.0 + z * (1.0 - sg)) * own[None]).astype(BF16)
        return carry

    finish(third, x_ref, mv_ref, gb_ref, each)
    wait_all(copies)
    first_matmul(act_ref, w_buf, a_ref, st_ref)


def top_kernel(
    place, third, x_ref, g, g_other, gb_ref, dy_ref,
    act_ref, xhat_ref, dz_ref, keep_ref, send_ref, mv_ref, sums_ref,
):
    merge_wide(merge_norm, place, g, g_other, mv_ref)

    def each(rows, lanes, xhat, z, sg, own, carry):
        if rows is None:
            sums_ref[:, lanes] = sums_of(*carry)
            return carry
        act_ref[rows, :, lanes] = (z * sg * own[None]).astype(BF16)
        xhat_ref[rows, :, lanes] = xhat.astype(BF16)
        dz = dy_ref[rows, :, lanes].astype(F32) * (sg * (1.0 + z * (1.0 - sg)) * own[None])
        dz_ref[rows, :, lanes] = dz.astype(BF16)
        return carry[0] + jnp.sum(dz, axis=0), carry[1] + jnp.sum(dz * xhat, axis=0)

    finish(third, x_ref, mv_ref, gb_ref, each)
    split_wide(place, sums_ref, keep_ref, send_ref)


class Shares:
    def __init__(self, kind, parts):
        self.kind, self.parts = kind, parts

    @property
    def count(self):
        return 2 if self.kind == "whole" else 4 * sum(1 for width in self.parts if width)

    def outs(self):
        if self.kind == "whole":
            width = sum(self.parts)
            return [((4, 2, 2, 16, width), BF16)] * 2
        return [((4, 2, 16, width), BF16) for width in self.parts if width for _ in range(4)]

    def store(self, place, refs, first, result, zs=ALL):
        core, y, x = place[0], place[1], place[2]
        width = result.shape[1]
        parts = result.astype(BF16).reshape(-1, 2, 2, 2, 16, width)
        lower, upper = parts[:, :, :, 0], parts[:, :, :, 1]
        sides = [jnp.where(core == 0, lower, upper), jnp.where(core == 0, upper, lower)]
        if self.kind == "whole":
            for ref, v in zip(refs, sides):
                ref[zs, :, :, :, pl.ds(first, width)] = v
            return
        is_p = first < self.parts[0]
        start = first if is_p else first - self.parts[0]
        lanes = pl.ds(start, width)
        refs = refs[:4] if is_p else refs[-4:]
        for k, v in enumerate(sides):
            if is_p:
                two, at = (v[:, 0], v[:, 1]), y
            else:
                two, at = (v[:, :, 0], v[:, :, 1]), x
            refs[2 * k][zs, :, :, lanes] = jnp.where(at == 0, two[0], two[1])
            refs[2 * k + 1][zs, :, :, lanes] = jnp.where(at == 0, two[1], two[0])


def wide_back_kernel(
    rows_total, wt, place, dz, xhat, mv3_ref, g, g_other, gbo_ref, second, mv2_ref, gb_ref, *rest
):
    refs, (dn2_ref, stb_ref, d3, s3_ref, buf, sems) = rest[: wt.count], rest[wt.count :]
    copies = wt.copies("out", place, refs, buf, sems)
    merge_wide(merge_sums, place, g, g_other, s3_ref)
    own = own_lines(512)

    def tile(j, _):
        lanes = pl.ds(pl.multiple_of(512 * j, 512), 512)
        k = lax.rsqrt(per_line(mv3_ref[4:7, lanes]) + EPS) * gbo_ref[0:1, lanes] * own
        dh = per_line(s3_ref[0:3, lanes]) / rows_total
        dg = per_line(s3_ref[4:7, lanes]) / rows_total

        def chunk(i, c):
            rows = pl.ds(i * SIDE, SIDE)
            v = dz[rows, :, lanes].astype(F32) - dh[None] - xhat[rows, :, lanes].astype(F32) * dg[None]
            d3[rows, :, lanes] = (k[None] * v).astype(BF16)
            return c

        return chunks(chunk, 0)

    lax.fori_loop(0, 4, tile, 0)
    wait_all(copies)
    dn2_ref[...] = jnp.zeros(dn2_ref.shape, F32)

    def product(j, _):
        lanes = pl.ds(pl.multiple_of(512 * j, 512), 512)
        w = buf[j].reshape(512, 512)
        dn2_ref[...] += dot(flat(d3[:, :, lanes]), w).reshape(PIX, LINE, 512)
        return 0

    lax.fori_loop(0, 4, product, 0)
    mean = per_line(mv2_ref[0:3])
    inv = lax.rsqrt(per_line(mv2_ref[4:7]) + EPS)
    gain, bias = gb_ref[2:3], gb_ref[3:4]

    def chunk(i, carry):
        rows = pl.ds(i * SIDE, SIDE)
        xh = (second[rows] - mean[None]) * inv[None]
        n2 = xh * gain[None] + bias[None]
        sg = sigmoid(n2)
        dn = dn2_ref[rows] * (sg * (1.0 + n2 * (1.0 - sg)))
        dn2_ref[rows] = dn
        return carry[0] + jnp.sum(dn, axis=0), carry[1] + jnp.sum(dn * xh, axis=0)

    zero = jnp.zeros((LINE, 512), F32)
    spread(sums_of(*chunks(chunk, (zero, zero))), stb_ref)


def wide_grad(sh, place, refs, start, d3, mid):
    for j in range(4):
        v = flat(d3[:, :, pl.ds(512 * j, 512)])
        res = dot_tn(v, flat(mid[...])).reshape(2, 2, 2, 4, 16, 512)
        for g in range(4):
            sh.store(place, refs, start + 512 * g, res[:, :, :, g].reshape(128, 512), slice(j, j + 1))


def middle_grad(sh, place, refs, start, d2, mixp):
    for tap in range(9):
        mixed = mixp[tap // 3 : tap // 3 + SIDE, tap % 3 : tap % 3 + SIDE].reshape(ROWS, 512)
        sh.store(place, refs, start + 512 * tap, dot_tn(flat(d2[...]), mixed))


def branch_grad(sh, place, refs, start, dlog, sq_ref, diff, dsq, patch):
    build_patches(flat(sq_ref[...]), patch)
    for j in range(3):
        pv = patch[:, :, :, pl.ds(768 * j, 768)].reshape(ROWS, 768)
        sh.store(place, refs, start + 128 + 768 * j, dot_tn(flat(dlog[...]), pv))
    sh.store(place, refs, start, dot_tn(flat(diff[...]), flat(dsq[...])))


def wide_grad_kernel(sh, place, d3, mid, *refs):
    wide_grad(sh, place, refs, 0, d3, mid)


def branch_grad_kernel(sh, place, dlog, sq_ref, diff, dsq, *rest):
    branch_grad(sh, place, rest[: sh.count], 0, dlog, sq_ref, diff, dsq, rest[sh.count])


def all_grad_kernel(sh, place, d3, mid, d2, mixp, dlog, sq_ref, diff, dsq, *rest):
    refs = rest[: sh.count]
    branch_grad(sh, place, refs, 0, dlog, sq_ref, diff, dsq, rest[sh.count])
    middle_grad(sh, place, refs, 2432, d2, mixp)
    wide_grad(sh, place, refs, 7040, d3, mid)


def second_back_kernel(rows_total, sh, place, dn2, second, mv2_ref, g, g_other, gb_ref, *rest):
    if sh is not None:
        mixp, refs, (d2, s2_ref) = rest[0], rest[1 : 1 + sh.count], rest[1 + sh.count :]
    else:
        d2, s2_ref = rest
    s2_ref[...] = merge_sums([g, g_other], OWN_ROWS)
    own = own_lines(512)
    mean2 = per_line(mv2_ref[0:3])
    inv2 = lax.rsqrt(per_line(mv2_ref[4:7]) + EPS)
    k2 = inv2 * gb_ref[2:3] * own
    dh2 = per_line(s2_ref[0:3]) / rows_total
    dg2 = per_line(s2_ref[4:7]) / rows_total

    def chunk(i, c):
        rows = pl.ds(i * SIDE, SIDE)
        xh = (second[rows] - mean2[None]) * inv2[None]
        d2[rows] = (k2[None] * (dn2[rows] - dh2[None] - xh * dg2[None])).astype(BF16)
        return c

    chunks(chunk)
    if sh is not None:
        middle_grad(sh, place, refs, 0, d2, mixp)


def middle_back_kernel(wt, place, d2, a_ref, mv1_ref, gb_ref, msk_ref, op_ref, *rest):
    refs = rest[: wt.count]
    (
        dn1_ref, stb_ref, dlog, dsq_ref,
        sq_buf, nf_buf, mid_buf, d2p, dmix, dsq, sq_sems, nf_sems, mid_sems,
    ) = rest[wt.count :]
    mid_copies = wt.copies("mid", place, refs, mid_buf, mid_sems)
    nf_copies = wt.copies("nf", place, refs, nf_buf, nf_sems)
    sq_copies = wt.copies("sq", place, refs, sq_buf, sq_sems)
    clear_border(d2p)
    for y in range(SIDE):
        d2p[y + 1, 1:8] = d2[SIDE * y : SIDE * y + SIDE]
    wait_all(mid_copies)
    dmix[...] = jnp.zeros(dmix.shape, F32)

    def tap_step(tap, _):
        ty, tx = tap // 3, tap % 3
        v = d2p[pl.ds(2 - ty, SIDE), pl.ds(2 - tx, SIDE)].reshape(ROWS, 512)
        w = mid_buf[..., pl.ds(pl.multiple_of(tap * 512, 512), 512)].reshape(512, 512)
        dmix[...] += dot(v, w).reshape(PIX, LINE, 512)
        return 0

    lax.fori_loop(0, 9, tap_step, 0)
    mean1 = per_line(mv1_ref[0:3])
    inv1 = lax.rsqrt(per_line(mv1_ref[4:7]) + EPS)
    gain1, bias1 = gb_ref[0:1], gb_ref[1:2]

    def log_chunk(i, c):
        rows = pl.ds(i * SIDE, SIDE)
        n1 = (a_ref[rows] - mean1[None]) * inv1[None] * gain1[None] + bias1[None]
        h = n1 * sigmoid(n1)
        op = op_ref[rows].astype(F32)
        dlog[rows] = (dmix[rows] * h * op * (1.0 - op)).astype(BF16)
        return c

    chunks(log_chunk)
    wait_all(nf_copies)
    dsq[...] = jnp.zeros(dsq.shape, F32)
    for k in (1, 2):
        for ty in range(3):
            w = nf_buf[..., pl.ds(((k - 1) * 9 + ty * 3) * 128, 384)].reshape(512, 384)
            res = dot(flat(dlog[...]), w).reshape(SIDE, SIDE, LINE, 384)
            for tx in range(3):
                dy, dx = k * (ty - 1), k * (tx - 1)
                (y0, y1), (x0, x1) = tap_ranges(dy), tap_ranges(dx)
                dsq[y0 + dy : y1 + dy, x0 + dx : x1 + dx] += res[
                    y0:y1, x0:x1, :, 128 * tx : 128 * tx + 128
                ]
    dsq_low = dsq[...].astype(BF16).reshape(ROWS, 128)
    dsq_ref[...] = dsq_low.reshape(PIX, LINE, 128)
    wait_all(sq_copies)
    dn1_ref[...] = dot_nt(dsq_low, sq_buf[...].reshape(512, 128)).reshape(PIX, LINE, 512)
    m = msk_ref[:, 0:1]

    def last_chunk(i, carry):
        rows = pl.ds(i * SIDE, SIDE)
        xh = (a_ref[rows] - mean1[None]) * inv1[None]
        n1 = xh * gain1[None] + bias1[None]
        sg = sigmoid(n1)
        e = dn1_ref[rows] * m[None]
        op = op_ref[rows].astype(F32)
        dhid = dmix[rows] * (0.5 + op) - e + pltpu.roll(e, 1, 1)
        dn = dhid * (sg * (1.0 + n1 * (1.0 - sg)))
        dn1_ref[rows] = dn
        return carry[0] + jnp.sum(dn, axis=0), carry[1] + jnp.sum(dn * xh, axis=0)

    zero = jnp.zeros((LINE, 512), F32)
    spread(sums_of(*chunks(last_chunk, (zero, zero))), stb_ref)


def first_d1(rows_total, place, dn1, dn1_other, a_ref, mv1_ref, s1_ref, gb_ref, d1):
    own = own_lines(512)
    r = line_of(512)
    first = ((r == 0) | (r == 5) | (r == 10)) & (place[0] == 1)
    mean = per_line(mv1_ref[0:3])
    inv = lax.rsqrt(per_line(mv1_ref[4:7]) + EPS)
    k = inv * gb_ref[0:1] * own
    dh = per_line(s1_ref[0:3]) / rows_total
    dg = per_line(s1_ref[4:7]) / rows_total

    def chunk(i, c):
        rows = pl.ds(i * SIDE, SIDE)
        xh = (a_ref[rows] - mean[None]) * inv[None]
        dn = dn1[rows] + jnp.where(first[None], pltpu.roll(dn1_other[rows], LINE - 4, 1), 0.0)
        d1[rows] = (k[None] * (dn - dh[None] - xh * dg[None])).astype(BF16)
        return c

    chunks(chunk)


def first_back_kernel(
    rows_total, wt, place, dn1, dn1_other, a_ref, mv1_ref, g, g_other, gb_ref, dz, slope, xhat, *rest
):
    refs, rest = rest[: wt.count], rest[wt.count :]
    dx_ref, d1, s1_ref, dz_ref, keep_ref, send_ref, w_buf, sums_ref, sems = rest
    copies = wt.copies("in", place, refs, w_buf, sems)
    s1_ref[...] = merge_sums([g, g_other], OWN_ROWS)
    first_d1(rows_total, place, dn1, dn1_other, a_ref, mv1_ref, s1_ref, gb_ref, d1)
    wait_all(copies)

    def tile(j, _):
        lanes = pl.ds(pl.multiple_of(512 * j, 512), 512)
        w = w_buf[..., lanes].reshape(512, 512)
        dx = dot(flat(d1[...]), w).reshape(PIX, LINE, 512) + dz[:, :, lanes].astype(F32)
        dx_low = dx.astype(BF16)
        dx_ref[:, :, lanes] = dx_low
        d = dx_low.astype(F32) * slope[:, :, lanes].astype(F32)
        dz_ref[:, :, lanes] = d.astype(BF16)
        sums_ref[:, lanes] = sums_of(
            jnp.sum(d, axis=0), jnp.sum(d * xhat[:, :, lanes].astype(F32), axis=0)
        )
        return 0

    lax.fori_loop(0, 4, tile, 0)
    split_wide(place, sums_ref, keep_ref, send_ref)


def first_grad(sh, place, refs, d1, x_ref):
    for j in range(4):
        x = flat(x_ref[:, :, pl.ds(512 * j, 512)])
        sh.store(place, refs, 512 * j, dot_tn(flat(d1[...]), x))


def first_grad_kernel(sh, place, d1, x_ref, *refs):
    first_grad(sh, place, refs, d1, x_ref)


def last_grad_kernel(
    rows_total, sh, place, dn1, dn1_other, a_ref, mv1_ref, g, g_other, gb_ref, x_ref, *rest
):
    refs, (d1, s1_ref) = rest[: sh.count], rest[sh.count :]
    s1_ref[...] = merge_sums([g, g_other], OWN_ROWS)
    first_d1(rows_total, place, dn1, dn1_other, a_ref, mv1_ref, s1_ref, gb_ref, d1)
    first_grad(sh, place, refs, d1, x_ref)


def last_back_kernel(wt, place, d1, dz, *rest):
    refs, (dx_ref, w_buf, sems) = rest[: wt.count], rest[wt.count :]
    wait_all(wt.copies("in", place, refs, w_buf, sems))

    def tile(j, _):
        lanes = pl.ds(pl.multiple_of(512 * j, 512), 512)
        w = w_buf[..., lanes].reshape(512, 512)
        dx = dot(flat(d1[...]), w).reshape(PIX, LINE, 512) + dz[:, :, lanes].astype(F32)
        dx_ref[:, :, lanes] = dx.astype(BF16)
        return 0

    lax.fori_loop(0, 4, tile, 0)


VM = pl.BlockSpec(memory_space=pltpu.VMEM)
HB = pl.BlockSpec(memory_space=pltpu.HBM)
SM = pl.BlockSpec(memory_space=pltpu.SMEM)


def call(kernel, specs, outs, scratch=(), us=5):
    return pl.pallas_call(
        kernel,
        in_specs=specs,
        out_specs=tuple(VM for _ in outs),
        out_shape=tuple(jax.ShapeDtypeStruct(s, d) for s, d in outs),
        scratch_shapes=list(scratch),
        compiler_params=pltpu.CompilerParams(vmem_limit_bytes=VMEM_BYTES),
        cost_estimate=pl.CostEstimate(flops=us * 10**9, bytes_accessed=us * 3 * 10**6, transcendentals=0),
    )


def pm(width, dtype):
    return ((PIX, LINE, width), dtype)


def wbuf(width):
    return pltpu.VMEM((4, 2, 2, 2, 16, width), BF16)


STAT = ((8, 512), F32)
WIDE_STAT = ((8, 2048), F32)
PAIR = [(0, 1), (1, 0)]


class Links:
    def __init__(self, dp, core):
        self.dp, self.core = dp, core
        self.at = lax.axis_index("dp")

    def bit(self, k):
        return (self.at // k) % 2

    def place(self):
        y, x = (self.bit(2), self.bit(1)) if self.split else (0, 0)
        return jnp.stack([self.core, jnp.int32(y), jnp.int32(x)]).astype(jnp.int32)

    split = True

    def swap(self, v):
        return lax.ppermute(v, "pipe", PAIR)

    def across(self, v, k):
        return lax.ppermute(v, "dp", [(i, i ^ k) for i in range(self.dp)])

    def to_all(self, spread, *meanwhile):
        g = lax.all_to_all(spread, "dp", 0, 0)
        if meanwhile:
            g = after(g, *meanwhile)
        return g, self.swap(g)

    def by_core(self, own, other):
        first = self.core == 0
        return jnp.where(first, own, other), jnp.where(first, other, own)

    def in_order(self, which, own, other, axis):
        pair = jnp.where(which == 0, jnp.stack([own, other], axis), jnp.stack([other, own], axis))
        return pair

    def halves(self, piece):
        two = piece.reshape(2, 16, piece.shape[1])
        keep = lax.dynamic_index_in_dim(two, self.core, 0, keepdims=False)
        recv = self.swap(lax.dynamic_index_in_dim(two, 1 - self.core, 0, keepdims=False))
        return self.by_core(keep, recv)

    def gather_z(self, own):
        v = self.in_order(self.bit(8), own, self.across(own, 8), 0)
        v = self.in_order(self.bit(4), v, self.across(v, 4), 1)
        return v.reshape(4, 16, -1)

    def gather_xy(self, v, cut, *then):
        p, q = v[..., :cut], v[..., cut:]
        p_other, q_other = self.across(p, 1), self.across(q, 2)
        if then:
            p_other, q_other = after((p_other, q_other), *then)
        p = self.in_order(self.bit(1), p, p_other, 1)
        q = self.in_order(self.bit(2), q, q_other, 1)
        mine = (p, self.across(p, 2), q, self.across(q, 1))
        return mine + tuple(self.swap(v) for v in mine)

    def gather_split(self, own, cut):
        return self.gather_xy(self.gather_z(own), cut)

    def gather_whole(self, own):
        return lax.all_gather(own, "dp").reshape(4, 2, 2, 16, -1)

    def gather_blocks(self, gains, inner, rest, wide):
        rows = jnp.concatenate([jnp.pad(v, ((0, 0), (0, 128 - v.shape[1]))) for v in gains], axis=0)
        tail = jnp.pad(rows, ((0, 32 - rows.shape[0]), (0, 0)))
        a = self.halves(jnp.concatenate([inner, tail], axis=1))
        b, c = self.halves(rest), self.halves(self.narrow_rows(wide))
        b0 = self.gather_whole(b[0])
        a0 = self.gather_split(a[0], 1024)
        ca = self.gather_z(after(jnp.concatenate([c[0], a[1]], axis=1), a0))
        block_0 = {
            "A": (Weights("split", SPLIT_A), a0),
        }
        return block_0, (ca, b0, jnp.concatenate([c[1], b[1]], axis=1))

    def gather_middle(self, blocks, then):
        block_0, (ca, b0, bc) = blocks
        b0 = after(b0, then)
        block_0["B"] = (Weights("whole", middle_at(0)), (b0, self.swap(b0)))
        return block_0, (ca, self.gather_whole(after(bc, b0)))

    def gather_next(self, blocks, second):
        block_0, (ca, bc) = blocks
        ca = self.gather_xy(ca, 2048, second)
        block_0["C"] = (Weights("split", SPLIT_C), ca)
        return block_0, (ca, bc)

    def gather_last(self, blocks, third):
        block_0, (ca, bc) = blocks
        bc = after(bc, third)
        bc = (bc, self.swap(bc))
        return block_0, {
            "A": (Weights("split", SPLIT_A1), ca),
            "B": (Weights("whole", middle_at(2048)), bc),
            "C": (Weights("whole", wide_at(0)), bc),
        }

    def gains_of(self, group, place):
        wt, refs = group
        return call(
            functools.partial(gains_kernel, wt), [SM] + [HB] * len(refs), [STAT, WIDE_STAT],
            [wbuf(128), pltpu.SemaphoreType.DMA((wt.sems("gain"),))],
        )(place, *refs)

    def add(self, a, b):
        return (a.astype(F32) + b.astype(F32)).astype(BF16)

    def halve(self, v, axis, k, then=None):
        which = self.bit(k)
        keep = lax.dynamic_index_in_dim(v, which, axis, keepdims=False)
        send = lax.dynamic_index_in_dim(v, 1 - which, axis, keepdims=False)
        moved = self.across(send, k)
        if then is not None:
            moved = after(moved, then)
        return self.add(keep, moved)

    def scatter_split(self, g, then=(None,) * 4):
        done = []
        for own, other, send_own, send_other, k in ((*g[:4], 2), (*g[4:], 1)):
            other = self.add(other, self.swap(send_other))
            moved = self.across(other, k)
            if then[0] is not None:
                moved = after(moved, then[0])
            v = self.add(self.add(own, self.swap(send_own)), moved)
            done.append(self.halve(v, 1, 3 - k, then[1]))
        v = jnp.concatenate(done, axis=-1)
        v = self.halve(v.reshape(2, 2, 16, -1), 1, 4, then[2])
        return self.halve(v, 0, 8, then[3])

    def half_sums(self, keep, send):
        return self.add(keep, self.swap(send)).reshape(16, 16, -1)

    def scatter_whole(self, v):
        return lax.psum_scatter(v, "dp", scatter_dimension=0, tiled=True)[0]

    def to_owner(self, early, late):
        early_other = lax.ppermute(early, "pipe", [(1, 0)])
        late_other = lax.ppermute(late, "pipe", [(0, 1)])
        at_0 = jnp.concatenate([early, early_other], axis=0)
        at_1 = jnp.concatenate([late_other, late], axis=0)
        return jnp.where(self.core == 0, at_0, at_1).astype(F32)

    def wide_rows(self, v):
        return v.reshape(2, 16, 4, -1).transpose(0, 2, 1, 3).reshape(128, -1)

    def narrow_rows(self, v):
        return v.reshape(2, 4, 16, -1).transpose(0, 2, 1, 3).reshape(32, -1)


class AnyLinks(Links):
    split = False

    def gather_blocks(self, gains, inner, rest, wide):
        full = [lax.all_gather(v, "dp", tiled=True) for v in (inner, wide, rest)]
        full[1] = jnp.stack([self.narrow_rows(f) for f in full[1].reshape(16, 128, -1)]).reshape(512, -1)
        own = jnp.concatenate(full, axis=1)
        vectors = [lax.all_gather(v, "dp", axis=1, tiled=True).astype(F32) for v in gains]
        mid = jnp.pad(jnp.concatenate(vectors[:4]), ((0, 4), (0, 0)))
        out = jnp.pad(jnp.concatenate(vectors[4:]), ((0, 6), (0, 0)))
        mids, outs = self.by_core(mid, self.swap(mid)), self.by_core(out, self.swap(out))
        blocks = []
        for s, full in enumerate(self.by_core(own, self.swap(own))):
            parts = full.reshape(16, 2, 16, -1)
            mine = lax.dynamic_index_in_dim(parts, self.core, 1, keepdims=False)
            theirs = lax.dynamic_index_in_dim(parts, 1 - self.core, 1, keepdims=False)
            refs = tuple(v.reshape(4, 2, 2, 16, -1) for v in (mine, theirs))
            groups = (("A", {"in": [("W", 0, 0, 2048)]}), ("B", middle_at(4096)), ("C", wide_at(2048)))
            blocks.append({k: (Weights("whole", v), refs) for k, v in groups})
            blocks[s]["gains"] = (mids[s], outs[s])
        return blocks

    def gather_middle(self, blocks, then):
        return blocks

    def gather_next(self, blocks, second):
        return blocks

    def gather_last(self, blocks, third):
        return blocks

    def gains_of(self, group, place):
        return group

    def scatter_pairs(self, early, late, wide):
        full = []
        for keep, send in (early, late):
            half = self.add(keep, self.swap(send)).reshape(16, 16, -1)
            full.append(jnp.stack(self.by_core(half, self.swap(half)), axis=1))
        total = jnp.where(self.core == 0, full[0], full[1])
        if wide:
            total = jnp.stack([self.wide_rows(v.reshape(32, -1)) for v in total])
        total = total.reshape(-1, total.shape[-1])
        return lax.psum_scatter(total, "dp", scatter_dimension=0, tiled=True).astype(F32)


def after(v, *others):
    return lax.optimization_barrier((v, others))[0]


SPLIT_A = {"in": [("P", 0, 0, 1024), ("Q", 0, 1024, 1024)], "gain": [("Q", 1024, 0, 128)]}
SPLIT_C = {"out": [("P", 512 * g, (g,), 512) for g in range(4)]}
SPLIT_A1 = {"in": [("Q", 0, 0, 2048)], "gain": [("Q", 2048, 0, 128)]}


def middle_at(first):
    return {
        "sq": [("W", first, 0, 128)],
        "nf": [("W", first + 128, 0, 2304)],
        "mid": [("W", first + 2432, 0, 4608)],
    }


def wide_at(first):
    return {"out": [("W", first + 512 * g, (g,), 512) for g in range(4)]}


def local(
    clips_in, cotangent, segment_ids, w_in, w_squeeze, w_near, w_far, w_mid, w_out,
    gain_mid, bias_mid, gain_out, bias_out,
):
    dp = lax.axis_size("dp")
    core = lax.axis_index("pipe")
    links = (Links if dp == 16 else AnyLinks)(dp, core)
    place = links.place()
    rows_total = float(clips_in.shape[1] * dp)

    def low(v):
        return v[0].astype(BF16)

    n = w_in.shape[2]
    gain_rows = [low(gain_mid)[0:1], low(bias_mid)[0:1], low(gain_mid)[1:2], low(bias_mid)[1:2]]
    gathered = links.gather_blocks(
        gain_rows + [low(gain_out)[None], low(bias_out)[None]],
        low(w_in).T,
        jnp.concatenate([low(w_squeeze), low(w_near).T, low(w_far).T, low(w_mid).T], axis=1),
        low(w_out).T,
    )

    def gains_of(s):
        return links.gains_of(gathered[s]["A" if links.split else "gains"], place)

    gains = [gains_of(0)]

    same = (segment_ids[:, 0, 1:] == segment_ids[:, 0, :-1]).astype(F32)
    same = jnp.concatenate([same, jnp.zeros((3, 1), F32)], axis=1)
    mine_seg = lax.dynamic_slice_in_dim(same, core * HALF, HALF, 1)
    msk = jnp.concatenate([mine_seg, jnp.zeros((3, 1), F32)], axis=1).reshape(15)
    msk = jnp.broadcast_to(jnp.concatenate([msk, jnp.zeros((1,), F32)])[:, None], (LINE, 128))

    permute = call(permute_kernel, [SM, VM], [pm(2048, BF16)])
    x0 = permute(place, clips_in)[0]
    dy = permute(place, cotangent)[0]

    dma = pltpu.SemaphoreType.DMA
    wide_buf = pltpu.VMEM((4, 2, 2, 2, 4, 16, 512), BF16)

    stb = ((dp, 8, 384), F32)
    half_stat = ((8, 1024), F32)
    buffers = {"in": wbuf(2048), "sq": wbuf(128), "nf": wbuf(2304), "mid": wbuf(4608), "out": wide_buf}
    groups = {"A": ("in",), "B": ("sq", "nf", "mid"), "C": ("out",)}

    def kernel(body, group, values, outs, scratch, *static):
        wt, refs = group[1]
        names = groups[group[0]]
        return call(
            functools.partial(body, *static, wt),
            [SM] + [VM] * len(values) + [HB] * len(refs),
            outs,
            [buffers[k] for k in names] + scratch + [dma((wt.sems(k),)) for k in names],
        )(place, *values, *refs)

    def group(s, k):
        return k, gathered[s][k]

    def first(s, x):
        return kernel(first_kernel, group(s, "A"), [x], [pm(512, F32), stb], [])

    def middle(s, *values):
        outs = [pm(512, F32), pm(512, BF16), pm(128, BF16), pm(512, BF16),
                ((9, 9, LINE, 512), BF16), pm(512, F32), stb, STAT]
        scratch = [pltpu.VMEM((PIX, LINE, 512), F32), pltpu.VMEM((SIDE, SIDE, LINE, 2304), BF16)]
        return kernel(middle_kernel, group(s, "B"), list(values), outs, scratch)

    def widen(s, *values):
        outs = [pm(512, BF16), pm(2048, F32), half_stat, half_stat, STAT]
        return kernel(wide_kernel, group(s, "C"), list(values), outs, [pltpu.VMEM((8, 2048), F32)])

    def turn(*values):
        outs = [pm(2048, BF16)] * 3 + [pm(512, F32), stb, WIDE_STAT]
        return kernel(turn_kernel, group(1, "A"), list(values), outs, [])

    top = call(
        top_kernel, [SM] + [VM] * 6, [pm(2048, BF16)] * 3 + [half_stat, half_stat, WIDE_STAT],
        [pltpu.VMEM((8, 2048), F32)],
    )

    def pairs(norm, keep, send, *meanwhile):
        recv = links.swap(send)
        v = call(functools.partial(pair_kernel, norm), [VM, VM], [((dp, 8, 768), F32)])(keep, recv)
        return links.to_all(v[0], *meanwhile)

    def wide_back(s, *values):
        outs = [pm(512, F32), stb, pm(2048, BF16), WIDE_STAT]
        return kernel(wide_back_kernel, group(s, "C"), list(values), outs, [], rows_total)

    def second_back(sh, *values):
        outs = [pm(512, BF16), STAT]
        return call(
            functools.partial(second_back_kernel, rows_total, sh), [SM] + [VM] * len(values),
            (sh.outs() if sh else []) + outs,
        )(place, *values)

    def middle_back(s, *values):
        outs = [pm(512, F32), stb, pm(512, BF16), pm(128, BF16)]
        scratch = [pltpu.VMEM((9, 9, LINE, 512), BF16), pltpu.VMEM((PIX, LINE, 512), F32),
                   pltpu.VMEM((SIDE, SIDE, LINE, 128), F32)]
        return kernel(middle_back_kernel, group(s, "B"), list(values), outs, scratch)

    def first_back(*values):
        outs = [pm(2048, BF16), pm(512, BF16), STAT, pm(2048, BF16), half_stat, half_stat]
        scratch = [pltpu.VMEM((8, 2048), F32)]
        return kernel(first_back_kernel, group(1, "A"), list(values), outs, scratch, rows_total)

    def last_grad(sh, *values):
        return call(
            functools.partial(last_grad_kernel, rows_total, sh), [SM] + [VM] * len(values),
            sh.outs() + [pm(512, BF16), STAT],
        )(place, *values)

    def last_back(*values):
        return kernel(last_back_kernel, group(0, "A"), list(values), [pm(2048, BF16)], [])[0]

    def shares_of(kind, *parts):
        return Shares(kind if links.split else "whole", parts)

    def grad(body, sh, values, scratch=()):
        return call(
            functools.partial(body, sh), [SM] + [VM] * len(values), sh.outs(), scratch
        )(place, *values)

    restore = call(
        restore_kernel, [SM, HB, HB, HB, HB], [((3, SEG * PIX, 2048), BF16)],
        [pltpu.VMEM((2, PIX, LINE, 2048), BF16), dma((2,))],
    )
    patch = [pltpu.VMEM((SIDE, SIDE, LINE, 2304), BF16)]

    def crossed(early, late):
        return lax.ppermute(early, "pipe", [(1, 0)]), lax.ppermute(late, "pipe", [(0, 1)])

    kept = []
    x = x0
    a, st = first(0, x)
    for s in range(2):
        gb, gbo = gains[s]
        sums = links.to_all(st, *([dy] if s == 0 else []))
        if s == 0:
            gathered = links.gather_middle(gathered, sums[0])
        a, diff, sq, op, mix, second, st, mv1 = middle(s, a, links.swap(a), *sums, gb, msk)
        if s == 0:
            gathered = links.gather_next(gathered, second)
        mid, third, keep, send, mv2 = widen(s, second, *links.to_all(st), gb)
        stats = pairs(True, keep, send)
        if s == 0:
            if links.split:
                gathered = (gathered[0], {"A": (Weights("split", SPLIT_A1), gathered[1][0])}, gathered[1])
                gains.append(gains_of(1))
            act0, xhat, slope0, a_next, st, mv3 = turn(third, x, *stats, gbo)
            if links.split:
                gathered = links.gather_last((gathered[0], gathered[2]), a_next)
            else:
                gains.append(gains_of(1))
        else:
            act1, xhat, dz, keep, send, mv3 = top(place, third, x, *stats, gbo, dy)
        kept.append((x, a, mv1, diff, sq, op, mix, second, mv2, mid, xhat, mv3))
        if s == 0:
            x, a = act0, a_next

    gb, gbo = gains[1]
    x, a, mv1, diff, sq, op, mix, second, mv2, mid, xhat, mv3 = kept[1]
    activations = restore(place, act0, act1, *crossed(act0, act1))[0]
    dn2, st, d3, s3 = wide_back(
        1, dz, xhat, mv3, *pairs(False, keep, send, activations), gbo, second, mv2, gb
    )
    d2, s2 = second_back(None, dn2, second, mv2, *links.to_all(st), gb)
    dn1, st, dlog, dsq = middle_back(1, d2, a, mv1, gb, msk, op)
    g_rest = grad(
        all_grad_kernel, shares_of("whole", 2432, 4608, 2048), [d3, mid, d2, mix, dlog, sq, diff, dsq], patch
    )
    dx1, d1, s1, dz, keep, send = first_back(
        dn1, links.swap(dn1), a, mv1, *links.to_all(st, *g_rest), gb, dz, slope0, kept[0][10]
    )
    norms_1 = (s1, s2, s3)
    g_in1 = grad(first_grad_kernel, shares_of("split", 2048, 0), [d1, x])
    meanwhile = g_in1
    if links.split:
        late = links.half_sums(*g_rest)
        meanwhile = (late, *g_in1)
        late = links.scatter_whole(late)

    gb, gbo = gains[0]
    x, a, mv1, diff, sq, op, mix, second, mv2, mid, xhat, mv3 = kept[0]
    dn2, st, d3, s3 = wide_back(
        0, dz, xhat, mv3, *pairs(False, keep, send, *meanwhile), gbo, second, mv2, gb
    )
    g_out = grad(wide_grad_kernel, shares_of("split", 0, 2048), [d3, mid])
    *g_mid, d2, s2 = second_back(
        shares_of("split", 2048, 2560), dn2, second, mv2, *links.to_all(st, *g_out), gb, mix
    )
    dn1, st, dlog, dsq = middle_back(0, d2, a, mv1, gb, msk, op)
    g_branch = grad(branch_grad_kernel, shares_of("split", 0, 2432), [dlog, sq, diff, dsq], patch)
    *g_in, d1, s1 = last_grad(
        shares_of("split", 2048, 0), dn1, links.swap(dn1), a, mv1, *links.to_all(st, *g_branch), gb, x
    )
    norms_0 = (s1, s2, s3)
    dx0 = last_back(after(d1, *g_in), dz)
    input_grads = restore(place, dx0, dx1, *crossed(dx0, dx1))[0]

    if links.split:
        pair = links.scatter_split((*g_in1, *g_out), (dn1, d1, None, None))
        in_1, out_0 = pair[:, :2048], pair[:, 2048:]
        mid_0 = links.scatter_split(g_mid, (d1, None, None, None))
        pair = links.scatter_split((*g_in, *g_branch), (d1, None, None, None))
        in_0, branch_0 = pair[:, :2048], pair[:, 2048:]
        f_in = links.to_owner(in_0, in_1)
        f_branch = links.to_owner(branch_0, late[:, :2432])
        f_mid = links.to_owner(mid_0, late[:, 2432:7040])
        f_out = links.wide_rows(links.to_owner(out_0, late[:, 7040:]))
    else:
        rest = [v[..., :2432] for v in g_rest], [v[..., 2432:7040] for v in g_rest], [v[..., 7040:] for v in g_rest]
        f_branch = links.scatter_pairs(g_branch, rest[0], False)
        f_mid = links.scatter_pairs(g_mid, rest[1], False)
        f_out = links.scatter_pairs(g_out, rest[2], True)
        f_in = links.scatter_pairs(g_in, g_in1, False)
    grad_w_in = f_in.T[None]
    grad_w_squeeze = f_branch[:, :128][None]
    grad_w_near = f_branch[:, 128:1280].T[None]
    grad_w_far = f_branch[:, 1280:].T[None]
    grad_w_mid = f_mid.T[None]
    grad_w_out = f_out.T[None]

    s1, s2, s3 = [jnp.where(core == 0, e, l) for e, l in zip(norms_0, norms_1)]
    dp_index = lax.axis_index("dp")
    mid_sums = jnp.stack(
        [jnp.stack([s1[0:3].sum(0), s2[0:3].sum(0)]), jnp.stack([s1[4:7].sum(0), s2[4:7].sum(0)])]
    )
    mid_sums = lax.dynamic_slice_in_dim(mid_sums, dp_index * n, n, 2)
    out_sums = jnp.stack([s3[0:3].sum(0), s3[4:7].sum(0)])
    out_sums = lax.dynamic_slice_in_dim(out_sums, dp_index * 4 * n, 4 * n, 1)
    return (
        activations[None], input_grads[None], grad_w_in, grad_w_squeeze, grad_w_near, grad_w_far,
        grad_w_mid, grad_w_out, mid_sums[1][None], mid_sums[0][None], out_sums[1][None],
        out_sums[0][None],
    )


def solution(mesh):
    split = P("pipe", None, "dp")
    rows = P("pipe", "dp", None)
    vec = P("pipe", "dp")
    clips = P(None, "dp", None)
    weights = (split, rows, split, split, split, split, split, split, vec, vec)
    whole = P("pipe", None, "dp", None)
    return jax.shard_map(
        local,
        mesh=mesh,
        in_specs=(clips, clips, clips) + weights,
        out_specs=(whole, whole) + weights,
        check_vma=False,
    )
```

time: 3170 us -> 735 us (0.23)
  blocking collectives: 1530 us -> 83.4 us
  local copies, waits for them, and re-layouts: 719 us -> 78 us
  waiting for transfers between devices: 461 us -> 210 us
  matrix products: 222 us -> 0 us
  Pallas kernels: 0 us -> 201 us
  other arithmetic: 181 us -> 27.6 us
  starting transfers between devices: 13.1 us -> 109 us
    psum x30 -> x0, blocking collectives: 1340 us -> none  [the longest x12 526 us: norm_forward(): spread = lax.psum(jnp.sum(centre * centre, axis=0), 'dp') / row_total]
    reduce_scatter x6 -> x1, waiting for transfers between devices: 458 us -> 0.01 us  [scatter_whole(): return lax.psum_scatter(v, 'dp', scatter_dimension=0, tiled=True)[0]]
    concatenate x216 -> x2, local copies, waits for them, and re-layouts: 273 us -> 0.04 us  [the longest x1 0.03 us: gather_blocks(): jnp.concatenate([jnp.pad(v, ((0, 0), (0, 128 - v.shape[1]))) for v in gai...]
    dot_general x72 -> x0, matrix products: 222 us -> none  [the longest x24 85.7 us: across(): lax.dot_general(left_side, right_side, (((0,), (0,)), ((), ())), preferre...]
    pallas_call x0 -> x30, Pallas kernels: none -> 201 us  [the longest x12 115 us: kernel(): call(functools.partial(body, *static, wt), [SM] + [VM] * len(values) + [H...]
    all_gather x5 -> x0, blocking collectives: 192 us -> none  [the longest x1 44.3 us: local(): lax.all_gather(lowered[6], 'dp', axis=1, tiled=True)]
    ppermute x6 -> x88, waiting for transfers between devices: 2.58 us -> 181 us  [the longest x30 162 us: across(): return lax.ppermute(v, 'dp', [(i, i ^ k) for i in range(self.dp)])]
    unnamed x889 -> x285, local copies, waits for them, and re-layouts: 235 us -> 66.1 us
  transfers between devices with their start and end apart: 17 -> 97, of which waited for: 6 -> 40; matrix products, arithmetic and copies ran while one was open for 14% -> 5% of each run, Pallas kernels for 0% -> 20%
where the time goes in v1:
time: 735 us; the launch traced here: 725 us
  waiting for transfers between devices  210 us (29%)
  Pallas kernels  201 us (27%)
  starting transfers between devices  109 us (15%)
  blocking collectives  83.4 us (11%)
  local copies, waits for them, and re-layouts  78 us (11%)
  other arithmetic  27.6 us (4%)
  between operations  16.3 us (2%)
    ppermute x30, waiting for transfers between devices, across(): return lax.ppermute(v, 'dp', [(i, i ^ k) for i in range(self.dp)])  162 us
    pallas_call x12, Pallas kernels, kernel(): call(functools.partial(body, *static, wt), [SM] + [VM] * len(values) + [H...  115 us
    all_to_all x6, blocking collectives, to_all(): g = lax.all_to_all(spread, 'dp', 0, 0)  83.4 us
    unnamed x285, local copies, waits for them, and re-layouts  66.1 us
    ppermute x30, starting transfers between devices, across(): return lax.ppermute(v, 'dp', [(i, i ^ k) for i in range(self.dp)])  48 us
    all_to_all x6, starting transfers between devices, to_all(): g = lax.all_to_all(spread, 'dp', 0, 0)  28.9 us
    pallas_call x4, Pallas kernels, grad(): call(functools.partial(body, sh), [SM] + [VM] * len(values), sh.outs(), s...  25.7 us
    all_to_all x6, waiting for transfers between devices, to_all(): g = lax.all_to_all(spread, 'dp', 0, 0)  21.5 us
  transfers between devices with their start and end apart: 97, of which 40 were waited for; matrix products, arithmetic and copies ran while one was open for 5% of the time, Pallas kernels for 20%

profile of v1, /device:TPU:0, one launch (start us, length us, event | category | flops | bytes accessed | tf_op | source)
XLA Modules:
  0.0 724.9 jit_solution(14590892141717446331)
XLA Ops:
  20.5 5.7 shard_map.220.x_ref
  29.6 6.0 collective-permute-done.2
  42.1 5.7 shard_map.222.dy_ref
  50.6 5.7 collective-permute-done.4
  64.3 5.5 all-to-all-start
  71.8 10.5 %all-to-all-done.g = f32[16,8,384]{2,1,0:T(8,128)S(1)} async-done(((f32[16,8,384]{2,1,0:T(8,128)}), f32[16,8,384]{2,1,0:T(8,128)S(1)}, u32[]{:S(2)}, u32[]{:S(2)}) %all-to-all-start) | async-done | bytes 196640 | tf_op jit(solution)/shard_map/all_to_all | solution.py:823
  82.3 7.6 %all-gather.5.cloned.1.call-done = bf16[256,7040]{1,0:T(8,128)(2,1)} async-done(((bf16[16,7040]{1,0:T(8,128)(2,1)}), bf16[256,7040]{1,0:T(8,128)(2,1)}) %all-gather.5.cloned.1.call-update) | async-done | bytes 3604496 | tf_op jit(solution)/shard_map/all_gather | solution.py:861
  101.3 12.5 %collective-permute-done.18 = bf16[2,16,4224]{2,1,0:T(8,128)(2,1)S(1)} collective-permute-done((bf16[2,16,4224]{2,1,0:T(8,128)(2,1)S(1)}, bf16[2,16,4224]{2,1,0:T(8,128)(2,1)S(1)}, u32[]{:S(2)}, u32[]{:S(2)}) %collective-permute-start.18) | collective-permute-done | bytes 270368 | tf_op jit(solution)/shard_map/ppermute | solution.py:820
  120.1 11.8 %shard_map.224 = (f32[49,16,512]{2,1,0:T(8,128)S(1)}, bf16[49,16,512]{2,1,0:T(8,128)(2,1)S(1)}, bf16[49,16,128]{2,1,0:T(8,128)(2,1)S(1)}, bf16[49,16,512]{2,1,0:...) custom-call(s32[3]{0:T(128)S(1)} %pad_add_fusion.core_ref.place, ...), custom_call_target="tpu_custom_call" | custom-call | flops 5000000000 | bytes 15000000 | tf_op jit(solution)/shard_map/pallas_call | solution.py:1065
  138.7 5.2 all-to-all-start.1
  144.0 15.3 %collective-permute-done.22.rest_3_ = bf16[4,2,16,2176]{3,2,1,0:T(8,128)(2,1)S(1)} collective-permute-done((bf16[4,2,16,2176]{3,2,1,0:T(8,128)(2,1)S(1)}, bf16[4,2,16,2176]{3,2,1,0:T(8,128)(2,1)S(1)}, u32[]{:S(2)}, u32[]{:S(2)}) %collective-permute-start.22) | collective-permute-done | bytes 557088 | tf_op jit(solution)/shard_map/ppermute | solution.py:820
  164.5 5.5 shard_map.225
  174.0 15.8 %all_to_all.60.g = f32[16,8,768]{2,1,0:T(8,128)S(1)} all-to-all(f32[16,8,768]{2,1,0:T(8,128)S(1)} %shard_map.226), channel_id=1, replica_groups=mesh['pipe'=2,'dp'=16] {'dp'}, dimensions={0} | all-to-all | bytes 786432 | tf_op jit(solution)/shard_map/all_to_all | solution.py:823
  191.5 13.2 %shard_map.227 = (bf16[49,16,2048]{2,1,0:T(8,128)(2,1)}, bf16[49,16,2048]{2,1,0:T(8,128)(2,1)S(1)}, bf16[49,16,2048]{2,1,0:T(8,128)(2,1)}, f32[49,16,512]{2,1,0:...) custom-call(s32[3]{0:T(128)S(1)} %pad_add_fusion.core_ref.place, f32[49,16,2048]{2,1,0:T(8,128)} %copy-done.68, ...), custom_call_target="tpu_custom_call" | custom-call | flops 5000000000 | bytes 15000000 | tf_op jit(solution)/shard_map/pallas_call | solution.py:1065
  208.6 12.9 %all_to_all.61.g = f32[16,8,384]{2,1,0:T(8,128)S(1)} all-to-all(f32[16,8,384]{2,1,0:T(8,128)S(1)} %get-tuple-element.147), channel_id=1, replica_groups=mesh['pipe'=2,'dp'=16] {'dp'}, dimensions={0} | all-to-all | bytes 393216 | tf_op jit(solution)/shard_map/all_to_all | solution.py:823
  225.7 10.9 %shard_map.229 = (f32[49,16,512]{2,1,0:T(8,128)S(1)}, bf16[49,16,512]{2,1,0:T(8,128)(2,1)S(1)}, bf16[49,16,128]{2,1,0:T(8,128)(2,1)S(1)}, bf16[49,16,512]{2,1,0:...) custom-call(s32[3]{0:T(128)S(1)} %pad_add_fusion.core_ref.place, ...), custom_call_target="tpu_custom_call" | custom-call | flops 5000000000 | bytes 15000000 | tf_op jit(solution)/shard_map/pallas_call | solution.py:1065
  237.8 12.1 %all_to_all.62.g = f32[16,8,384]{2,1,0:T(8,128)S(1)} all-to-all(f32[16,8,384]{2,1,0:T(8,128)S(1)} %get-tuple-element.152), channel_id=1, replica_groups=mesh['pipe'=2,'dp'=16] {'dp'}, dimensions={0} | all-to-all | bytes 393216 | tf_op jit(solution)/shard_map/all_to_all | solution.py:823
  251.3 7.9 %shard_map.230 = (bf16[49,16,512]{2,1,0:T(8,128)(2,1)S(1)}, f32[49,16,2048]{2,1,0:T(8,128)}, f32[8,1024]{1,0:T(8,128)S(1)}, f32[8,1024]{1,0:T(8,128)S(1)}, f32[8,512]{1,0:T(8,128)S(1)}) custom-call(s32[3]{0:T(128)S(1)} %pad_add_fusion.core_ref.place, f32[49,16,512]{2,1,0:T(8,128)S(1)} %get-tuple-element.151.second, f32[16,8,384]{2,1,0:T(8,128)S(1)} %all_to_all.62.g, ...), custom_call_target="tpu_custom_call" | custom-call | flops 5000000000 | bytes 15000000 | tf_op jit(solution)/shard_map/pallas_call | solution.py:1065
  260.7 16.4 %all_to_all.63.g = f32[16,8,768]{2,1,0:T(8,128)S(1)} all-to-all(f32[16,8,768]{2,1,0:T(8,128)S(1)} %shard_map.231), channel_id=1, replica_groups=mesh['pipe'=2,'dp'=16] {'dp'}, dimensions={0} | all-to-all | bytes 786432 | tf_op jit(solution)/shard_map/all_to_all | solution.py:823
  278.8 12.0 %shard_map.232 = (bf16[49,16,2048]{2,1,0:T(8,128)(2,1)}, bf16[49,16,2048]{2,1,0:T(8,128)(2,1)S(1)}, bf16[49,16,2048]{2,1,0:T(8,128)(2,1)S(1)}, f32[8,1024]{1,0:T...) custom-call(s32[3]{0:T(128)S(1)} %pad_add_fusion.core_ref.place, f32[49,16,2048]{2,1,0:T(8,128)} %get-tuple-element.153.third, ...), custom_call_target="tpu_custom_call" | custom-call | flops 5000000000 | bytes 15000000 | tf_op jit(solution)/shard_map/pallas_call | solution.py:1173
  292.6 6.1 collective-permute-start.36
  307.3 11.1 %shard_map.233 = bf16[3,392,2048]{2,1,0:T(8,128)(2,1)} custom-call(s32[3]{0:T(128)S(1)} %pad_add_fusion.core_ref.place, bf16[49,16,2048]{2,1,0:T(8,128)(2,1)} %get-tuple-element.145.x_ref.early_ref, bf16[49,16,2048]{2,1,0:T(8,128)(2,1)} %get-tuple-element.157.late_ref, bf16[49,16,2048]{2,1,0:T(8,128)(2,1)} %collective-permute-done.35.early_in, ...), custom_call_target="tpu_custom_call" | custom-call | flops 5000000000 | bytes 15000000 | tf_op jit(solution)/shard_map/pallas_call | solution.py:1180
  325.7 6.4 shard_map.235
  332.1 13.9 %all_to_all.64.g = f32[16,8,384]{2,1,0:T(8,128)S(1)} all-to-all(f32[16,8,384]{2,1,0:T(8,128)S(1)} %get-tuple-element.166), channel_id=1, replica_groups=mesh['pipe'=2,'dp'=16] {'dp'}, dimensions={0} | all-to-all | bytes 393216 | tf_op jit(solution)/shard_map/all_to_all | solution.py:823
  349.2 14.7 %shard_map.237 = (f32[49,16,512]{2,1,0:T(8,128)}, f32[16,8,384]{2,1,0:T(8,128)S(1)}, bf16[49,16,512]{2,1,0:T(8,128)(2,1)S(1)}, bf16[49,16,128]{2,1,0:T(8,128)(2,1)S(1)}) custom-call(s32[3]{0:T(128)S(1)} %pad_add_fusion.core_ref.place, bf16[49,16,512]{2,1,0:T(8,128)(2,1)S(1)} %get-tuple-element.167.d2, f32[49,16,512]{2,1,0:T(8,128)S(1)} %copy-done.14, ...), custom_call_target="tpu_custom_call" | custom-call | flops 5000000000 | bytes 15000000 | tf_op jit(solution)/shard_map/pallas_call | solution.py:1065
  365.0 13.0 %shard_map.238 = (bf16[4,2,2,16,9088]{4,3,2,1,0:T(8,128)(2,1)S(1)}, bf16[4,2,2,16,9088]{4,3,2,1,0:T(8,128)(2,1)}) custom-call(s32[3]{0:T(128)S(1)} %pad_add_fusion.core_ref.place, bf16[49,16,2048]{2,1,0:T(8,128)(2,1)S(1)} %get-tuple-element.173.d3, bf16[49,16,512]{2,1,0:T(8,128)(2,1)S(1)} %copy-done.93, bf16[49,16,512]{2,1,0:T(8,128)(2,1)S(1)} %get-tuple-element.167.d2, ...), custom_call_target="tpu_custom_call" | custom-call | flops 5000000000 | bytes 15000000 | tf_op jit(solution)/shard_map/pallas_call | solution.py:1137
  380.8 12.3 %all_to_all.65.g = f32[16,8,384]{2,1,0:T(8,128)S(1)} all-to-all(f32[16,8,384]{2,1,0:T(8,128)S(1)} %get-tuple-element.172), channel_id=1, replica_groups=mesh['pipe'=2,'dp'=16] {'dp'}, dimensions={0} | all-to-all | bytes 393216 | tf_op jit(solution)/shard_map/all_to_all | solution.py:823
  396.1 12.7 %shard_map.239 = (bf16[49,16,2048]{2,1,0:T(8,128)(2,1)}, bf16[49,16,512]{2,1,0:T(8,128)(2,1)S(1)}, f32[8,512]{1,0:T(8,128)S(1)}, bf16[49,16,2048]{2,1,0:T(8,128)...) custom-call(s32[3]{0:T(128)S(1)} %pad_add_fusion.core_ref.place, f32[49,16,512]{2,1,0:T(8,128)} %get-tuple-element.171.dn1, ...), custom_call_target="tpu_custom_call" | custom-call | flops 5000000000 | bytes 15000000 | tf_op jit(solution)/shard_map/pallas_call | solution.py:1065
  421.5 7.0 add_convert_fusion
  428.4 6.2 all-to-all-done.9.g
  439.4 9.5 %shard_map.242 = (f32[49,16,512]{2,1,0:T(8,128)S(1)}, f32[16,8,384]{2,1,0:T(8,128)}, bf16[49,16,2048]{2,1,0:T(8,128)(2,1)S(1)}, f32[8,2048]{1,0:T(8,128)S(1)}) custom-call(s32[3]{0:T(128)S(1)} %pad_add_fusion.core_ref.place, bf16[49,16,2048]{2,1,0:T(8,128)(2,1)} %get-tuple-element.185.dz, bf16[49,16,2048]{2,1,0:T(8,128)(2,1)} %copy-done.1, ...), custom_call_target="tpu_custom_call" | custom-call | flops 5000000000 | bytes 15000000 | tf_op jit(solution)/shard_map/pallas_call | solution.py:1065
  473.0 6.1 shard_map.244
  483.5 13.5 %shard_map.245 = (f32[49,16,512]{2,1,0:T(8,128)}, f32[16,8,384]{2,1,0:T(8,128)}, bf16[49,16,512]{2,1,0:T(8,128)(2,1)S(1)}, bf16[49,16,128]{2,1,0:T(8,128)(2,1)S(1)}) custom-call(s32[3]{0:T(128)S(1)} %pad_add_fusion.core_ref.place, bf16[49,16,512]{2,1,0:T(8,128)(2,1)S(1)} %get-tuple-element.206.d2, f32[49,16,512]{2,1,0:T(8,128)S(1)} %copy-done.84, ...), custom_call_target="tpu_custom_call" | custom-call | flops 5000000000 | bytes 15000000 | tf_op jit(solution)/shard_map/pallas_call | solution.py:1065
  498.0 5.8 all-to-all-start.11
  508.0 4.6 shard_map.246
  527.4 31.0 %collective-permute-done.56 = bf16[4,2,16,2432]{3,2,1,0:T(8,128)(2,1)S(1)} collective-permute-done((bf16[4,2,16,2432]{3,2,1,0:T(8,128)(2,1)S(1)}, bf16[4,2,16,2432]{3,2,1,0:T(8,128)(2,1)S(1)}, u32[]{:S(2)}, u32[]{:S(2)}) %collective-permute-start.56) | collective-permute-done | bytes 622624 | tf_op jit(solution)/shard_map/ppermute | solution.py:820
  562.2 5.0 shard_map.247
  573.5 13.5 %collective-permute-done.64 = bf16[4,16,2048]{2,1,0:T(8,128)(2,1)S(1)} collective-permute-done((bf16[4,16,2048]{2,1,0:T(8,128)(2,1)S(1)}, bf16[4,16,2048]{2,1,0:T(8,128)(2,1)S(1)}, u32[]{:S(2)}, u32[]{:S(2)}) %collective-permute-start.64) | collective-permute-done | bytes 262176 | tf_op jit(solution)/shard_map/ppermute | solution.py:820
  588.4 5.0 shard_map.248.early_ref
  598.3 5.6 collective-permute-done.77
  605.6 6.6 collective-permute-done.69
  613.1 8.9 %collective-permute-done.57 = bf16[4,16,2432]{2,1,0:T(8,128)(2,1)S(1)} collective-permute-done((bf16[4,16,2432]{2,1,0:T(8,128)(2,1)S(1)}, bf16[4,16,2432]{2,1,0:T(8,128)(2,1)S(1)}, u32[]{:S(2)}, u32[]{:S(2)}) %collective-permute-start.57) | collective-permute-done | bytes 311328 | tf_op jit(solution)/shard_map/ppermute | solution.py:820
  623.1 8.4 %collective-permute-done.81 = bf16[4,16,2560]{2,1,0:T(8,128)(2,1)S(1)} collective-permute-done((bf16[4,16,2560]{2,1,0:T(8,128)(2,1)S(1)}, bf16[4,16,2560]{2,1,0:T(8,128)(2,1)S(1)}, u32[]{:S(2)}, u32[]{:S(2)}) %collective-permute-start.81) | collective-permute-done | bytes 327712 | tf_op jit(solution)/shard_map/ppermute | solution.py:820
  641.8 9.6 %collective-permute-done.52 = bf16[4,2,16,2048]{3,2,1,0:T(8,128)(2,1)S(1)} collective-permute-done((bf16[4,2,16,2048]{3,2,1,0:T(8,128)(2,1)S(1)}, bf16[4,2,16,2048]{3,2,1,0:T(8,128)(2,1)S(1)}, u32[]{:S(2)}, u32[]{:S(2)}) %collective-permute-start.52) | collective-permute-done | bytes 524320 | tf_op jit(solution)/shard_map/ppermute | solution.py:820
  663.8 7.3 %collective-permute-done.58 = bf16[2,16,4480]{2,1,0:T(8,128)(2,1)S(1)} collective-permute-done((bf16[2,16,4480]{2,1,0:T(8,128)(2,1)S(1)}, bf16[2,16,4480]{2,1,0:T(8,128)(2,1)S(1)}, u32[]{:S(2)}, u32[]{:S(2)}) %collective-permute-start.58) | collective-permute-done | bytes 286752 | tf_op jit(solution)/shard_map/ppermute | solution.py:820
  674.8 7.2 collective-permute-done.59
  682.0 9.4 %collective-permute-done.83 = bf16[16,4608]{1,0:T(8,128)(2,1)S(1)} collective-permute-done((bf16[16,4608]{1,0:T(8,128)(2,1)S(1)}, bf16[16,4608]{1,0:T(8,128)(2,1)S(1)}, u32[]{:S(2)}, u32[]{:S(2)}) %collective-permute-start.83) | collective-permute-done | bytes 147488 | tf_op jit(solution)/shard_map/ppermute | solution.py:820
  700.9 11.1 %shard_map.249 = bf16[3,392,2048]{2,1,0:T(8,128)(2,1)} custom-call(s32[3]{0:T(128)S(1)} %pad_add_fusion.core_ref.place, bf16[49,16,2048]{2,1,0:T(8,128)(2,1)} %shard_map.248.early_ref, bf16[49,16,2048]{2,1,0:T(8,128)(2,1)} %get-tuple-element.227.late_ref, bf16[49,16,2048]{2,1,0:T(8,128)(2,1)} %collective-permute-done.48.early_in, ...), custom_call_target="tpu_custom_call" | custom-call | flops 5000000000 | bytes 15000000 | tf_op jit(solution)/shard_map/pallas_call | solution.py:1216
  (599 shorter events, 239.0 us)
Async XLA Ops:
  7.2 82.7 %all-gather.5.cloned.1.call-start = ((), (), s32[]{:S(2)}) async-start(), calls=%async_computation.14 | async-start | bytes 3829760 | tf_op jit(solution)/shard_map/all_gather | solution.py:861
  13.3 43.8 %collective-permute-start.16 = (bf16[16,2048]{1,0:T(8,128)(2,1)S(1)}, bf16[16,2048]{1,0:T(8,128)(2,1)S(1)}, u32[]{:S(2)}, u32[]{:S(2)}) collective-permute-start(bf16[16,2048]{1,0:T(8,128)(2,1)S(1)} %dynamic-slice_bitcast_fusion.14), channel_id=1, source_target_pairs={{0,16},{16,0},{1,17},{17,1},{2,18},{18,2},{3,19},{19,3},{4,20},{20... | collective-permute-start | bytes 196616 | tf_op jit(solution)/shard_map/ppermute | solution.py:817
  14.1 13.8 %collective-permute-start.1 = (bf16[16,2176]{1,0:T(8,128)(2,1)S(1)}, bf16[16,2176]{1,0:T(8,128)(2,1)S(1)}, u32[]{:S(2)}, u32[]{:S(2)}) collective-permute-start(bf16[16,2176]{1,0:T(8,128)(2,1)S(1)} %get-tuple-element.293), channel_id=1, source_target_pairs={{0,8},{1,9},{2,10},{3,11},{4,12},{5,13},{6,14},{7,15},{8,0},{9,1},... | collective-permute-start | bytes 208904 | tf_op jit(solution)/shard_map/ppermute | solution.py:820
  35.7 13.8 %collective-permute-start.3 = (bf16[4,16,1024]{2,1,0:T(8,128)(2,1)S(1)}, bf16[4,16,1024]{2,1,0:T(8,128)(2,1)S(1)}, u32[]{:S(2)}, u32[]{:S(2)}) collective-permute-start(bf16[4,16,1024]{2,1,0:T(8,128)(2,1)S(1)} %get-tuple-element.291), channel_id=1, source_target_pairs={{0,1},{1,0},{2,3},{3,2},{4,5},{5,4},{6,7},{7,6},{8,9},{9,8},{10,11... | collective-permute-start | bytes 393224 | tf_op jit(solution)/shard_map/ppermute | solution.py:820
  64.3 18.0 %all-to-all-start = ((f32[16,8,384]{2,1,0:T(8,128)}), f32[16,8,384]{2,1,0:T(8,128)S(1)}, u32[]{:S(2)}, u32[]{:S(2)}) async-start(f32[16,8,384]{2,1,0:T(8,128)} %get-tuple-element.132), calls=%async_computation | async-start | bytes 393216 | tf_op jit(solution)/shard_map/all_to_all | solution.py:823
  69.9 138.3 %all-gather.7.cloned.1.call-start = ((), (), s32[]{:S(2)}) async-start(), calls=%async_computation.15 | async-start | bytes 4943872 | tf_op jit(solution)/shard_map/all_gather | solution.py:861
  90.2 28.0 %collective-permute-start.14 = (bf16[4,2,2,16,7040]{4,3,2,1,0:T(8,128)(2,1)}, bf16[4,2,2,16,7040]{4,3,2,1,0:T(8,128)(2,1)S(1)}, u32[]{:S(2)}, u32[]{:S(2)}) collective-permute-start(bf16[4,2,2,16,7040]{4,3,2,1,0:T(8,128)(2,1)} %bitcast.200), channel_id=1, source_target_pairs={{0,16},{16,0},{1,17},{17,1},{2,18},{18,2},{3,19},{19,3},{4,20},{20... | collective-permute-start | bytes 10813448 | tf_op jit(solution)/shard_map/ppermute | solution.py:817
  91.1 27.2 %collective-permute-start.11 = (f32[49,16,512]{2,1,0:T(8,128)S(1)}, f32[49,16,512]{2,1,0:T(8,128)S(1)}, u32[]{:S(2)}, u32[]{:S(2)}) collective-permute-start(f32[49,16,512]{2,1,0:T(8,128)S(1)} %get-tuple-element.131.a_in), channel_id=1, source_target_pairs={{0,16},{16,0},{1,17},{17,1},{2,18},{18,2},{3,19},{19,3},{4,20},{20... | collective-permute-start | bytes 4816904 | tf_op jit(solution)/shard_map/ppermute | solution.py:817
  101.1 12.7 %collective-permute-start.18 = (bf16[2,16,4224]{2,1,0:T(8,128)(2,1)S(1)}, bf16[2,16,4224]{2,1,0:T(8,128)(2,1)S(1)}, u32[]{:S(2)}, u32[]{:S(2)}) collective-permute-start(bf16[2,16,4224]{2,1,0:T(8,128)(2,1)S(1)} %maximum_select_fusion.7), channel_id=1, source_target_pairs={{0,4},{1,5},{2,6},{3,7},{4,0},{5,1},{6,2},{7,3},{8,12},{9,13},{10,... | collective-permute-start | bytes 811016 | tf_op jit(solution)/shard_map/ppermute | solution.py:820
  101.2 17.1 %collective-permute-start.12 = (f32[16,8,384]{2,1,0:T(8,128)S(1)}, f32[16,8,384]{2,1,0:T(8,128)S(1)}, u32[]{:S(2)}, u32[]{:S(2)}) collective-permute-start(f32[16,8,384]{2,1,0:T(8,128)S(1)} %all-to-all-done.g), channel_id=1, source_target_pairs={{0,16},{16,0},{1,17},{17,1},{2,18},{18,2},{3,19},{19,3},{4,20},{20... | collective-permute-start | bytes 589832 | tf_op jit(solution)/shard_map/ppermute | solution.py:817
  114.1 23.1 %collective-permute-start.19 = (bf16[4,16,2048]{2,1,0:T(8,128)(2,1)S(1)}, bf16[4,16,2048]{2,1,0:T(8,128)(2,1)S(1)}, u32[]{:S(2)}, u32[]{:S(2)}) collective-permute-start(bf16[4,16,2048]{2,1,0:T(8,128)(2,1)S(1)} %get-tuple-element.285), channel_id=1, source_target_pairs={{0,1},{1,0},{2,3},{3,2},{4,5},{5,4},{6,7},{7,6},{8,9},{9,8},{10,11... | collective-permute-start | bytes 786440 | tf_op jit(solution)/shard_map/ppermute | solution.py:820
  115.4 21.8 %collective-permute-start.20 = (bf16[4,16,2176]{2,1,0:T(8,128)(2,1)S(1)}, bf16[4,16,2176]{2,1,0:T(8,128)(2,1)S(1)}, u32[]{:S(2)}, u32[]{:S(2)}) collective-permute-start(bf16[4,16,2176]{2,1,0:T(8,128)(2,1)S(1)} %get-tuple-element.283), channel_id=1, source_target_pairs={{0,2},{1,3},{2,0},{3,1},{4,6},{5,7},{6,4},{7,5},{8,10},{9,11},{10,... | collective-permute-start | bytes 835592 | tf_op jit(solution)/shard_map/ppermute | solution.py:820
  137.3 22.0 %collective-permute-start.22 = (bf16[4,2,16,2176]{3,2,1,0:T(8,128)(2,1)S(1)}, bf16[4,2,16,2176]{3,2,1,0:T(8,128)(2,1)S(1)}, u32[]{:S(2)}, u32[]{:S(2)}) collective-permute-start(bf16[4,2,16,2176]{3,2,1,0:T(8,128)(2,1)S(1)} %maximum_select_fusion.rest_2_), channel_id=1, source_target_pairs={{0,1},{1,0},{2,3},{3,2},{4,5},{5,4},{6,7},{7,6},{8,9},{9,8},{10,11... | collective-permute-start | bytes 1671176 | tf_op jit(solution)/shard_map/ppermute | solution.py:820
  137.5 22.3 %collective-permute-start.21 = (bf16[4,2,16,2048]{3,2,0,1:T(8,128)(2,1)S(1)}, bf16[4,2,16,2048]{3,2,0,1:T(8,128)(2,1)}, u32[]{:S(2)}, u32[]{:S(2)}) collective-permute-start(bf16[4,2,16,2048]{3,2,0,1:T(8,128)(2,1)S(1)} %maximum_select_fusion.2), channel_id=1, source_target_pairs={{0,2},{1,3},{2,0},{3,1},{4,6},{5,7},{6,4},{7,5},{8,10},{9,11},{10,... | collective-permute-start | bytes 1572872 | tf_op jit(solution)/shard_map/ppermute | solution.py:820
  138.7 21.4 %all-to-all-start.1 = ((f32[16,8,384]{2,1,0:T(8,128)}), f32[16,8,384]{2,1,0:T(8,128)S(1)}, u32[]{:S(2)}, u32[]{:S(2)}) async-start(f32[16,8,384]{2,1,0:T(8,128)} %get-tuple-element.137), calls=%async_computation.1 | async-start | bytes 393216 | tf_op jit(solution)/shard_map/all_to_all | solution.py:823
  143.9 20.6 %collective-permute-start.25 = (bf16[4,2,16,2176]{3,2,1,0:T(8,128)(2,1)S(1)}, bf16[4,2,16,2176]{3,2,1,0:T(8,128)(2,1)}, u32[]{:S(2)}, u32[]{:S(2)}) collective-permute-start(bf16[4,2,16,2176]{3,2,1,0:T(8,128)(2,1)S(1)} %maximum_select_fusion.rest_2_), channel_id=1, source_target_pairs={{0,16},{16,0},{1,17},{17,1},{2,18},{18,2},{3,19},{19,3},{4,20},{20... | collective-permute-start | bytes 1671176 | tf_op jit(solution)/shard_map/ppermute | solution.py:817
  208.1 15.4 %collective-permute-start.31 = (bf16[4,2,2,16,9088]{4,3,2,1,0:T(8,128)(2,1)}, bf16[4,2,2,16,9088]{4,3,2,1,0:T(8,128)(2,1)S(1)}, u32[]{:S(2)}, u32[]{:S(2)}) collective-permute-start(bf16[4,2,2,16,9088]{4,3,2,1,0:T(8,128)(2,1)} %bitcast.191), channel_id=1, source_target_pairs={{0,16},{16,0},{1,17},{17,1},{2,18},{18,2},{3,19},{19,3},{4,20},{20... | collective-permute-start | bytes 13959176 | tf_op jit(solution)/shard_map/ppermute | solution.py:817
  208.3 15.3 %collective-permute-start.29 = (f32[49,16,512]{2,1,0:T(8,128)}, f32[49,16,512]{2,1,0:T(8,128)S(1)}, u32[]{:S(2)}, u32[]{:S(2)}) collective-permute-start(f32[49,16,512]{2,1,0:T(8,128)} %copy-done.49), channel_id=1, source_target_pairs={{0,16},{16,0},{1,17},{17,1},{2,18},{18,2},{3,19},{19,3},{4,20},{20... | collective-permute-start | bytes 4816904 | tf_op jit(solution)/shard_map/ppermute | solution.py:817
  277.1 30.2 %collective-permute-start.35 = (bf16[49,16,2048]{2,1,0:T(8,128)(2,1)}, bf16[49,16,2048]{2,1,0:T(8,128)(2,1)}, u32[]{:S(2)}, u32[]{:S(2)}) collective-permute-start(bf16[49,16,2048]{2,1,0:T(8,128)(2,1)} %get-tuple-element.145.x_ref.early_ref), channel_id=1, source_target_pairs={{16,0},{17,1},{18,2},{19,3},{20,4},{21,5},{22,6},{23,7},{24,8},{25... | collective-permute-start | bytes 9633800 | tf_op jit(solution)/shard_map/ppermute | solution.py:1148
  292.6 14.7 %collective-permute-start.36 = (bf16[49,16,2048]{2,1,0:T(8,128)(2,1)}, bf16[49,16,2048]{2,1,0:T(8,128)(2,1)}, u32[]{:S(2)}, u32[]{:S(2)}) collective-permute-start(bf16[49,16,2048]{2,1,0:T(8,128)(2,1)} %get-tuple-element.157.late_ref), channel_id=1, source_target_pairs={{0,16},{1,17},{2,18},{3,19},{4,20},{5,21},{6,22},{7,23},{8,24},{9,... | collective-permute-start | bytes 9633800 | tf_op jit(solution)/shard_map/ppermute | solution.py:1148
  303.0 17.4 %all-to-all-start.6 = ((f32[16,8,768]{2,1,0:T(8,128)}), f32[16,8,768]{2,1,0:T(8,128)}, u32[]{:S(2)}, u32[]{:S(2)}) async-start(f32[16,8,768]{2,1,0:T(8,128)} %copy-done.28), calls=%async_computation.6 | async-start | bytes 786432 | tf_op jit(solution)/shard_map/all_to_all | solution.py:823
  380.3 41.2 %collective-permute-start.43 = (bf16[4,2,2,16,9088]{4,3,2,1,0:T(8,128)(2,1)}, bf16[4,2,2,16,9088]{4,3,2,1,0:T(8,128)(2,1)}, u32[]{:S(2)}, u32[]{:S(2)}) collective-permute-start(bf16[4,2,2,16,9088]{4,3,2,1,0:T(8,128)(2,1)} %get-tuple-element.181), channel_id=1, source_target_pairs={{0,16},{16,0},{1,17},{17,1},{2,18},{18,2},{3,19},{19,3},{4,20},{20... | collective-permute-start | bytes 13959176 | tf_op jit(solution)/shard_map/ppermute | solution.py:817
  380.4 14.2 %collective-permute-start.40 = (f32[49,16,512]{2,1,0:T(8,128)}, f32[49,16,512]{2,1,0:T(8,128)}, u32[]{:S(2)}, u32[]{:S(2)}) collective-permute-start(f32[49,16,512]{2,1,0:T(8,128)} %get-tuple-element.171.dn1), channel_id=1, source_target_pairs={{0,16},{16,0},{1,17},{17,1},{2,18},{18,2},{3,19},{19,3},{4,20},{20... | collective-permute-start | bytes 4816904 | tf_op jit(solution)/shard_map/ppermute | solution.py:817
  415.1 19.5 %collective-permute-start.62 = (bf16[4,2,16,2048]{3,2,0,1:T(8,128)(2,1)}, bf16[4,2,16,2048]{3,2,0,1:T(8,128)(2,1)}, u32[]{:S(2)}, u32[]{:S(2)}) collective-permute-start(bf16[4,2,16,2048]{3,2,0,1:T(8,128)(2,1)} %copy.156), channel_id=1, source_target_pairs={{0,16},{16,0},{1,17},{17,1},{2,18},{18,2},{3,19},{19,3},{4,20},{20... | collective-permute-start | bytes 1572872 | tf_op jit(solution)/shard_map/ppermute | solution.py:817
  416.3 97.4 %collective-permute-start.61 = (bf16[4,2,16,2048]{3,2,0,1:T(8,128)(2,1)}, bf16[4,2,16,2048]{3,2,0,1:T(8,128)(2,1)}, u32[]{:S(2)}, u32[]{:S(2)}) collective-permute-start(bf16[4,2,16,2048]{3,2,0,1:T(8,128)(2,1)} %copy.154), channel_id=1, source_target_pairs={{0,16},{16,0},{1,17},{17,1},{2,18},{18,2},{3,19},{19,3},{4,20},{20... | collective-permute-start | bytes 1572872 | tf_op jit(solution)/shard_map/ppermute | solution.py:817
  417.2 17.4 %all-to-all-start.9 = ((f32[16,8,768]{2,1,0:T(8,128)}), f32[16,8,768]{2,1,0:T(8,128)}, u32[]{:S(2)}, u32[]{:S(2)}) async-start(f32[16,8,768]{2,1,0:T(8,128)} %copy-done.29), calls=%async_computation.9 | async-start | bytes 786432 | tf_op jit(solution)/shard_map/all_to_all | solution.py:823
  421.4 275.2 %reduce-scatter.2.cloned.1.call-start = ((), (), s32[]{:S(2)}) async-start(), calls=%async_computation.13 | async-start | bytes 4943872 | tf_op jit(solution)/shard_map/reduce_scatter | solution.py:934
  436.7 75.8 %collective-permute-start.63 = (bf16[4,2,16,2048]{3,2,0,1:T(8,128)(2,1)}, bf16[4,2,16,2048]{3,2,0,1:T(8,128)(2,1)}, u32[]{:S(2)}, u32[]{:S(2)}) collective-permute-start(bf16[4,2,16,2048]{3,2,0,1:T(8,128)(2,1)} %add_convert_fusion.14), channel_id=1, source_target_pairs={{0,2},{1,3},{2,0},{3,1},{4,6},{5,7},{6,4},{7,5},{8,10},{9,11},{10,... | collective-permute-start | bytes 1572872 | tf_op jit(solution)/shard_map/ppermute | solution.py:820
  451.8 15.2 %all-to-all-start.10 = ((f32[16,8,384]{2,1,0:T(8,128)}), f32[16,8,384]{2,1,0:T(8,128)S(1)}, u32[]{:S(2)}, u32[]{:S(2)}) async-start(f32[16,8,384]{2,1,0:T(8,128)} %get-tuple-element.197), calls=%async_computation.10 | async-start | bytes 393216 | tf_op jit(solution)/shard_map/all_to_all | solution.py:823
  463.6 53.9 %collective-permute-start.65 = (bf16[4,2,16,2048]{3,2,1,0:T(8,128)(2,1)}, bf16[4,2,16,2048]{3,2,1,0:T(8,128)(2,1)}, u32[]{:S(2)}, u32[]{:S(2)}) collective-permute-start(bf16[4,2,16,2048]{3,2,1,0:T(8,128)(2,1)} %get-tuple-element.202), channel_id=1, source_target_pairs={{0,16},{16,0},{1,17},{17,1},{2,18},{18,2},{3,19},{19,3},{4,20},{20... | collective-permute-start | bytes 1572872 | tf_op jit(solution)/shard_map/ppermute | solution.py:817
  468.0 49.2 %collective-permute-start.67 = (bf16[4,2,16,2048]{3,2,1,0:T(8,128)(2,1)}, bf16[4,2,16,2048]{3,2,1,0:T(8,128)(2,1)}, u32[]{:S(2)}, u32[]{:S(2)}) collective-permute-start(bf16[4,2,16,2048]{3,2,1,0:T(8,128)(2,1)} %add_convert_fusion.11), channel_id=1, source_target_pairs={{0,1},{1,0},{2,3},{3,2},{4,5},{5,4},{6,7},{7,6},{8,9},{9,8},{10,11... | collective-permute-start | bytes 1572872 | tf_op jit(solution)/shard_map/ppermute | solution.py:820
  498.0 62.9 %collective-permute-start.46 = (f32[49,16,512]{2,1,0:T(8,128)}, f32[49,16,512]{2,1,0:T(8,128)}, u32[]{:S(2)}, u32[]{:S(2)}) collective-permute-start(f32[49,16,512]{2,1,0:T(8,128)} %get-tuple-element.210.dn1), channel_id=1, source_target_pairs={{0,16},{16,0},{1,17},{17,1},{2,18},{18,2},{3,19},{19,3},{4,20},{20... | collective-permute-start | bytes 4816904 | tf_op jit(solution)/shard_map/ppermute | solution.py:817
  498.0 19.2 %all-to-all-start.11 = ((f32[16,8,384]{2,1,0:T(8,128)}), f32[16,8,384]{2,1,0:T(8,128)S(1)}, u32[]{:S(2)}, u32[]{:S(2)}) async-start(f32[16,8,384]{2,1,0:T(8,128)} %get-tuple-element.211), calls=%async_computation.11 | async-start | bytes 393216 | tf_op jit(solution)/shard_map/all_to_all | solution.py:823
  520.7 67.1 %collective-permute-start.76 = (bf16[4,2,16,2048]{3,2,0,1:T(8,128)(2,1)S(1)}, bf16[4,2,16,2048]{3,2,0,1:T(8,128)(2,1)S(1)}, u32[]{:S(2)}, u32[]{:S(2)}) collective-permute-start(bf16[4,2,16,2048]{3,2,0,1:T(8,128)(2,1)S(1)} %add_convert_fusion.8), channel_id=1, source_target_pairs={{0,2},{1,3},{2,0},{3,1},{4,6},{5,7},{6,4},{7,5},{8,10},{9,11},{10,... | collective-permute-start | bytes 1572872 | tf_op jit(solution)/shard_map/ppermute | solution.py:820
  524.2 34.2 %collective-permute-start.56 = (bf16[4,2,16,2432]{3,2,1,0:T(8,128)(2,1)S(1)}, bf16[4,2,16,2432]{3,2,1,0:T(8,128)(2,1)S(1)}, u32[]{:S(2)}, u32[]{:S(2)}) collective-permute-start(bf16[4,2,16,2432]{3,2,1,0:T(8,128)(2,1)S(1)} %add_convert_fusion.5), channel_id=1, source_target_pairs={{0,1},{1,0},{2,3},{3,2},{4,5},{5,4},{6,7},{7,6},{8,9},{9,8},{10,11... | collective-permute-start | bytes 1867784 | tf_op jit(solution)/shard_map/ppermute | solution.py:820
  525.9 61.9 %collective-permute-start.80 = (bf16[4,2,16,2560]{3,2,1,0:T(8,128)(2,1)S(1)}, bf16[4,2,16,2560]{3,2,1,0:T(8,128)(2,1)S(1)}, u32[]{:S(2)}, u32[]{:S(2)}) collective-permute-start(bf16[4,2,16,2560]{3,2,1,0:T(8,128)(2,1)S(1)} %add_convert_fusion.2), channel_id=1, source_target_pairs={{0,1},{1,0},{2,3},{3,2},{4,5},{5,4},{6,7},{7,6},{8,9},{9,8},{10,11... | collective-permute-start | bytes 1966088 | tf_op jit(solution)/shard_map/ppermute | solution.py:820
  527.3 66.0 %collective-permute-start.54 = (bf16[4,2,16,2432]{3,2,1,0:T(8,128)(2,1)S(1)}, bf16[4,2,16,2432]{3,2,1,0:T(8,128)(2,1)S(1)}, u32[]{:S(2)}, u32[]{:S(2)}) collective-permute-start(bf16[4,2,16,2432]{3,2,1,0:T(8,128)(2,1)S(1)} %copy-done.55), channel_id=1, source_target_pairs={{0,16},{16,0},{1,17},{17,1},{2,18},{18,2},{3,19},{19,3},{4,20},{20... | collective-permute-start | bytes 1867784 | tf_op jit(solution)/shard_map/ppermute | solution.py:817
  558.4 28.7 %collective-permute-start.64 = (bf16[4,16,2048]{2,1,0:T(8,128)(2,1)S(1)}, bf16[4,16,2048]{2,1,0:T(8,128)(2,1)S(1)}, u32[]{:S(2)}, u32[]{:S(2)}) collective-permute-start(bf16[4,16,2048]{2,1,0:T(8,128)(2,1)S(1)} %copy-done.125), channel_id=1, source_target_pairs={{0,1},{1,0},{2,3},{3,2},{4,5},{5,4},{6,7},{7,6},{8,9},{9,8},{10,11... | collective-permute-start | bytes 786440 | tf_op jit(solution)/shard_map/ppermute | solution.py:820
  570.5 126.9 %collective-permute-start.49 = (bf16[49,16,2048]{2,1,0:T(8,128)(2,1)}, bf16[49,16,2048]{2,1,0:T(8,128)(2,1)}, u32[]{:S(2)}, u32[]{:S(2)}) collective-permute-start(bf16[49,16,2048]{2,1,0:T(8,128)(2,1)} %get-tuple-element.227.late_ref), channel_id=1, source_target_pairs={{0,16},{1,17},{2,18},{3,19},{4,20},{5,21},{6,22},{7,23},{8,24},{9,... | collective-permute-start | bytes 9633800 | tf_op jit(solution)/shard_map/ppermute | solution.py:1148
  587.8 46.7 %collective-permute-start.51 = (bf16[4,2,16,2048]{3,2,1,0:T(8,128)(2,1)S(1)}, bf16[4,2,16,2048]{3,2,1,0:T(8,128)(2,1)S(1)}, u32[]{:S(2)}, u32[]{:S(2)}) collective-permute-start(bf16[4,2,16,2048]{3,2,1,0:T(8,128)(2,1)S(1)} %get-tuple-element.225), channel_id=1, source_target_pairs={{0,16},{16,0},{1,17},{17,1},{2,18},{18,2},{3,19},{19,3},{4,20},{20... | collective-permute-start | bytes 1572872 | tf_op jit(solution)/shard_map/ppermute | solution.py:817
  593.4 58.0 %collective-permute-start.50 = (bf16[4,2,16,2048]{3,2,1,0:T(8,128)(2,1)S(1)}, bf16[4,2,16,2048]{3,2,1,0:T(8,128)(2,1)S(1)}, u32[]{:S(2)}, u32[]{:S(2)}) collective-permute-start(bf16[4,2,16,2048]{3,2,1,0:T(8,128)(2,1)S(1)} %get-tuple-element.224), channel_id=1, source_target_pairs={{0,16},{16,0},{1,17},{17,1},{2,18},{18,2},{3,19},{19,3},{4,20},{20... | collective-permute-start | bytes 1572872 | tf_op jit(solution)/shard_map/ppermute | solution.py:817
  593.8 107.1 %collective-permute-start.48 = (bf16[49,16,2048]{2,1,0:T(8,128)(2,1)}, bf16[49,16,2048]{2,1,0:T(8,128)(2,1)}, u32[]{:S(2)}, u32[]{:S(2)}) collective-permute-start(bf16[49,16,2048]{2,1,0:T(8,128)(2,1)} %shard_map.248.early_ref), channel_id=1, source_target_pairs={{16,0},{17,1},{18,2},{19,3},{20,4},{21,5},{22,6},{23,7},{24,8},{25... | collective-permute-start | bytes 9633800 | tf_op jit(solution)/shard_map/ppermute | solution.py:1148
  634.6 25.5 %collective-permute-start.82 = (bf16[2,16,4608]{2,1,0:T(8,128)(2,1)S(1)}, bf16[2,16,4608]{2,1,0:T(8,128)(2,1)S(1)}, u32[]{:S(2)}, u32[]{:S(2)}) collective-permute-start(bf16[2,16,4608]{2,1,0:T(8,128)(2,1)S(1)} %dynamic-slice_bitcast_fusion.2), channel_id=1, source_target_pairs={{0,4},{1,5},{2,6},{3,7},{4,0},{5,1},{6,2},{7,3},{8,12},{9,13},{10,... | collective-permute-start | bytes 884744 | tf_op jit(solution)/shard_map/ppermute | solution.py:820
  654.3 38.5 %collective-permute-start.71 = (bf16[16,2048]{1,0:T(8,128)(2,1)S(1)}, bf16[16,2048]{1,0:T(8,128)(2,1)S(1)}, u32[]{:S(2)}, u32[]{:S(2)}) collective-permute-start(bf16[16,2048]{1,0:T(8,128)(2,1)S(1)} %get-tuple-element.297), channel_id=1, source_target_pairs={{0,16},{1,17},{2,18},{3,19},{4,20},{5,21},{6,22},{7,23},{8,24},{9,... | collective-permute-start | bytes 196616 | tf_op jit(solution)/shard_map/ppermute | solution.py:938
  658.6 54.7 %collective-permute-start.86 = (bf16[16,2048]{1,0:T(8,128)(2,1)S(1)}, bf16[16,2048]{1,0:T(8,128)(2,1)S(1)}, u32[]{:S(2)}, u32[]{:S(2)}) collective-permute-start(bf16[16,2048]{1,0:T(8,128)(2,1)S(1)} %get-tuple-element.296), channel_id=1, source_target_pairs={{16,0},{17,1},{18,2},{19,3},{20,4},{21,5},{22,6},{23,7},{24,8},{25... | collective-permute-start | bytes 196616 | tf_op jit(solution)/shard_map/ppermute | solution.py:937
  692.8 24.4 %collective-permute-start.84 = (bf16[16,4608]{1,0:T(8,128)(2,1)S(1)}, bf16[16,4608]{1,0:T(8,128)(2,1)S(1)}, u32[]{:S(2)}, u32[]{:S(2)}) collective-permute-start(bf16[16,4608]{1,0:T(8,128)(2,1)S(1)} %fusion.9), channel_id=1, source_target_pairs={{16,0},{17,1},{18,2},{19,3},{20,4},{21,5},{22,6},{23,7},{24,8},{25... | collective-permute-start | bytes 442376 | tf_op jit(solution)/shard_map/ppermute | solution.py:937
  694.6 21.2 %collective-permute-start.72 = (bf16[16,2432]{1,0:T(8,128)(2,1)S(1)}, bf16[16,2432]{1,0:T(8,128)(2,1)S(1)}, u32[]{:S(2)}, u32[]{:S(2)}) collective-permute-start(bf16[16,2432]{1,0:T(8,128)(2,1)S(1)} %slice.142), channel_id=1, source_target_pairs={{16,0},{17,1},{18,2},{19,3},{20,4},{21,5},{22,6},{23,7},{24,8},{25... | collective-permute-start | bytes 233480 | tf_op jit(solution)/shard_map/ppermute | solution.py:937
  697.5 17.2 %collective-permute-start.87 = (bf16[16,2048]{1,0:T(8,128)(2,1)S(1)}, bf16[16,2048]{1,0:T(8,128)(2,1)S(1)}, u32[]{:S(2)}, u32[]{:S(2)}) collective-permute-start(bf16[16,2048]{1,0:T(8,128)(2,1)S(1)} %slice.149), channel_id=1, source_target_pairs={{0,16},{1,17},{2,18},{3,19},{4,20},{5,21},{6,22},{7,23},{8,24},{9,... | collective-permute-start | bytes 196616 | tf_op jit(solution)/shard_map/ppermute | solution.py:938
  (190 other events, 2643.6 us)
Sparse Core Ops, SparseCore 0:
  12.8 77.1 all-gather.4
  93.3 86.6 all-gather.6
  438.0 144.5 reduce-scatter.1

commit v2 on v1

v2 whole, which is shorter than its diff:
```python
import functools

import jax
import jax.numpy as jnp
from jax import lax
from jax.experimental import pallas as pl
from jax.experimental.pallas import tpu as pltpu
from jax.sharding import PartitionSpec as P

SEG = 8
SIDE = 7
PIX = SIDE * SIDE
HALF = SEG // 2
STRIDE = HALF + 1
LINE = 16
ROWS = PIX * LINE
EPS = 1e-05
F32 = jnp.float32
BF16 = jnp.bfloat16
VMEM_BYTES = 36 * 1024 * 1024


def dot(left, right):
    return lax.dot_general(left, right, (((1,), (0,)), ((), ())), preferred_element_type=F32)


def dot_nt(left, right):
    return lax.dot_general(left, right, (((1,), (1,)), ((), ())), preferred_element_type=F32)


def dot_tn(left, right):
    return lax.dot_general(left, right, (((0,), (0,)), ((), ())), preferred_element_type=F32)


def sigmoid(v):
    return 0.5 * jnp.tanh(0.5 * v) + 0.5


def line_of(width):
    return lax.broadcasted_iota(jnp.int32, (LINE, width), 0)


def own_lines(width):
    r = line_of(width)
    inside = (r < 4) | ((r >= 5) & (r < 9)) | ((r >= 10) & (r < 14))
    return inside.astype(F32)


def per_line(values):
    width = values.shape[1]
    r = line_of(width)
    return jnp.where(r < 5, values[0:1], jnp.where(r < 10, values[1:2], values[2:3]))


def per_batch(lines, count):
    r = line_of(lines.shape[1])
    pieces = []
    for b in range(3):
        keep = (r >= 5 * b) & (r < 5 * b + count)
        pieces.append(jnp.sum(jnp.where(keep, lines, 0.0), axis=0, keepdims=True))
    return pieces


def flat(v):
    return v.reshape(-1, v.shape[-1])


def chunks(body, init=0):
    return lax.fori_loop(0, SIDE, body, init)


def ref_stats(a_ref, first, width):
    lanes = pl.ds(first, width)

    def add(i, s):
        return s + jnp.sum(a_ref[pl.ds(i * SIDE, SIDE), :, lanes], axis=0)

    sums = per_batch(chunks(add, jnp.zeros((LINE, width), F32)), HALF)
    means = [s / (HALF * PIX) for s in sums]
    mean_lines = per_line(jnp.concatenate(means, axis=0))

    def add_sq(i, s):
        d = a_ref[pl.ds(i * SIDE, SIDE), :, lanes] - mean_lines[None]
        return s + jnp.sum(d * d, axis=0)

    sq = per_batch(chunks(add_sq, jnp.zeros((LINE, width), F32)), HALF)
    zero = jnp.zeros((1, width), F32)
    return jnp.concatenate(means + [zero] + sq + [zero], axis=0)


def pack(st):
    cut = st.shape[1] * 3 // 4
    rest = [
        jnp.concatenate([st[r : r + 1, cut:] for r in rows], axis=1)
        for rows in ((0, 1, 2), (4, 5, 6))
    ]
    return jnp.concatenate([st[0:3, :cut], st[4:7, :cut]] + rest, axis=0)


def unpack(p, group):
    third = p.shape[1] // 3
    row = p[6 + group : 7 + group]
    rest = jnp.concatenate([row[:, third * k : third * (k + 1)] for k in range(3)], axis=0)
    return jnp.concatenate([p[3 * group : 3 * group + 3], rest], axis=1)


def spread(st, out_ref):
    packed = pack(st)
    for k in range(out_ref.shape[0]):
        out_ref[k] = packed


def merge_norm(gs, rows_each):
    count = sum(g.shape[0] for g in gs)
    total = sum(jnp.sum(g[...], axis=0) for g in gs)
    mean = total / count
    off = 0.0
    for g in gs:
        d = g[...] - mean[None]
        off = off + jnp.sum(d * d, axis=0)
    var = (unpack(total, 1) + rows_each * unpack(off, 0)) / (rows_each * count)
    return eight(unpack(mean, 0), var)


def merge_sums(gs, rows_each):
    total = sum(jnp.sum(g[...], axis=0) for g in gs)
    return eight(unpack(total, 0), unpack(total, 1))


def eight(first, second):
    zero = jnp.zeros((1, first.shape[1]), F32)
    return jnp.concatenate([first, zero, second, zero], axis=0)


def merge_wide(merge, place, g, g_other, out_ref):
    core = place[0]
    rows_each = float(2 * HALF * PIX)
    half = out_ref.shape[1] // 2
    out_ref[:, pl.ds(pl.multiple_of(core * half, half), half)] = merge([g], rows_each)
    out_ref[:, pl.ds(pl.multiple_of((1 - core) * half, half), half)] = merge([g_other], rows_each)


def split_wide(place, st, keep_ref, send_ref):
    core = place[0]
    half = st.shape[1] // 2
    keep_ref[...] = st[:, pl.ds(pl.multiple_of(core * half, half), half)]
    send_ref[...] = st[:, pl.ds(pl.multiple_of((1 - core) * half, half), half)]


def pair_kernel(norm, keep, recv, out_ref):
    a, b = keep[...], recv[...]
    if norm:
        d = a[0:3] - b[0:3]
        mean = 0.5 * (a[0:3] + b[0:3])
        st = eight(mean, a[4:7] + b[4:7] + (HALF * PIX / 2.0) * d * d)
    else:
        st = a + b
    spread(st, out_ref)


OWN_ROWS = float(HALF * PIX)


def gains_kernel(wt, place, *rest):
    refs, (gb_ref, gbo_ref, buf, sems) = rest[: wt.count], rest[wt.count :]
    wait_all(wt.copies("gain", place, refs, buf, Moves(sems)))
    i = lax.broadcasted_iota(jnp.int32, (128, 512), 0)
    j = lax.broadcasted_iota(jnp.int32, (128, 512), 1)
    mid = jnp.zeros((16, 512), F32)
    for k in range(16):
        g = buf[k // 4, k // 2 % 2, k % 2, 0]
        hot = jnp.where((i < 32) & (j == 32 * k + i), 1.0, 0.0).astype(BF16)
        mid = mid + dot(g, hot)
        gbo_ref[:, 128 * k : 128 * k + 128] = g[4:12].astype(F32)
    gb_ref[...] = mid[0:8]


class Moves:
    def __init__(self, sems):
        self.sems, self.used, self.leaving = sems, 0, []

    def fetch(self, source, target):
        copy = pltpu.make_async_copy(source, target, self.sems.at[self.used])
        self.used += 1
        copy.start()
        return copy

    def store(self, source, target):
        self.leaving.append(self.fetch(source, target))

    def chunks_of(self, source, target):
        return [self.fetch(source.at[rows], target.at[rows]) for rows in CHUNKS]

    def tiles_of(self, source, target):
        return [self.fetch(source.at[:, :, lanes], target.at[:, :, lanes]) for lanes in TILES]

    def finish(self):
        wait_all(self.leaving)


CHUNKS = [pl.ds(SIDE * i, SIDE) for i in range(SIDE)]
TILES = [pl.ds(512 * j, 512) for j in range(4)]


def wait_all(copies):
    for c in copies:
        c.wait()


class Weights:
    def __init__(self, kind, segments):
        self.kind, self.segments = kind, segments

    @property
    def count(self):
        return 2 if self.kind == "whole" else 8

    def copies(self, name, place, refs, buf, moves):
        core, y, x = place[0], place[1], place[2]
        found = []
        for part, start, at, width in self.segments[name]:
            for side in range(2):
                c = core if side == 0 else 1 - core
                if self.kind == "whole":
                    pairs = [(refs[side], (ALL, ALL, ALL))]
                elif part == "P":
                    pairs = [(refs[4 * side], (ALL, y, ALL)), (refs[4 * side + 1], (ALL, 1 - y, ALL))]
                else:
                    pairs = [(refs[4 * side + 2], (ALL, ALL, x)), (refs[4 * side + 3], (ALL, ALL, 1 - x))]
                for ref, where in pairs:
                    source = ref.at[..., pl.ds(start, width)]
                    if isinstance(at, tuple):
                        target = buf.at[where + (c, at[0])]
                    else:
                        target = buf.at[where + (c, ALL, pl.ds(at, width))]
                    found.append(moves.fetch(source, target))
        return found


ALL = slice(None)


def first_matmul(x_buf, w_buf, a_ref, stb_ref):
    for j in range(2):
        w = w_buf[2 * j : 2 * j + 2].reshape(256, 2048)
        a_ref[:, :, pl.ds(256 * j, 256)] = dot_nt(flat(x_buf[...]), w).reshape(PIX, LINE, 256)
    spread(ref_stats(a_ref, 0, 512), stb_ref)


def permute_kernel(core_ref, x_ref, out_ref, x_buf, buf, sems):
    moves = Moves(sems)
    loads = moves.tiles_of(x_ref, x_buf)
    core = core_ref[0]
    i = lax.broadcasted_iota(jnp.int32, (ROWS, SEG * PIX), 0)
    j = lax.broadcasted_iota(jnp.int32, (ROWS, SEG * PIX), 1)
    pixel, line = i >> 4, i & 15
    hots = []
    for b in range(3):
        t = line - 5 * b
        target = (HALF * core + t) * PIX + pixel
        hots.append(jnp.where((t >= 0) & (t < HALF) & (j == target), 1.0, 0.0).astype(BF16))
    for load, lanes in zip(loads, TILES):
        load.wait()
        total = dot(hots[0], x_buf[0, :, lanes])
        total = total + dot(hots[1], x_buf[1, :, lanes])
        total = total + dot(hots[2], x_buf[2, :, lanes])
        buf[:, :, lanes] = total.astype(BF16).reshape(PIX, LINE, 512)
        moves.store(buf.at[:, :, lanes], out_ref.at[:, :, lanes])
    moves.finish()


def restore_kernel(place, early_ref, late_ref, early_in, late_in, out_ref, buf, out_buf, sems):
    core = place[0]

    def copies(mine, received):
        found = []
        for k, lanes in enumerate(TILES):
            for n, (v, side) in enumerate(((mine, core), (received, 1 - core))):
                found.append(
                    pltpu.make_async_copy(
                        v.at[:, :, lanes], buf.at[side, :, :, lanes], sems.at[2 * k + n]
                    )
                )
        return found

    @pl.when(core == 0)
    def _():
        for c in copies(early_ref, early_in):
            c.start()

    @pl.when(core == 1)
    def _():
        for c in copies(late_ref, late_in):
            c.start()

    def hot(first, count, side, b):
        j = lax.broadcasted_iota(jnp.int32, (count, ROWS), 0) + first
        i = lax.broadcasted_iota(jnp.int32, (count, ROWS), 1)
        seg = jnp.zeros_like(j)
        for k in range(1, SEG):
            seg = seg + jnp.where(j >= PIX * k, 1, 0)
        t = seg - HALF * side
        target = (j - PIX * seg) * LINE + 5 * b + t
        return jnp.where((t >= 0) & (t < HALF) & (i == target), 1.0, 0.0).astype(BF16)

    hots = [(hot(0, 208, 0, b), hot(192, 200, 1, b)) for b in range(3)]
    loads = copies(early_ref, early_in)
    leaving = []
    for k, lanes in enumerate(TILES):
        wait_all(loads[2 * k : 2 * k + 2])
        for b, (lower, upper) in enumerate(hots):
            low = dot(lower, flat(buf[0, :, :, lanes])).astype(BF16)
            high = dot(upper, flat(buf[1, :, :, lanes])).astype(BF16)
            out_buf[b, 0:192, lanes] = low[:192]
            out_buf[b, 192:208, lanes] = low[192:] + high[:16]
            out_buf[b, 208:392, lanes] = high[16:]
        copy = pltpu.make_async_copy(out_buf.at[:, :, lanes], out_ref.at[:, :, lanes], sems.at[8 + k])
        copy.start()
        leaving.append(copy)
    wait_all(leaving)


def first_kernel(wt, place, x_ref, *rest):
    refs, (a_ref, stb_ref, w_buf, sems) = rest[: wt.count], rest[wt.count :]
    wait_all(wt.copies("in", place, refs, w_buf, Moves(sems)))
    first_matmul(x_ref, w_buf, a_ref, stb_ref)


def tap_ranges(shift):
    return max(0, -shift), min(SIDE, SIDE - shift)


def build_patches(sq, patch):
    patch[...] = jnp.zeros(patch.shape, BF16)
    sq4 = sq.reshape(SIDE, SIDE, LINE, 128)
    for k in (1, 2):
        for tap in range(9):
            dy, dx = k * (tap // 3 - 1), k * (tap % 3 - 1)
            (y0, y1), (x0, x1) = tap_ranges(dy), tap_ranges(dx)
            col = ((k - 1) * 9 + tap) * 128
            patch[y0:y1, x0:x1, :, col : col + 128] = sq4[y0 + dy : y1 + dy, x0 + dx : x1 + dx]


def clear_border(pad):
    zero_row = jnp.zeros((9, LINE, 512), BF16)
    pad[0] = zero_row
    pad[8] = zero_row
    for y in range(1, 8):
        pad[y, 0] = jnp.zeros((LINE, 512), BF16)
        pad[y, 8] = jnp.zeros((LINE, 512), BF16)


def middle_kernel(wt, place, a_in, a_other, g, g_other, gb_ref, msk_ref, *rest):
    refs = rest[: wt.count]
    (
        a_ref, diff_ref, sq_ref, op_ref, mix_ref, second, second_ref, st_ref, mv_ref,
        sq_buf, nf_buf, mid_buf, a_buf, diff, sq_out, op, mixp, hid, patch, sems,
    ) = rest[wt.count :]
    core = place[0]
    moves = Moves(sems)
    sq_copies = wt.copies("sq", place, refs, sq_buf, moves)
    nf_copies = wt.copies("nf", place, refs, nf_buf, moves)
    mid_copies = wt.copies("mid", place, refs, mid_buf, moves)
    clear_border(mixp)
    mv_ref[...] = merge_norm([g, g_other], OWN_ROWS)
    r = line_of(512)
    halo = ((r == 4) | (r == 9) | (r == 14)) & (core == 0)
    mean = per_line(mv_ref[0:3])
    scale = lax.rsqrt(per_line(mv_ref[4:7]) + EPS) * gb_ref[0:1]
    shift = gb_ref[1:2]
    m = msk_ref[:, 0:1]
    for rows in CHUNKS:
        a = jnp.where(halo[None], pltpu.roll(a_other[rows], 4, 1), a_in[rows])
        a_buf[rows] = a
        n1 = (a - mean[None]) * scale[None] + shift[None]
        h = n1 * sigmoid(n1)
        hid[rows] = h
        diff[rows] = (m[None] * (pltpu.roll(h, LINE - 1, 1) - h)).astype(BF16)
    moves.store(a_buf, a_ref)
    moves.store(diff, diff_ref)
    wait_all(sq_copies)
    sq = dot(flat(diff[...]), sq_buf[...].reshape(512, 128)).astype(BF16)
    sq_out[...] = sq.reshape(PIX, LINE, 128)
    moves.store(sq_out, sq_ref)
    build_patches(sq, patch)
    wait_all(nf_copies)
    for j in range(2):
        lanes = pl.ds(256 * j, 256)
        w = nf_buf[2 * j : 2 * j + 2].reshape(256, 2304)
        logits = dot_nt(patch[...].reshape(ROWS, 2304), w).reshape(PIX, LINE, 256)
        opening = sigmoid(logits)
        op[:, :, lanes] = opening.astype(BF16)
        mixed = (hid[:, :, lanes] * (0.5 + opening)).astype(BF16)
        mixp[1:8, 1:8, :, lanes] = mixed.reshape(SIDE, SIDE, LINE, 256)
    moves.store(op, op_ref)
    moves.store(mixp, mix_ref)
    wait_all(mid_copies)

    total = 0.0
    for k in range(9):
        v = mixp[k // 3 : k // 3 + SIDE, k % 3 : k % 3 + SIDE].reshape(ROWS, 512)
        total = total + dot_nt(v, mid_buf[..., pl.ds(512 * k, 512)].reshape(512, 512))
    second[...] = total.reshape(PIX, LINE, 512)
    moves.store(second, second_ref)
    spread(ref_stats(second, 0, 512), st_ref)
    moves.finish()


def wide_kernel(wt, place, second, g, g_other, gb_ref, *rest):
    refs = rest[: wt.count]
    mid_ref, keep_ref, send_ref, mv_ref, buf, mid, third, st_ref, sems = rest[wt.count :]
    moves = Moves(sems)
    copies = wt.copies("out", place, refs, buf, moves)
    mv_ref[...] = merge_norm([g, g_other], OWN_ROWS)
    mean = per_line(mv_ref[0:3])
    scale = lax.rsqrt(per_line(mv_ref[4:7]) + EPS) * gb_ref[2:3]
    shift = gb_ref[3:4]
    for rows in CHUNKS:
        n2 = (second[rows] - mean[None]) * scale[None] + shift[None]
        mid[rows] = (n2 * sigmoid(n2)).astype(BF16)
    moves.store(mid, mid_ref)
    wait_all(copies)
    for j, lanes in enumerate(TILES):
        w = buf[j].reshape(512, 512)
        third[...] = dot_nt(flat(mid[...]), w).reshape(PIX, LINE, 512)
        st_ref[:, lanes] = ref_stats(third, 0, 512)
    split_wide(place, st_ref, keep_ref, send_ref)
    moves.finish()


def finish(mid, wide_buf, third, x_buf, loads, mv_ref, gb_ref, each, after_tile):
    for j, lanes in enumerate(TILES):
        third[...] = dot_nt(flat(mid[...]), wide_buf[j].reshape(512, 512)).reshape(PIX, LINE, 512)
        wait_all([load[j] for load in loads])
        mean = per_line(mv_ref[0:3, lanes])
        inv = lax.rsqrt(per_line(mv_ref[4:7, lanes]) + EPS)
        gain, bias = gb_ref[0:1, lanes], gb_ref[1:2, lanes]

        def chunk(i, carry):
            rows = pl.ds(i * SIDE, SIDE)
            xhat = (third[rows] - mean[None]) * inv[None]
            z = x_buf[rows, :, lanes].astype(F32) + xhat * gain[None] + bias[None]
            sg = sigmoid(z)
            return each(rows, lanes, xhat, z * sg, sg, carry)

        zero = jnp.zeros((LINE, 512), F32)
        after_tile(lanes, chunks(chunk, (zero, zero)))


def sums_of(dh, dg):
    zero = jnp.zeros((1, dh.shape[1]), F32)
    return jnp.concatenate(per_batch(dh, STRIDE) + [zero] + per_batch(dg, STRIDE) + [zero], axis=0)


def turn_kernel(wide_wt, wt, place, mid, x_ref, g, g_other, gb_ref, *rest):
    wide_refs, rest = rest[: wide_wt.count], rest[wide_wt.count :]
    refs = rest[: wt.count]
    (
        act_ref, xhat_ref, slope_ref, a_ref, st_ref, mv_ref,
        wide_buf, w_buf, third, x_buf, act, xhat_buf, slope, sems,
    ) = rest[wt.count :]
    moves = Moves(sems)
    wide_copies = wide_wt.copies("out", place, wide_refs, wide_buf, moves)
    loads = [moves.tiles_of(x_ref, x_buf)]
    copies = wt.copies("in", place, refs, w_buf, moves)
    merge_wide(merge_norm, place, g, g_other, mv_ref)

    def each(rows, lanes, xhat, y, sg, carry):
        act[rows, :, lanes] = y.astype(BF16)
        xhat_buf[rows, :, lanes] = xhat.astype(BF16)
        slope[rows, :, lanes] = (sg + y * (1.0 - sg)).astype(BF16)
        return carry

    def after_tile(lanes, _):
        for buf, ref in ((act, act_ref), (xhat_buf, xhat_ref), (slope, slope_ref)):
            moves.store(buf.at[:, :, lanes], ref.at[:, :, lanes])

    wait_all(wide_copies)
    finish(mid, wide_buf, third, x_buf, loads, mv_ref, gb_ref, each, after_tile)
    wait_all(copies)
    first_matmul(act, w_buf, a_ref, st_ref)
    moves.finish()


def top_kernel(
    wide_wt, place, mid, x_ref, g, g_other, gb_ref, dy_ref, *rest,
):
    wide_refs, rest = rest[: wide_wt.count], rest[wide_wt.count :]
    (
        act_ref, xhat_ref, dz, keep_ref, send_ref, mv_ref,
        wide_buf, third, x_buf, dy, act, xhat_buf, sums_ref, sems,
    ) = rest
    moves = Moves(sems)
    wide_copies = wide_wt.copies("out", place, wide_refs, wide_buf, moves)
    loads = [moves.tiles_of(r, b) for r, b in ((x_ref, x_buf), (dy_ref, dy))]
    merge_wide(merge_norm, place, g, g_other, mv_ref)

    def each(rows, lanes, xhat, y, sg, carry):
        act[rows, :, lanes] = y.astype(BF16)
        xhat_buf[rows, :, lanes] = xhat.astype(BF16)
        d = dy[rows, :, lanes].astype(F32) * (sg + y * (1.0 - sg))
        dz[rows, :, lanes] = d.astype(BF16)
        return carry[0] + jnp.sum(d, axis=0), carry[1] + jnp.sum(d * xhat, axis=0)

    def after_tile(lanes, carry):
        for buf, ref in ((act, act_ref), (xhat_buf, xhat_ref)):
            moves.store(buf.at[:, :, lanes], ref.at[:, :, lanes])
        sums_ref[:, lanes] = sums_of(*carry)

    wait_all(wide_copies)
    finish(mid, wide_buf, third, x_buf, loads, mv_ref, gb_ref, each, after_tile)
    split_wide(place, sums_ref, keep_ref, send_ref)
    moves.finish()


class Shares:
    def __init__(self, kind, parts):
        self.kind, self.parts = kind, parts

    @property
    def count(self):
        return 2 if self.kind == "whole" else 4 * sum(1 for width in self.parts if width)

    def outs(self):
        if self.kind == "whole":
            width = sum(self.parts)
            return [((4, 2, 2, 16, width), BF16)] * 2
        return [((4, 2, 16, width), BF16) for width in self.parts if width for _ in range(4)]

    def buffers(self):
        return [pltpu.VMEM(shape, dtype) for shape, dtype in self.outs()]

    def store(self, place, out, first, result, zs=ALL):
        refs, bufs, moves = out

        def put(ref, buf, v, lanes):
            buf[zs, ..., lanes] = v
            moves.store(buf.at[zs, ..., lanes], ref.at[zs, ..., lanes])

        core, y, x = place[0], place[1], place[2]
        width = result.shape[1]
        parts = result.astype(BF16).reshape(-1, 2, 2, 2, 16, width)
        lower, upper = parts[:, :, :, 0], parts[:, :, :, 1]
        sides = [jnp.where(core == 0, lower, upper), jnp.where(core == 0, upper, lower)]
        if self.kind == "whole":
            for ref, buf, v in zip(refs, bufs, sides):
                put(ref, buf, v, pl.ds(first, width))
            return
        is_p = first < self.parts[0]
        start = first if is_p else first - self.parts[0]
        lanes = pl.ds(start, width)
        refs = refs[:4] if is_p else refs[-4:]
        bufs = bufs[:4] if is_p else bufs[-4:]
        for k, v in enumerate(sides):
            if is_p:
                two, at = (v[:, 0], v[:, 1]), y
            else:
                two, at = (v[:, :, 0], v[:, :, 1]), x
            put(refs[2 * k], bufs[2 * k], jnp.where(at == 0, two[0], two[1]), lanes)
            put(refs[2 * k + 1], bufs[2 * k + 1], jnp.where(at == 0, two[1], two[0]), lanes)


def wide_back_kernel(
    rows_total, wt, place, dz, xhat_ref, mv3_ref, g, g_other, gbo_ref, second_ref, mv2_ref, gb_ref, *rest
):
    refs = rest[: wt.count]
    dn2, stb_ref, d3_ref, s3_ref, buf, xhat, second, d3, lines, sems = rest[wt.count :]
    moves = Moves(sems)
    loads = moves.chunks_of(xhat_ref, xhat)
    copies = wt.copies("out", place, refs, buf, moves)
    second_load = moves.fetch(second_ref, second)
    merge_wide(merge_sums, place, g, g_other, s3_ref)
    own = own_lines(512)
    for lanes in TILES:
        lines[0, :, lanes] = lax.rsqrt(per_line(mv3_ref[4:7, lanes]) + EPS) * gbo_ref[0:1, lanes] * own
        lines[1, :, lanes] = per_line(s3_ref[0:3, lanes]) / rows_total
        lines[2, :, lanes] = per_line(s3_ref[4:7, lanes]) / rows_total
    for load, rows in zip(loads, CHUNKS):
        load.wait()
        for lanes in TILES:
            v = dz[rows, :, lanes].astype(F32) - lines[1, :, lanes][None]
            v = v - xhat[rows, :, lanes].astype(F32) * lines[2, :, lanes][None]
            d3[rows, :, lanes] = (lines[0, :, lanes][None] * v).astype(BF16)
    moves.store(d3, d3_ref)
    wait_all(copies)
    for j, lanes in enumerate(TILES):
        part = dot(flat(d3[:, :, lanes]), buf[j].reshape(512, 512)).reshape(PIX, LINE, 512)
        dn2[...] = part if j == 0 else dn2[...] + part
    second_load.wait()
    mean = per_line(mv2_ref[0:3])
    inv = lax.rsqrt(per_line(mv2_ref[4:7]) + EPS)
    gain, bias = gb_ref[2:3], gb_ref[3:4]

    def chunk(i, carry):
        rows = pl.ds(i * SIDE, SIDE)
        xh = (second[rows] - mean[None]) * inv[None]
        n2 = xh * gain[None] + bias[None]
        sg = sigmoid(n2)
        dn = dn2[rows] * (sg * (1.0 + n2 * (1.0 - sg)))
        dn2[rows] = dn
        return carry[0] + jnp.sum(dn, axis=0), carry[1] + jnp.sum(dn * xh, axis=0)

    zero = jnp.zeros((LINE, 512), F32)
    spread(sums_of(*chunks(chunk, (zero, zero))), stb_ref)
    moves.finish()


def wide_grad(sh, place, refs, start, d3, mid):
    for j in range(4):
        v = flat(d3[:, :, pl.ds(512 * j, 512)])
        res = dot_tn(v, flat(mid[...])).reshape(2, 2, 2, 4, 16, 512)
        for g in range(4):
            sh.store(place, refs, start + 512 * g, res[:, :, :, g].reshape(128, 512), slice(j, j + 1))


def middle_grad(sh, place, refs, start, d2, mixp):
    for tap in range(9):
        mixed = mixp[tap // 3 : tap // 3 + SIDE, tap % 3 : tap % 3 + SIDE].reshape(ROWS, 512)
        sh.store(place, refs, start + 512 * tap, dot_tn(flat(d2[...]), mixed))


def branch_grad(sh, place, refs, start, dlog, sq_ref, diff, dsq, patch):
    build_patches(flat(sq_ref[...]), patch)
    for j in range(3):
        pv = patch[:, :, :, pl.ds(768 * j, 768)].reshape(ROWS, 768)
        sh.store(place, refs, start + 128 + 768 * j, dot_tn(flat(dlog[...]), pv))
    sh.store(place, refs, start, dot_tn(flat(diff[...]), flat(dsq[...])))


def fetch_all(moves, refs, bufs):
    return [moves.fetch(r, b) for r, b in zip(refs, bufs)]


def branch_grad_kernel(sh, place, dlog, dsq, sq_ref, diff_ref, *rest):
    refs, (sq, diff, patch), bufs = rest[: sh.count], rest[sh.count : -1 - sh.count], rest[-1 - sh.count : -1]
    moves = Moves(rest[-1])
    wait_all(fetch_all(moves, (sq_ref, diff_ref), (sq, diff)))
    branch_grad(sh, place, (refs, bufs, moves), 0, dlog, sq, diff, dsq, patch)
    moves.finish()


def all_grad_kernel(sh, place, d2, dlog, dsq, d3_ref, mid_ref, mix_ref, sq_ref, diff_ref, *rest):
    refs, (d3, mid, mixp, sq, diff, patch) = rest[: sh.count], rest[sh.count : -1 - sh.count]
    bufs, moves = rest[-1 - sh.count : -1], Moves(rest[-1])
    out = (refs, bufs, moves)
    mix_load = moves.fetch(mix_ref, mixp)
    loads = fetch_all(moves, (sq_ref, diff_ref, d3_ref, mid_ref), (sq, diff, d3, mid))
    mix_load.wait()
    middle_grad(sh, place, out, 2432, d2, mixp)
    wait_all(loads)
    wide_grad(sh, place, out, 7040, d3, mid)
    branch_grad(sh, place, out, 0, dlog, sq, diff, dsq, patch)
    moves.finish()


def mixed_grad_kernel(sh, place, d3, mid_ref, d1, x_ref, *rest):
    refs, (mid, x), bufs = rest[: sh.count], rest[sh.count : -1 - sh.count], rest[-1 - sh.count : -1]
    moves = Moves(rest[-1])
    wait_all(fetch_all(moves, (mid_ref, x_ref), (mid, x)))
    wide_grad(sh, place, (refs, bufs, moves), 0, d3, mid)
    first_grad(sh, place, (refs, bufs, moves), 2048, d1, x)
    moves.finish()


def second_back_kernel(rows_total, sh, place, dn2, second_ref, mv2_ref, g, g_other, gb_ref, *rest):
    if sh is not None:
        mix_ref, refs, rest = rest[0], rest[1 : 1 + sh.count], rest[1 + sh.count :]
        d2, s2_ref, second, mixp, *bufs, sems = rest
    else:
        d2, s2_ref, second, sems = rest
    moves = Moves(sems)
    second_loads = moves.chunks_of(second_ref, second)
    if sh is not None:
        mix_load = moves.fetch(mix_ref, mixp)
    s2_ref[...] = merge_sums([g, g_other], OWN_ROWS)
    own = own_lines(512)
    mean2 = per_line(mv2_ref[0:3])
    inv2 = lax.rsqrt(per_line(mv2_ref[4:7]) + EPS)
    k2 = inv2 * gb_ref[2:3] * own
    dh2 = per_line(s2_ref[0:3]) / rows_total
    dg2 = per_line(s2_ref[4:7]) / rows_total
    for i, rows in enumerate(CHUNKS):
        second_loads[i].wait()
        xh = (second[rows] - mean2[None]) * inv2[None]
        d2[rows] = (k2[None] * (dn2[rows] - dh2[None] - xh * dg2[None])).astype(BF16)
    if sh is not None:
        mix_load.wait()
        middle_grad(sh, place, (refs, bufs, moves), 0, d2, mixp)
    moves.finish()


def middle_back_kernel(wt, place, d2, a_ref, mv1_ref, gb_ref, msk_ref, op_ref, *rest):
    refs = rest[: wt.count]
    (
        dn1, stb_ref, dlog, dsq_out,
        sq_buf, nf_buf, mid_buf, d2p, a, op, dmix, dsq, sems,
    ) = rest[wt.count :]
    moves = Moves(sems)
    mid_copies = wt.copies("mid", place, refs, mid_buf, moves)
    late_loads = [moves.fetch(a_ref, a), moves.fetch(op_ref, op)]
    nf_copies = wt.copies("nf", place, refs, nf_buf, moves)
    sq_copies = wt.copies("sq", place, refs, sq_buf, moves)
    clear_border(d2p)
    for i, rows in enumerate(CHUNKS):
        d2p[i + 1, 1:8] = d2[rows]
    wait_all(mid_copies)

    total = 0.0
    for k in range(9):
        y, x = 2 - k // 3, 2 - k % 3
        v = d2p[y : y + SIDE, x : x + SIDE].reshape(ROWS, 512)
        total = total + dot(v, mid_buf[..., pl.ds(512 * k, 512)].reshape(512, 512))
    dmix[...] = total.reshape(PIX, LINE, 512)
    wait_all(late_loads)
    mean1 = per_line(mv1_ref[0:3])
    inv1 = lax.rsqrt(per_line(mv1_ref[4:7]) + EPS)
    gain1, bias1 = gb_ref[0:1], gb_ref[1:2]

    def log_chunk(i, c):
        rows = pl.ds(i * SIDE, SIDE)
        n1 = (a[rows] - mean1[None]) * inv1[None] * gain1[None] + bias1[None]
        h = n1 * sigmoid(n1)
        o = op[rows].astype(F32)
        dlog[rows] = (dmix[rows] * h * o * (1.0 - o)).astype(BF16)
        return c

    chunks(log_chunk)
    wait_all(nf_copies)
    dsq[...] = jnp.zeros(dsq.shape, F32)
    for k in (1, 2):
        for ty in range(3):
            w = nf_buf[..., pl.ds(((k - 1) * 9 + ty * 3) * 128, 384)].reshape(512, 384)
            res = dot(flat(dlog[...]), w).reshape(SIDE, SIDE, LINE, 384)
            for tx in range(3):
                dy, dx = k * (ty - 1), k * (tx - 1)
                (y0, y1), (x0, x1) = tap_ranges(dy), tap_ranges(dx)
                dsq[y0 + dy : y1 + dy, x0 + dx : x1 + dx] += res[
                    y0:y1, x0:x1, :, 128 * tx : 128 * tx + 128
                ]
    dsq_low = dsq[...].astype(BF16).reshape(ROWS, 128)
    dsq_out[...] = dsq_low.reshape(PIX, LINE, 128)
    wait_all(sq_copies)
    dn1[...] = dot_nt(dsq_low, sq_buf[...].reshape(512, 128)).reshape(PIX, LINE, 512)
    m = msk_ref[:, 0:1]

    def last_chunk(i, carry):
        rows = pl.ds(i * SIDE, SIDE)
        xh = (a[rows] - mean1[None]) * inv1[None]
        n1 = xh * gain1[None] + bias1[None]
        sg = sigmoid(n1)
        e = dn1[rows] * m[None]
        o = op[rows].astype(F32)
        dhid = dmix[rows] * (0.5 + o) - e + pltpu.roll(e, 1, 1)
        dn = dhid * (sg * (1.0 + n1 * (1.0 - sg)))
        dn1[rows] = dn
        return carry[0] + jnp.sum(dn, axis=0), carry[1] + jnp.sum(dn * xh, axis=0)

    zero = jnp.zeros((LINE, 512), F32)
    spread(sums_of(*chunks(last_chunk, (zero, zero))), stb_ref)


def first_d1(rows_total, place, loads, dn1, dn1_other, a, mv1_ref, s1_ref, gb_ref, d1):
    own = own_lines(512)
    r = line_of(512)
    first = ((r == 0) | (r == 5) | (r == 10)) & (place[0] == 1)
    mean = per_line(mv1_ref[0:3])
    inv = lax.rsqrt(per_line(mv1_ref[4:7]) + EPS)
    k = inv * gb_ref[0:1] * own
    dh = per_line(s1_ref[0:3]) / rows_total
    dg = per_line(s1_ref[4:7]) / rows_total
    for i, rows in enumerate(CHUNKS):
        loads[i].wait()
        xh = (a[rows] - mean[None]) * inv[None]
        dn = dn1[rows] + jnp.where(first[None], pltpu.roll(dn1_other[rows], LINE - 4, 1), 0.0)
        d1[rows] = (k[None] * (dn - dh[None] - xh * dg[None])).astype(BF16)


def first_back_kernel(
    rows_total, wt, place, dn1, other, a_ref, mv1_ref, g, g_other, gb_ref, dz_ref, slope_ref, xhat_ref, *rest
):
    refs = rest[: wt.count]
    (
        dx_ref, d1, s1_ref, below, keep_ref, send_ref,
        w_buf, a, dz, slope, xhat, dx, sums_ref, sems,
    ) = rest[wt.count :]
    moves = Moves(sems)
    loads = moves.chunks_of(a_ref, a)
    copies = wt.copies("in", place, refs, w_buf, moves)
    tiles = [moves.tiles_of(r, b) for r, b in ((dz_ref, dz), (slope_ref, slope), (xhat_ref, xhat))]
    s1_ref[...] = merge_sums([g, g_other], OWN_ROWS)
    first_d1(rows_total, place, loads, dn1, other, a, mv1_ref, s1_ref, gb_ref, d1)
    wait_all(copies)
    for j, lanes in enumerate(TILES):
        wait_all([load[j] for load in tiles])
        w = w_buf[..., lanes].reshape(512, 512)
        v = dot(flat(d1[...]), w).reshape(PIX, LINE, 512) + dz[:, :, lanes].astype(F32)
        low = v.astype(BF16)
        dx[:, :, lanes] = low
        d = low.astype(F32) * slope[:, :, lanes].astype(F32)
        below[:, :, lanes] = d.astype(BF16)
        moves.store(dx.at[:, :, lanes], dx_ref.at[:, :, lanes])
        sums_ref[:, lanes] = sums_of(
            jnp.sum(d, axis=0), jnp.sum(d * xhat[:, :, lanes].astype(F32), axis=0)
        )
    split_wide(place, sums_ref, keep_ref, send_ref)
    moves.finish()


def first_grad(sh, place, out, start, d1, x_ref):
    for j in range(4):
        x = flat(x_ref[:, :, pl.ds(512 * j, 512)])
        sh.store(place, out, start + 512 * j, dot_tn(flat(d1[...]), x))


def last_grad_kernel(rows_total, sh, place, dn1, other, a_ref, mv1_ref, g, g_other, gb_ref, x_ref, *rest):
    refs, rest = rest[: sh.count], rest[sh.count :]
    d1, s1_ref, a, x, *bufs, sems = rest
    moves = Moves(sems)
    loads = moves.chunks_of(a_ref, a)
    x_load = moves.fetch(x_ref, x)
    s1_ref[...] = merge_sums([g, g_other], OWN_ROWS)
    first_d1(rows_total, place, loads, dn1, other, a, mv1_ref, s1_ref, gb_ref, d1)
    x_load.wait()
    first_grad(sh, place, (refs, bufs, moves), 0, d1, x)
    moves.finish()


def last_back_kernel(wt, place, d1, dz_ref, *rest):
    refs, (dx_ref, w_buf, dz, dx, sems) = rest[: wt.count], rest[wt.count :]
    moves = Moves(sems)
    copies = wt.copies("in", place, refs, w_buf, moves)
    loads = moves.tiles_of(dz_ref, dz)
    wait_all(copies)
    for j, lanes in enumerate(TILES):
        loads[j].wait()
        w = w_buf[..., lanes].reshape(512, 512)
        v = dot(flat(d1[...]), w).reshape(PIX, LINE, 512) + dz[:, :, lanes].astype(F32)
        dx[:, :, lanes] = v.astype(BF16)
        moves.store(dx.at[:, :, lanes], dx_ref.at[:, :, lanes])
    moves.finish()


VM = pl.BlockSpec(memory_space=pltpu.VMEM)
HB = pl.BlockSpec(memory_space=pltpu.HBM)
SM = pl.BlockSpec(memory_space=pltpu.SMEM)
AN = pl.BlockSpec(memory_space=pl.ANY)


class Near:
    def __init__(self, value):
        self.value = value


class Near2(Near):
    pass


def is_big(shape):
    return len(shape) >= 4 or (len(shape) == 3 and shape[0] in (PIX, 3))


def size_of(shape, dtype):
    size = jnp.dtype(dtype).itemsize
    for k in shape:
        size *= k
    return size


def call(kernel, outs, scratch=(), us=5):
    def run(place, *values):
        specs = [SM]
        need = 6 * 1024 * 1024
        need += sum(size_of(v.shape, v.dtype) for v in scratch)
        need += sum(size_of(*o[:2]) for o in outs if not (is_big(o[0]) and len(o) == 2))
        for v in values:
            u = v.value if isinstance(v, Near) else v
            if not is_big(u.shape) or (isinstance(v, Near) and not isinstance(v, Near2)):
                need += size_of(u.shape, u.dtype)
        for v in values:
            if isinstance(v, Near):
                specs.append(AN if isinstance(v, Near2) else VM)
            else:
                specs.append(HB if is_big(v.shape) else VM)
        return pl.pallas_call(
            kernel,
            in_specs=specs,
            out_specs=tuple(HB if is_big(o[0]) and len(o) == 2 else VM for o in outs),
            out_shape=tuple(jax.ShapeDtypeStruct(o[0], o[1]) for o in outs),
            scratch_shapes=list(scratch) + [pltpu.SemaphoreType.DMA((96,))],
            compiler_params=pltpu.CompilerParams(vmem_limit_bytes=52 * 1024 * 1024),
            cost_estimate=pl.CostEstimate(flops=us * 10**9, bytes_accessed=us * 3 * 10**6, transcendentals=0),
        )(place, *[v.value if isinstance(v, Near) else v for v in values])

    return run


def near(width, dtype):
    return ((PIX, LINE, width), dtype, True)


def pm(width, dtype):
    return ((PIX, LINE, width), dtype)


def buf(width, dtype):
    return pltpu.VMEM((PIX, LINE, width), dtype)


def wbuf(width):
    return pltpu.VMEM((4, 2, 2, 2, 16, width), BF16)


STAT = ((8, 512), F32)
WIDE_STAT = ((8, 2048), F32)
PAIR = [(0, 1), (1, 0)]


class Links:
    def __init__(self, dp, core):
        self.dp, self.core = dp, core
        self.at = lax.axis_index("dp")

    def bit(self, k):
        return (self.at // k) % 2

    def place(self):
        y, x = (self.bit(2), self.bit(1)) if self.split else (0, 0)
        return jnp.stack([self.core, jnp.int32(y), jnp.int32(x)]).astype(jnp.int32)

    split = True

    def swap(self, v):
        return lax.ppermute(v, "pipe", PAIR)

    def across(self, v, k):
        return lax.ppermute(v, "dp", [(i, i ^ k) for i in range(self.dp)])

    def to_all(self, spread, *meanwhile):
        g = lax.all_to_all(spread, "dp", 0, 0)
        if meanwhile:
            g = after(g, *meanwhile)
        return g, self.swap(g)

    def by_core(self, own, other):
        first = self.core == 0
        return jnp.where(first, own, other), jnp.where(first, other, own)

    def in_order(self, which, own, other, axis):
        pair = jnp.where(which == 0, jnp.stack([own, other], axis), jnp.stack([other, own], axis))
        return pair

    def halves(self, piece):
        two = piece.reshape(2, 16, piece.shape[1])
        keep = lax.dynamic_index_in_dim(two, self.core, 0, keepdims=False)
        recv = self.swap(lax.dynamic_index_in_dim(two, 1 - self.core, 0, keepdims=False))
        return self.by_core(keep, recv)

    def gather_first(self, v, cut):
        p, q = v[..., :cut], v[..., cut:]
        p_other, q_other = self.across(p, 1), self.across(q, 2)
        return self.in_order(self.bit(1), p, p_other, 1), self.in_order(self.bit(2), q, q_other, 1)

    def gather_second(self, p, q):
        mine = (p, self.across(p, 2), q, self.across(q, 1))
        return mine + tuple(self.swap(v) for v in mine)

    def gather_whole(self, own):
        return lax.all_gather(own, "dp").reshape(4, 2, 2, 16, -1)

    def gather_blocks(self, gains, inner, rest, wide, permute, clips, cotangent):
        rows = jnp.concatenate([jnp.pad(v, ((0, 0), (0, 128 - v.shape[1]))) for v in gains], axis=0)
        tail = jnp.pad(rows, ((0, 32 - rows.shape[0]), (0, 0)))
        a = self.halves(jnp.concatenate([inner, tail], axis=1))
        b, c = self.halves(rest), self.halves(self.narrow_rows(wide))
        b0 = self.gather_whole(b[0])
        v = after(a[0], b[0])
        v = self.in_order(self.bit(8), v, self.across(v, 8), 0)
        x = permute(after(clips, v, b[0]))
        moved = after(self.across(v, 4), x)
        v = self.in_order(self.bit(4), v, moved, 1).reshape(4, 16, -1)
        ca = jnp.concatenate([c[0], a[1]], axis=1)
        ca = self.in_order(self.bit(8), ca, self.across(after(ca, v), 8), 0)
        dy = permute(after(cotangent, v))
        moved = after(self.across(ca, 4), dy)
        ca = self.in_order(self.bit(4), ca, moved, 1).reshape(4, 16, -1)
        a0 = self.gather_second(*self.gather_first(v, 1024))
        block_0 = {"A": (Weights("split", SPLIT_A), a0)}
        return (block_0, (ca, b0, jnp.concatenate([c[1], b[1]], axis=1))), x, dy

    def gather_middle(self, blocks, pieces, then):
        block_0, (_, b0, bc) = blocks
        ca = self.gather_second(*pieces)
        block_0["C"] = (Weights("split", SPLIT_C), ca)
        b0 = after(b0, then)
        block_0["B"] = (Weights("whole", middle_at(0)), (b0, self.swap(b0)))
        return block_0, (ca, self.gather_whole(after(bc, b0)))

    def gather_last(self, blocks, third):
        block_0, (ca, bc) = blocks
        bc = after(bc, third)
        bc = (bc, self.swap(bc))
        return block_0, {
            "A": (Weights("split", SPLIT_A1), ca),
            "B": (Weights("whole", middle_at(2048)), bc),
            "C": (Weights("whole", wide_at(0)), bc),
        }

    def gains_of(self, group, place):
        wt, refs = group
        return call(functools.partial(gains_kernel, wt), [STAT, WIDE_STAT], [wbuf(128)])(place, *refs)

    def add(self, a, b):
        return (a.astype(F32) + b.astype(F32)).astype(BF16)

    def halve(self, v, axis, k, then=None):
        which = self.bit(k)
        keep = lax.dynamic_index_in_dim(v, which, axis, keepdims=False)
        send = lax.dynamic_index_in_dim(v, 1 - which, axis, keepdims=False)
        moved = self.across(send, k)
        if then is not None:
            moved = after(moved, then)
        return self.add(keep, moved)

    def scatter_first(self, g):
        return [self.add(g[k], self.swap(g[k + 2])) for k in (1, 5)]

    def scatter_xy(self, g, sent, then=(None, None)):
        done = []
        for own, send_own, other, k in ((g[0], g[2], sent[0], 2), (g[4], g[6], sent[1], 1)):
            moved = self.across(other, k)
            if then[0] is not None:
                moved = after(moved, then[0])
            v = self.add(self.add(own, self.swap(send_own)), moved)
            done.append(self.halve(v, 1, 3 - k, then[1]))
        return jnp.concatenate(done, axis=-1)

    def scatter_z(self, v, then=(None, None)):
        half = self.halve(v.reshape(2, 2, 16, -1), 1, 4, then[0])
        return self.halve(half, 0, 8, then[1]), half

    def half_sums(self, keep, send):
        return self.add(keep, self.swap(send)).reshape(16, 16, -1)

    def scatter_whole(self, v):
        return lax.psum_scatter(v, "dp", scatter_dimension=0, tiled=True)[0]

    def scatter_at_once(self, v, *then):
        v = lax.all_to_all(v, "dp", 0, 0)
        if then:
            v = after(v, *then)
        return jnp.sum(v.astype(F32), axis=0)

    def handed(self, early, late):
        return lax.ppermute(early, "pipe", [(1, 0)]), lax.ppermute(late, "pipe", [(0, 1)])

    def to_owner(self, early, early_other, late, late_other):
        at_0 = jnp.concatenate([early, early_other], axis=0).astype(F32)
        at_1 = jnp.concatenate([late_other, late], axis=0).astype(F32)
        return jnp.where(self.core == 0, at_0, at_1)

    def wide_rows(self, v):
        return v.reshape(2, 16, 4, -1).transpose(0, 2, 1, 3).reshape(128, -1)

    def narrow_rows(self, v):
        return v.reshape(2, 4, 16, -1).transpose(0, 2, 1, 3).reshape(32, -1)


class AnyLinks(Links):
    split = False

    def gather_blocks(self, gains, inner, rest, wide, permute, clips, cotangent):
        full = [lax.all_gather(v, "dp", tiled=True) for v in (inner, wide, rest)]
        full[1] = jnp.stack([self.narrow_rows(f) for f in full[1].reshape(16, 128, -1)]).reshape(512, -1)
        own = jnp.concatenate(full, axis=1)
        vectors = [lax.all_gather(v, "dp", axis=1, tiled=True).astype(F32) for v in gains]
        mid = jnp.pad(jnp.concatenate(vectors[:4]), ((0, 4), (0, 0)))
        out = jnp.pad(jnp.concatenate(vectors[4:]), ((0, 6), (0, 0)))
        mids, outs = self.by_core(mid, self.swap(mid)), self.by_core(out, self.swap(out))
        blocks = []
        for s, full in enumerate(self.by_core(own, self.swap(own))):
            parts = full.reshape(16, 2, 16, -1)
            mine = lax.dynamic_index_in_dim(parts, self.core, 1, keepdims=False)
            theirs = lax.dynamic_index_in_dim(parts, 1 - self.core, 1, keepdims=False)
            refs = tuple(v.reshape(4, 2, 2, 16, -1) for v in (mine, theirs))
            groups = (("A", {"in": [("W", 0, 0, 2048)]}), ("B", middle_at(4096)), ("C", wide_at(2048)))
            blocks.append({k: (Weights("whole", v), refs) for k, v in groups})
            blocks[s]["gains"] = (mids[s], outs[s])
        return blocks, permute(clips), permute(cotangent)

    def gather_middle(self, blocks, pieces, then):
        return blocks

    def gather_last(self, blocks, third):
        return blocks

    def gains_of(self, group, place):
        return group

    def scatter_pairs(self, early, late, wide):
        full = []
        for keep, send in (early, late):
            half = self.add(keep, self.swap(send)).reshape(16, 16, -1)
            full.append(jnp.stack(self.by_core(half, self.swap(half)), axis=1))
        total = jnp.where(self.core == 0, full[0], full[1])
        if wide:
            total = jnp.stack([self.wide_rows(v.reshape(32, -1)) for v in total])
        total = total.reshape(-1, total.shape[-1])
        return lax.psum_scatter(total, "dp", scatter_dimension=0, tiled=True).astype(F32)


def after(v, *others):
    return lax.optimization_barrier((v, others))[0]


SPLIT_A = {"in": [("P", 0, 0, 1024), ("Q", 0, 1024, 1024)], "gain": [("Q", 1024, 0, 128)]}
SPLIT_C = {"out": [("P", 512 * g, (g,), 512) for g in range(4)]}
SPLIT_A1 = {"in": [("Q", 0, 0, 2048)], "gain": [("Q", 2048, 0, 128)]}


def middle_at(first):
    return {
        "sq": [("W", first, 0, 128)],
        "nf": [("W", first + 128, 0, 2304)],
        "mid": [("W", first + 2432, 0, 4608)],
    }


def wide_at(first):
    return {"out": [("W", first + 512 * g, (g,), 512) for g in range(4)]}


def local(
    clips_in, cotangent, segment_ids, w_in, w_squeeze, w_near, w_far, w_mid, w_out,
    gain_mid, bias_mid, gain_out, bias_out,
):
    dp = lax.axis_size("dp")
    core = lax.axis_index("pipe")
    links = (Links if dp == 16 else AnyLinks)(dp, core)
    place = links.place()
    rows_total = float(clips_in.shape[1] * dp)

    def low(v):
        return v[0].astype(BF16)

    n = w_in.shape[2]
    gain_rows = [low(gain_mid)[0:1], low(bias_mid)[0:1], low(gain_mid)[1:2], low(bias_mid)[1:2]]
    def permute(v):
        scratch = [pltpu.VMEM((3, SEG * PIX, 2048), BF16), buf(2048, BF16)]
        return call(permute_kernel, [pm(2048, BF16)], scratch)(place, v)[0]

    gathered, x0, dy = links.gather_blocks(
        gain_rows + [low(gain_out)[None], low(bias_out)[None]],
        low(w_in).T,
        jnp.concatenate([low(w_squeeze), low(w_near).T, low(w_far).T, low(w_mid).T], axis=1),
        low(w_out).T,
        permute, clips_in, cotangent,
    )

    def gains_of(s):
        return links.gains_of(gathered[s]["A" if links.split else "gains"], place)

    gains = [gains_of(0)]

    same = (segment_ids[:, 0, 1:] == segment_ids[:, 0, :-1]).astype(F32)
    same = jnp.concatenate([same, jnp.zeros((3, 1), F32)], axis=1)
    mine_seg = lax.dynamic_slice_in_dim(same, core * HALF, HALF, 1)
    msk = jnp.concatenate([mine_seg, jnp.zeros((3, 1), F32)], axis=1).reshape(15)
    msk = jnp.broadcast_to(jnp.concatenate([msk, jnp.zeros((1,), F32)])[:, None], (LINE, 128))


    wide_buf = pltpu.VMEM((4, 2, 2, 2, 4, 16, 512), BF16)

    stb = ((dp, 8, 384), F32)
    half_stat = ((8, 1024), F32)
    buffers = {"in": wbuf(2048), "sq": wbuf(128), "nf": wbuf(2304), "mid": wbuf(4608), "out": wide_buf}
    groups = {"A": ("in",), "B": ("sq", "nf", "mid"), "C": ("out",)}

    def kernel(body, group, values, outs, scratch, *static):
        wt, refs = group[1]
        names = groups[group[0]]
        refs = [Near2(v) if names == ("out",) and wt.kind == "split" else v for v in refs]
        return call(functools.partial(body, *static, wt), outs, [buffers[k] for k in names] + scratch)(
            place, *values, *refs
        )

    def group(s, k):
        return k, gathered[s][k]

    wide_sums = pltpu.VMEM((8, 2048), F32)
    lines = pltpu.VMEM((3, LINE, 2048), F32)
    padded = pltpu.VMEM((9, 9, LINE, 512), BF16)
    patch = pltpu.VMEM((SIDE, SIDE, LINE, 2304), BF16)

    def first(s, x):
        return kernel(first_kernel, group(s, "A"), [Near(x)], [near(512, F32), stb], [])

    def middle(s, a, other, *values):
        outs = [pm(512, F32), pm(512, BF16), pm(128, BF16), pm(512, BF16),
                ((9, 9, LINE, 512), BF16), near(512, F32), pm(512, F32), stb, STAT]
        scratch = [buf(512, F32), buf(512, BF16), buf(128, BF16), buf(512, BF16), padded, buf(512, F32), patch]
        return kernel(middle_kernel, group(s, "B"), [Near(a), Near(other), *values], outs, scratch)

    def widen(s, second, *values):
        outs = [pm(512, BF16), half_stat, half_stat, STAT]
        scratch = [buf(512, BF16), buf(512, F32), wide_sums]
        return kernel(wide_kernel, group(s, "C"), [Near(second), *values], outs, scratch)

    def turn(mid, *values):
        outs = [pm(2048, BF16)] * 3 + [near(512, F32), stb, WIDE_STAT]
        wide_wt, wide_refs = gathered[0]["C"]
        scratch = [buf(512, F32)] + [buf(2048, BF16)] * 4
        wt, refs = gathered[1]["A"]
        return call(
            functools.partial(turn_kernel, wide_wt, wt), outs, [wide_buf, buffers["in"]] + scratch
        )(place, Near(mid), *values, *[Near2(v) for v in wide_refs], *refs)

    def top(mid, *values):
        outs = [pm(2048, BF16)] * 2 + [near(2048, BF16), half_stat, half_stat, WIDE_STAT]
        wide_wt, wide_refs = gathered[1]["C"]
        scratch = [wide_buf, buf(512, F32)] + [buf(2048, BF16)] * 4 + [wide_sums]
        return call(functools.partial(top_kernel, wide_wt), outs, scratch)(
            place, Near(mid), *values, *wide_refs
        )

    def pairs(norm, keep, send, *meanwhile):
        recv = links.swap(send)
        v = pl.pallas_call(
            functools.partial(pair_kernel, norm), in_specs=[VM, VM], out_specs=VM,
            out_shape=jax.ShapeDtypeStruct((dp, 8, 768), F32),
            compiler_params=pltpu.CompilerParams(vmem_limit_bytes=8 * 1024 * 1024),
        )(keep, recv)
        return links.to_all(v, *meanwhile)

    def wide_back(s, dz, *values):
        outs = [near(512, F32), stb, pm(2048, BF16), WIDE_STAT]
        scratch = [buf(2048, BF16), buf(512, F32), buf(2048, BF16), lines]
        return kernel(wide_back_kernel, group(s, "C"), [Near(dz), *values], outs, scratch, rows_total)

    def second_back(sh, dn2, *values):
        outs = [near(512, BF16), STAT]
        scratch = [buf(512, F32)]
        if sh:
            outs, scratch = sh.outs() + outs, scratch + [padded] + sh.buffers()
        return call(functools.partial(second_back_kernel, rows_total, sh), outs, scratch)(
            place, Near(dn2), *values
        )

    def middle_back(s, d2, *values):
        outs = [near(512, F32), stb, near(512, BF16), near(128, BF16)]
        scratch = [padded, buf(512, F32), buf(512, BF16), buf(512, F32), pltpu.VMEM((SIDE, SIDE, LINE, 128), F32)]
        return kernel(middle_back_kernel, group(s, "B"), [Near(d2), *values], outs, scratch)

    def first_back(dn1, other, *values):
        outs = [pm(2048, BF16), near(512, BF16), STAT, near(2048, BF16), half_stat, half_stat]
        scratch = [buf(512, F32)] + [buf(2048, BF16)] * 4 + [wide_sums]
        return kernel(
            first_back_kernel, group(1, "A"), [Near(dn1), Near(other), *values], outs, scratch, rows_total
        )

    def last_grad(sh, dn1, other, *values):
        scratch = [buf(512, F32), buf(2048, BF16)] + sh.buffers()
        return call(
            functools.partial(last_grad_kernel, rows_total, sh), sh.outs() + [near(512, BF16), STAT], scratch
        )(place, Near(dn1), Near(other), *values)

    def last_back(d1, *values):
        scratch = [buf(2048, BF16), buf(2048, BF16)]
        return kernel(last_back_kernel, group(0, "A"), [Near(d1), *values], [pm(2048, BF16)], scratch)[0]

    def shares_of(kind, *parts):
        return Shares(kind if links.split else "whole", parts)

    def grad(body, sh, values, *scratch):
        bufs = [pltpu.VMEM(v.shape, v.dtype) for v in values if not isinstance(v, Near)]
        return call(
            functools.partial(body, sh), sh.outs(), bufs + list(scratch) + sh.buffers()
        )(place, *values)

    restore = call(
        restore_kernel, [((3, SEG * PIX, 2048), BF16)],
        [pltpu.VMEM((2, PIX, LINE, 2048), BF16), pltpu.VMEM((3, SEG * PIX, 2048), BF16)],
    )

    def crossed(early, late):
        return lax.ppermute(early, "pipe", [(1, 0)]), lax.ppermute(late, "pipe", [(0, 1)])

    kept = []
    x = x0
    if links.split:
        x = after(x, gathered[1][0])
    a, st = first(0, x)
    for s in range(2):
        gb, gbo = gains[s]
        if s == 0:
            pieces = links.gather_first(after(gathered[1][0], a), 2048) if links.split else ()
            sums = links.to_all(st, dy, *pieces, gb)
            gathered = links.gather_middle(gathered, pieces, sums[0])
        else:
            sums = links.to_all(st, gb)
        a, diff, sq, op, mix, second, second_far, st, mv1 = middle(s, a, links.swap(a), *sums, gb, msk)
        mid, keep, send, mv2 = widen(s, second, *links.to_all(st), gb)
        stats = pairs(True, keep, send)
        if s == 0:
            if links.split:
                gathered = (gathered[0], {"A": (Weights("split", SPLIT_A1), gathered[1][0])}, gathered[1])
                gains.append(gains_of(1))
            act0, xhat, slope0, a_next, st, mv3 = turn(mid, x, *stats, gbo)
            if links.split:
                gathered = links.gather_last((gathered[0], gathered[2]), a_next)
            else:
                gains.append(gains_of(1))
        else:
            act1, xhat, dz, keep, send, mv3 = top(mid, x, *stats, gbo, dy)
        kept.append((x, a, mv1, diff, sq, op, mix, second_far, mv2, mid, xhat, mv3))
        if s == 0:
            x, a = act0, a_next

    gb, gbo = gains[1]
    x, a, mv1, diff, sq, op, mix, second, mv2, mid, xhat, mv3 = kept[1]
    dn2, st, d3, s3 = wide_back(
        1, dz, xhat, mv3, *pairs(False, keep, send), gbo, second, mv2, gb
    )
    d2, s2 = second_back(None, dn2, second, mv2, *links.to_all(st), gb)
    dn1, st, dlog, dsq = middle_back(1, d2, a, mv1, gb, msk, op)
    g_rest = grad(
        all_grad_kernel, shares_of("whole", 2432, 4608, 2048),
        [Near(d2), Near(dlog), Near(dsq), d3, mid, mix, sq, diff], patch,
    )
    split = links.split
    sums = links.to_all(st, *g_rest)
    dx1, d1_late, s1, dz, keep, send = first_back(
        dn1, links.swap(dn1), a, mv1, *sums, gb, dz, slope0, kept[0][10]
    )
    meanwhile = []
    if split:
        late = links.half_sums(g_rest[0], after(g_rest[1], sums[0]))
        keep = after(keep, late)
        late = links.scatter_whole(late)
    norms_1 = (s1, s2, s3)
    x_late = x

    gb, gbo = gains[0]
    x, a, mv1, diff, sq, op, mix, second, mv2, mid, xhat, mv3 = kept[0]
    dn2, st, d3, s3 = wide_back(
        0, dz, xhat, mv3, *pairs(False, keep, send, *meanwhile), gbo, second, mv2, gb
    )
    g_mixed = grad(
        mixed_grad_kernel, shares_of("whole", 4096), [Near(d3), mid, Near(d1_late), x_late]
    )
    *g_mid, d2, s2 = second_back(
        shares_of("split", 2048, 2560), dn2, second, mv2, *links.to_all(st, *g_mixed), gb, mix
    )
    dn1, st, dlog, dsq = middle_back(0, d2, a, mv1, gb, msk, op)
    if split:
        sent = links.scatter_first(g_mid)
        mixed = links.half_sums(*g_mixed)
        dlog = after(dlog, mixed, *sent)
        mixed = links.scatter_whole(mixed)
    g_branch = grad(branch_grad_kernel, shares_of("whole", 2432), [Near(dlog), Near(dsq), sq, diff], patch)
    meanwhile = g_branch
    if split:
        rest_0 = [links.half_sums(*g_branch)]
    *g_in, d1, s1 = last_grad(
        shares_of("whole", 2048), dn1, links.swap(dn1), a, mv1, *links.to_all(st, *meanwhile), gb, x
    )
    norms_0 = (s1, s2, s3)
    if split:
        last = jnp.concatenate([links.half_sums(*g_in), *rest_0], axis=-1)
        dx0 = last_back(after(d1, last), dz)
        act0, act1 = after((act0, act1), last)
        early = links.scatter_xy(g_mid, sent, (d1, None))
        activations = restore(place, act0, act1, *crossed(act0, act1))[0]
        input_grads = restore(place, after(dx0, activations), dx1, *crossed(dx0, dx1))[0]
        mid_0, _ = links.scatter_z(early, (input_grads, None))
        last = links.scatter_at_once(last, input_grads, mid_0)
        in_0, branch_0 = jnp.split(last, [2048], axis=-1)
        mixed = after(mixed, late)
        out_0, in_1 = jnp.split(mixed, 2, axis=-1)
        branch_1, mid_1, out_1 = jnp.split(late, [2432, 7040], axis=-1)
        mid_other, late_other = links.handed(mid_0, late)
        branch_1o, mid_1o, out_1o = jnp.split(late_other, [2432, 7040], axis=-1)
        out_0o, in_1o = links.handed(out_0, in_1)
        in_0o, branch_0o = jnp.split(lax.ppermute(last, "pipe", [(1, 0)]), [2048], axis=-1)
        f_in = links.to_owner(in_0, in_0o, in_1, in_1o)
        f_branch = links.to_owner(branch_0, branch_0o, branch_1, branch_1o)
        f_mid = links.to_owner(mid_0, mid_other, mid_1, mid_1o)
        f_out = links.wide_rows(links.to_owner(out_0, out_0o, out_1, out_1o))
    else:
        activations = restore(place, act0, act1, *crossed(act0, act1))[0]
        dx0 = last_back(d1, dz)
        input_grads = restore(place, dx0, dx1, *crossed(dx0, dx1))[0]
        rest = [v[..., :2432] for v in g_rest], [v[..., 2432:7040] for v in g_rest], [v[..., 7040:] for v in g_rest]
        f_branch = links.scatter_pairs(g_branch, rest[0], False)
        f_mid = links.scatter_pairs(g_mid, rest[1], False)
        g_out, in_1 = [v[..., :2048] for v in g_mixed], [v[..., 2048:] for v in g_mixed]
        f_out = links.scatter_pairs(g_out, rest[2], True)
        f_in = links.scatter_pairs(g_in, in_1, False)

    grad_w_in = f_in.T[None]
    grad_w_squeeze = f_branch[:, :128][None]
    grad_w_near = f_branch[:, 128:1280].T[None]
    grad_w_far = f_branch[:, 1280:].T[None]
    grad_w_mid = f_mid.T[None]
    grad_w_out = f_out.T[None]

    s1, s2, s3 = [jnp.where(core == 0, e, l) for e, l in zip(norms_0, norms_1)]
    dp_index = lax.axis_index("dp")
    mid_sums = jnp.stack(
        [jnp.stack([s1[0:3].sum(0), s2[0:3].sum(0)]), jnp.stack([s1[4:7].sum(0), s2[4:7].sum(0)])]
    )
    mid_sums = lax.dynamic_slice_in_dim(mid_sums, dp_index * n, n, 2)
    out_sums = jnp.stack([s3[0:3].sum(0), s3[4:7].sum(0)])
    out_sums = lax.dynamic_slice_in_dim(out_sums, dp_index * 4 * n, 4 * n, 1)
    return (
        activations[None], input_grads[None], grad_w_in, grad_w_squeeze, grad_w_near, grad_w_far,
        grad_w_mid, grad_w_out, mid_sums[1][None], mid_sums[0][None], out_sums[1][None],
        out_sums[0][None],
    )


def solution(mesh):
    split = P("pipe", None, "dp")
    rows = P("pipe", "dp", None)
    vec = P("pipe", "dp")
    clips = P(None, "dp", None)
    weights = (split, rows, split, split, split, split, split, split, vec, vec)
    whole = P("pipe", None, "dp", None)
    return jax.shard_map(
        local,
        mesh=mesh,
        in_specs=(clips, clips, clips) + weights,
        out_specs=(whole, whole) + weights,
        check_vma=False,
    )
```

time: 735 us -> 681 us (0.927)
  waiting for transfers between devices: 210 us -> 136 us
  Pallas kernels: 201 us -> 246 us
  local copies, waits for them, and re-layouts: 78 us -> 34 us
  blocking collectives: 83.4 us -> 104 us
  starting transfers between devices: 109 us -> 101 us
    ppermute x30 -> x18, waiting for transfers between devices: 162 us -> 72.7 us  [across(): return lax.ppermute(v, 'dp', [(i, i ^ k) for i in range(self.dp)])]
    unnamed x285 -> x89, local copies, waits for them, and re-layouts: 66.1 us -> 18.2 us
    pallas_call x30 -> x29, Pallas kernels: 201 us -> 246 us  [the longest x25 246 us: run(): pl.pallas_call(kernel, in_specs=specs, out_specs=tuple((HB if is_big(o[0]...]
    all_to_all x6, blocking collectives: 83.4 us -> 104 us  [to_all(): g = lax.all_to_all(spread, 'dp', 0, 0)]
    ppermute x46 -> x41, waiting for transfers between devices: 18 us -> 38.8 us  [swap(): return lax.ppermute(v, 'pipe', PAIR)]
    ppermute x30 -> x18, starting transfers between devices: 48 us -> 30.4 us  [across(): return lax.ppermute(v, 'dp', [(i, i ^ k) for i in range(self.dp)])]
    convert_element_type x25 -> x12, other arithmetic: 17.7 us -> 17.5 us  [add(): return (a.astype(F32) + b.astype(F32)).astype(BF16)]
  transfers between devices with their start and end apart: 97 -> 79, of which waited for: 40 -> 32; matrix products, arithmetic and copies ran while one was open for 5% -> 6% of each run, Pallas kernels for 20% -> 27%
where the time goes in v2:
time: 681 us; the launch traced here: 669 us
  Pallas kernels  246 us (36%)
  waiting for transfers between devices  136 us (20%)
  blocking collectives  104 us (15%)
  starting transfers between devices  101 us (15%)
  local copies, waits for them, and re-layouts  34 us (5%)
  other arithmetic  31.7 us (5%)
  between operations  15.3 us (2%)
    pallas_call x25, Pallas kernels, run(): pl.pallas_call(kernel, in_specs=specs, out_specs=tuple((HB if is_big(o[0]...  246 us
    all_to_all x6, blocking collectives, to_all(): g = lax.all_to_all(spread, 'dp', 0, 0)  104 us
    ppermute x18, waiting for transfers between devices, across(): return lax.ppermute(v, 'dp', [(i, i ^ k) for i in range(self.dp)])  72.7 us
    ppermute x41, waiting for transfers between devices, swap(): return lax.ppermute(v, 'pipe', PAIR)  38.8 us
    all_to_all x6, starting transfers between devices, to_all(): g = lax.all_to_all(spread, 'dp', 0, 0)  34.9 us
    ppermute x18, starting transfers between devices, across(): return lax.ppermute(v, 'dp', [(i, i ^ k) for i in range(self.dp)])  30.4 us
    unnamed x89, local copies, waits for them, and re-layouts  18.2 us
    all_to_all x6, waiting for transfers between devices, to_all(): g = lax.all_to_all(spread, 'dp', 0, 0)  17.8 us
  transfers between devices with their start and end apart: 79, of which 32 were waited for; matrix products, arithmetic and copies ran while one was open for 6% of the time, Pallas kernels for 27%

profile of v2, /device:TPU:0, one launch (start us, length us, event | category | flops | bytes accessed | tf_op | source)
XLA Modules:
  0.0 669.0 jit_solution(3875926119694654180)
XLA Ops:
  17.0 4.0 collective-permute-start.2
  25.9 9.3 %shard_map.220.x_ref = bf16[49,16,2048]{2,1,0:T(8,128)(2,1)} custom-call(s32[3]{0:T(128)S(1)} %pad_add_fusion.core_ref.place, bf16[3,392,2048]{2,1,0:T(8,128)(2,1)} %x_ref), custom_call_target="tpu_custom_call" | custom-call | flops 5000000000 | bytes 15000000 | tf_op jit(solution)/shard_map/pallas_call | solution.py:884
  40.3 9.2 %shard_map.221.dy_ref = bf16[49,16,2048]{2,1,0:T(8,128)(2,1)} custom-call(s32[3]{0:T(128)S(1)} %pad_add_fusion.core_ref.place, bf16[3,392,2048]{2,1,0:T(8,128)(2,1)} %x_ref.1), custom_call_target="tpu_custom_call" | custom-call | flops 5000000000 | bytes 15000000 | tf_op jit(solution)/shard_map/pallas_call | solution.py:884
  51.9 6.2 collective-permute-done.9
  69.2 7.5 %shard_map.222 = (f32[49,16,512]{2,1,0:T(8,128)}, f32[16,8,384]{2,1,0:T(8,128)}) custom-call(s32[3]{0:T(128)S(1)} %pad_add_fusion.core_ref.place, bf16[49,16,2048]{2,1,0:T(8,128)(2,1)} %shard_map.220.x_ref, bf16[4,2,16,1024]{3,2,1,0:T(8,128)(2,1)S(1)} %copy.116.rest_0_, bf16[4,2,16,1024]{3,2,1,0:T(8,128)(2,1)S(1)} %copy.117.rest_1_, ...), custom_call_target="tpu_custom_call" | custom-call | flops 5000000000 | bytes 15000000 | tf_op jit(solution)/shard_map/pallas_call | solution.py:884
  76.8 4.3 all-to-all-start
  88.1 7.9 %collective-permute-done.16 = bf16[4,16,2048]{2,1,0:T(8,128)(2,1)S(1)} collective-permute-done((bf16[4,16,2048]{2,1,0:T(8,128)(2,1)S(1)}, bf16[4,16,2048]{2,1,0:T(8,128)(2,1)S(1)}, u32[]{:S(2)}, u32[]{:S(2)}) %collective-permute-start.16) | collective-permute-done | bytes 262176 | tf_op jit(solution)/shard_map/ppermute | solution.py:936
  97.8 6.5 all-gather.5.cloned.1.call-done
  107.1 4.1 collective-permute-done.18.g_other
  113.7 14.1 %shard_map.224 = (f32[49,16,512]{2,1,0:T(8,128)}, bf16[49,16,512]{2,1,0:T(8,128)(2,1)S(1)}, bf16[49,16,128]{2,1,0:T(8,128)(2,1)S(1)}, bf16[49,16,512]{2,1,0:T(8,...) custom-call(s32[3]{0:T(128)S(1)} %pad_add_fusion.core_ref.place, ...), custom_call_target="tpu_custom_call" | custom-call | flops 5000000000 | bytes 15000000 | tf_op jit(solution)/shard_map/pallas_call | solution.py:884
  130.0 4.9 all-to-all-start.1
  135.9 11.3 %all-to-all-done.1.g = f32[16,8,384]{2,1,0:T(8,128)S(1)} async-done(((f32[16,8,384]{2,1,0:T(8,128)}), f32[16,8,384]{2,1,0:T(8,128)S(1)}, u32[]{:S(2)}, u32[]{:S(2)}) %all-to-all-start.1) | async-done | bytes 196640 | tf_op jit(solution)/shard_map/all_to_all | solution.py:939
  153.4 7.4 %shard_map.225 = (bf16[49,16,512]{2,1,0:T(8,128)(2,1)}, f32[8,1024]{1,0:T(8,128)S(1)}, f32[8,1024]{1,0:T(8,128)S(1)}, f32[8,512]{1,0:T(8,128)S(1)}) custom-call(s32[3]{0:T(128)S(1)} %pad_add_fusion.core_ref.place, f32[49,16,512]{2,1,0:T(8,128)} %get-tuple-element.141.second, f32[16,8,384]{2,1,0:T(8,128)S(1)} %all-to-all-done.1.g, ...), custom_call_target="tpu_custom_call" | custom-call | flops 5000000000 | bytes 15000000 | tf_op jit(solution)/shard_map/pallas_call | solution.py:884
  162.3 24.2 %all_to_all.65.g = f32[16,8,768]{2,1,0:T(8,128)S(1)} all-to-all(f32[16,8,768]{2,1,0:T(8,128)S(1)} %shard_map.226), channel_id=1, replica_groups=mesh['pipe'=2,'dp'=16] {'dp'}, dimensions={0} | all-to-all | bytes 786432 | tf_op jit(solution)/shard_map/all_to_all | solution.py:939
  188.3 13.0 %shard_map.227 = (bf16[49,16,2048]{2,1,0:T(8,128)(2,1)}, bf16[49,16,2048]{2,1,0:T(8,128)(2,1)}, bf16[49,16,2048]{2,1,0:T(8,128)(2,1)}, f32[49,16,512]{2,1,0:T(8,...) custom-call(s32[3]{0:T(128)S(1)} %pad_add_fusion.core_ref.place, ...), custom_call_target="tpu_custom_call" | custom-call | flops 5000000000 | bytes 15000000 | tf_op jit(solution)/shard_map/pallas_call | solution.py:884
  202.4 9.4 %all-to-all-start.3 = ((f32[16,8,384]{2,1,0:T(8,128)}), f32[16,8,384]{2,1,0:T(8,128)S(1)}, u32[]{:S(2)}, u32[]{:S(2)}) async-start(f32[16,8,384]{2,1,0:T(8,128)} %get-tuple-element.149), calls=%async_computation.3 | async-start | bytes 393216 | tf_op jit(solution)/shard_map/all_to_all | solution.py:939
  214.3 6.5 all-to-all-done.3.g
  222.2 14.0 %shard_map.229 = (f32[49,16,512]{2,1,0:T(8,128)}, bf16[49,16,512]{2,1,0:T(8,128)(2,1)S(1)}, bf16[49,16,128]{2,1,0:T(8,128)(2,1)S(1)}, bf16[49,16,512]{2,1,0:T(8,...) custom-call(s32[3]{0:T(128)S(1)} %pad_add_fusion.core_ref.place, ...), custom_call_target="tpu_custom_call" | custom-call | flops 5000000000 | bytes 15000000 | tf_op jit(solution)/shard_map/pallas_call | solution.py:884
  236.9 12.1 %all_to_all.66.g = f32[16,8,384]{2,1,0:T(8,128)S(1)} all-to-all(f32[16,8,384]{2,1,0:T(8,128)S(1)} %get-tuple-element.155), channel_id=1, replica_groups=mesh['pipe'=2,'dp'=16] {'dp'}, dimensions={0} | all-to-all | bytes 393216 | tf_op jit(solution)/shard_map/all_to_all | solution.py:939
  250.4 7.6 %shard_map.230 = (bf16[49,16,512]{2,1,0:T(8,128)(2,1)S(1)}, f32[8,1024]{1,0:T(8,128)S(1)}, f32[8,1024]{1,0:T(8,128)S(1)}, f32[8,512]{1,0:T(8,128)S(1)}) custom-call(s32[3]{0:T(128)S(1)} %pad_add_fusion.core_ref.place, f32[49,16,512]{2,1,0:T(8,128)} %get-tuple-element.154.second, f32[16,8,384]{2,1,0:T(8,128)S(1)} %all_to_all.66.g, ...), custom_call_target="tpu_custom_call" | custom-call | flops 5000000000 | bytes 15000000 | tf_op jit(solution)/shard_map/pallas_call | solution.py:884
  259.3 16.3 %all_to_all.67.g = f32[16,8,768]{2,1,0:T(8,128)S(1)} all-to-all(f32[16,8,768]{2,1,0:T(8,128)S(1)} %shard_map.231), channel_id=1, replica_groups=mesh['pipe'=2,'dp'=16] {'dp'}, dimensions={0} | all-to-all | bytes 786432 | tf_op jit(solution)/shard_map/all_to_all | solution.py:939
  277.3 13.5 %shard_map.232 = (bf16[49,16,2048]{2,1,0:T(8,128)(2,1)}, bf16[49,16,2048]{2,1,0:T(8,128)(2,1)}, bf16[49,16,2048]{2,1,0:T(8,128)(2,1)}, f32[8,1024]{1,0:T(8,128)S...) custom-call(s32[3]{0:T(128)S(1)} %pad_add_fusion.core_ref.place, ...), custom_call_target="tpu_custom_call" | custom-call | flops 5000000000 | bytes 15000000 | tf_op jit(solution)/shard_map/pallas_call | solution.py:884
  292.1 16.3 %all_to_all.68.g = f32[16,8,768]{2,1,0:T(8,128)S(1)} all-to-all(f32[16,8,768]{2,1,0:T(8,128)S(1)} %shard_map.233), channel_id=1, replica_groups=mesh['pipe'=2,'dp'=16] {'dp'}, dimensions={0} | all-to-all | bytes 786432 | tf_op jit(solution)/shard_map/all_to_all | solution.py:939
  310.2 9.4 %shard_map.234 = (f32[49,16,512]{2,1,0:T(8,128)}, f32[16,8,384]{2,1,0:T(8,128)S(1)}, bf16[49,16,2048]{2,1,0:T(8,128)(2,1)}, f32[8,2048]{1,0:T(8,128)S(1)}) custom-call(s32[3]{0:T(128)S(1)} %pad_add_fusion.core_ref.place, bf16[49,16,2048]{2,1,0:T(8,128)(2,1)} %get-tuple-element.161.dz.dz_ref, bf16[49,16,2048]{2,1,0:T(8,128)(2,1)} %get-tuple-element.162.xhat_ref, ...), custom_call_target="tpu_custom_call" | custom-call | flops 5000000000 | bytes 15000000 | tf_op jit(solution)/shard_map/pallas_call | solution.py:884
  319.6 12.4 %all_to_all.69.g = f32[16,8,384]{2,1,0:T(8,128)S(1)} all-to-all(f32[16,8,384]{2,1,0:T(8,128)S(1)} %get-tuple-element.169), channel_id=1, replica_groups=mesh['pipe'=2,'dp'=16] {'dp'}, dimensions={0} | all-to-all | bytes 393216 | tf_op jit(solution)/shard_map/all_to_all | solution.py:939
  338.1 15.3 %shard_map.236 = (f32[49,16,512]{2,1,0:T(8,128)}, f32[16,8,384]{2,1,0:T(8,128)}, bf16[49,16,512]{2,1,0:T(8,128)(2,1)S(1)}, bf16[49,16,128]{2,1,0:T(8,128)(2,1)S(1)}) custom-call(s32[3]{0:T(128)S(1)} %pad_add_fusion.core_ref.place, bf16[49,16,512]{2,1,0:T(8,128)(2,1)} %copy-done.10, f32[49,16,512]{2,1,0:T(8,128)} %get-tuple-element.171.a_ref, ...), custom_call_target="tpu_custom_call" | custom-call | flops 5000000000 | bytes 15000000 | tf_op jit(solution)/shard_map/pallas_call | solution.py:884
  360.2 14.3 %shard_map.237 = (bf16[4,2,2,16,9088]{4,3,2,1,0:T(8,128)(2,1)}, bf16[4,2,2,16,9088]{4,3,2,1,0:T(8,128)(2,1)}) custom-call(s32[3]{0:T(128)S(1)} %pad_add_fusion.core_ref.place, bf16[49,16,512]{2,1,0:T(8,128)(2,1)S(1)} %copy-done.11, bf16[49,16,512]{2,1,0:T(8,128)(2,1)S(1)} %copy-done.13, bf16[49,16,128]{2,1,0:T(8,128)(2,1)S(1)} %get-tuple-element.177.dsq, ...), custom_call_target="tpu_custom_call" | custom-call | flops 5000000000 | bytes 15000000 | tf_op jit(solution)/shard_map/pallas_call | solution.py:884
  374.7 7.9 %collective-permute-done.40 = bf16[4,2,2,16,9088]{4,3,2,1,0:T(8,128)(2,1)S(1)} collective-permute-done((bf16[4,2,2,16,9088]{4,3,2,1,0:T(8,128)(2,1)}, bf16[4,2,2,16,9088]{4,3,2,1,0:T(8,128)(2,1)S(1)}, u32[]{:S(2)}, u32[]{:S(2)}) %collective-permute-start.40) | collective-permute-done | bytes 4653088 | tf_op jit(solution)/shard_map/ppermute | solution.py:933
  382.6 5.8 add_convert_fusion
  393.5 14.0 %shard_map.238 = (bf16[49,16,2048]{2,1,0:T(8,128)(2,1)}, bf16[49,16,512]{2,1,0:T(8,128)(2,1)}, f32[8,512]{1,0:T(8,128)S(1)}, bf16[49,16,2048]{2,1,0:T(8,128)(2,1...) custom-call(s32[3]{0:T(128)S(1)} %pad_add_fusion.core_ref.place, f32[49,16,512]{2,1,0:T(8,128)} %get-tuple-element.174.dn1, ...), custom_call_target="tpu_custom_call" | custom-call | flops 5000000000 | bytes 15000000 | tf_op jit(solution)/shard_map/pallas_call | solution.py:884
  408.9 22.9 %all_to_all.70.g = f32[16,8,768]{2,1,0:T(8,128)S(1)} all-to-all(f32[16,8,768]{2,1,0:T(8,128)S(1)} %shard_map.239), channel_id=1, replica_groups=mesh['pipe'=2,'dp'=16] {'dp'}, dimensions={0} | all-to-all | bytes 786432 | tf_op jit(solution)/shard_map/all_to_all | solution.py:939
  433.7 9.5 %shard_map.240 = (f32[49,16,512]{2,1,0:T(8,128)}, f32[16,8,384]{2,1,0:T(8,128)}, bf16[49,16,2048]{2,1,0:T(8,128)(2,1)}, f32[8,2048]{1,0:T(8,128)S(1)}) custom-call(s32[3]{0:T(128)S(1)} %pad_add_fusion.core_ref.place, bf16[49,16,2048]{2,1,0:T(8,128)(2,1)} %get-tuple-element.187.dz.dz_ref, bf16[49,16,2048]{2,1,0:T(8,128)(2,1)} %get-tuple-element.186.xhat_ref, ...), custom_call_target="tpu_custom_call" | custom-call | flops 5000000000 | bytes 15000000 | tf_op jit(solution)/shard_map/pallas_call | solution.py:884
  443.2 5.9 all-to-all-start.10
  451.4 10.3 %shard_map.241 = (bf16[4,2,2,16,4096]{4,3,2,1,0:T(8,128)(2,1)}, bf16[4,2,2,16,4096]{4,3,2,1,0:T(8,128)(2,1)}) custom-call(s32[3]{0:T(128)S(1)} %pad_add_fusion.core_ref.place, bf16[49,16,2048]{2,1,0:T(8,128)(2,1)} %get-tuple-element.197.d3, bf16[49,16,512]{2,1,0:T(8,128)(2,1)S(1)} %copy-done.8, bf16[49,16,512]{2,1,0:T(8,128)(2,1)S(1)} %copy-done.3, ...), custom_call_target="tpu_custom_call" | custom-call | flops 5000000000 | bytes 15000000 | tf_op jit(solution)/shard_map/pallas_call | solution.py:884
  465.9 12.3 %shard_map.242 = (bf16[4,2,16,2048]{3,2,1,0:T(8,128)(2,1)S(1)}, bf16[4,2,16,2048]{3,2,1,0:T(8,128)(2,1)S(1)}, bf16[4,2,16,2048]{3,2,1,0:T(8,128)(2,1)S(1)}, bf16...) custom-call(s32[3]{0:T(128)S(1)} %pad_add_fusion.core_ref.place, ...), custom_call_target="tpu_custom_call" | custom-call | flops 5000000000 | bytes 15000000 | tf_op jit(solution)/shard_map/pallas_call | solution.py:884
  481.1 15.6 %shard_map.243 = (f32[49,16,512]{2,1,0:T(8,128)}, f32[16,8,384]{2,1,0:T(8,128)}, bf16[49,16,512]{2,1,0:T(8,128)(2,1)S(1)}, bf16[49,16,128]{2,1,0:T(8,128)(2,1)S(1)}) custom-call(s32[3]{0:T(128)S(1)} %pad_add_fusion.core_ref.place, bf16[49,16,512]{2,1,0:T(8,128)(2,1)} %get-tuple-element.203.d2, f32[49,16,512]{2,1,0:T(8,128)} %get-tuple-element.204.a_ref, ...), custom_call_target="tpu_custom_call" | custom-call | flops 5000000000 | bytes 15000000 | tf_op jit(solution)/shard_map/pallas_call | solution.py:884
  498.7 6.9 %all-to-all-start.11 = ((f32[16,8,384]{2,1,0:T(8,128)}), f32[16,8,384]{2,1,0:T(8,128)S(1)}, u32[]{:S(2)}, u32[]{:S(2)}) async-start(f32[16,8,384]{2,1,0:T(8,128)} %get-tuple-element.208), calls=%async_computation.11 | async-start | bytes 393216 | tf_op jit(solution)/shard_map/all_to_all | solution.py:939
  518.4 6.0 shard_map.244
  526.1 3.8 collective-permute-start.54
  529.9 8.7 %shard_map.245 = (bf16[4,2,2,16,2048]{4,3,2,1,0:T(8,128)(2,1)}, bf16[4,2,2,16,2048]{4,3,2,1,0:T(8,128)(2,1)}, bf16[49,16,512]{2,1,0:T(8,128)(2,1)S(1)}, f32[8,512]{1,0:T(8,128)S(1)}) custom-call(s32[3]{0:T(128)S(1)} %pad_add_fusion.core_ref.place, f32[49,16,512]{2,1,0:T(8,128)} %get-tuple-element.207.dn1, f32[49,16,512]{2,1,0:T(8,128)} %collective-permute-done.44.other, ...), custom_call_target="tpu_custom_call" | custom-call | flops 5000000000 | bytes 15000000 | tf_op jit(solution)/shard_map/pallas_call | solution.py:884
  550.2 6.5 collective-permute-start.52
  556.7 6.7 shard_map.247.early_ref
  567.0 10.1 %collective-permute-done.60 = bf16[4,16,2560]{2,1,0:T(8,128)(2,1)S(1)} collective-permute-done((bf16[4,16,2560]{2,1,0:T(8,128)(2,1)S(1)}, bf16[4,16,2560]{2,1,0:T(8,128)(2,1)S(1)}, u32[]{:S(2)}, u32[]{:S(2)}) %collective-permute-start.60) | collective-permute-done | bytes 327712 | tf_op jit(solution)/shard_map/ppermute | solution.py:936
  577.2 7.3 %all-to-all-start.12 = ((bf16[16,16,4480]{2,1,0:T(8,128)(2,1)}), bf16[16,16,4480]{2,1,0:T(8,128)(2,1)S(1)}, u32[]{:S(2)}, u32[]{:S(2)}) async-start(bf16[16,16,4480]{2,1,0:T(8,128)(2,1)} %pad_maximum_fusion), calls=%async_computation.12 | async-start | bytes 4587520 | tf_op jit(solution)/shard_map/all_to_all | solution.py:1048
  586.6 9.8 %shard_map.246 = bf16[3,392,2048]{2,1,0:T(8,128)(2,1)} custom-call(s32[3]{0:T(128)S(1)} %pad_add_fusion.core_ref.place, bf16[49,16,2048]{2,1,0:T(8,128)(2,1)} %get-tuple-element.223.x_ref.early_ref, bf16[49,16,2048]{2,1,0:T(8,128)(2,1)} %get-tuple-element.224.late_ref, bf16[49,16,2048]{2,1,0:T(8,128)(2,1)} %collective-permute-done.51.early_in, ...), custom_call_target="tpu_custom_call" | custom-call | flops 5000000000 | bytes 15000000 | tf_op jit(solution)/shard_map/pallas_call | solution.py:884
  596.5 9.8 %shard_map.248 = bf16[3,392,2048]{2,1,0:T(8,128)(2,1)} custom-call(s32[3]{0:T(128)S(1)} %pad_add_fusion.core_ref.place, bf16[49,16,2048]{2,1,0:T(8,128)(2,1)} %shard_map.247.early_ref, bf16[49,16,2048]{2,1,0:T(8,128)(2,1)} %get-tuple-element.228.late_ref, bf16[49,16,2048]{2,1,0:T(8,128)(2,1)} %collective-permute-done.53.early_in, ...), custom_call_target="tpu_custom_call" | custom-call | flops 5000000000 | bytes 15000000 | tf_op jit(solution)/shard_map/pallas_call | solution.py:884
  606.4 25.7 %collective-permute-done.61 = bf16[2,16,4608]{2,1,0:T(8,128)(2,1)S(1)} collective-permute-done((bf16[2,16,4608]{2,1,0:T(8,128)(2,1)S(1)}, bf16[2,16,4608]{2,1,0:T(8,128)(2,1)S(1)}, u32[]{:S(2)}, u32[]{:S(2)}) %collective-permute-start.61) | collective-permute-done | bytes 294944 | tf_op jit(solution)/shard_map/ppermute | solution.py:936
  635.5 9.4 %collective-permute-done.62 = bf16[16,4608]{1,0:T(8,128)(2,1)S(1)} collective-permute-done((bf16[16,4608]{1,0:T(8,128)(2,1)S(1)}, bf16[16,4608]{1,0:T(8,128)(2,1)S(1)}, u32[]{:S(2)}, u32[]{:S(2)}) %collective-permute-start.62) | collective-permute-done | bytes 147488 | tf_op jit(solution)/shard_map/ppermute | solution.py:936
  (347 shorter events, 157.8 us)
Async XLA Ops:
  7.2 97.1 %all-gather.5.cloned.1.call-start = ((), (), s32[]{:S(2)}) async-start(), calls=%async_computation.17 | async-start | bytes 3829760 | tf_op jit(solution)/shard_map/all_gather | solution.py:968
  25.1 10.1 %collective-permute-start.4 = (bf16[2,16,2176]{2,1,0:T(8,128)(2,1)S(1)}, bf16[2,16,2176]{2,1,0:T(8,128)(2,1)S(1)}, u32[]{:S(2)}, u32[]{:S(2)}) collective-permute-start(bf16[2,16,2176]{2,1,0:T(8,128)(2,1)S(1)} %maximum_select_fusion.10), channel_id=1, source_target_pairs={{0,4},{1,5},{2,6},{3,7},{4,0},{5,1},{6,2},{7,3},{8,12},{9,13},{10,... | collective-permute-start | bytes 417800 | tf_op jit(solution)/shard_map/ppermute | solution.py:936
  35.2 16.5 %collective-permute-start.5 = (bf16[16,4224]{1,0:T(8,128)(2,1)S(1)}, bf16[16,4224]{1,0:T(8,128)(2,1)S(1)}, u32[]{:S(2)}, u32[]{:S(2)}) collective-permute-start(bf16[16,4224]{1,0:T(8,128)(2,1)S(1)} %get-tuple-element.131), channel_id=1, source_target_pairs={{0,8},{1,9},{2,10},{3,11},{4,12},{5,13},{6,14},{7,15},{8,0},{9,1},... | collective-permute-start | bytes 405512 | tf_op jit(solution)/shard_map/ppermute | solution.py:936
  38.7 12.4 %collective-permute-start.7 = (bf16[4,16,1024]{2,1,0:T(8,128)(2,1)S(1)}, bf16[4,16,1024]{2,1,0:T(8,128)(2,1)S(1)}, u32[]{:S(2)}, u32[]{:S(2)}) collective-permute-start(bf16[4,16,1024]{2,1,0:T(8,128)(2,1)S(1)} %get-tuple-element.285), channel_id=1, source_target_pairs={{0,1},{1,0},{2,3},{3,2},{4,5},{5,4},{6,7},{7,6},{8,9},{9,8},{10,11... | collective-permute-start | bytes 393224 | tf_op jit(solution)/shard_map/ppermute | solution.py:936
  51.1 11.9 %collective-permute-start.8 = (bf16[4,2,16,1024]{3,2,0,1:T(8,128)(2,1)S(1)}, bf16[4,2,16,1024]{3,2,0,1:T(8,128)(2,1)S(1)}, u32[]{:S(2)}, u32[]{:S(2)}) collective-permute-start(bf16[4,2,16,1024]{3,2,0,1:T(8,128)(2,1)S(1)} %maximum_select_fusion.8), channel_id=1, source_target_pairs={{0,2},{1,3},{2,0},{3,1},{4,6},{5,7},{6,4},{7,5},{8,10},{9,11},{10,... | collective-permute-start | bytes 786440 | tf_op jit(solution)/shard_map/ppermute | solution.py:936
  51.7 11.4 %collective-permute-start.11 = (bf16[4,2,16,1024]{3,2,0,1:T(8,128)(2,1)S(1)}, bf16[4,2,16,1024]{3,2,0,1:T(8,128)(2,1)S(1)}, u32[]{:S(2)}, u32[]{:S(2)}) collective-permute-start(bf16[4,2,16,1024]{3,2,0,1:T(8,128)(2,1)S(1)} %maximum_select_fusion.8), channel_id=1, source_target_pairs={{0,16},{16,0},{1,17},{17,1},{2,18},{18,2},{3,19},{19,3},{4,20},{20... | collective-permute-start | bytes 786440 | tf_op jit(solution)/shard_map/ppermute | solution.py:933
  51.8 15.2 %collective-permute-start.6 = (bf16[2,16,4224]{2,1,0:T(8,128)(2,1)S(1)}, bf16[2,16,4224]{2,1,0:T(8,128)(2,1)S(1)}, u32[]{:S(2)}, u32[]{:S(2)}) collective-permute-start(bf16[2,16,4224]{2,1,0:T(8,128)(2,1)S(1)} %maximum_select_fusion.7), channel_id=1, source_target_pairs={{0,4},{1,5},{2,6},{3,7},{4,0},{5,1},{6,2},{7,3},{8,12},{9,13},{10,... | collective-permute-start | bytes 811016 | tf_op jit(solution)/shard_map/ppermute | solution.py:936
  58.1 8.8 %collective-permute-start.10 = (bf16[4,2,16,1152]{3,2,1,0:T(8,128)(2,1)S(1)}, bf16[4,2,16,1152]{3,2,1,0:T(8,128)(2,1)S(1)}, u32[]{:S(2)}, u32[]{:S(2)}) collective-permute-start(bf16[4,2,16,1152]{3,2,1,0:T(8,128)(2,1)S(1)} %maximum_select_fusion.4.rest_2_), channel_id=1, source_target_pairs={{0,1},{1,0},{2,3},{3,2},{4,5},{5,4},{6,7},{7,6},{8,9},{9,8},{10,11... | collective-permute-start | bytes 884744 | tf_op jit(solution)/shard_map/ppermute | solution.py:936
  76.8 21.0 %all-to-all-start = ((f32[16,8,384]{2,1,0:T(8,128)}), f32[16,8,384]{2,1,0:T(8,128)S(1)}, u32[]{:S(2)}, u32[]{:S(2)}) async-start(f32[16,8,384]{2,1,0:T(8,128)} %get-tuple-element.136), calls=%async_computation | async-start | bytes 393216 | tf_op jit(solution)/shard_map/all_to_all | solution.py:939
  81.1 120.8 %all-gather.7.cloned.1.call-start = ((), (), s32[]{:S(2)}) async-start(), calls=%async_computation.18 | async-start | bytes 4943872 | tf_op jit(solution)/shard_map/all_gather | solution.py:968
  81.2 14.8 %collective-permute-start.16 = (bf16[4,16,2048]{2,1,0:T(8,128)(2,1)S(1)}, bf16[4,16,2048]{2,1,0:T(8,128)(2,1)S(1)}, u32[]{:S(2)}, u32[]{:S(2)}) collective-permute-start(bf16[4,16,2048]{2,1,0:T(8,128)(2,1)S(1)} %get-tuple-element.279), channel_id=1, source_target_pairs={{0,1},{1,0},{2,3},{3,2},{4,5},{5,4},{6,7},{7,6},{8,9},{9,8},{10,11... | collective-permute-start | bytes 786440 | tf_op jit(solution)/shard_map/ppermute | solution.py:936
  83.2 13.7 %collective-permute-start.17 = (bf16[4,16,2176]{2,1,0:T(8,128)(2,1)S(1)}, bf16[4,16,2176]{2,1,0:T(8,128)(2,1)S(1)}, u32[]{:S(2)}, u32[]{:S(2)}) collective-permute-start(bf16[4,16,2176]{2,1,0:T(8,128)(2,1)S(1)} %get-tuple-element.277), channel_id=1, source_target_pairs={{0,2},{1,3},{2,0},{3,1},{4,6},{5,7},{6,4},{7,5},{8,10},{9,11},{10,... | collective-permute-start | bytes 835592 | tf_op jit(solution)/shard_map/ppermute | solution.py:936
  104.3 9.3 %collective-permute-start.19 = (bf16[4,2,2,16,7040]{4,3,2,1,0:T(8,128)(2,1)}, bf16[4,2,2,16,7040]{4,3,2,1,0:T(8,128)(2,1)}, u32[]{:S(2)}, u32[]{:S(2)}) collective-permute-start(bf16[4,2,2,16,7040]{4,3,2,1,0:T(8,128)(2,1)} %bitcast.200), channel_id=1, source_target_pairs={{0,16},{16,0},{1,17},{17,1},{2,18},{18,2},{3,19},{19,3},{4,20},{20... | collective-permute-start | bytes 10813448 | tf_op jit(solution)/shard_map/ppermute | solution.py:933
  104.4 9.2 %collective-permute-start.15 = (f32[49,16,512]{2,1,0:T(8,128)}, f32[49,16,512]{2,1,0:T(8,128)}, u32[]{:S(2)}, u32[]{:S(2)}) collective-permute-start(f32[49,16,512]{2,1,0:T(8,128)} %get-tuple-element.135.a_in), channel_id=1, source_target_pairs={{0,16},{16,0},{1,17},{17,1},{2,18},{18,2},{3,19},{19,3},{4,20},{20... | collective-permute-start | bytes 4816904 | tf_op jit(solution)/shard_map/ppermute | solution.py:933
  105.3 30.2 %collective-permute-start.21 = (bf16[4,2,16,2048]{3,2,0,1:T(8,128)(2,1)}, bf16[4,2,16,2048]{3,2,0,1:T(8,128)(2,1)}, u32[]{:S(2)}, u32[]{:S(2)}) collective-permute-start(bf16[4,2,16,2048]{3,2,0,1:T(8,128)(2,1)} %maximum_select_fusion.2), channel_id=1, source_target_pairs={{0,2},{1,3},{2,0},{3,1},{4,6},{5,7},{6,4},{7,5},{8,10},{9,11},{10,... | collective-permute-start | bytes 1572872 | tf_op jit(solution)/shard_map/ppermute | solution.py:936
  106.8 28.2 %collective-permute-start.22 = (bf16[4,2,16,2176]{3,2,1,0:T(8,128)(2,1)}, bf16[4,2,16,2176]{3,2,1,0:T(8,128)(2,1)}, u32[]{:S(2)}, u32[]{:S(2)}) collective-permute-start(bf16[4,2,16,2176]{3,2,1,0:T(8,128)(2,1)} %maximum_select_fusion.rest_2_.rest_10_), channel_id=1, source_target_pairs={{0,1},{1,0},{2,3},{3,2},{4,5},{5,4},{6,7},{7,6},{8,9},{9,8},{10,11... | collective-permute-start | bytes 1671176 | tf_op jit(solution)/shard_map/ppermute | solution.py:936
  130.0 17.2 %all-to-all-start.1 = ((f32[16,8,384]{2,1,0:T(8,128)}), f32[16,8,384]{2,1,0:T(8,128)S(1)}, u32[]{:S(2)}, u32[]{:S(2)}) async-start(f32[16,8,384]{2,1,0:T(8,128)} %get-tuple-element.142), calls=%async_computation.1 | async-start | bytes 393216 | tf_op jit(solution)/shard_map/all_to_all | solution.py:939
  134.9 18.5 %collective-permute-start.25 = (bf16[4,2,16,2176]{3,2,1,0:T(8,128)(2,1)}, bf16[4,2,16,2176]{3,2,1,0:T(8,128)(2,1)}, u32[]{:S(2)}, u32[]{:S(2)}) collective-permute-start(bf16[4,2,16,2176]{3,2,1,0:T(8,128)(2,1)} %maximum_select_fusion.rest_2_.rest_10_), channel_id=1, source_target_pairs={{0,16},{16,0},{1,17},{17,1},{2,18},{18,2},{3,19},{19,3},{4,20},{20... | collective-permute-start | bytes 1671176 | tf_op jit(solution)/shard_map/ppermute | solution.py:933
  134.9 18.4 %collective-permute-start.26 = (bf16[4,2,16,2176]{3,2,1,0:T(8,128)(2,1)}, bf16[4,2,16,2176]{3,2,1,0:T(8,128)(2,1)}, u32[]{:S(2)}, u32[]{:S(2)}) collective-permute-start(bf16[4,2,16,2176]{3,2,1,0:T(8,128)(2,1)} %collective-permute-done.22.rest_3_.rest_11_), channel_id=1, source_target_pairs={{0,16},{16,0},{1,17},{17,1},{2,18},{18,2},{3,19},{19,3},{4,20},{20... | collective-permute-start | bytes 1671176 | tf_op jit(solution)/shard_map/ppermute | solution.py:933
  135.4 14.0 %collective-permute-start.23 = (bf16[4,2,16,2048]{3,2,0,1:T(8,128)(2,1)}, bf16[4,2,16,2048]{3,2,0,1:T(8,128)(2,1)}, u32[]{:S(2)}, u32[]{:S(2)}) collective-permute-start(bf16[4,2,16,2048]{3,2,0,1:T(8,128)(2,1)} %maximum_select_fusion.2), channel_id=1, source_target_pairs={{0,16},{16,0},{1,17},{17,1},{2,18},{18,2},{3,19},{19,3},{4,20},{20... | collective-permute-start | bytes 1572872 | tf_op jit(solution)/shard_map/ppermute | solution.py:933
  135.5 16.0 %collective-permute-start.24 = (bf16[4,2,16,2048]{3,2,0,1:T(8,128)(2,1)}, bf16[4,2,16,2048]{3,2,0,1:T(8,128)(2,1)}, u32[]{:S(2)}, u32[]{:S(2)}) collective-permute-start(bf16[4,2,16,2048]{3,2,0,1:T(8,128)(2,1)} %collective-permute-done.21), channel_id=1, source_target_pairs={{0,16},{16,0},{1,17},{17,1},{2,18},{18,2},{3,19},{19,3},{4,20},{20... | collective-permute-start | bytes 1572872 | tf_op jit(solution)/shard_map/ppermute | solution.py:933
  201.9 20.3 %collective-permute-start.31 = (bf16[4,2,2,16,9088]{4,3,2,1,0:T(8,128)(2,1)}, bf16[4,2,2,16,9088]{4,3,2,1,0:T(8,128)(2,1)}, u32[]{:S(2)}, u32[]{:S(2)}) collective-permute-start(bf16[4,2,2,16,9088]{4,3,2,1,0:T(8,128)(2,1)} %bitcast.194), channel_id=1, source_target_pairs={{0,16},{16,0},{1,17},{17,1},{2,18},{18,2},{3,19},{19,3},{4,20},{20... | collective-permute-start | bytes 13959176 | tf_op jit(solution)/shard_map/ppermute | solution.py:933
  202.1 20.1 %collective-permute-start.29 = (f32[49,16,512]{2,1,0:T(8,128)}, f32[49,16,512]{2,1,0:T(8,128)}, u32[]{:S(2)}, u32[]{:S(2)}) collective-permute-start(f32[49,16,512]{2,1,0:T(8,128)} %get-tuple-element.148.a_in), channel_id=1, source_target_pairs={{0,16},{16,0},{1,17},{17,1},{2,18},{18,2},{3,19},{19,3},{4,20},{20... | collective-permute-start | bytes 4816904 | tf_op jit(solution)/shard_map/ppermute | solution.py:933
  202.4 18.3 %all-to-all-start.3 = ((f32[16,8,384]{2,1,0:T(8,128)}), f32[16,8,384]{2,1,0:T(8,128)S(1)}, u32[]{:S(2)}, u32[]{:S(2)}) async-start(f32[16,8,384]{2,1,0:T(8,128)} %get-tuple-element.149), calls=%async_computation.3 | async-start | bytes 393216 | tf_op jit(solution)/shard_map/all_to_all | solution.py:939
  354.3 20.2 %all-to-all-start.8 = ((f32[16,8,384]{2,1,0:T(8,128)}), f32[16,8,384]{2,1,0:T(8,128)S(1)}, u32[]{:S(2)}, u32[]{:S(2)}) async-start(f32[16,8,384]{2,1,0:T(8,128)} %get-tuple-element.175), calls=%async_computation.8 | async-start | bytes 393216 | tf_op jit(solution)/shard_map/all_to_all | solution.py:939
  357.8 288.8 %reduce-scatter.5.cloned.1.call-start = ((), (), s32[]{:S(2)}) async-start(), calls=%async_computation.16 | async-start | bytes 4943872 | tf_op jit(solution)/shard_map/reduce_scatter | solution.py:1045
  443.2 18.6 %all-to-all-start.10 = ((f32[16,8,384]{2,1,0:T(8,128)}), f32[16,8,384]{2,1,0:T(8,128)S(1)}, u32[]{:S(2)}, u32[]{:S(2)}) async-start(f32[16,8,384]{2,1,0:T(8,128)} %get-tuple-element.196), calls=%async_computation.10 | async-start | bytes 393216 | tf_op jit(solution)/shard_map/all_to_all | solution.py:939
  461.7 51.0 %collective-permute-start.45 = (bf16[4,2,2,16,4096]{4,3,2,1,0:T(8,128)(2,1)}, bf16[4,2,2,16,4096]{4,3,2,1,0:T(8,128)(2,1)}, u32[]{:S(2)}, u32[]{:S(2)}) collective-permute-start(bf16[4,2,2,16,4096]{4,3,2,1,0:T(8,128)(2,1)} %get-tuple-element.200), channel_id=1, source_target_pairs={{0,16},{16,0},{1,17},{17,1},{2,18},{18,2},{3,19},{19,3},{4,20},{20... | collective-permute-start | bytes 6291464 | tf_op jit(solution)/shard_map/ppermute | solution.py:933
  480.0 26.5 %collective-permute-start.46 = (bf16[4,2,16,2048]{3,2,0,1:T(8,128)(2,1)}, bf16[4,2,16,2048]{3,2,0,1:T(8,128)(2,1)}, u32[]{:S(2)}, u32[]{:S(2)}) collective-permute-start(bf16[4,2,16,2048]{3,2,0,1:T(8,128)(2,1)} %copy.149), channel_id=1, source_target_pairs={{0,16},{16,0},{1,17},{17,1},{2,18},{18,2},{3,19},{19,3},{4,20},{20... | collective-permute-start | bytes 1572872 | tf_op jit(solution)/shard_map/ppermute | solution.py:933
  480.9 27.7 %collective-permute-start.47 = (bf16[4,2,16,2560]{3,2,1,0:T(8,128)(2,1)}, bf16[4,2,16,2560]{3,2,1,0:T(8,128)(2,1)}, u32[]{:S(2)}, u32[]{:S(2)}) collective-permute-start(bf16[4,2,16,2560]{3,2,1,0:T(8,128)(2,1)} %get-tuple-element.213), channel_id=1, source_target_pairs={{0,16},{16,0},{1,17},{17,1},{2,18},{18,2},{3,19},{19,3},{4,20},{20... | collective-permute-start | bytes 1966088 | tf_op jit(solution)/shard_map/ppermute | solution.py:933
  498.3 27.7 %collective-permute-start.44 = (f32[49,16,512]{2,1,0:T(8,128)}, f32[49,16,512]{2,1,0:T(8,128)}, u32[]{:S(2)}, u32[]{:S(2)}) collective-permute-start(f32[49,16,512]{2,1,0:T(8,128)} %get-tuple-element.207.dn1), channel_id=1, source_target_pairs={{0,16},{16,0},{1,17},{17,1},{2,18},{18,2},{3,19},{19,3},{4,20},{20... | collective-permute-start | bytes 4816904 | tf_op jit(solution)/shard_map/ppermute | solution.py:933
  498.7 25.7 %all-to-all-start.11 = ((f32[16,8,384]{2,1,0:T(8,128)}), f32[16,8,384]{2,1,0:T(8,128)S(1)}, u32[]{:S(2)}, u32[]{:S(2)}) async-start(f32[16,8,384]{2,1,0:T(8,128)} %get-tuple-element.208), calls=%async_computation.11 | async-start | bytes 393216 | tf_op jit(solution)/shard_map/all_to_all | solution.py:939
  505.6 144.1 %reduce-scatter.3.cloned.1.call-start = ((), (), s32[]{:S(2)}) async-start(), calls=%async_computation.15 | async-start | bytes 2228224 | tf_op jit(solution)/shard_map/reduce_scatter | solution.py:1045
  506.5 35.3 %collective-permute-start.55 = (bf16[4,2,16,2048]{3,2,0,1:T(8,128)(2,1)}, bf16[4,2,16,2048]{3,2,0,1:T(8,128)(2,1)}, u32[]{:S(2)}, u32[]{:S(2)}) collective-permute-start(bf16[4,2,16,2048]{3,2,0,1:T(8,128)(2,1)} %copy.155), channel_id=1, source_target_pairs={{0,16},{16,0},{1,17},{17,1},{2,18},{18,2},{3,19},{19,3},{4,20},{20... | collective-permute-start | bytes 1572872 | tf_op jit(solution)/shard_map/ppermute | solution.py:933
  510.8 27.9 %collective-permute-start.59 = (bf16[4,2,16,2560]{3,2,1,0:T(8,128)(2,1)}, bf16[4,2,16,2560]{3,2,1,0:T(8,128)(2,1)}, u32[]{:S(2)}, u32[]{:S(2)}) collective-permute-start(bf16[4,2,16,2560]{3,2,1,0:T(8,128)(2,1)} %add_convert_fusion.6), channel_id=1, source_target_pairs={{0,1},{1,0},{2,3},{3,2},{4,5},{5,4},{6,7},{7,6},{8,9},{9,8},{10,11... | collective-permute-start | bytes 1966088 | tf_op jit(solution)/shard_map/ppermute | solution.py:936
  524.6 17.2 %collective-permute-start.56 = (bf16[4,2,16,2048]{3,2,0,1:T(8,128)(2,1)}, bf16[4,2,16,2048]{3,2,0,1:T(8,128)(2,1)}, u32[]{:S(2)}, u32[]{:S(2)}) collective-permute-start(bf16[4,2,16,2048]{3,2,0,1:T(8,128)(2,1)} %add_convert_fusion.9), channel_id=1, source_target_pairs={{0,2},{1,3},{2,0},{3,1},{4,6},{5,7},{6,4},{7,5},{8,10},{9,11},{10,... | collective-permute-start | bytes 1572872 | tf_op jit(solution)/shard_map/ppermute | solution.py:936
  526.1 70.4 %collective-permute-start.54 = (bf16[49,16,2048]{2,1,0:T(8,128)(2,1)}, bf16[49,16,2048]{2,1,0:T(8,128)(2,1)}, u32[]{:S(2)}, u32[]{:S(2)}) collective-permute-start(bf16[49,16,2048]{2,1,0:T(8,128)(2,1)} %get-tuple-element.228.late_ref), channel_id=1, source_target_pairs={{0,16},{1,17},{2,18},{3,19},{4,20},{5,21},{6,22},{7,23},{8,24},{9,... | collective-permute-start | bytes 9633800 | tf_op jit(solution)/shard_map/ppermute | solution.py:1285
  529.9 14.5 %collective-permute-start.58 = (bf16[4,2,16,2560]{3,2,1,0:T(8,128)(2,1)}, bf16[4,2,16,2560]{3,2,1,0:T(8,128)(2,1)S(1)}, u32[]{:S(2)}, u32[]{:S(2)}) collective-permute-start(bf16[4,2,16,2560]{3,2,1,0:T(8,128)(2,1)} %get-tuple-element.233), channel_id=1, source_target_pairs={{0,16},{16,0},{1,17},{17,1},{2,18},{18,2},{3,19},{19,3},{4,20},{20... | collective-permute-start | bytes 1966088 | tf_op jit(solution)/shard_map/ppermute | solution.py:933
  543.4 21.4 %collective-permute-start.57 = (bf16[4,16,2048]{2,1,0:T(8,128)(2,1)S(1)}, bf16[4,16,2048]{2,1,0:T(8,128)(2,1)S(1)}, u32[]{:S(2)}, u32[]{:S(2)}) collective-permute-start(bf16[4,16,2048]{2,1,0:T(8,128)(2,1)S(1)} %dynamic-slice_bitcast_fusion.2), channel_id=1, source_target_pairs={{0,1},{1,0},{2,3},{3,2},{4,5},{5,4},{6,7},{7,6},{8,9},{9,8},{10,11... | collective-permute-start | bytes 786440 | tf_op jit(solution)/shard_map/ppermute | solution.py:936
  548.9 37.7 %collective-permute-start.51 = (bf16[49,16,2048]{2,1,0:T(8,128)(2,1)}, bf16[49,16,2048]{2,1,0:T(8,128)(2,1)}, u32[]{:S(2)}, u32[]{:S(2)}) collective-permute-start(bf16[49,16,2048]{2,1,0:T(8,128)(2,1)} %get-tuple-element.223.x_ref.early_ref), channel_id=1, source_target_pairs={{16,0},{17,1},{18,2},{19,3},{20,4},{21,5},{22,6},{23,7},{24,8},{25... | collective-permute-start | bytes 9633800 | tf_op jit(solution)/shard_map/ppermute | solution.py:1285
  550.2 36.4 %collective-permute-start.52 = (bf16[49,16,2048]{2,1,0:T(8,128)(2,1)}, bf16[49,16,2048]{2,1,0:T(8,128)(2,1)}, u32[]{:S(2)}, u32[]{:S(2)}) collective-permute-start(bf16[49,16,2048]{2,1,0:T(8,128)(2,1)} %get-tuple-element.224.late_ref), channel_id=1, source_target_pairs={{0,16},{1,17},{2,18},{3,19},{4,20},{5,21},{6,22},{7,23},{8,24},{9,... | collective-permute-start | bytes 9633800 | tf_op jit(solution)/shard_map/ppermute | solution.py:1285
  563.4 33.1 %collective-permute-start.53 = (bf16[49,16,2048]{2,1,0:T(8,128)(2,1)}, bf16[49,16,2048]{2,1,0:T(8,128)(2,1)}, u32[]{:S(2)}, u32[]{:S(2)}) collective-permute-start(bf16[49,16,2048]{2,1,0:T(8,128)(2,1)} %shard_map.247.early_ref), channel_id=1, source_target_pairs={{16,0},{17,1},{18,2},{19,3},{20,4},{21,5},{22,6},{23,7},{24,8},{25... | collective-permute-start | bytes 9633800 | tf_op jit(solution)/shard_map/ppermute | solution.py:1285
  564.7 12.3 %collective-permute-start.60 = (bf16[4,16,2560]{2,1,0:T(8,128)(2,1)S(1)}, bf16[4,16,2560]{2,1,0:T(8,128)(2,1)S(1)}, u32[]{:S(2)}, u32[]{:S(2)}) collective-permute-start(bf16[4,16,2560]{2,1,0:T(8,128)(2,1)S(1)} %dynamic-slice_bitcast_fusion), channel_id=1, source_target_pairs={{0,2},{1,3},{2,0},{3,1},{4,6},{5,7},{6,4},{7,5},{8,10},{9,11},{10,... | collective-permute-start | bytes 983048 | tf_op jit(solution)/shard_map/ppermute | solution.py:936
  577.2 67.8 %all-to-all-start.12 = ((bf16[16,16,4480]{2,1,0:T(8,128)(2,1)}), bf16[16,16,4480]{2,1,0:T(8,128)(2,1)S(1)}, u32[]{:S(2)}, u32[]{:S(2)}) async-start(bf16[16,16,4480]{2,1,0:T(8,128)(2,1)} %pad_maximum_fusion), calls=%async_computation.12 | async-start | bytes 4587520 | tf_op jit(solution)/shard_map/all_to_all | solution.py:1048
  584.5 47.6 %collective-permute-start.61 = (bf16[2,16,4608]{2,1,0:T(8,128)(2,1)S(1)}, bf16[2,16,4608]{2,1,0:T(8,128)(2,1)S(1)}, u32[]{:S(2)}, u32[]{:S(2)}) collective-permute-start(bf16[2,16,4608]{2,1,0:T(8,128)(2,1)S(1)} %dynamic-slice_bitcast_fusion.1), channel_id=1, source_target_pairs={{0,4},{1,5},{2,6},{3,7},{4,0},{5,1},{6,2},{7,3},{8,12},{9,13},{10,... | collective-permute-start | bytes 884744 | tf_op jit(solution)/shard_map/ppermute | solution.py:936
  632.2 12.7 %collective-permute-start.62 = (bf16[16,4608]{1,0:T(8,128)(2,1)S(1)}, bf16[16,4608]{1,0:T(8,128)(2,1)S(1)}, u32[]{:S(2)}, u32[]{:S(2)}) collective-permute-start(bf16[16,4608]{1,0:T(8,128)(2,1)S(1)} %dynamic-slice_bitcast_fusion.4), channel_id=1, source_target_pairs={{0,8},{1,9},{2,10},{3,11},{4,12},{5,13},{6,14},{7,15},{8,0},{9,1},... | collective-permute-start | bytes 442376 | tf_op jit(solution)/shard_map/ppermute | solution.py:936
  646.6 11.9 %collective-permute-start.65 = (bf16[16,9088]{1,0:T(8,128)(2,1)}, bf16[16,9088]{1,0:T(8,128)(2,1)S(1)}, u32[]{:S(2)}, u32[]{:S(2)}) collective-permute-start(bf16[16,9088]{1,0:T(8,128)(2,1)} %bitcast.174), channel_id=1, source_target_pairs={{0,16},{1,17},{2,18},{3,19},{4,20},{5,21},{6,22},{7,23},{8,24},{9,... | collective-permute-start | bytes 872456 | tf_op jit(solution)/shard_map/ppermute | solution.py:1054
  652.5 8.9 %collective-permute-start.66 = (bf16[16,4608]{1,0:T(8,128)(2,1)S(1)}, bf16[16,4608]{1,0:T(8,128)(2,1)S(1)}, u32[]{:S(2)}, u32[]{:S(2)}) collective-permute-start(bf16[16,4608]{1,0:T(8,128)(2,1)S(1)} %fusion.3), channel_id=1, source_target_pairs={{16,0},{17,1},{18,2},{19,3},{20,4},{21,5},{22,6},{23,7},{24,8},{25... | collective-permute-start | bytes 442376 | tf_op jit(solution)/shard_map/ppermute | solution.py:1054
  (74 other events, 630.5 us)
Sparse Core Ops, SparseCore 0:
  17.2 87.0 all-gather.4
  107.0 89.1 all-gather.6
  388.5 113.0 reduce-scatter.4
  526.2 84.6 reduce-scatter.2

commit v3 on v2

--- a/solution.py
+++ b/solution.py
@@ -1328,12 +1328,14 @@
     )
     split = links.split
     sums = links.to_all(st, *g_rest)
+    dn1_other = links.swap(dn1)
     dx1, d1_late, s1, dz, keep, send = first_back(
-        dn1, links.swap(dn1), a, mv1, *sums, gb, dz, slope0, kept[0][10]
+        dn1, dn1_other, a, mv1, *sums, gb, dz, slope0, kept[0][10]
     )
     meanwhile = []
     if split:
-        late = links.half_sums(g_rest[0], after(g_rest[1], sums[0]))
+        recv = after(links.swap(after(g_rest[1], sums[1], dn1_other)), dx1)
+        late = links.add(g_rest[0], recv).reshape(16, 16, -1)
         keep = after(keep, late)
         late = links.scatter_whole(late)
     norms_1 = (s1, s2, s3)
@@ -1347,13 +1349,13 @@
     g_mixed = grad(
         mixed_grad_kernel, shares_of("whole", 4096), [Near(d3), mid, Near(d1_late), x_late]
     )
-    *g_mid, d2, s2 = second_back(
-        shares_of("split", 2048, 2560), dn2, second, mv2, *links.to_all(st, *g_mixed), gb, mix
-    )
+    sums = links.to_all(st, *g_mixed)
+    mixed_sums = sums
+    *g_mid, d2, s2 = second_back(shares_of("split", 2048, 2560), dn2, second, mv2, *sums, gb, mix)
     dn1, st, dlog, dsq = middle_back(0, d2, a, mv1, gb, msk, op)
     if split:
         sent = links.scatter_first(g_mid)
-        mixed = links.half_sums(*g_mixed)
+        mixed = links.half_sums(g_mixed[0], after(g_mixed[1], mixed_sums[1]))
         dlog = after(dlog, mixed, *sent)
         mixed = links.scatter_whole(mixed)
     g_branch = grad(branch_grad_kernel, shares_of("whole", 2432), [Near(dlog), Near(dsq), sq, diff], patch)
@@ -1367,12 +1369,12 @@
     if split:
         last = jnp.concatenate([links.half_sums(*g_in), *rest_0], axis=-1)
         dx0 = last_back(after(d1, last), dz)
-        act0, act1 = after((act0, act1), last)
+        act0, act1, dx1 = after((act0, act1, dx1), last)
         early = links.scatter_xy(g_mid, sent, (d1, None))
         activations = restore(place, act0, act1, *crossed(act0, act1))[0]
-        input_grads = restore(place, after(dx0, activations), dx1, *crossed(dx0, dx1))[0]
-        mid_0, _ = links.scatter_z(early, (input_grads, None))
-        last = links.scatter_at_once(last, input_grads, mid_0)
+        last = links.scatter_at_once(last, activations)
+        input_grads = restore(place, after(dx0, last), dx1, *crossed(dx0, dx1))[0]
+        mid_0, _ = links.scatter_z(early, (activations, input_grads))
         in_0, branch_0 = jnp.split(last, [2048], axis=-1)
         mixed = after(mixed, late)
         out_0, in_1 = jnp.split(mixed, 2, axis=-1)

time: 681 us -> 668 us (0.981)
  waiting for transfers between devices: 136 us -> 122 us
    ppermute x18, waiting for transfers between devices: 72.7 us -> 58 us  [across(): return lax.ppermute(v, 'dp', [(i, i ^ k) for i in range(self.dp)])]
    reduce_scatter x2, waiting for transfers between devices: 0.04 us -> 13 us  [scatter_whole(): return lax.psum_scatter(v, 'dp', scatter_dimension=0, tiled=True)[0]]
    ppermute x41, waiting for transfers between devices: 38.8 us -> 26.5 us  [swap(): return lax.ppermute(v, 'pipe', PAIR)]
    unnamed x89 -> x97, local copies, waits for them, and re-layouts: 18.2 us -> 17.4 us
  transfers between devices with their start and end apart: 79 -> 79, of which waited for: 32 -> 29; matrix products, arithmetic and copies ran while one was open for 6% -> 6% of each run, Pallas kernels for 27% -> 28%
where the time goes in v3:
time: 668 us; the launch traced here: 656 us
  Pallas kernels  246 us (37%)
  waiting for transfers between devices  122 us (18%)
  blocking collectives  106 us (16%)
  starting transfers between devices  102 us (15%)
  other arithmetic  34.2 us (5%)
  local copies, waits for them, and re-layouts  30.5 us (5%)
  between operations  15.4 us (2%)
    pallas_call x25, Pallas kernels, run(): pl.pallas_call(kernel, in_specs=specs, out_specs=tuple((HB if is_big(o[0]...  246 us
    all_to_all x6, blocking collectives, to_all(): g = lax.all_to_all(spread, 'dp', 0, 0)  106 us
    ppermute x18, waiting for transfers between devices, across(): return lax.ppermute(v, 'dp', [(i, i ^ k) for i in range(self.dp)])  58 us
    all_to_all x6, starting transfers between devices, to_all(): g = lax.all_to_all(spread, 'dp', 0, 0)  33 us
    ppermute x18, starting transfers between devices, across(): return lax.ppermute(v, 'dp', [(i, i ^ k) for i in range(self.dp)])  27.9 us
    ppermute x41, waiting for transfers between devices, swap(): return lax.ppermute(v, 'pipe', PAIR)  26.5 us
    convert_element_type x12, other arithmetic, add(): return (a.astype(F32) + b.astype(F32)).astype(BF16)  18.3 us
    all_to_all x6, waiting for transfers between devices, to_all(): g = lax.all_to_all(spread, 'dp', 0, 0)  17.8 us
  transfers between devices with their start and end apart: 79, of which 29 were waited for; matrix products, arithmetic and copies ran while one was open for 6% of the time, Pallas kernels for 28%

profile of v3, /device:TPU:0, one launch (start us, length us, event | category | flops | bytes accessed | tf_op | source)
XLA Modules:
  0.0 655.9 jit_solution(267015517814289763)
XLA Ops:
  17.0 4.0 collective-permute-start.2
  25.9 9.3 %shard_map.220.x_ref = bf16[49,16,2048]{2,1,0:T(8,128)(2,1)} custom-call(s32[3]{0:T(128)S(1)} %pad_add_fusion.core_ref.place, bf16[3,392,2048]{2,1,0:T(8,128)(2,1)} %x_ref), custom_call_target="tpu_custom_call" | custom-call | flops 5000000000 | bytes 15000000 | tf_op jit(solution)/shard_map/pallas_call | solution.py:884
  40.3 9.2 %shard_map.221.dy_ref = bf16[49,16,2048]{2,1,0:T(8,128)(2,1)} custom-call(s32[3]{0:T(128)S(1)} %pad_add_fusion.core_ref.place, bf16[3,392,2048]{2,1,0:T(8,128)(2,1)} %x_ref.1), custom_call_target="tpu_custom_call" | custom-call | flops 5000000000 | bytes 15000000 | tf_op jit(solution)/shard_map/pallas_call | solution.py:884
  51.9 6.2 collective-permute-done.9
  63.2 3.8 collective-permute-done.6
  69.3 7.5 %shard_map.222 = (f32[49,16,512]{2,1,0:T(8,128)}, f32[16,8,384]{2,1,0:T(8,128)}) custom-call(s32[3]{0:T(128)S(1)} %pad_add_fusion.core_ref.place, bf16[49,16,2048]{2,1,0:T(8,128)(2,1)} %shard_map.220.x_ref, bf16[4,2,16,1024]{3,2,1,0:T(8,128)(2,1)S(1)} %copy.116.rest_0_, bf16[4,2,16,1024]{3,2,1,0:T(8,128)(2,1)S(1)} %copy.117.rest_1_, ...), custom_call_target="tpu_custom_call" | custom-call | flops 5000000000 | bytes 15000000 | tf_op jit(solution)/shard_map/pallas_call | solution.py:884
  76.8 4.3 all-to-all-start
  88.1 7.8 %collective-permute-done.16 = bf16[4,16,2048]{2,1,0:T(8,128)(2,1)S(1)} collective-permute-done((bf16[4,16,2048]{2,1,0:T(8,128)(2,1)S(1)}, bf16[4,16,2048]{2,1,0:T(8,128)(2,1)S(1)}, u32[]{:S(2)}, u32[]{:S(2)}) %collective-permute-start.16) | collective-permute-done | bytes 262176 | tf_op jit(solution)/shard_map/ppermute | solution.py:936
  97.7 6.5 all-gather.5.cloned.1.call-done
  107.1 4.1 collective-permute-done.18.g_other
  113.6 14.1 %shard_map.224 = (f32[49,16,512]{2,1,0:T(8,128)}, bf16[49,16,512]{2,1,0:T(8,128)(2,1)S(1)}, bf16[49,16,128]{2,1,0:T(8,128)(2,1)S(1)}, bf16[49,16,512]{2,1,0:T(8,...) custom-call(s32[3]{0:T(128)S(1)} %pad_add_fusion.core_ref.place, ...), custom_call_target="tpu_custom_call" | custom-call | flops 5000000000 | bytes 15000000 | tf_op jit(solution)/shard_map/pallas_call | solution.py:884
  130.0 4.9 all-to-all-start.1
  135.9 11.3 %all-to-all-done.1.g = f32[16,8,384]{2,1,0:T(8,128)S(1)} async-done(((f32[16,8,384]{2,1,0:T(8,128)}), f32[16,8,384]{2,1,0:T(8,128)S(1)}, u32[]{:S(2)}, u32[]{:S(2)}) %all-to-all-start.1) | async-done | bytes 196640 | tf_op jit(solution)/shard_map/all_to_all | solution.py:939
  153.4 7.4 %shard_map.225 = (bf16[49,16,512]{2,1,0:T(8,128)(2,1)}, f32[8,1024]{1,0:T(8,128)S(1)}, f32[8,1024]{1,0:T(8,128)S(1)}, f32[8,512]{1,0:T(8,128)S(1)}) custom-call(s32[3]{0:T(128)S(1)} %pad_add_fusion.core_ref.place, f32[49,16,512]{2,1,0:T(8,128)} %get-tuple-element.145.second, f32[16,8,384]{2,1,0:T(8,128)S(1)} %all-to-all-done.1.g, ...), custom_call_target="tpu_custom_call" | custom-call | flops 5000000000 | bytes 15000000 | tf_op jit(solution)/shard_map/pallas_call | solution.py:884
  162.3 24.2 %all_to_all.65.g = f32[16,8,768]{2,1,0:T(8,128)S(1)} all-to-all(f32[16,8,768]{2,1,0:T(8,128)S(1)} %shard_map.226), channel_id=1, replica_groups=mesh['pipe'=2,'dp'=16] {'dp'}, dimensions={0} | all-to-all | bytes 786432 | tf_op jit(solution)/shard_map/all_to_all | solution.py:939
  188.3 13.0 %shard_map.227 = (bf16[49,16,2048]{2,1,0:T(8,128)(2,1)}, bf16[49,16,2048]{2,1,0:T(8,128)(2,1)}, bf16[49,16,2048]{2,1,0:T(8,128)(2,1)}, f32[49,16,512]{2,1,0:T(8,...) custom-call(s32[3]{0:T(128)S(1)} %pad_add_fusion.core_ref.place, ...), custom_call_target="tpu_custom_call" | custom-call | flops 5000000000 | bytes 15000000 | tf_op jit(solution)/shard_map/pallas_call | solution.py:884
  202.4 9.3 %all-to-all-start.3 = ((f32[16,8,384]{2,1,0:T(8,128)}), f32[16,8,384]{2,1,0:T(8,128)S(1)}, u32[]{:S(2)}, u32[]{:S(2)}) async-start(f32[16,8,384]{2,1,0:T(8,128)} %get-tuple-element.153), calls=%async_computation.3 | async-start | bytes 393216 | tf_op jit(solution)/shard_map/all_to_all | solution.py:939
  214.2 6.5 all-to-all-done.3.g
  222.2 13.9 %shard_map.229 = (f32[49,16,512]{2,1,0:T(8,128)}, bf16[49,16,512]{2,1,0:T(8,128)(2,1)S(1)}, bf16[49,16,128]{2,1,0:T(8,128)(2,1)S(1)}, bf16[49,16,512]{2,1,0:T(8,...) custom-call(s32[3]{0:T(128)S(1)} %pad_add_fusion.core_ref.place, ...), custom_call_target="tpu_custom_call" | custom-call | flops 5000000000 | bytes 15000000 | tf_op jit(solution)/shard_map/pallas_call | solution.py:884
  237.7 12.1 %all_to_all.66.g = f32[16,8,384]{2,1,0:T(8,128)S(1)} all-to-all(f32[16,8,384]{2,1,0:T(8,128)S(1)} %get-tuple-element.159), channel_id=1, replica_groups=mesh['pipe'=2,'dp'=16] {'dp'}, dimensions={0} | all-to-all | bytes 393216 | tf_op jit(solution)/shard_map/all_to_all | solution.py:939
  251.2 7.6 %shard_map.230 = (bf16[49,16,512]{2,1,0:T(8,128)(2,1)S(1)}, f32[8,1024]{1,0:T(8,128)S(1)}, f32[8,1024]{1,0:T(8,128)S(1)}, f32[8,512]{1,0:T(8,128)S(1)}) custom-call(s32[3]{0:T(128)S(1)} %pad_add_fusion.core_ref.place, f32[49,16,512]{2,1,0:T(8,128)} %get-tuple-element.158.second, f32[16,8,384]{2,1,0:T(8,128)S(1)} %all_to_all.66.g, ...), custom_call_target="tpu_custom_call" | custom-call | flops 5000000000 | bytes 15000000 | tf_op jit(solution)/shard_map/pallas_call | solution.py:884
  260.1 16.3 %all_to_all.67.g = f32[16,8,768]{2,1,0:T(8,128)S(1)} all-to-all(f32[16,8,768]{2,1,0:T(8,128)S(1)} %shard_map.231), channel_id=1, replica_groups=mesh['pipe'=2,'dp'=16] {'dp'}, dimensions={0} | all-to-all | bytes 786432 | tf_op jit(solution)/shard_map/all_to_all | solution.py:939
  278.1 13.4 %shard_map.232 = (bf16[49,16,2048]{2,1,0:T(8,128)(2,1)}, bf16[49,16,2048]{2,1,0:T(8,128)(2,1)}, bf16[49,16,2048]{2,1,0:T(8,128)(2,1)}, f32[8,1024]{1,0:T(8,128)S...) custom-call(s32[3]{0:T(128)S(1)} %pad_add_fusion.core_ref.place, ...), custom_call_target="tpu_custom_call" | custom-call | flops 5000000000 | bytes 15000000 | tf_op jit(solution)/shard_map/pallas_call | solution.py:884
  292.8 16.3 %all_to_all.68.g = f32[16,8,768]{2,1,0:T(8,128)S(1)} all-to-all(f32[16,8,768]{2,1,0:T(8,128)S(1)} %shard_map.233), channel_id=1, replica_groups=mesh['pipe'=2,'dp'=16] {'dp'}, dimensions={0} | all-to-all | bytes 786432 | tf_op jit(solution)/shard_map/all_to_all | solution.py:939
  310.9 9.4 %shard_map.234 = (f32[49,16,512]{2,1,0:T(8,128)}, f32[16,8,384]{2,1,0:T(8,128)S(1)}, bf16[49,16,2048]{2,1,0:T(8,128)(2,1)}, f32[8,2048]{1,0:T(8,128)S(1)}) custom-call(s32[3]{0:T(128)S(1)} %pad_add_fusion.core_ref.place, bf16[49,16,2048]{2,1,0:T(8,128)(2,1)} %get-tuple-element.165.dz.dz_ref, bf16[49,16,2048]{2,1,0:T(8,128)(2,1)} %get-tuple-element.166.xhat_ref, ...), custom_call_target="tpu_custom_call" | custom-call | flops 5000000000 | bytes 15000000 | tf_op jit(solution)/shard_map/pallas_call | solution.py:884
  320.3 12.4 %all_to_all.69.g = f32[16,8,384]{2,1,0:T(8,128)S(1)} all-to-all(f32[16,8,384]{2,1,0:T(8,128)S(1)} %get-tuple-element.173), channel_id=1, replica_groups=mesh['pipe'=2,'dp'=16] {'dp'}, dimensions={0} | all-to-all | bytes 393216 | tf_op jit(solution)/shard_map/all_to_all | solution.py:939
  334.1 3.8 shard_map.235
  338.8 15.2 %shard_map.236 = (f32[49,16,512]{2,1,0:T(8,128)}, f32[16,8,384]{2,1,0:T(8,128)}, bf16[49,16,512]{2,1,0:T(8,128)(2,1)S(1)}, bf16[49,16,128]{2,1,0:T(8,128)(2,1)S(1)}) custom-call(s32[3]{0:T(128)S(1)} %pad_add_fusion.core_ref.place, bf16[49,16,512]{2,1,0:T(8,128)(2,1)} %copy-done.10, f32[49,16,512]{2,1,0:T(8,128)} %get-tuple-element.175.a_ref, ...), custom_call_target="tpu_custom_call" | custom-call | flops 5000000000 | bytes 15000000 | tf_op jit(solution)/shard_map/pallas_call | solution.py:884
  360.9 14.3 %shard_map.237 = (bf16[4,2,2,16,9088]{4,3,2,1,0:T(8,128)(2,1)}, bf16[4,2,2,16,9088]{4,3,2,1,0:T(8,128)(2,1)}) custom-call(s32[3]{0:T(128)S(1)} %pad_add_fusion.core_ref.place, bf16[49,16,512]{2,1,0:T(8,128)(2,1)S(1)} %copy-done.11, bf16[49,16,512]{2,1,0:T(8,128)(2,1)S(1)} %copy-done.13, bf16[49,16,128]{2,1,0:T(8,128)(2,1)S(1)} %get-tuple-element.181.dsq, ...), custom_call_target="tpu_custom_call" | custom-call | flops 5000000000 | bytes 15000000 | tf_op jit(solution)/shard_map/pallas_call | solution.py:884
  377.1 14.4 %shard_map.238 = (bf16[49,16,2048]{2,1,0:T(8,128)(2,1)}, bf16[49,16,512]{2,1,0:T(8,128)(2,1)}, f32[8,512]{1,0:T(8,128)S(1)}, bf16[49,16,2048]{2,1,0:T(8,128)(2,1...) custom-call(s32[3]{0:T(128)S(1)} %pad_add_fusion.core_ref.place, f32[49,16,512]{2,1,0:T(8,128)} %get-tuple-element.178.dn1, ...), custom_call_target="tpu_custom_call" | custom-call | flops 5000000000 | bytes 15000000 | tf_op jit(solution)/shard_map/pallas_call | solution.py:884
  391.6 5.7 add_convert_fusion
  398.6 24.9 %all_to_all.70.g = f32[16,8,768]{2,1,0:T(8,128)S(1)} all-to-all(f32[16,8,768]{2,1,0:T(8,128)S(1)} %shard_map.239), channel_id=1, replica_groups=mesh['pipe'=2,'dp'=16] {'dp'}, dimensions={0} | all-to-all | bytes 786432 | tf_op jit(solution)/shard_map/all_to_all | solution.py:939
  425.4 9.5 %shard_map.240 = (f32[49,16,512]{2,1,0:T(8,128)}, f32[16,8,384]{2,1,0:T(8,128)}, bf16[49,16,2048]{2,1,0:T(8,128)(2,1)}, f32[8,2048]{1,0:T(8,128)S(1)}) custom-call(s32[3]{0:T(128)S(1)} %pad_add_fusion.core_ref.place, bf16[49,16,2048]{2,1,0:T(8,128)(2,1)} %get-tuple-element.192.dz.dz_ref, bf16[49,16,2048]{2,1,0:T(8,128)(2,1)} %get-tuple-element.190.xhat_ref, ...), custom_call_target="tpu_custom_call" | custom-call | flops 5000000000 | bytes 15000000 | tf_op jit(solution)/shard_map/pallas_call | solution.py:884
  434.9 4.1 all-to-all-start.10
  441.2 10.3 %shard_map.241 = (bf16[4,2,2,16,4096]{4,3,2,1,0:T(8,128)(2,1)}, bf16[4,2,2,16,4096]{4,3,2,1,0:T(8,128)(2,1)}) custom-call(s32[3]{0:T(128)S(1)} %pad_add_fusion.core_ref.place, bf16[49,16,2048]{2,1,0:T(8,128)(2,1)} %get-tuple-element.203.d3, bf16[49,16,512]{2,1,0:T(8,128)(2,1)S(1)} %copy-done.8, bf16[49,16,512]{2,1,0:T(8,128)(2,1)S(1)} %copy-done.3, ...), custom_call_target="tpu_custom_call" | custom-call | flops 5000000000 | bytes 15000000 | tf_op jit(solution)/shard_map/pallas_call | solution.py:884
  453.2 12.3 %shard_map.242 = (bf16[4,2,16,2048]{3,2,1,0:T(8,128)(2,1)S(1)}, bf16[4,2,16,2048]{3,2,1,0:T(8,128)(2,1)S(1)}, bf16[4,2,16,2048]{3,2,1,0:T(8,128)(2,1)S(1)}, bf16...) custom-call(s32[3]{0:T(128)S(1)} %pad_add_fusion.core_ref.place, ...), custom_call_target="tpu_custom_call" | custom-call | flops 5000000000 | bytes 15000000 | tf_op jit(solution)/shard_map/pallas_call | solution.py:884
  468.4 15.6 %shard_map.243 = (f32[49,16,512]{2,1,0:T(8,128)}, f32[16,8,384]{2,1,0:T(8,128)}, bf16[49,16,512]{2,1,0:T(8,128)(2,1)S(1)}, bf16[49,16,128]{2,1,0:T(8,128)(2,1)S(1)}) custom-call(s32[3]{0:T(128)S(1)} %pad_add_fusion.core_ref.place, bf16[49,16,512]{2,1,0:T(8,128)(2,1)} %get-tuple-element.209.d2, f32[49,16,512]{2,1,0:T(8,128)} %get-tuple-element.210.a_ref, ...), custom_call_target="tpu_custom_call" | custom-call | flops 5000000000 | bytes 15000000 | tf_op jit(solution)/shard_map/pallas_call | solution.py:884
  486.1 6.9 %all-to-all-start.11 = ((f32[16,8,384]{2,1,0:T(8,128)}), f32[16,8,384]{2,1,0:T(8,128)S(1)}, u32[]{:S(2)}, u32[]{:S(2)}) async-start(f32[16,8,384]{2,1,0:T(8,128)} %get-tuple-element.214), calls=%async_computation.11 | async-start | bytes 393216 | tf_op jit(solution)/shard_map/all_to_all | solution.py:939
  506.2 5.9 shard_map.244
  514.0 8.6 %shard_map.245 = (bf16[4,2,2,16,2048]{4,3,2,1,0:T(8,128)(2,1)}, bf16[4,2,2,16,2048]{4,3,2,1,0:T(8,128)(2,1)}, bf16[49,16,512]{2,1,0:T(8,128)(2,1)S(1)}, f32[8,512]{1,0:T(8,128)S(1)}) custom-call(s32[3]{0:T(128)S(1)} %pad_add_fusion.core_ref.place, f32[49,16,512]{2,1,0:T(8,128)} %get-tuple-element.213.dn1, f32[49,16,512]{2,1,0:T(8,128)} %collective-permute-done.44.other, ...), custom_call_target="tpu_custom_call" | custom-call | flops 5000000000 | bytes 15000000 | tf_op jit(solution)/shard_map/pallas_call | solution.py:884
  533.6 6.5 collective-permute-start.52
  543.4 9.0 %all-to-all-start.12 = ((bf16[16,16,4480]{2,1,0:T(8,128)(2,1)}), bf16[16,16,4480]{2,1,0:T(8,128)(2,1)}, u32[]{:S(2)}, u32[]{:S(2)}) async-start(bf16[16,16,4480]{2,1,0:T(8,128)(2,1)} %pad_maximum_fusion), calls=%async_computation.12 | async-start | bytes 4587520 | tf_op jit(solution)/shard_map/all_to_all | solution.py:1048
  553.5 6.6 %shard_map.247.early_ref = bf16[49,16,2048]{2,1,0:T(8,128)(2,1)} custom-call(s32[3]{0:T(128)S(1)} %pad_add_fusion.core_ref.place, bf16[49,16,512]{2,1,0:T(8,128)(2,1)} %copy-done.18, bf16[49,16,2048]{2,1,0:T(8,128)(2,1)} %get-tuple-element.192.dz.dz_ref, bf16[4,2,16,1024]{3,2,1,0:T(8,128)(2,1)S(1)} %copy.116.rest_0_, ...), custom_call_target="tpu_custom_call" | custom-call | flops 5000000000 | bytes 15000000 | tf_op jit(solution)/shard_map/pallas_call | solution.py:884
  561.4 6.6 %collective-permute-start.54 = (bf16[49,16,2048]{2,1,0:T(8,128)(2,1)}, bf16[49,16,2048]{2,1,0:T(8,128)(2,1)}, u32[]{:S(2)}, u32[]{:S(2)}) collective-permute-start(bf16[49,16,2048]{2,1,0:T(8,128)(2,1)} %get-tuple-element.236.late_ref), channel_id=1, source_target_pairs={{0,16},{1,17},{2,18},{3,19},{4,20},{5,21},{6,22},{7,23},{8,24},{9,... | collective-permute-start | bytes 9633800 | tf_op jit(solution)/shard_map/ppermute | solution.py:1285
  570.1 9.8 %shard_map.246 = bf16[3,392,2048]{2,1,0:T(8,128)(2,1)} custom-call(s32[3]{0:T(128)S(1)} %pad_add_fusion.core_ref.place, bf16[49,16,2048]{2,1,0:T(8,128)(2,1)} %get-tuple-element.230.x_ref.early_ref, bf16[49,16,2048]{2,1,0:T(8,128)(2,1)} %get-tuple-element.231.late_ref, bf16[49,16,2048]{2,1,0:T(8,128)(2,1)} %collective-permute-done.51.early_in, ...), custom_call_target="tpu_custom_call" | custom-call | flops 5000000000 | bytes 15000000 | tf_op jit(solution)/shard_map/pallas_call | solution.py:884
  579.9 29.5 %collective-permute-done.64 = bf16[2,16,4608]{2,1,0:T(8,128)(2,1)S(1)} collective-permute-done((bf16[2,16,4608]{2,1,0:T(8,128)(2,1)S(1)}, bf16[2,16,4608]{2,1,0:T(8,128)(2,1)S(1)}, u32[]{:S(2)}, u32[]{:S(2)}) %collective-permute-start.64) | collective-permute-done | bytes 294944 | tf_op jit(solution)/shard_map/ppermute | solution.py:936
  612.8 13.0 %reduce-scatter.3.cloned.1.call-done = bf16[1,16,4096]{2,1,0:T(8,128)(2,1)} async-done(((bf16[16,16,4096]{2,1,0:T(8,128)(2,1)}), bf16[1,16,4096]{2,1,0:T(8,128)(2,1)}) %reduce-scatter.3.cloned.1.call-update) | async-done | bytes 131088 | tf_op jit(solution)/shard_map/reduce_scatter | solution.py:1045
  627.9 9.8 %shard_map.248 = bf16[3,392,2048]{2,1,0:T(8,128)(2,1)} custom-call(s32[3]{0:T(128)S(1)} %pad_add_fusion.core_ref.place, bf16[49,16,2048]{2,1,0:T(8,128)(2,1)} %shard_map.247.early_ref, bf16[49,16,2048]{2,1,0:T(8,128)(2,1)} %get-tuple-element.236.late_ref, bf16[49,16,2048]{2,1,0:T(8,128)(2,1)} %collective-permute-done.53.early_in, ...), custom_call_target="tpu_custom_call" | custom-call | flops 5000000000 | bytes 15000000 | tf_op jit(solution)/shard_map/pallas_call | solution.py:884
  (356 shorter events, 143.2 us)
Async XLA Ops:
  7.2 97.1 %all-gather.5.cloned.1.call-start = ((), (), s32[]{:S(2)}) async-start(), calls=%async_computation.17 | async-start | bytes 3829760 | tf_op jit(solution)/shard_map/all_gather | solution.py:968
  25.1 10.1 %collective-permute-start.4 = (bf16[2,16,2176]{2,1,0:T(8,128)(2,1)S(1)}, bf16[2,16,2176]{2,1,0:T(8,128)(2,1)S(1)}, u32[]{:S(2)}, u32[]{:S(2)}) collective-permute-start(bf16[2,16,2176]{2,1,0:T(8,128)(2,1)S(1)} %maximum_select_fusion.10), channel_id=1, source_target_pairs={{0,4},{1,5},{2,6},{3,7},{4,0},{5,1},{6,2},{7,3},{8,12},{9,13},{10,... | collective-permute-start | bytes 417800 | tf_op jit(solution)/shard_map/ppermute | solution.py:936
  35.2 16.5 %collective-permute-start.5 = (bf16[16,4224]{1,0:T(8,128)(2,1)S(1)}, bf16[16,4224]{1,0:T(8,128)(2,1)S(1)}, u32[]{:S(2)}, u32[]{:S(2)}) collective-permute-start(bf16[16,4224]{1,0:T(8,128)(2,1)S(1)} %get-tuple-element.135), channel_id=1, source_target_pairs={{0,8},{1,9},{2,10},{3,11},{4,12},{5,13},{6,14},{7,15},{8,0},{9,1},... | collective-permute-start | bytes 405512 | tf_op jit(solution)/shard_map/ppermute | solution.py:936
  38.7 12.4 %collective-permute-start.7 = (bf16[4,16,1024]{2,1,0:T(8,128)(2,1)S(1)}, bf16[4,16,1024]{2,1,0:T(8,128)(2,1)S(1)}, u32[]{:S(2)}, u32[]{:S(2)}) collective-permute-start(bf16[4,16,1024]{2,1,0:T(8,128)(2,1)S(1)} %get-tuple-element.293), channel_id=1, source_target_pairs={{0,1},{1,0},{2,3},{3,2},{4,5},{5,4},{6,7},{7,6},{8,9},{9,8},{10,11... | collective-permute-start | bytes 393224 | tf_op jit(solution)/shard_map/ppermute | solution.py:936
  51.1 11.9 %collective-permute-start.8 = (bf16[4,2,16,1024]{3,2,0,1:T(8,128)(2,1)S(1)}, bf16[4,2,16,1024]{3,2,0,1:T(8,128)(2,1)S(1)}, u32[]{:S(2)}, u32[]{:S(2)}) collective-permute-start(bf16[4,2,16,1024]{3,2,0,1:T(8,128)(2,1)S(1)} %maximum_select_fusion.8), channel_id=1, source_target_pairs={{0,2},{1,3},{2,0},{3,1},{4,6},{5,7},{6,4},{7,5},{8,10},{9,11},{10,... | collective-permute-start | bytes 786440 | tf_op jit(solution)/shard_map/ppermute | solution.py:936
  51.7 11.4 %collective-permute-start.11 = (bf16[4,2,16,1024]{3,2,0,1:T(8,128)(2,1)S(1)}, bf16[4,2,16,1024]{3,2,0,1:T(8,128)(2,1)S(1)}, u32[]{:S(2)}, u32[]{:S(2)}) collective-permute-start(bf16[4,2,16,1024]{3,2,0,1:T(8,128)(2,1)S(1)} %maximum_select_fusion.8), channel_id=1, source_target_pairs={{0,16},{16,0},{1,17},{17,1},{2,18},{18,2},{3,19},{19,3},{4,20},{20... | collective-permute-start | bytes 786440 | tf_op jit(solution)/shard_map/ppermute | solution.py:933
  51.8 15.2 %collective-permute-start.6 = (bf16[2,16,4224]{2,1,0:T(8,128)(2,1)S(1)}, bf16[2,16,4224]{2,1,0:T(8,128)(2,1)S(1)}, u32[]{:S(2)}, u32[]{:S(2)}) collective-permute-start(bf16[2,16,4224]{2,1,0:T(8,128)(2,1)S(1)} %maximum_select_fusion.7), channel_id=1, source_target_pairs={{0,4},{1,5},{2,6},{3,7},{4,0},{5,1},{6,2},{7,3},{8,12},{9,13},{10,... | collective-permute-start | bytes 811016 | tf_op jit(solution)/shard_map/ppermute | solution.py:936
  76.8 21.0 %all-to-all-start = ((f32[16,8,384]{2,1,0:T(8,128)}), f32[16,8,384]{2,1,0:T(8,128)S(1)}, u32[]{:S(2)}, u32[]{:S(2)}) async-start(f32[16,8,384]{2,1,0:T(8,128)} %get-tuple-element.140), calls=%async_computation | async-start | bytes 393216 | tf_op jit(solution)/shard_map/all_to_all | solution.py:939
  81.1 120.8 %all-gather.7.cloned.1.call-start = ((), (), s32[]{:S(2)}) async-start(), calls=%async_computation.18 | async-start | bytes 4943872 | tf_op jit(solution)/shard_map/all_gather | solution.py:968
  81.2 14.8 %collective-permute-start.16 = (bf16[4,16,2048]{2,1,0:T(8,128)(2,1)S(1)}, bf16[4,16,2048]{2,1,0:T(8,128)(2,1)S(1)}, u32[]{:S(2)}, u32[]{:S(2)}) collective-permute-start(bf16[4,16,2048]{2,1,0:T(8,128)(2,1)S(1)} %get-tuple-element.287), channel_id=1, source_target_pairs={{0,1},{1,0},{2,3},{3,2},{4,5},{5,4},{6,7},{7,6},{8,9},{9,8},{10,11... | collective-permute-start | bytes 786440 | tf_op jit(solution)/shard_map/ppermute | solution.py:936
  83.2 13.6 %collective-permute-start.17 = (bf16[4,16,2176]{2,1,0:T(8,128)(2,1)S(1)}, bf16[4,16,2176]{2,1,0:T(8,128)(2,1)S(1)}, u32[]{:S(2)}, u32[]{:S(2)}) collective-permute-start(bf16[4,16,2176]{2,1,0:T(8,128)(2,1)S(1)} %get-tuple-element.285), channel_id=1, source_target_pairs={{0,2},{1,3},{2,0},{3,1},{4,6},{5,7},{6,4},{7,5},{8,10},{9,11},{10,... | collective-permute-start | bytes 835592 | tf_op jit(solution)/shard_map/ppermute | solution.py:936
  104.3 9.3 %collective-permute-start.19 = (bf16[4,2,2,16,7040]{4,3,2,1,0:T(8,128)(2,1)}, bf16[4,2,2,16,7040]{4,3,2,1,0:T(8,128)(2,1)}, u32[]{:S(2)}, u32[]{:S(2)}) collective-permute-start(bf16[4,2,2,16,7040]{4,3,2,1,0:T(8,128)(2,1)} %bitcast.202), channel_id=1, source_target_pairs={{0,16},{16,0},{1,17},{17,1},{2,18},{18,2},{3,19},{19,3},{4,20},{20... | collective-permute-start | bytes 10813448 | tf_op jit(solution)/shard_map/ppermute | solution.py:933
  105.3 30.3 %collective-permute-start.21 = (bf16[4,2,16,2048]{3,2,0,1:T(8,128)(2,1)}, bf16[4,2,16,2048]{3,2,0,1:T(8,128)(2,1)}, u32[]{:S(2)}, u32[]{:S(2)}) collective-permute-start(bf16[4,2,16,2048]{3,2,0,1:T(8,128)(2,1)} %maximum_select_fusion.2), channel_id=1, source_target_pairs={{0,2},{1,3},{2,0},{3,1},{4,6},{5,7},{6,4},{7,5},{8,10},{9,11},{10,... | collective-permute-start | bytes 1572872 | tf_op jit(solution)/shard_map/ppermute | solution.py:936
  106.7 28.2 %collective-permute-start.22 = (bf16[4,2,16,2176]{3,2,1,0:T(8,128)(2,1)}, bf16[4,2,16,2176]{3,2,1,0:T(8,128)(2,1)}, u32[]{:S(2)}, u32[]{:S(2)}) collective-permute-start(bf16[4,2,16,2176]{3,2,1,0:T(8,128)(2,1)} %maximum_select_fusion.rest_2_.rest_10_), channel_id=1, source_target_pairs={{0,1},{1,0},{2,3},{3,2},{4,5},{5,4},{6,7},{7,6},{8,9},{9,8},{10,11... | collective-permute-start | bytes 1671176 | tf_op jit(solution)/shard_map/ppermute | solution.py:936
  130.0 17.2 %all-to-all-start.1 = ((f32[16,8,384]{2,1,0:T(8,128)}), f32[16,8,384]{2,1,0:T(8,128)S(1)}, u32[]{:S(2)}, u32[]{:S(2)}) async-start(f32[16,8,384]{2,1,0:T(8,128)} %get-tuple-element.146), calls=%async_computation.1 | async-start | bytes 393216 | tf_op jit(solution)/shard_map/all_to_all | solution.py:939
  134.8 18.5 %collective-permute-start.25 = (bf16[4,2,16,2176]{3,2,1,0:T(8,128)(2,1)}, bf16[4,2,16,2176]{3,2,1,0:T(8,128)(2,1)}, u32[]{:S(2)}, u32[]{:S(2)}) collective-permute-start(bf16[4,2,16,2176]{3,2,1,0:T(8,128)(2,1)} %maximum_select_fusion.rest_2_.rest_10_), channel_id=1, source_target_pairs={{0,16},{16,0},{1,17},{17,1},{2,18},{18,2},{3,19},{19,3},{4,20},{20... | collective-permute-start | bytes 1671176 | tf_op jit(solution)/shard_map/ppermute | solution.py:933
  134.9 18.4 %collective-permute-start.26 = (bf16[4,2,16,2176]{3,2,1,0:T(8,128)(2,1)}, bf16[4,2,16,2176]{3,2,1,0:T(8,128)(2,1)}, u32[]{:S(2)}, u32[]{:S(2)}) collective-permute-start(bf16[4,2,16,2176]{3,2,1,0:T(8,128)(2,1)} %collective-permute-done.22.rest_3_.rest_11_), channel_id=1, source_target_pairs={{0,16},{16,0},{1,17},{17,1},{2,18},{18,2},{3,19},{19,3},{4,20},{20... | collective-permute-start | bytes 1671176 | tf_op jit(solution)/shard_map/ppermute | solution.py:933
  135.4 14.0 %collective-permute-start.23 = (bf16[4,2,16,2048]{3,2,0,1:T(8,128)(2,1)}, bf16[4,2,16,2048]{3,2,0,1:T(8,128)(2,1)}, u32[]{:S(2)}, u32[]{:S(2)}) collective-permute-start(bf16[4,2,16,2048]{3,2,0,1:T(8,128)(2,1)} %maximum_select_fusion.2), channel_id=1, source_target_pairs={{0,16},{16,0},{1,17},{17,1},{2,18},{18,2},{3,19},{19,3},{4,20},{20... | collective-permute-start | bytes 1572872 | tf_op jit(solution)/shard_map/ppermute | solution.py:933
  135.5 16.0 %collective-permute-start.24 = (bf16[4,2,16,2048]{3,2,0,1:T(8,128)(2,1)}, bf16[4,2,16,2048]{3,2,0,1:T(8,128)(2,1)}, u32[]{:S(2)}, u32[]{:S(2)}) collective-permute-start(bf16[4,2,16,2048]{3,2,0,1:T(8,128)(2,1)} %collective-permute-done.21), channel_id=1, source_target_pairs={{0,16},{16,0},{1,17},{17,1},{2,18},{18,2},{3,19},{19,3},{4,20},{20... | collective-permute-start | bytes 1572872 | tf_op jit(solution)/shard_map/ppermute | solution.py:933
  201.9 20.2 %collective-permute-start.31 = (bf16[4,2,2,16,9088]{4,3,2,1,0:T(8,128)(2,1)}, bf16[4,2,2,16,9088]{4,3,2,1,0:T(8,128)(2,1)}, u32[]{:S(2)}, u32[]{:S(2)}) collective-permute-start(bf16[4,2,2,16,9088]{4,3,2,1,0:T(8,128)(2,1)} %bitcast.196), channel_id=1, source_target_pairs={{0,16},{16,0},{1,17},{17,1},{2,18},{18,2},{3,19},{19,3},{4,20},{20... | collective-permute-start | bytes 13959176 | tf_op jit(solution)/shard_map/ppermute | solution.py:933
  202.1 20.1 %collective-permute-start.29 = (f32[49,16,512]{2,1,0:T(8,128)}, f32[49,16,512]{2,1,0:T(8,128)}, u32[]{:S(2)}, u32[]{:S(2)}) collective-permute-start(f32[49,16,512]{2,1,0:T(8,128)} %get-tuple-element.152.a_in), channel_id=1, source_target_pairs={{0,16},{16,0},{1,17},{17,1},{2,18},{18,2},{3,19},{19,3},{4,20},{20... | collective-permute-start | bytes 4816904 | tf_op jit(solution)/shard_map/ppermute | solution.py:933
  202.4 18.3 %all-to-all-start.3 = ((f32[16,8,384]{2,1,0:T(8,128)}), f32[16,8,384]{2,1,0:T(8,128)S(1)}, u32[]{:S(2)}, u32[]{:S(2)}) async-start(f32[16,8,384]{2,1,0:T(8,128)} %get-tuple-element.153), calls=%async_computation.3 | async-start | bytes 393216 | tf_op jit(solution)/shard_map/all_to_all | solution.py:939
  354.9 21.8 %collective-permute-start.38 = (f32[49,16,512]{2,1,0:T(8,128)}, f32[49,16,512]{2,1,0:T(8,128)}, u32[]{:S(2)}, u32[]{:S(2)}) collective-permute-start(f32[49,16,512]{2,1,0:T(8,128)} %get-tuple-element.178.dn1), channel_id=1, source_target_pairs={{0,16},{16,0},{1,17},{17,1},{2,18},{18,2},{3,19},{19,3},{4,20},{20... | collective-permute-start | bytes 4816904 | tf_op jit(solution)/shard_map/ppermute | solution.py:933
  355.1 20.1 %all-to-all-start.8 = ((f32[16,8,384]{2,1,0:T(8,128)}), f32[16,8,384]{2,1,0:T(8,128)S(1)}, u32[]{:S(2)}, u32[]{:S(2)}) async-start(f32[16,8,384]{2,1,0:T(8,128)} %get-tuple-element.179), calls=%async_computation.8 | async-start | bytes 393216 | tf_op jit(solution)/shard_map/all_to_all | solution.py:939
  358.6 252.9 %reduce-scatter.5.cloned.1.call-start = ((), (), s32[]{:S(2)}) async-start(), calls=%async_computation.16 | async-start | bytes 4943872 | tf_op jit(solution)/shard_map/reduce_scatter | solution.py:1045
  376.7 14.8 %collective-permute-start.40 = (bf16[4,2,2,16,9088]{4,3,2,1,0:T(8,128)(2,1)}, bf16[4,2,2,16,9088]{4,3,2,1,0:T(8,128)(2,1)}, u32[]{:S(2)}, u32[]{:S(2)}) collective-permute-start(bf16[4,2,2,16,9088]{4,3,2,1,0:T(8,128)(2,1)} %get-tuple-element.195), channel_id=1, source_target_pairs={{0,16},{16,0},{1,17},{17,1},{2,18},{18,2},{3,19},{19,3},{4,20},{20... | collective-permute-start | bytes 13959176 | tf_op jit(solution)/shard_map/ppermute | solution.py:933
  434.9 16.7 %all-to-all-start.10 = ((f32[16,8,384]{2,1,0:T(8,128)}), f32[16,8,384]{2,1,0:T(8,128)S(1)}, u32[]{:S(2)}, u32[]{:S(2)}) async-start(f32[16,8,384]{2,1,0:T(8,128)} %get-tuple-element.202), calls=%async_computation.10 | async-start | bytes 393216 | tf_op jit(solution)/shard_map/all_to_all | solution.py:939
  453.1 47.3 %collective-permute-start.45 = (bf16[4,2,2,16,4096]{4,3,2,1,0:T(8,128)(2,1)}, bf16[4,2,2,16,4096]{4,3,2,1,0:T(8,128)(2,1)}, u32[]{:S(2)}, u32[]{:S(2)}) collective-permute-start(bf16[4,2,2,16,4096]{4,3,2,1,0:T(8,128)(2,1)} %get-tuple-element.216), channel_id=1, source_target_pairs={{0,16},{16,0},{1,17},{17,1},{2,18},{18,2},{3,19},{19,3},{4,20},{20... | collective-permute-start | bytes 6291464 | tf_op jit(solution)/shard_map/ppermute | solution.py:933
  467.4 26.5 %collective-permute-start.46 = (bf16[4,2,16,2048]{3,2,0,1:T(8,128)(2,1)}, bf16[4,2,16,2048]{3,2,0,1:T(8,128)(2,1)}, u32[]{:S(2)}, u32[]{:S(2)}) collective-permute-start(bf16[4,2,16,2048]{3,2,0,1:T(8,128)(2,1)} %copy.149), channel_id=1, source_target_pairs={{0,16},{16,0},{1,17},{17,1},{2,18},{18,2},{3,19},{19,3},{4,20},{20... | collective-permute-start | bytes 1572872 | tf_op jit(solution)/shard_map/ppermute | solution.py:933
  468.3 28.1 %collective-permute-start.47 = (bf16[4,2,16,2560]{3,2,1,0:T(8,128)(2,1)}, bf16[4,2,16,2560]{3,2,1,0:T(8,128)(2,1)}, u32[]{:S(2)}, u32[]{:S(2)}) collective-permute-start(bf16[4,2,16,2560]{3,2,1,0:T(8,128)(2,1)} %get-tuple-element.220), channel_id=1, source_target_pairs={{0,16},{16,0},{1,17},{17,1},{2,18},{18,2},{3,19},{19,3},{4,20},{20... | collective-permute-start | bytes 1966088 | tf_op jit(solution)/shard_map/ppermute | solution.py:933
  485.7 26.6 %collective-permute-start.44 = (f32[49,16,512]{2,1,0:T(8,128)}, f32[49,16,512]{2,1,0:T(8,128)}, u32[]{:S(2)}, u32[]{:S(2)}) collective-permute-start(f32[49,16,512]{2,1,0:T(8,128)} %get-tuple-element.213.dn1), channel_id=1, source_target_pairs={{0,16},{16,0},{1,17},{17,1},{2,18},{18,2},{3,19},{19,3},{4,20},{20... | collective-permute-start | bytes 4816904 | tf_op jit(solution)/shard_map/ppermute | solution.py:933
  486.1 26.1 %all-to-all-start.11 = ((f32[16,8,384]{2,1,0:T(8,128)}), f32[16,8,384]{2,1,0:T(8,128)S(1)}, u32[]{:S(2)}, u32[]{:S(2)}) async-start(f32[16,8,384]{2,1,0:T(8,128)} %get-tuple-element.214), calls=%async_computation.11 | async-start | bytes 393216 | tf_op jit(solution)/shard_map/all_to_all | solution.py:939
  492.9 132.9 %reduce-scatter.3.cloned.1.call-start = ((), (), s32[]{:S(2)}) async-start(), calls=%async_computation.15 | async-start | bytes 2228224 | tf_op jit(solution)/shard_map/reduce_scatter | solution.py:1045
  493.0 30.8 %collective-permute-start.61 = (bf16[4,2,16,2560]{3,2,1,0:T(8,128)(2,1)}, bf16[4,2,16,2560]{3,2,1,0:T(8,128)(2,1)}, u32[]{:S(2)}, u32[]{:S(2)}) collective-permute-start(bf16[4,2,16,2560]{3,2,1,0:T(8,128)(2,1)} %get-tuple-element.242), channel_id=1, source_target_pairs={{0,16},{16,0},{1,17},{17,1},{2,18},{18,2},{3,19},{19,3},{4,20},{20... | collective-permute-start | bytes 1966088 | tf_op jit(solution)/shard_map/ppermute | solution.py:933
  493.9 33.9 %collective-permute-start.58 = (bf16[4,2,16,2048]{3,2,0,1:T(8,128)(2,1)}, bf16[4,2,16,2048]{3,2,0,1:T(8,128)(2,1)}, u32[]{:S(2)}, u32[]{:S(2)}) collective-permute-start(bf16[4,2,16,2048]{3,2,0,1:T(8,128)(2,1)} %copy.155), channel_id=1, source_target_pairs={{0,16},{16,0},{1,17},{17,1},{2,18},{18,2},{3,19},{19,3},{4,20},{20... | collective-permute-start | bytes 1572872 | tf_op jit(solution)/shard_map/ppermute | solution.py:933
  498.5 25.3 %collective-permute-start.62 = (bf16[4,2,16,2560]{3,2,1,0:T(8,128)(2,1)}, bf16[4,2,16,2560]{3,2,1,0:T(8,128)(2,1)}, u32[]{:S(2)}, u32[]{:S(2)}) collective-permute-start(bf16[4,2,16,2560]{3,2,1,0:T(8,128)(2,1)} %add_convert_fusion.6), channel_id=1, source_target_pairs={{0,1},{1,0},{2,3},{3,2},{4,5},{5,4},{6,7},{7,6},{8,9},{9,8},{10,11... | collective-permute-start | bytes 1966088 | tf_op jit(solution)/shard_map/ppermute | solution.py:936
  512.3 15.5 %collective-permute-start.59 = (bf16[4,2,16,2048]{3,2,0,1:T(8,128)(2,1)}, bf16[4,2,16,2048]{3,2,0,1:T(8,128)(2,1)S(1)}, u32[]{:S(2)}, u32[]{:S(2)}) collective-permute-start(bf16[4,2,16,2048]{3,2,0,1:T(8,128)(2,1)} %add_convert_fusion.9), channel_id=1, source_target_pairs={{0,2},{1,3},{2,0},{3,1},{4,6},{5,7},{6,4},{7,5},{8,10},{9,11},{10,... | collective-permute-start | bytes 1572872 | tf_op jit(solution)/shard_map/ppermute | solution.py:936
  513.8 15.8 %collective-permute-start.50 = (bf16[4,2,2,16,2432]{4,3,2,1,0:T(8,128)(2,1)}, bf16[4,2,2,16,2432]{4,3,2,1,0:T(8,128)(2,1)S(1)}, u32[]{:S(2)}, u32[]{:S(2)}) collective-permute-start(bf16[4,2,2,16,2432]{4,3,2,1,0:T(8,128)(2,1)} %get-tuple-element.226), channel_id=1, source_target_pairs={{0,16},{16,0},{1,17},{17,1},{2,18},{18,2},{3,19},{19,3},{4,20},{20... | collective-permute-start | bytes 3735560 | tf_op jit(solution)/shard_map/ppermute | solution.py:933
  526.1 26.3 %collective-permute-start.63 = (bf16[4,16,2560]{2,1,0:T(8,128)(2,1)}, bf16[4,16,2560]{2,1,0:T(8,128)(2,1)}, u32[]{:S(2)}, u32[]{:S(2)}) collective-permute-start(bf16[4,16,2560]{2,1,0:T(8,128)(2,1)} %dynamic-slice_bitcast_fusion), channel_id=1, source_target_pairs={{0,2},{1,3},{2,0},{3,1},{4,6},{5,7},{6,4},{7,5},{8,10},{9,11},{10,... | collective-permute-start | bytes 983048 | tf_op jit(solution)/shard_map/ppermute | solution.py:936
  529.2 14.1 %collective-permute-start.60 = (bf16[4,16,2048]{2,1,0:T(8,128)(2,1)S(1)}, bf16[4,16,2048]{2,1,0:T(8,128)(2,1)S(1)}, u32[]{:S(2)}, u32[]{:S(2)}) collective-permute-start(bf16[4,16,2048]{2,1,0:T(8,128)(2,1)S(1)} %dynamic-slice_bitcast_fusion.2), channel_id=1, source_target_pairs={{0,1},{1,0},{2,3},{3,2},{4,5},{5,4},{6,7},{7,6},{8,9},{9,8},{10,11... | collective-permute-start | bytes 786440 | tf_op jit(solution)/shard_map/ppermute | solution.py:936
  532.3 37.8 %collective-permute-start.51 = (bf16[49,16,2048]{2,1,0:T(8,128)(2,1)}, bf16[49,16,2048]{2,1,0:T(8,128)(2,1)}, u32[]{:S(2)}, u32[]{:S(2)}) collective-permute-start(bf16[49,16,2048]{2,1,0:T(8,128)(2,1)} %get-tuple-element.230.x_ref.early_ref), channel_id=1, source_target_pairs={{16,0},{17,1},{18,2},{19,3},{20,4},{21,5},{22,6},{23,7},{24,8},{25... | collective-permute-start | bytes 9633800 | tf_op jit(solution)/shard_map/ppermute | solution.py:1285
  533.6 36.5 %collective-permute-start.52 = (bf16[49,16,2048]{2,1,0:T(8,128)(2,1)}, bf16[49,16,2048]{2,1,0:T(8,128)(2,1)}, u32[]{:S(2)}, u32[]{:S(2)}) collective-permute-start(bf16[49,16,2048]{2,1,0:T(8,128)(2,1)} %get-tuple-element.231.late_ref), channel_id=1, source_target_pairs={{0,16},{1,17},{2,18},{3,19},{4,20},{5,21},{6,22},{7,23},{8,24},{9,... | collective-permute-start | bytes 9633800 | tf_op jit(solution)/shard_map/ppermute | solution.py:1285
  543.4 82.5 %all-to-all-start.12 = ((bf16[16,16,4480]{2,1,0:T(8,128)(2,1)}), bf16[16,16,4480]{2,1,0:T(8,128)(2,1)}, u32[]{:S(2)}, u32[]{:S(2)}) async-start(bf16[16,16,4480]{2,1,0:T(8,128)(2,1)} %pad_maximum_fusion), calls=%async_computation.12 | async-start | bytes 4587520 | tf_op jit(solution)/shard_map/all_to_all | solution.py:1048
  560.1 67.7 %collective-permute-start.53 = (bf16[49,16,2048]{2,1,0:T(8,128)(2,1)}, bf16[49,16,2048]{2,1,0:T(8,128)(2,1)}, u32[]{:S(2)}, u32[]{:S(2)}) collective-permute-start(bf16[49,16,2048]{2,1,0:T(8,128)(2,1)} %shard_map.247.early_ref), channel_id=1, source_target_pairs={{16,0},{17,1},{18,2},{19,3},{20,4},{21,5},{22,6},{23,7},{24,8},{25... | collective-permute-start | bytes 9633800 | tf_op jit(solution)/shard_map/ppermute | solution.py:1285
  561.4 66.4 %collective-permute-start.54 = (bf16[49,16,2048]{2,1,0:T(8,128)(2,1)}, bf16[49,16,2048]{2,1,0:T(8,128)(2,1)}, u32[]{:S(2)}, u32[]{:S(2)}) collective-permute-start(bf16[49,16,2048]{2,1,0:T(8,128)(2,1)} %get-tuple-element.236.late_ref), channel_id=1, source_target_pairs={{0,16},{1,17},{2,18},{3,19},{4,20},{5,21},{6,22},{7,23},{8,24},{9,... | collective-permute-start | bytes 9633800 | tf_op jit(solution)/shard_map/ppermute | solution.py:1285
  568.1 41.3 %collective-permute-start.64 = (bf16[2,16,4608]{2,1,0:T(8,128)(2,1)S(1)}, bf16[2,16,4608]{2,1,0:T(8,128)(2,1)S(1)}, u32[]{:S(2)}, u32[]{:S(2)}) collective-permute-start(bf16[2,16,4608]{2,1,0:T(8,128)(2,1)S(1)} %dynamic-slice_bitcast_fusion.1), channel_id=1, source_target_pairs={{0,4},{1,5},{2,6},{3,7},{4,0},{5,1},{6,2},{7,3},{8,12},{9,13},{10,... | collective-permute-start | bytes 884744 | tf_op jit(solution)/shard_map/ppermute | solution.py:936
  609.5 28.2 %collective-permute-start.65 = (bf16[16,4608]{1,0:T(8,128)(2,1)S(1)}, bf16[16,4608]{1,0:T(8,128)(2,1)S(1)}, u32[]{:S(2)}, u32[]{:S(2)}) collective-permute-start(bf16[16,4608]{1,0:T(8,128)(2,1)S(1)} %dynamic-slice_bitcast_fusion.4), channel_id=1, source_target_pairs={{0,8},{1,9},{2,10},{3,11},{4,12},{5,13},{6,14},{7,15},{8,0},{9,1},... | collective-permute-start | bytes 442376 | tf_op jit(solution)/shard_map/ppermute | solution.py:936
  611.5 33.3 %collective-permute-start.57 = (bf16[16,9088]{1,0:T(8,128)(2,1)}, bf16[16,9088]{1,0:T(8,128)(2,1)S(1)}, u32[]{:S(2)}, u32[]{:S(2)}) collective-permute-start(bf16[16,9088]{1,0:T(8,128)(2,1)} %bitcast.176), channel_id=1, source_target_pairs={{0,16},{1,17},{2,18},{3,19},{4,20},{5,21},{6,22},{7,23},{8,24},{9,... | collective-permute-start | bytes 872456 | tf_op jit(solution)/shard_map/ppermute | solution.py:1054
  (78 other events, 633.2 us)
Sparse Core Ops, SparseCore 0:
  17.2 87.0 all-gather.4
  107.0 89.1 all-gather.6
  397.4 121.1 reduce-scatter.4
  520.8 105.0 reduce-scatter.2

commit v4 on v3

--- a/solution.py
+++ b/solution.py
@@ -1376,7 +1376,7 @@
         input_grads = restore(place, after(dx0, last), dx1, *crossed(dx0, dx1))[0]
         mid_0, _ = links.scatter_z(early, (activations, input_grads))
         in_0, branch_0 = jnp.split(last, [2048], axis=-1)
-        mixed = after(mixed, late)
+        mixed = after(mixed, late, input_grads)
         out_0, in_1 = jnp.split(mixed, 2, axis=-1)
         branch_1, mid_1, out_1 = jnp.split(late, [2432, 7040], axis=-1)
         mid_other, late_other = links.handed(mid_0, late)

time: 668 us -> 665 us (level)
  the two profiles are of different devices: /device:TPU:0 before, /device:TPU:19 now
where the time goes in v4:
time: 665 us; the launch traced here: 654 us
  Pallas kernels  246 us (37%)
  starting transfers between devices  119 us (18%)
  waiting for transfers between devices  104 us (16%)
  blocking collectives  102 us (15%)
  other arithmetic  34.2 us (5%)
  local copies, waits for them, and re-layouts  33.7 us (5%)
  between operations  15.2 us (2%)
    pallas_call x25, Pallas kernels, run(): pl.pallas_call(kernel, in_specs=specs, out_specs=tuple((HB if is_big(o[0]...  246 us
    all_to_all x6, blocking collectives, to_all(): g = lax.all_to_all(spread, 'dp', 0, 0)  102 us
    ppermute x18, waiting for transfers between devices, across(): return lax.ppermute(v, 'dp', [(i, i ^ k) for i in range(self.dp)])  40.5 us
    all_to_all x6, starting transfers between devices, to_all(): g = lax.all_to_all(spread, 'dp', 0, 0)  37 us
    ppermute x41, starting transfers between devices, swap(): return lax.ppermute(v, 'pipe', PAIR)  32.3 us
    ppermute x41, waiting for transfers between devices, swap(): return lax.ppermute(v, 'pipe', PAIR)  23.2 us
    all_to_all x1, waiting for transfers between devices, scatter_at_once(): v = lax.all_to_all(v, 'dp', 0, 0)  21.4 us
    convert_element_type x12, other arithmetic, add(): return (a.astype(F32) + b.astype(F32)).astype(BF16)  18.2 us
  transfers between devices with their start and end apart: 79, of which 30 were waited for; matrix products, arithmetic and copies ran while one was open for 6% of the time, Pallas kernels for 28%

profile of v4, /device:TPU:19, one launch (start us, length us, event | category | flops | bytes accessed | tf_op | source)
XLA Modules:
  0.0 654.4 jit_solution(8964883510029226915)
XLA Ops:
  25.1 9.3 %shard_map.220.x_ref = bf16[49,16,2048]{2,1,0:T(8,128)(2,1)} custom-call(s32[3]{0:T(128)S(1)} %pad_add_fusion.core_ref.place, bf16[3,392,2048]{2,1,0:T(8,128)(2,1)} %x_ref), custom_call_target="tpu_custom_call" | custom-call | flops 5000000000 | bytes 15000000 | tf_op jit(solution)/shard_map/pallas_call | solution.py:884
  34.9 9.2 %shard_map.221.dy_ref = bf16[49,16,2048]{2,1,0:T(8,128)(2,1)} custom-call(s32[3]{0:T(128)S(1)} %pad_add_fusion.core_ref.place, bf16[3,392,2048]{2,1,0:T(8,128)(2,1)} %x_ref.1), custom_call_target="tpu_custom_call" | custom-call | flops 5000000000 | bytes 15000000 | tf_op jit(solution)/shard_map/pallas_call | solution.py:884
  51.4 5.4 collective-permute-start.13
  64.7 7.5 %shard_map.222 = (f32[49,16,512]{2,1,0:T(8,128)}, f32[16,8,384]{2,1,0:T(8,128)}) custom-call(s32[3]{0:T(128)S(1)} %pad_add_fusion.core_ref.place, bf16[49,16,2048]{2,1,0:T(8,128)(2,1)} %shard_map.220.x_ref, bf16[4,2,16,1024]{3,2,1,0:T(8,128)(2,1)S(1)} %copy.116.rest_0_, bf16[4,2,16,1024]{3,2,1,0:T(8,128)(2,1)S(1)} %copy.117.rest_1_, ...), custom_call_target="tpu_custom_call" | custom-call | flops 5000000000 | bytes 15000000 | tf_op jit(solution)/shard_map/pallas_call | solution.py:884
  72.2 7.4 %all-to-all-start = ((f32[16,8,384]{2,1,0:T(8,128)}), f32[16,8,384]{2,1,0:T(8,128)S(1)}, u32[]{:S(2)}, u32[]{:S(2)}) async-start(f32[16,8,384]{2,1,0:T(8,128)} %get-tuple-element.140), calls=%async_computation | async-start | bytes 393216 | tf_op jit(solution)/shard_map/all_to_all | solution.py:939
  84.7 8.7 %collective-permute-done.16 = bf16[4,16,2048]{2,1,0:T(8,128)(2,1)S(1)} collective-permute-done((bf16[4,16,2048]{2,1,0:T(8,128)(2,1)S(1)}, bf16[4,16,2048]{2,1,0:T(8,128)(2,1)S(1)}, u32[]{:S(2)}, u32[]{:S(2)}) %collective-permute-start.16) | collective-permute-done | bytes 262176 | tf_op jit(solution)/shard_map/ppermute | solution.py:936
  95.5 5.9 all-gather.5.cloned.1.call-done
  105.4 4.2 collective-permute-done.18.g_other
  112.0 14.2 %shard_map.224 = (f32[49,16,512]{2,1,0:T(8,128)}, bf16[49,16,512]{2,1,0:T(8,128)(2,1)S(1)}, bf16[49,16,128]{2,1,0:T(8,128)(2,1)S(1)}, bf16[49,16,512]{2,1,0:T(8,...) custom-call(s32[3]{0:T(128)S(1)} %pad_add_fusion.core_ref.place, ...), custom_call_target="tpu_custom_call" | custom-call | flops 5000000000 | bytes 15000000 | tf_op jit(solution)/shard_map/pallas_call | solution.py:884
  128.4 5.0 all-to-all-start.1
  135.0 9.3 %all-to-all-done.1.g = f32[16,8,384]{2,1,0:T(8,128)S(1)} async-done(((f32[16,8,384]{2,1,0:T(8,128)}), f32[16,8,384]{2,1,0:T(8,128)S(1)}, u32[]{:S(2)}, u32[]{:S(2)}) %all-to-all-start.1) | async-done | bytes 196640 | tf_op jit(solution)/shard_map/all_to_all | solution.py:939
  152.3 7.4 %shard_map.225 = (bf16[49,16,512]{2,1,0:T(8,128)(2,1)}, f32[8,1024]{1,0:T(8,128)S(1)}, f32[8,1024]{1,0:T(8,128)S(1)}, f32[8,512]{1,0:T(8,128)S(1)}) custom-call(s32[3]{0:T(128)S(1)} %pad_add_fusion.core_ref.place, f32[49,16,512]{2,1,0:T(8,128)} %get-tuple-element.145.second, f32[16,8,384]{2,1,0:T(8,128)S(1)} %all-to-all-done.1.g, ...), custom_call_target="tpu_custom_call" | custom-call | flops 5000000000 | bytes 15000000 | tf_op jit(solution)/shard_map/pallas_call | solution.py:884
  161.1 26.0 %all_to_all.65.g = f32[16,8,768]{2,1,0:T(8,128)S(1)} all-to-all(f32[16,8,768]{2,1,0:T(8,128)S(1)} %shard_map.226), channel_id=1, replica_groups=mesh['pipe'=2,'dp'=16] {'dp'}, dimensions={0} | all-to-all | bytes 786432 | tf_op jit(solution)/shard_map/all_to_all | solution.py:939
  190.4 13.0 %shard_map.227 = (bf16[49,16,2048]{2,1,0:T(8,128)(2,1)}, bf16[49,16,2048]{2,1,0:T(8,128)(2,1)}, bf16[49,16,2048]{2,1,0:T(8,128)(2,1)}, f32[49,16,512]{2,1,0:T(8,...) custom-call(s32[3]{0:T(128)S(1)} %pad_add_fusion.core_ref.place, ...), custom_call_target="tpu_custom_call" | custom-call | flops 5000000000 | bytes 15000000 | tf_op jit(solution)/shard_map/pallas_call | solution.py:884
  204.6 5.8 all-to-all-start.3
  212.9 3.9 all-to-all-done.3.g
  218.6 13.9 %shard_map.229 = (f32[49,16,512]{2,1,0:T(8,128)}, bf16[49,16,512]{2,1,0:T(8,128)(2,1)S(1)}, bf16[49,16,128]{2,1,0:T(8,128)(2,1)S(1)}, bf16[49,16,512]{2,1,0:T(8,...) custom-call(s32[3]{0:T(128)S(1)} %pad_add_fusion.core_ref.place, ...), custom_call_target="tpu_custom_call" | custom-call | flops 5000000000 | bytes 15000000 | tf_op jit(solution)/shard_map/pallas_call | solution.py:884
  234.1 11.7 %all_to_all.66.g = f32[16,8,384]{2,1,0:T(8,128)S(1)} all-to-all(f32[16,8,384]{2,1,0:T(8,128)S(1)} %get-tuple-element.159), channel_id=1, replica_groups=mesh['pipe'=2,'dp'=16] {'dp'}, dimensions={0} | all-to-all | bytes 393216 | tf_op jit(solution)/shard_map/all_to_all | solution.py:939
  247.7 7.6 %shard_map.230 = (bf16[49,16,512]{2,1,0:T(8,128)(2,1)S(1)}, f32[8,1024]{1,0:T(8,128)S(1)}, f32[8,1024]{1,0:T(8,128)S(1)}, f32[8,512]{1,0:T(8,128)S(1)}) custom-call(s32[3]{0:T(128)S(1)} %pad_add_fusion.core_ref.place, f32[49,16,512]{2,1,0:T(8,128)} %get-tuple-element.158.second, f32[16,8,384]{2,1,0:T(8,128)S(1)} %all_to_all.66.g, ...), custom_call_target="tpu_custom_call" | custom-call | flops 5000000000 | bytes 15000000 | tf_op jit(solution)/shard_map/pallas_call | solution.py:884
  256.6 15.8 %all_to_all.67.g = f32[16,8,768]{2,1,0:T(8,128)S(1)} all-to-all(f32[16,8,768]{2,1,0:T(8,128)S(1)} %shard_map.231), channel_id=1, replica_groups=mesh['pipe'=2,'dp'=16] {'dp'}, dimensions={0} | all-to-all | bytes 786432 | tf_op jit(solution)/shard_map/all_to_all | solution.py:939
  274.8 13.4 %shard_map.232 = (bf16[49,16,2048]{2,1,0:T(8,128)(2,1)}, bf16[49,16,2048]{2,1,0:T(8,128)(2,1)}, bf16[49,16,2048]{2,1,0:T(8,128)(2,1)}, f32[8,1024]{1,0:T(8,128)S...) custom-call(s32[3]{0:T(128)S(1)} %pad_add_fusion.core_ref.place, ...), custom_call_target="tpu_custom_call" | custom-call | flops 5000000000 | bytes 15000000 | tf_op jit(solution)/shard_map/pallas_call | solution.py:884
  289.6 15.6 %all_to_all.68.g = f32[16,8,768]{2,1,0:T(8,128)S(1)} all-to-all(f32[16,8,768]{2,1,0:T(8,128)S(1)} %shard_map.233), channel_id=1, replica_groups=mesh['pipe'=2,'dp'=16] {'dp'}, dimensions={0} | all-to-all | bytes 786432 | tf_op jit(solution)/shard_map/all_to_all | solution.py:939
  307.6 9.4 %shard_map.234 = (f32[49,16,512]{2,1,0:T(8,128)}, f32[16,8,384]{2,1,0:T(8,128)S(1)}, bf16[49,16,2048]{2,1,0:T(8,128)(2,1)}, f32[8,2048]{1,0:T(8,128)S(1)}) custom-call(s32[3]{0:T(128)S(1)} %pad_add_fusion.core_ref.place, bf16[49,16,2048]{2,1,0:T(8,128)(2,1)} %get-tuple-element.165.dz.dz_ref, bf16[49,16,2048]{2,1,0:T(8,128)(2,1)} %get-tuple-element.166.xhat_ref, ...), custom_call_target="tpu_custom_call" | custom-call | flops 5000000000 | bytes 15000000 | tf_op jit(solution)/shard_map/pallas_call | solution.py:884
  317.0 11.7 %all_to_all.69.g = f32[16,8,384]{2,1,0:T(8,128)S(1)} all-to-all(f32[16,8,384]{2,1,0:T(8,128)S(1)} %get-tuple-element.173), channel_id=1, replica_groups=mesh['pipe'=2,'dp'=16] {'dp'}, dimensions={0} | all-to-all | bytes 393216 | tf_op jit(solution)/shard_map/all_to_all | solution.py:939
  335.3 15.2 %shard_map.236 = (f32[49,16,512]{2,1,0:T(8,128)}, f32[16,8,384]{2,1,0:T(8,128)}, bf16[49,16,512]{2,1,0:T(8,128)(2,1)S(1)}, bf16[49,16,128]{2,1,0:T(8,128)(2,1)S(1)}) custom-call(s32[3]{0:T(128)S(1)} %pad_add_fusion.core_ref.place, bf16[49,16,512]{2,1,0:T(8,128)(2,1)} %copy-done.10, f32[49,16,512]{2,1,0:T(8,128)} %get-tuple-element.175.a_ref, ...), custom_call_target="tpu_custom_call" | custom-call | flops 5000000000 | bytes 15000000 | tf_op jit(solution)/shard_map/pallas_call | solution.py:884
  351.8 5.8 all-to-all-start.8
  359.9 14.3 %shard_map.237 = (bf16[4,2,2,16,9088]{4,3,2,1,0:T(8,128)(2,1)}, bf16[4,2,2,16,9088]{4,3,2,1,0:T(8,128)(2,1)}) custom-call(s32[3]{0:T(128)S(1)} %pad_add_fusion.core_ref.place, bf16[49,16,512]{2,1,0:T(8,128)(2,1)S(1)} %copy-done.11, bf16[49,16,512]{2,1,0:T(8,128)(2,1)S(1)} %copy-done.13, bf16[49,16,128]{2,1,0:T(8,128)(2,1)S(1)} %get-tuple-element.181.dsq, ...), custom_call_target="tpu_custom_call" | custom-call | flops 5000000000 | bytes 15000000 | tf_op jit(solution)/shard_map/pallas_call | solution.py:884
  376.2 14.5 %shard_map.238 = (bf16[49,16,2048]{2,1,0:T(8,128)(2,1)}, bf16[49,16,512]{2,1,0:T(8,128)(2,1)}, f32[8,512]{1,0:T(8,128)S(1)}, bf16[49,16,2048]{2,1,0:T(8,128)(2,1...) custom-call(s32[3]{0:T(128)S(1)} %pad_add_fusion.core_ref.place, f32[49,16,512]{2,1,0:T(8,128)} %get-tuple-element.178.dn1, ...), custom_call_target="tpu_custom_call" | custom-call | flops 5000000000 | bytes 15000000 | tf_op jit(solution)/shard_map/pallas_call | solution.py:884
  390.7 5.7 add_convert_fusion
  397.7 21.0 %all_to_all.70.g = f32[16,8,768]{2,1,0:T(8,128)S(1)} all-to-all(f32[16,8,768]{2,1,0:T(8,128)S(1)} %shard_map.239), channel_id=1, replica_groups=mesh['pipe'=2,'dp'=16] {'dp'}, dimensions={0} | all-to-all | bytes 786432 | tf_op jit(solution)/shard_map/all_to_all | solution.py:939
  421.5 9.5 %shard_map.240 = (f32[49,16,512]{2,1,0:T(8,128)}, f32[16,8,384]{2,1,0:T(8,128)}, bf16[49,16,2048]{2,1,0:T(8,128)(2,1)}, f32[8,2048]{1,0:T(8,128)S(1)}) custom-call(s32[3]{0:T(128)S(1)} %pad_add_fusion.core_ref.place, bf16[49,16,2048]{2,1,0:T(8,128)(2,1)} %get-tuple-element.192.dz.dz_ref, bf16[49,16,2048]{2,1,0:T(8,128)(2,1)} %get-tuple-element.190.xhat_ref, ...), custom_call_target="tpu_custom_call" | custom-call | flops 5000000000 | bytes 15000000 | tf_op jit(solution)/shard_map/pallas_call | solution.py:884
  431.0 6.5 all-to-all-start.10
  439.8 10.3 %shard_map.241 = (bf16[4,2,2,16,4096]{4,3,2,1,0:T(8,128)(2,1)}, bf16[4,2,2,16,4096]{4,3,2,1,0:T(8,128)(2,1)}) custom-call(s32[3]{0:T(128)S(1)} %pad_add_fusion.core_ref.place, bf16[49,16,2048]{2,1,0:T(8,128)(2,1)} %get-tuple-element.203.d3, bf16[49,16,512]{2,1,0:T(8,128)(2,1)S(1)} %copy-done.8, bf16[49,16,512]{2,1,0:T(8,128)(2,1)S(1)} %copy-done.3, ...), custom_call_target="tpu_custom_call" | custom-call | flops 5000000000 | bytes 15000000 | tf_op jit(solution)/shard_map/pallas_call | solution.py:884
  452.6 12.3 %shard_map.242 = (bf16[4,2,16,2048]{3,2,1,0:T(8,128)(2,1)S(1)}, bf16[4,2,16,2048]{3,2,1,0:T(8,128)(2,1)S(1)}, bf16[4,2,16,2048]{3,2,1,0:T(8,128)(2,1)S(1)}, bf16...) custom-call(s32[3]{0:T(128)S(1)} %pad_add_fusion.core_ref.place, ...), custom_call_target="tpu_custom_call" | custom-call | flops 5000000000 | bytes 15000000 | tf_op jit(solution)/shard_map/pallas_call | solution.py:884
  467.8 15.6 %shard_map.243 = (f32[49,16,512]{2,1,0:T(8,128)}, f32[16,8,384]{2,1,0:T(8,128)}, bf16[49,16,512]{2,1,0:T(8,128)(2,1)S(1)}, bf16[49,16,128]{2,1,0:T(8,128)(2,1)S(1)}) custom-call(s32[3]{0:T(128)S(1)} %pad_add_fusion.core_ref.place, bf16[49,16,512]{2,1,0:T(8,128)(2,1)} %get-tuple-element.209.d2, f32[49,16,512]{2,1,0:T(8,128)} %get-tuple-element.210.a_ref, ...), custom_call_target="tpu_custom_call" | custom-call | flops 5000000000 | bytes 15000000 | tf_op jit(solution)/shard_map/pallas_call | solution.py:884
  485.1 6.4 all-to-all-start.11
  503.6 6.0 shard_map.244
  512.0 8.6 %shard_map.245 = (bf16[4,2,2,16,2048]{4,3,2,1,0:T(8,128)(2,1)}, bf16[4,2,2,16,2048]{4,3,2,1,0:T(8,128)(2,1)}, bf16[49,16,512]{2,1,0:T(8,128)(2,1)S(1)}, f32[8,512]{1,0:T(8,128)S(1)}) custom-call(s32[3]{0:T(128)S(1)} %pad_add_fusion.core_ref.place, f32[49,16,512]{2,1,0:T(8,128)} %get-tuple-element.213.dn1, f32[49,16,512]{2,1,0:T(8,128)} %collective-permute-done.44.other, ...), custom_call_target="tpu_custom_call" | custom-call | flops 5000000000 | bytes 15000000 | tf_op jit(solution)/shard_map/pallas_call | solution.py:884
  530.7 4.2 collective-permute-start.51
  536.8 5.1 collective-permute-done.60
  542.0 8.0 %all-to-all-start.12 = ((bf16[16,16,4480]{2,1,0:T(8,128)(2,1)}), bf16[16,16,4480]{2,1,0:T(8,128)(2,1)}, u32[]{:S(2)}, u32[]{:S(2)}) async-start(bf16[16,16,4480]{2,1,0:T(8,128)(2,1)} %pad_maximum_fusion), calls=%async_computation.12 | async-start | bytes 4587520 | tf_op jit(solution)/shard_map/all_to_all | solution.py:1048
  551.1 6.6 %shard_map.247.early_ref = bf16[49,16,2048]{2,1,0:T(8,128)(2,1)} custom-call(s32[3]{0:T(128)S(1)} %pad_add_fusion.core_ref.place, bf16[49,16,512]{2,1,0:T(8,128)(2,1)} %copy-done.18, bf16[49,16,2048]{2,1,0:T(8,128)(2,1)} %get-tuple-element.192.dz.dz_ref, bf16[4,2,16,1024]{3,2,1,0:T(8,128)(2,1)S(1)} %copy.116.rest_0_, ...), custom_call_target="tpu_custom_call" | custom-call | flops 5000000000 | bytes 15000000 | tf_op jit(solution)/shard_map/pallas_call | solution.py:884
  557.8 5.3 collective-permute-start.53
  565.9 9.8 %shard_map.246 = bf16[3,392,2048]{2,1,0:T(8,128)(2,1)} custom-call(s32[3]{0:T(128)S(1)} %pad_add_fusion.core_ref.place, bf16[49,16,2048]{2,1,0:T(8,128)(2,1)} %get-tuple-element.230.x_ref.early_ref, bf16[49,16,2048]{2,1,0:T(8,128)(2,1)} %get-tuple-element.231.late_ref, bf16[49,16,2048]{2,1,0:T(8,128)(2,1)} %collective-permute-done.51.early_in, ...), custom_call_target="tpu_custom_call" | custom-call | flops 5000000000 | bytes 15000000 | tf_op jit(solution)/shard_map/pallas_call | solution.py:884
  575.7 18.5 %collective-permute-done.64 = bf16[2,16,4608]{2,1,0:T(8,128)(2,1)S(1)} collective-permute-done((bf16[2,16,4608]{2,1,0:T(8,128)(2,1)S(1)}, bf16[2,16,4608]{2,1,0:T(8,128)(2,1)S(1)}, u32[]{:S(2)}, u32[]{:S(2)}) %collective-permute-start.64) | collective-permute-done | bytes 294944 | tf_op jit(solution)/shard_map/ppermute | solution.py:936
  598.4 21.4 %all-to-all-done.12 = bf16[16,16,4480]{2,1,0:T(8,128)(2,1)} async-done(((bf16[16,16,4480]{2,1,0:T(8,128)(2,1)}), bf16[16,16,4480]{2,1,0:T(8,128)(2,1)}, u32[]{:S(2)}, u32[]{:S(2)}) %all-to-all-start.12) | async-done | bytes 2293792 | tf_op jit(solution)/shard_map/all_to_all | solution.py:1048
  621.8 5.1 collective-permute-start.55
  626.9 9.8 %shard_map.248 = bf16[3,392,2048]{2,1,0:T(8,128)(2,1)} custom-call(s32[3]{0:T(128)S(1)} %pad_add_fusion.core_ref.place, bf16[49,16,2048]{2,1,0:T(8,128)(2,1)} %shard_map.247.early_ref, bf16[49,16,2048]{2,1,0:T(8,128)(2,1)} %get-tuple-element.236.late_ref, bf16[49,16,2048]{2,1,0:T(8,128)(2,1)} %collective-permute-done.53.early_in, ...), custom_call_target="tpu_custom_call" | custom-call | flops 5000000000 | bytes 15000000 | tf_op jit(solution)/shard_map/pallas_call | solution.py:884
  (352 shorter events, 152.2 us)
Async XLA Ops:
  7.2 94.2 %all-gather.5.cloned.1.call-start = ((), (), s32[]{:S(2)}) async-start(), calls=%async_computation.17 | async-start | bytes 3829760 | tf_op jit(solution)/shard_map/all_gather | solution.py:968
  21.5 13.0 %collective-permute-start.4 = (bf16[2,16,2176]{2,1,0:T(8,128)(2,1)S(1)}, bf16[2,16,2176]{2,1,0:T(8,128)(2,1)S(1)}, u32[]{:S(2)}, u32[]{:S(2)}) collective-permute-start(bf16[2,16,2176]{2,1,0:T(8,128)(2,1)S(1)} %maximum_select_fusion.10), channel_id=1, source_target_pairs={{0,4},{1,5},{2,6},{3,7},{4,0},{5,1},{6,2},{7,3},{8,12},{9,13},{10,... | collective-permute-start | bytes 417800 | tf_op jit(solution)/shard_map/ppermute | solution.py:936
  34.5 12.9 %collective-permute-start.5 = (bf16[16,4224]{1,0:T(8,128)(2,1)S(1)}, bf16[16,4224]{1,0:T(8,128)(2,1)S(1)}, u32[]{:S(2)}, u32[]{:S(2)}) collective-permute-start(bf16[16,4224]{1,0:T(8,128)(2,1)S(1)} %get-tuple-element.135), channel_id=1, source_target_pairs={{0,8},{1,9},{2,10},{3,11},{4,12},{5,13},{6,14},{7,15},{8,0},{9,1},... | collective-permute-start | bytes 405512 | tf_op jit(solution)/shard_map/ppermute | solution.py:936
  45.5 12.0 %collective-permute-start.8 = (bf16[4,2,16,1024]{3,2,0,1:T(8,128)(2,1)S(1)}, bf16[4,2,16,1024]{3,2,0,1:T(8,128)(2,1)S(1)}, u32[]{:S(2)}, u32[]{:S(2)}) collective-permute-start(bf16[4,2,16,1024]{3,2,0,1:T(8,128)(2,1)S(1)} %maximum_select_fusion.8), channel_id=1, source_target_pairs={{0,2},{1,3},{2,0},{3,1},{4,6},{5,7},{6,4},{7,5},{8,10},{9,11},{10,... | collective-permute-start | bytes 786440 | tf_op jit(solution)/shard_map/ppermute | solution.py:936
  45.8 13.6 %collective-permute-start.11 = (bf16[4,2,16,1024]{3,2,0,1:T(8,128)(2,1)S(1)}, bf16[4,2,16,1024]{3,2,0,1:T(8,128)(2,1)S(1)}, u32[]{:S(2)}, u32[]{:S(2)}) collective-permute-start(bf16[4,2,16,1024]{3,2,0,1:T(8,128)(2,1)S(1)} %maximum_select_fusion.8), channel_id=1, source_target_pairs={{0,16},{16,0},{1,17},{17,1},{2,18},{18,2},{3,19},{19,3},{4,20},{20... | collective-permute-start | bytes 786440 | tf_op jit(solution)/shard_map/ppermute | solution.py:933
  47.5 14.3 %collective-permute-start.6 = (bf16[2,16,4224]{2,1,0:T(8,128)(2,1)S(1)}, bf16[2,16,4224]{2,1,0:T(8,128)(2,1)S(1)}, u32[]{:S(2)}, u32[]{:S(2)}) collective-permute-start(bf16[2,16,4224]{2,1,0:T(8,128)(2,1)S(1)} %maximum_select_fusion.7), channel_id=1, source_target_pairs={{0,4},{1,5},{2,6},{3,7},{4,0},{5,1},{6,2},{7,3},{8,12},{9,13},{10,... | collective-permute-start | bytes 811016 | tf_op jit(solution)/shard_map/ppermute | solution.py:936
  48.6 13.2 %collective-permute-start.10 = (bf16[4,2,16,1152]{3,2,1,0:T(8,128)(2,1)S(1)}, bf16[4,2,16,1152]{3,2,1,0:T(8,128)(2,1)S(1)}, u32[]{:S(2)}, u32[]{:S(2)}) collective-permute-start(bf16[4,2,16,1152]{3,2,1,0:T(8,128)(2,1)S(1)} %maximum_select_fusion.4.rest_2_), channel_id=1, source_target_pairs={{0,1},{1,0},{2,3},{3,2},{4,5},{5,4},{6,7},{7,6},{8,9},{9,8},{10,11... | collective-permute-start | bytes 884744 | tf_op jit(solution)/shard_map/ppermute | solution.py:936
  72.2 23.3 %all-to-all-start = ((f32[16,8,384]{2,1,0:T(8,128)}), f32[16,8,384]{2,1,0:T(8,128)S(1)}, u32[]{:S(2)}, u32[]{:S(2)}) async-start(f32[16,8,384]{2,1,0:T(8,128)} %get-tuple-element.140), calls=%async_computation | async-start | bytes 393216 | tf_op jit(solution)/shard_map/all_to_all | solution.py:939
  79.6 124.5 %all-gather.7.cloned.1.call-start = ((), (), s32[]{:S(2)}) async-start(), calls=%async_computation.18 | async-start | bytes 4943872 | tf_op jit(solution)/shard_map/all_gather | solution.py:968
  79.7 13.7 %collective-permute-start.16 = (bf16[4,16,2048]{2,1,0:T(8,128)(2,1)S(1)}, bf16[4,16,2048]{2,1,0:T(8,128)(2,1)S(1)}, u32[]{:S(2)}, u32[]{:S(2)}) collective-permute-start(bf16[4,16,2048]{2,1,0:T(8,128)(2,1)S(1)} %get-tuple-element.287), channel_id=1, source_target_pairs={{0,1},{1,0},{2,3},{3,2},{4,5},{5,4},{6,7},{7,6},{8,9},{9,8},{10,11... | collective-permute-start | bytes 786440 | tf_op jit(solution)/shard_map/ppermute | solution.py:936
  80.1 14.5 %collective-permute-start.17 = (bf16[4,16,2176]{2,1,0:T(8,128)(2,1)S(1)}, bf16[4,16,2176]{2,1,0:T(8,128)(2,1)S(1)}, u32[]{:S(2)}, u32[]{:S(2)}) collective-permute-start(bf16[4,16,2176]{2,1,0:T(8,128)(2,1)S(1)} %get-tuple-element.285), channel_id=1, source_target_pairs={{0,2},{1,3},{2,0},{3,1},{4,6},{5,7},{6,4},{7,5},{8,10},{9,11},{10,... | collective-permute-start | bytes 835592 | tf_op jit(solution)/shard_map/ppermute | solution.py:936
  103.9 31.0 %collective-permute-start.21 = (bf16[4,2,16,2048]{3,2,0,1:T(8,128)(2,1)}, bf16[4,2,16,2048]{3,2,0,1:T(8,128)(2,1)}, u32[]{:S(2)}, u32[]{:S(2)}) collective-permute-start(bf16[4,2,16,2048]{3,2,0,1:T(8,128)(2,1)} %maximum_select_fusion.2), channel_id=1, source_target_pairs={{0,2},{1,3},{2,0},{3,1},{4,6},{5,7},{6,4},{7,5},{8,10},{9,11},{10,... | collective-permute-start | bytes 1572872 | tf_op jit(solution)/shard_map/ppermute | solution.py:936
  103.9 30.5 %collective-permute-start.22 = (bf16[4,2,16,2176]{3,2,1,0:T(8,128)(2,1)}, bf16[4,2,16,2176]{3,2,1,0:T(8,128)(2,1)}, u32[]{:S(2)}, u32[]{:S(2)}) collective-permute-start(bf16[4,2,16,2176]{3,2,1,0:T(8,128)(2,1)} %maximum_select_fusion.rest_2_.rest_10_), channel_id=1, source_target_pairs={{0,1},{1,0},{2,3},{3,2},{4,5},{5,4},{6,7},{7,6},{8,9},{9,8},{10,11... | collective-permute-start | bytes 1671176 | tf_op jit(solution)/shard_map/ppermute | solution.py:936
  128.4 16.0 %all-to-all-start.1 = ((f32[16,8,384]{2,1,0:T(8,128)}), f32[16,8,384]{2,1,0:T(8,128)S(1)}, u32[]{:S(2)}, u32[]{:S(2)}) async-start(f32[16,8,384]{2,1,0:T(8,128)} %get-tuple-element.146), calls=%async_computation.1 | async-start | bytes 393216 | tf_op jit(solution)/shard_map/all_to_all | solution.py:939
  133.4 18.9 %collective-permute-start.25 = (bf16[4,2,16,2176]{3,2,1,0:T(8,128)(2,1)}, bf16[4,2,16,2176]{3,2,1,0:T(8,128)(2,1)}, u32[]{:S(2)}, u32[]{:S(2)}) collective-permute-start(bf16[4,2,16,2176]{3,2,1,0:T(8,128)(2,1)} %maximum_select_fusion.rest_2_.rest_10_), channel_id=1, source_target_pairs={{0,16},{16,0},{1,17},{17,1},{2,18},{18,2},{3,19},{19,3},{4,20},{20... | collective-permute-start | bytes 1671176 | tf_op jit(solution)/shard_map/ppermute | solution.py:933
  134.4 17.9 %collective-permute-start.26 = (bf16[4,2,16,2176]{3,2,1,0:T(8,128)(2,1)}, bf16[4,2,16,2176]{3,2,1,0:T(8,128)(2,1)}, u32[]{:S(2)}, u32[]{:S(2)}) collective-permute-start(bf16[4,2,16,2176]{3,2,1,0:T(8,128)(2,1)} %collective-permute-done.22.rest_3_.rest_11_), channel_id=1, source_target_pairs={{0,16},{16,0},{1,17},{17,1},{2,18},{18,2},{3,19},{19,3},{4,20},{20... | collective-permute-start | bytes 1671176 | tf_op jit(solution)/shard_map/ppermute | solution.py:933
  134.5 13.8 %collective-permute-start.23 = (bf16[4,2,16,2048]{3,2,0,1:T(8,128)(2,1)}, bf16[4,2,16,2048]{3,2,0,1:T(8,128)(2,1)}, u32[]{:S(2)}, u32[]{:S(2)}) collective-permute-start(bf16[4,2,16,2048]{3,2,0,1:T(8,128)(2,1)} %maximum_select_fusion.2), channel_id=1, source_target_pairs={{0,16},{16,0},{1,17},{17,1},{2,18},{18,2},{3,19},{19,3},{4,20},{20... | collective-permute-start | bytes 1572872 | tf_op jit(solution)/shard_map/ppermute | solution.py:933
  135.0 15.5 %collective-permute-start.24 = (bf16[4,2,16,2048]{3,2,0,1:T(8,128)(2,1)}, bf16[4,2,16,2048]{3,2,0,1:T(8,128)(2,1)}, u32[]{:S(2)}, u32[]{:S(2)}) collective-permute-start(bf16[4,2,16,2048]{3,2,0,1:T(8,128)(2,1)} %collective-permute-done.21), channel_id=1, source_target_pairs={{0,16},{16,0},{1,17},{17,1},{2,18},{18,2},{3,19},{19,3},{4,20},{20... | collective-permute-start | bytes 1572872 | tf_op jit(solution)/shard_map/ppermute | solution.py:933
  204.1 14.6 %collective-permute-start.31 = (bf16[4,2,2,16,9088]{4,3,2,1,0:T(8,128)(2,1)}, bf16[4,2,2,16,9088]{4,3,2,1,0:T(8,128)(2,1)}, u32[]{:S(2)}, u32[]{:S(2)}) collective-permute-start(bf16[4,2,2,16,9088]{4,3,2,1,0:T(8,128)(2,1)} %bitcast.196), channel_id=1, source_target_pairs={{0,16},{16,0},{1,17},{17,1},{2,18},{18,2},{3,19},{19,3},{4,20},{20... | collective-permute-start | bytes 13959176 | tf_op jit(solution)/shard_map/ppermute | solution.py:933
  204.4 14.2 %collective-permute-start.29 = (f32[49,16,512]{2,1,0:T(8,128)}, f32[49,16,512]{2,1,0:T(8,128)}, u32[]{:S(2)}, u32[]{:S(2)}) collective-permute-start(f32[49,16,512]{2,1,0:T(8,128)} %get-tuple-element.152.a_in), channel_id=1, source_target_pairs={{0,16},{16,0},{1,17},{17,1},{2,18},{18,2},{3,19},{19,3},{4,20},{20... | collective-permute-start | bytes 4816904 | tf_op jit(solution)/shard_map/ppermute | solution.py:933
  204.6 12.2 %all-to-all-start.3 = ((f32[16,8,384]{2,1,0:T(8,128)}), f32[16,8,384]{2,1,0:T(8,128)S(1)}, u32[]{:S(2)}, u32[]{:S(2)}) async-start(f32[16,8,384]{2,1,0:T(8,128)} %get-tuple-element.153), calls=%async_computation.3 | async-start | bytes 393216 | tf_op jit(solution)/shard_map/all_to_all | solution.py:939
  351.4 24.4 %collective-permute-start.38 = (f32[49,16,512]{2,1,0:T(8,128)}, f32[49,16,512]{2,1,0:T(8,128)}, u32[]{:S(2)}, u32[]{:S(2)}) collective-permute-start(f32[49,16,512]{2,1,0:T(8,128)} %get-tuple-element.178.dn1), channel_id=1, source_target_pairs={{0,16},{16,0},{1,17},{17,1},{2,18},{18,2},{3,19},{19,3},{4,20},{20... | collective-permute-start | bytes 4816904 | tf_op jit(solution)/shard_map/ppermute | solution.py:933
  351.8 22.4 %all-to-all-start.8 = ((f32[16,8,384]{2,1,0:T(8,128)}), f32[16,8,384]{2,1,0:T(8,128)S(1)}, u32[]{:S(2)}, u32[]{:S(2)}) async-start(f32[16,8,384]{2,1,0:T(8,128)} %get-tuple-element.179), calls=%async_computation.8 | async-start | bytes 393216 | tf_op jit(solution)/shard_map/all_to_all | solution.py:939
  357.6 236.9 %reduce-scatter.5.cloned.1.call-start = ((), (), s32[]{:S(2)}) async-start(), calls=%async_computation.16 | async-start | bytes 4943872 | tf_op jit(solution)/shard_map/reduce_scatter | solution.py:1045
  375.8 14.9 %collective-permute-start.40 = (bf16[4,2,2,16,9088]{4,3,2,1,0:T(8,128)(2,1)}, bf16[4,2,2,16,9088]{4,3,2,1,0:T(8,128)(2,1)}, u32[]{:S(2)}, u32[]{:S(2)}) collective-permute-start(bf16[4,2,2,16,9088]{4,3,2,1,0:T(8,128)(2,1)} %get-tuple-element.195), channel_id=1, source_target_pairs={{0,16},{16,0},{1,17},{17,1},{2,18},{18,2},{3,19},{19,3},{4,20},{20... | collective-permute-start | bytes 13959176 | tf_op jit(solution)/shard_map/ppermute | solution.py:933
  431.0 19.1 %all-to-all-start.10 = ((f32[16,8,384]{2,1,0:T(8,128)}), f32[16,8,384]{2,1,0:T(8,128)S(1)}, u32[]{:S(2)}, u32[]{:S(2)}) async-start(f32[16,8,384]{2,1,0:T(8,128)} %get-tuple-element.202), calls=%async_computation.10 | async-start | bytes 393216 | tf_op jit(solution)/shard_map/all_to_all | solution.py:939
  452.2 45.6 %collective-permute-start.45 = (bf16[4,2,2,16,4096]{4,3,2,1,0:T(8,128)(2,1)}, bf16[4,2,2,16,4096]{4,3,2,1,0:T(8,128)(2,1)}, u32[]{:S(2)}, u32[]{:S(2)}) collective-permute-start(bf16[4,2,2,16,4096]{4,3,2,1,0:T(8,128)(2,1)} %get-tuple-element.216), channel_id=1, source_target_pairs={{0,16},{16,0},{1,17},{17,1},{2,18},{18,2},{3,19},{19,3},{4,20},{20... | collective-permute-start | bytes 6291464 | tf_op jit(solution)/shard_map/ppermute | solution.py:933
  466.8 26.6 %collective-permute-start.46 = (bf16[4,2,16,2048]{3,2,0,1:T(8,128)(2,1)}, bf16[4,2,16,2048]{3,2,0,1:T(8,128)(2,1)}, u32[]{:S(2)}, u32[]{:S(2)}) collective-permute-start(bf16[4,2,16,2048]{3,2,0,1:T(8,128)(2,1)} %copy.149), channel_id=1, source_target_pairs={{0,16},{16,0},{1,17},{17,1},{2,18},{18,2},{3,19},{19,3},{4,20},{20... | collective-permute-start | bytes 1572872 | tf_op jit(solution)/shard_map/ppermute | solution.py:933
  467.4 28.0 %collective-permute-start.47 = (bf16[4,2,16,2560]{3,2,1,0:T(8,128)(2,1)}, bf16[4,2,16,2560]{3,2,1,0:T(8,128)(2,1)}, u32[]{:S(2)}, u32[]{:S(2)}) collective-permute-start(bf16[4,2,16,2560]{3,2,1,0:T(8,128)(2,1)} %get-tuple-element.220), channel_id=1, source_target_pairs={{0,16},{16,0},{1,17},{17,1},{2,18},{18,2},{3,19},{19,3},{4,20},{20... | collective-permute-start | bytes 1966088 | tf_op jit(solution)/shard_map/ppermute | solution.py:933
  485.0 25.5 %collective-permute-start.44 = (f32[49,16,512]{2,1,0:T(8,128)}, f32[49,16,512]{2,1,0:T(8,128)}, u32[]{:S(2)}, u32[]{:S(2)}) collective-permute-start(f32[49,16,512]{2,1,0:T(8,128)} %get-tuple-element.213.dn1), channel_id=1, source_target_pairs={{0,16},{16,0},{1,17},{17,1},{2,18},{18,2},{3,19},{19,3},{4,20},{20... | collective-permute-start | bytes 4816904 | tf_op jit(solution)/shard_map/ppermute | solution.py:933
  485.1 24.4 %all-to-all-start.11 = ((f32[16,8,384]{2,1,0:T(8,128)}), f32[16,8,384]{2,1,0:T(8,128)S(1)}, u32[]{:S(2)}, u32[]{:S(2)}) async-start(f32[16,8,384]{2,1,0:T(8,128)} %get-tuple-element.214), calls=%async_computation.11 | async-start | bytes 393216 | tf_op jit(solution)/shard_map/all_to_all | solution.py:939
  491.5 145.3 %reduce-scatter.3.cloned.1.call-start = ((), (), s32[]{:S(2)}) async-start(), calls=%async_computation.15 | async-start | bytes 2228224 | tf_op jit(solution)/shard_map/reduce_scatter | solution.py:1045
  491.6 30.6 %collective-permute-start.61 = (bf16[4,2,16,2560]{3,2,1,0:T(8,128)(2,1)}, bf16[4,2,16,2560]{3,2,1,0:T(8,128)(2,1)}, u32[]{:S(2)}, u32[]{:S(2)}) collective-permute-start(bf16[4,2,16,2560]{3,2,1,0:T(8,128)(2,1)} %get-tuple-element.242), channel_id=1, source_target_pairs={{0,16},{16,0},{1,17},{17,1},{2,18},{18,2},{3,19},{19,3},{4,20},{20... | collective-permute-start | bytes 1966088 | tf_op jit(solution)/shard_map/ppermute | solution.py:933
  493.4 32.8 %collective-permute-start.58 = (bf16[4,2,16,2048]{3,2,0,1:T(8,128)(2,1)}, bf16[4,2,16,2048]{3,2,0,1:T(8,128)(2,1)}, u32[]{:S(2)}, u32[]{:S(2)}) collective-permute-start(bf16[4,2,16,2048]{3,2,0,1:T(8,128)(2,1)} %copy.155), channel_id=1, source_target_pairs={{0,16},{16,0},{1,17},{17,1},{2,18},{18,2},{3,19},{19,3},{4,20},{20... | collective-permute-start | bytes 1572872 | tf_op jit(solution)/shard_map/ppermute | solution.py:933
  497.5 24.1 %collective-permute-start.62 = (bf16[4,2,16,2560]{3,2,1,0:T(8,128)(2,1)}, bf16[4,2,16,2560]{3,2,1,0:T(8,128)(2,1)}, u32[]{:S(2)}, u32[]{:S(2)}) collective-permute-start(bf16[4,2,16,2560]{3,2,1,0:T(8,128)(2,1)} %add_convert_fusion.6), channel_id=1, source_target_pairs={{0,1},{1,0},{2,3},{3,2},{4,5},{5,4},{6,7},{7,6},{8,9},{9,8},{10,11... | collective-permute-start | bytes 1966088 | tf_op jit(solution)/shard_map/ppermute | solution.py:936
  510.5 15.7 %collective-permute-start.59 = (bf16[4,2,16,2048]{3,2,0,1:T(8,128)(2,1)}, bf16[4,2,16,2048]{3,2,0,1:T(8,128)(2,1)S(1)}, u32[]{:S(2)}, u32[]{:S(2)}) collective-permute-start(bf16[4,2,16,2048]{3,2,0,1:T(8,128)(2,1)} %add_convert_fusion.9), channel_id=1, source_target_pairs={{0,2},{1,3},{2,0},{3,1},{4,6},{5,7},{6,4},{7,5},{8,10},{9,11},{10,... | collective-permute-start | bytes 1572872 | tf_op jit(solution)/shard_map/ppermute | solution.py:936
  511.7 16.5 %collective-permute-start.50 = (bf16[4,2,2,16,2432]{4,3,2,1,0:T(8,128)(2,1)}, bf16[4,2,2,16,2432]{4,3,2,1,0:T(8,128)(2,1)S(1)}, u32[]{:S(2)}, u32[]{:S(2)}) collective-permute-start(bf16[4,2,2,16,2432]{4,3,2,1,0:T(8,128)(2,1)} %get-tuple-element.226), channel_id=1, source_target_pairs={{0,16},{16,0},{1,17},{17,1},{2,18},{18,2},{3,19},{19,3},{4,20},{20... | collective-permute-start | bytes 3735560 | tf_op jit(solution)/shard_map/ppermute | solution.py:933
  524.4 25.6 %collective-permute-start.63 = (bf16[4,16,2560]{2,1,0:T(8,128)(2,1)}, bf16[4,16,2560]{2,1,0:T(8,128)(2,1)}, u32[]{:S(2)}, u32[]{:S(2)}) collective-permute-start(bf16[4,16,2560]{2,1,0:T(8,128)(2,1)} %dynamic-slice_bitcast_fusion), channel_id=1, source_target_pairs={{0,2},{1,3},{2,0},{3,1},{4,6},{5,7},{6,4},{7,5},{8,10},{9,11},{10,... | collective-permute-start | bytes 983048 | tf_op jit(solution)/shard_map/ppermute | solution.py:936
  527.5 14.4 %collective-permute-start.60 = (bf16[4,16,2048]{2,1,0:T(8,128)(2,1)S(1)}, bf16[4,16,2048]{2,1,0:T(8,128)(2,1)S(1)}, u32[]{:S(2)}, u32[]{:S(2)}) collective-permute-start(bf16[4,16,2048]{2,1,0:T(8,128)(2,1)S(1)} %dynamic-slice_bitcast_fusion.2), channel_id=1, source_target_pairs={{0,1},{1,0},{2,3},{3,2},{4,5},{5,4},{6,7},{7,6},{8,9},{9,8},{10,11... | collective-permute-start | bytes 786440 | tf_op jit(solution)/shard_map/ppermute | solution.py:936
  530.7 35.2 %collective-permute-start.51 = (bf16[49,16,2048]{2,1,0:T(8,128)(2,1)}, bf16[49,16,2048]{2,1,0:T(8,128)(2,1)}, u32[]{:S(2)}, u32[]{:S(2)}) collective-permute-start(bf16[49,16,2048]{2,1,0:T(8,128)(2,1)} %get-tuple-element.230.x_ref.early_ref), channel_id=1, source_target_pairs={{16,0},{17,1},{18,2},{19,3},{20,4},{21,5},{22,6},{23,7},{24,8},{25... | collective-permute-start | bytes 9633800 | tf_op jit(solution)/shard_map/ppermute | solution.py:1285
  534.8 31.0 %collective-permute-start.52 = (bf16[49,16,2048]{2,1,0:T(8,128)(2,1)}, bf16[49,16,2048]{2,1,0:T(8,128)(2,1)}, u32[]{:S(2)}, u32[]{:S(2)}) collective-permute-start(bf16[49,16,2048]{2,1,0:T(8,128)(2,1)} %get-tuple-element.231.late_ref), channel_id=1, source_target_pairs={{0,16},{1,17},{2,18},{3,19},{4,20},{5,21},{6,22},{7,23},{8,24},{9,... | collective-permute-start | bytes 9633800 | tf_op jit(solution)/shard_map/ppermute | solution.py:1285
  542.0 77.8 %all-to-all-start.12 = ((bf16[16,16,4480]{2,1,0:T(8,128)(2,1)}), bf16[16,16,4480]{2,1,0:T(8,128)(2,1)}, u32[]{:S(2)}, u32[]{:S(2)}) async-start(bf16[16,16,4480]{2,1,0:T(8,128)(2,1)} %pad_maximum_fusion), calls=%async_computation.12 | async-start | bytes 4587520 | tf_op jit(solution)/shard_map/all_to_all | solution.py:1048
  557.8 69.1 %collective-permute-start.53 = (bf16[49,16,2048]{2,1,0:T(8,128)(2,1)}, bf16[49,16,2048]{2,1,0:T(8,128)(2,1)}, u32[]{:S(2)}, u32[]{:S(2)}) collective-permute-start(bf16[49,16,2048]{2,1,0:T(8,128)(2,1)} %shard_map.247.early_ref), channel_id=1, source_target_pairs={{16,0},{17,1},{18,2},{19,3},{20,4},{21,5},{22,6},{23,7},{24,8},{25... | collective-permute-start | bytes 9633800 | tf_op jit(solution)/shard_map/ppermute | solution.py:1285
  563.1 63.9 %collective-permute-start.54 = (bf16[49,16,2048]{2,1,0:T(8,128)(2,1)}, bf16[49,16,2048]{2,1,0:T(8,128)(2,1)}, u32[]{:S(2)}, u32[]{:S(2)}) collective-permute-start(bf16[49,16,2048]{2,1,0:T(8,128)(2,1)} %get-tuple-element.236.late_ref), channel_id=1, source_target_pairs={{0,16},{1,17},{2,18},{3,19},{4,20},{5,21},{6,22},{7,23},{8,24},{9,... | collective-permute-start | bytes 9633800 | tf_op jit(solution)/shard_map/ppermute | solution.py:1285
  564.6 29.7 %collective-permute-start.64 = (bf16[2,16,4608]{2,1,0:T(8,128)(2,1)S(1)}, bf16[2,16,4608]{2,1,0:T(8,128)(2,1)S(1)}, u32[]{:S(2)}, u32[]{:S(2)}) collective-permute-start(bf16[2,16,4608]{2,1,0:T(8,128)(2,1)S(1)} %dynamic-slice_bitcast_fusion.1), channel_id=1, source_target_pairs={{0,4},{1,5},{2,6},{3,7},{4,0},{5,1},{6,2},{7,3},{8,12},{9,13},{10,... | collective-permute-start | bytes 884744 | tf_op jit(solution)/shard_map/ppermute | solution.py:936
  594.4 42.5 %collective-permute-start.65 = (bf16[16,4608]{1,0:T(8,128)(2,1)S(1)}, bf16[16,4608]{1,0:T(8,128)(2,1)S(1)}, u32[]{:S(2)}, u32[]{:S(2)}) collective-permute-start(bf16[16,4608]{1,0:T(8,128)(2,1)S(1)} %dynamic-slice_bitcast_fusion.4), channel_id=1, source_target_pairs={{0,8},{1,9},{2,10},{3,11},{4,12},{5,13},{6,14},{7,15},{8,0},{9,1},... | collective-permute-start | bytes 442376 | tf_op jit(solution)/shard_map/ppermute | solution.py:936
  595.4 48.1 %collective-permute-start.57 = (bf16[16,9088]{1,0:T(8,128)(2,1)}, bf16[16,9088]{1,0:T(8,128)(2,1)S(1)}, u32[]{:S(2)}, u32[]{:S(2)}) collective-permute-start(bf16[16,9088]{1,0:T(8,128)(2,1)} %bitcast.177), channel_id=1, source_target_pairs={{0,16},{1,17},{2,18},{3,19},{4,20},{5,21},{6,22},{7,23},{8,24},{9,... | collective-permute-start | bytes 872456 | tf_op jit(solution)/shard_map/ppermute | solution.py:1054
  621.8 23.8 %collective-permute-start.55 = (f32[16,4480]{1,0:T(8,128)S(1)}, f32[16,4480]{1,0:T(8,128)S(1)}, u32[]{:S(2)}, u32[]{:S(2)}) collective-permute-start(f32[16,4480]{1,0:T(8,128)S(1)} %convert_reduce_fusion), channel_id=1, source_target_pairs={{16,0},{17,1},{18,2},{19,3},{20,4},{21,5},{22,6},{23,7},{24,8},{25... | collective-permute-start | bytes 860168 | tf_op jit(solution)/shard_map/ppermute | solution.py:1385
  (76 other events, 616.1 us)
Sparse Core Ops, SparseCore 0:
  17.4 83.9 all-gather.4
  104.2 87.0 all-gather.6
  396.5 119.5 reduce-scatter.4
  518.3 97.3 reduce-scatter.2

commit v5 on v4

--- a/solution.py
+++ b/solution.py
@@ -703,10 +703,10 @@
     clear_border(d2p)
     for i, rows in enumerate(CHUNKS):
         d2p[i + 1, 1:8] = d2[rows]
-    wait_all(mid_copies)
 
     total = 0.0
     for k in range(9):
+        wait_all(mid_copies[2 * k : 2 * k + 2])
         y, x = 2 - k // 3, 2 - k % 3
         v = d2p[y : y + SIDE, x : x + SIDE].reshape(ROWS, 512)
         total = total + dot(v, mid_buf[..., pl.ds(512 * k, 512)].reshape(512, 512))
@@ -1121,7 +1121,7 @@
     return {
         "sq": [("W", first, 0, 128)],
         "nf": [("W", first + 128, 0, 2304)],
-        "mid": [("W", first + 2432, 0, 4608)],
+        "mid": [("W", first + 2432 + 512 * k, 512 * k, 512) for k in range(9)],
     }
 
 

time: 665 us -> 665 us (level)
  no operation moved by 1% of the time
where the time goes in v5:
time: 665 us; the launch traced here: 654 us
  Pallas kernels  245 us (37%)
  starting transfers between devices  119 us (18%)
  waiting for transfers between devices  105 us (16%)
  blocking collectives  102 us (15%)
  other arithmetic  34.2 us (5%)
  local copies, waits for them, and re-layouts  33.7 us (5%)
  between operations  15.2 us (2%)
    pallas_call x25, Pallas kernels, run(): pl.pallas_call(kernel, in_specs=specs, out_specs=tuple((HB if is_big(o[0]...  245 us
    all_to_all x6, blocking collectives, to_all(): g = lax.all_to_all(spread, 'dp', 0, 0)  102 us
    ppermute x18, waiting for transfers between devices, across(): return lax.ppermute(v, 'dp', [(i, i ^ k) for i in range(self.dp)])  41.5 us
    all_to_all x6, starting transfers between devices, to_all(): g = lax.all_to_all(spread, 'dp', 0, 0)  36.9 us
    ppermute x41, starting transfers between devices, swap(): return lax.ppermute(v, 'pipe', PAIR)  32.4 us
    ppermute x41, waiting for transfers between devices, swap(): return lax.ppermute(v, 'pipe', PAIR)  23.2 us
    all_to_all x1, waiting for transfers between devices, scatter_at_once(): v = lax.all_to_all(v, 'dp', 0, 0)  21.6 us
    convert_element_type x12, other arithmetic, add(): return (a.astype(F32) + b.astype(F32)).astype(BF16)  18.3 us
  transfers between devices with their start and end apart: 79, of which 30 were waited for; matrix products, arithmetic and copies ran while one was open for 6% of the time, Pallas kernels for 28%

profile of v5, /device:TPU:19, one launch (start us, length us, event | category | flops | bytes accessed | tf_op | source)
XLA Modules:
  0.0 653.9 jit_solution(4541025346424807616)
XLA Ops:
  25.1 9.3 %shard_map.220.x_ref = bf16[49,16,2048]{2,1,0:T(8,128)(2,1)} custom-call(s32[3]{0:T(128)S(1)} %pad_add_fusion.core_ref.place, bf16[3,392,2048]{2,1,0:T(8,128)(2,1)} %x_ref), custom_call_target="tpu_custom_call" | custom-call | flops 5000000000 | bytes 15000000 | tf_op jit(solution)/shard_map/pallas_call | solution.py:884
  34.9 9.2 %shard_map.221.dy_ref = bf16[49,16,2048]{2,1,0:T(8,128)(2,1)} custom-call(s32[3]{0:T(128)S(1)} %pad_add_fusion.core_ref.place, bf16[3,392,2048]{2,1,0:T(8,128)(2,1)} %x_ref.1), custom_call_target="tpu_custom_call" | custom-call | flops 5000000000 | bytes 15000000 | tf_op jit(solution)/shard_map/pallas_call | solution.py:884
  51.4 5.4 collective-permute-start.13
  64.7 7.5 %shard_map.222 = (f32[49,16,512]{2,1,0:T(8,128)}, f32[16,8,384]{2,1,0:T(8,128)}) custom-call(s32[3]{0:T(128)S(1)} %pad_add_fusion.core_ref.place, bf16[49,16,2048]{2,1,0:T(8,128)(2,1)} %shard_map.220.x_ref, bf16[4,2,16,1024]{3,2,1,0:T(8,128)(2,1)S(1)} %copy.116.rest_0_, bf16[4,2,16,1024]{3,2,1,0:T(8,128)(2,1)S(1)} %copy.117.rest_1_, ...), custom_call_target="tpu_custom_call" | custom-call | flops 5000000000 | bytes 15000000 | tf_op jit(solution)/shard_map/pallas_call | solution.py:884
  72.2 7.4 %all-to-all-start = ((f32[16,8,384]{2,1,0:T(8,128)}), f32[16,8,384]{2,1,0:T(8,128)S(1)}, u32[]{:S(2)}, u32[]{:S(2)}) async-start(f32[16,8,384]{2,1,0:T(8,128)} %get-tuple-element.140), calls=%async_computation | async-start | bytes 393216 | tf_op jit(solution)/shard_map/all_to_all | solution.py:939
  84.7 8.7 %collective-permute-done.16 = bf16[4,16,2048]{2,1,0:T(8,128)(2,1)S(1)} collective-permute-done((bf16[4,16,2048]{2,1,0:T(8,128)(2,1)S(1)}, bf16[4,16,2048]{2,1,0:T(8,128)(2,1)S(1)}, u32[]{:S(2)}, u32[]{:S(2)}) %collective-permute-start.16) | collective-permute-done | bytes 262176 | tf_op jit(solution)/shard_map/ppermute | solution.py:936
  95.5 5.9 all-gather.5.cloned.1.call-done
  105.4 4.2 collective-permute-done.18.g_other
  112.0 14.3 %shard_map.224 = (f32[49,16,512]{2,1,0:T(8,128)}, bf16[49,16,512]{2,1,0:T(8,128)(2,1)S(1)}, bf16[49,16,128]{2,1,0:T(8,128)(2,1)S(1)}, bf16[49,16,512]{2,1,0:T(8,...) custom-call(s32[3]{0:T(128)S(1)} %pad_add_fusion.core_ref.place, ...), custom_call_target="tpu_custom_call" | custom-call | flops 5000000000 | bytes 15000000 | tf_op jit(solution)/shard_map/pallas_call | solution.py:884
  128.5 5.0 all-to-all-start.1
  135.1 9.2 %all-to-all-done.1.g = f32[16,8,384]{2,1,0:T(8,128)S(1)} async-done(((f32[16,8,384]{2,1,0:T(8,128)}), f32[16,8,384]{2,1,0:T(8,128)S(1)}, u32[]{:S(2)}, u32[]{:S(2)}) %all-to-all-start.1) | async-done | bytes 196640 | tf_op jit(solution)/shard_map/all_to_all | solution.py:939
  152.5 7.4 %shard_map.225 = (bf16[49,16,512]{2,1,0:T(8,128)(2,1)}, f32[8,1024]{1,0:T(8,128)S(1)}, f32[8,1024]{1,0:T(8,128)S(1)}, f32[8,512]{1,0:T(8,128)S(1)}) custom-call(s32[3]{0:T(128)S(1)} %pad_add_fusion.core_ref.place, f32[49,16,512]{2,1,0:T(8,128)} %get-tuple-element.145.second, f32[16,8,384]{2,1,0:T(8,128)S(1)} %all-to-all-done.1.g, ...), custom_call_target="tpu_custom_call" | custom-call | flops 5000000000 | bytes 15000000 | tf_op jit(solution)/shard_map/pallas_call | solution.py:884
  161.2 25.9 %all_to_all.65.g = f32[16,8,768]{2,1,0:T(8,128)S(1)} all-to-all(f32[16,8,768]{2,1,0:T(8,128)S(1)} %shard_map.226), channel_id=1, replica_groups=mesh['pipe'=2,'dp'=16] {'dp'}, dimensions={0} | all-to-all | bytes 786432 | tf_op jit(solution)/shard_map/all_to_all | solution.py:939
  190.5 13.0 %shard_map.227 = (bf16[49,16,2048]{2,1,0:T(8,128)(2,1)}, bf16[49,16,2048]{2,1,0:T(8,128)(2,1)}, bf16[49,16,2048]{2,1,0:T(8,128)(2,1)}, f32[49,16,512]{2,1,0:T(8,...) custom-call(s32[3]{0:T(128)S(1)} %pad_add_fusion.core_ref.place, ...), custom_call_target="tpu_custom_call" | custom-call | flops 5000000000 | bytes 15000000 | tf_op jit(solution)/shard_map/pallas_call | solution.py:884
  204.7 5.8 all-to-all-start.3
  213.0 3.9 all-to-all-done.3.g
  218.7 14.0 %shard_map.229 = (f32[49,16,512]{2,1,0:T(8,128)}, bf16[49,16,512]{2,1,0:T(8,128)(2,1)S(1)}, bf16[49,16,128]{2,1,0:T(8,128)(2,1)S(1)}, bf16[49,16,512]{2,1,0:T(8,...) custom-call(s32[3]{0:T(128)S(1)} %pad_add_fusion.core_ref.place, ...), custom_call_target="tpu_custom_call" | custom-call | flops 5000000000 | bytes 15000000 | tf_op jit(solution)/shard_map/pallas_call | solution.py:884
  234.3 11.7 %all_to_all.66.g = f32[16,8,384]{2,1,0:T(8,128)S(1)} all-to-all(f32[16,8,384]{2,1,0:T(8,128)S(1)} %get-tuple-element.159), channel_id=1, replica_groups=mesh['pipe'=2,'dp'=16] {'dp'}, dimensions={0} | all-to-all | bytes 393216 | tf_op jit(solution)/shard_map/all_to_all | solution.py:939
  247.9 7.6 %shard_map.230 = (bf16[49,16,512]{2,1,0:T(8,128)(2,1)S(1)}, f32[8,1024]{1,0:T(8,128)S(1)}, f32[8,1024]{1,0:T(8,128)S(1)}, f32[8,512]{1,0:T(8,128)S(1)}) custom-call(s32[3]{0:T(128)S(1)} %pad_add_fusion.core_ref.place, f32[49,16,512]{2,1,0:T(8,128)} %get-tuple-element.158.second, f32[16,8,384]{2,1,0:T(8,128)S(1)} %all_to_all.66.g, ...), custom_call_target="tpu_custom_call" | custom-call | flops 5000000000 | bytes 15000000 | tf_op jit(solution)/shard_map/pallas_call | solution.py:884
  256.8 15.8 %all_to_all.67.g = f32[16,8,768]{2,1,0:T(8,128)S(1)} all-to-all(f32[16,8,768]{2,1,0:T(8,128)S(1)} %shard_map.231), channel_id=1, replica_groups=mesh['pipe'=2,'dp'=16] {'dp'}, dimensions={0} | all-to-all | bytes 786432 | tf_op jit(solution)/shard_map/all_to_all | solution.py:939
  275.0 13.4 %shard_map.232 = (bf16[49,16,2048]{2,1,0:T(8,128)(2,1)}, bf16[49,16,2048]{2,1,0:T(8,128)(2,1)}, bf16[49,16,2048]{2,1,0:T(8,128)(2,1)}, f32[8,1024]{1,0:T(8,128)S...) custom-call(s32[3]{0:T(128)S(1)} %pad_add_fusion.core_ref.place, ...), custom_call_target="tpu_custom_call" | custom-call | flops 5000000000 | bytes 15000000 | tf_op jit(solution)/shard_map/pallas_call | solution.py:884
  289.8 15.6 %all_to_all.68.g = f32[16,8,768]{2,1,0:T(8,128)S(1)} all-to-all(f32[16,8,768]{2,1,0:T(8,128)S(1)} %shard_map.233), channel_id=1, replica_groups=mesh['pipe'=2,'dp'=16] {'dp'}, dimensions={0} | all-to-all | bytes 786432 | tf_op jit(solution)/shard_map/all_to_all | solution.py:939
  307.8 9.4 %shard_map.234 = (f32[49,16,512]{2,1,0:T(8,128)}, f32[16,8,384]{2,1,0:T(8,128)S(1)}, bf16[49,16,2048]{2,1,0:T(8,128)(2,1)}, f32[8,2048]{1,0:T(8,128)S(1)}) custom-call(s32[3]{0:T(128)S(1)} %pad_add_fusion.core_ref.place, bf16[49,16,2048]{2,1,0:T(8,128)(2,1)} %get-tuple-element.165.dz.dz_ref, bf16[49,16,2048]{2,1,0:T(8,128)(2,1)} %get-tuple-element.166.xhat_ref, ...), custom_call_target="tpu_custom_call" | custom-call | flops 5000000000 | bytes 15000000 | tf_op jit(solution)/shard_map/pallas_call | solution.py:884
  317.2 11.7 %all_to_all.69.g = f32[16,8,384]{2,1,0:T(8,128)S(1)} all-to-all(f32[16,8,384]{2,1,0:T(8,128)S(1)} %get-tuple-element.173), channel_id=1, replica_groups=mesh['pipe'=2,'dp'=16] {'dp'}, dimensions={0} | all-to-all | bytes 393216 | tf_op jit(solution)/shard_map/all_to_all | solution.py:939
  330.8 3.8 shard_map.235
  335.5 14.4 %shard_map.236 = (f32[49,16,512]{2,1,0:T(8,128)}, f32[16,8,384]{2,1,0:T(8,128)}, bf16[49,16,512]{2,1,0:T(8,128)(2,1)S(1)}, bf16[49,16,128]{2,1,0:T(8,128)(2,1)S(1)}) custom-call(s32[3]{0:T(128)S(1)} %pad_add_fusion.core_ref.place, bf16[49,16,512]{2,1,0:T(8,128)(2,1)} %copy-done.10, f32[49,16,512]{2,1,0:T(8,128)} %get-tuple-element.175.a_ref, ...), custom_call_target="tpu_custom_call" | custom-call | flops 5000000000 | bytes 15000000 | tf_op jit(solution)/shard_map/pallas_call | solution.py:884
  351.2 5.8 all-to-all-start.8
  359.3 14.3 %shard_map.237 = (bf16[4,2,2,16,9088]{4,3,2,1,0:T(8,128)(2,1)}, bf16[4,2,2,16,9088]{4,3,2,1,0:T(8,128)(2,1)}) custom-call(s32[3]{0:T(128)S(1)} %pad_add_fusion.core_ref.place, bf16[49,16,512]{2,1,0:T(8,128)(2,1)S(1)} %copy-done.11, bf16[49,16,512]{2,1,0:T(8,128)(2,1)S(1)} %copy-done.13, bf16[49,16,128]{2,1,0:T(8,128)(2,1)S(1)} %get-tuple-element.181.dsq, ...), custom_call_target="tpu_custom_call" | custom-call | flops 5000000000 | bytes 15000000 | tf_op jit(solution)/shard_map/pallas_call | solution.py:884
  375.5 14.5 %shard_map.238 = (bf16[49,16,2048]{2,1,0:T(8,128)(2,1)}, bf16[49,16,512]{2,1,0:T(8,128)(2,1)}, f32[8,512]{1,0:T(8,128)S(1)}, bf16[49,16,2048]{2,1,0:T(8,128)(2,1...) custom-call(s32[3]{0:T(128)S(1)} %pad_add_fusion.core_ref.place, f32[49,16,512]{2,1,0:T(8,128)} %get-tuple-element.178.dn1, ...), custom_call_target="tpu_custom_call" | custom-call | flops 5000000000 | bytes 15000000 | tf_op jit(solution)/shard_map/pallas_call | solution.py:884
  390.1 5.7 add_convert_fusion
  397.1 21.0 %all_to_all.70.g = f32[16,8,768]{2,1,0:T(8,128)S(1)} all-to-all(f32[16,8,768]{2,1,0:T(8,128)S(1)} %shard_map.239), channel_id=1, replica_groups=mesh['pipe'=2,'dp'=16] {'dp'}, dimensions={0} | all-to-all | bytes 786432 | tf_op jit(solution)/shard_map/all_to_all | solution.py:939
  420.9 9.5 %shard_map.240 = (f32[49,16,512]{2,1,0:T(8,128)}, f32[16,8,384]{2,1,0:T(8,128)}, bf16[49,16,2048]{2,1,0:T(8,128)(2,1)}, f32[8,2048]{1,0:T(8,128)S(1)}) custom-call(s32[3]{0:T(128)S(1)} %pad_add_fusion.core_ref.place, bf16[49,16,2048]{2,1,0:T(8,128)(2,1)} %get-tuple-element.192.dz.dz_ref, bf16[49,16,2048]{2,1,0:T(8,128)(2,1)} %get-tuple-element.190.xhat_ref, ...), custom_call_target="tpu_custom_call" | custom-call | flops 5000000000 | bytes 15000000 | tf_op jit(solution)/shard_map/pallas_call | solution.py:884
  430.4 6.5 all-to-all-start.10
  439.2 10.3 %shard_map.241 = (bf16[4,2,2,16,4096]{4,3,2,1,0:T(8,128)(2,1)}, bf16[4,2,2,16,4096]{4,3,2,1,0:T(8,128)(2,1)}) custom-call(s32[3]{0:T(128)S(1)} %pad_add_fusion.core_ref.place, bf16[49,16,2048]{2,1,0:T(8,128)(2,1)} %get-tuple-element.203.d3, bf16[49,16,512]{2,1,0:T(8,128)(2,1)S(1)} %copy-done.8, bf16[49,16,512]{2,1,0:T(8,128)(2,1)S(1)} %copy-done.3, ...), custom_call_target="tpu_custom_call" | custom-call | flops 5000000000 | bytes 15000000 | tf_op jit(solution)/shard_map/pallas_call | solution.py:884
  452.0 12.3 %shard_map.242 = (bf16[4,2,16,2048]{3,2,1,0:T(8,128)(2,1)S(1)}, bf16[4,2,16,2048]{3,2,1,0:T(8,128)(2,1)S(1)}, bf16[4,2,16,2048]{3,2,1,0:T(8,128)(2,1)S(1)}, bf16...) custom-call(s32[3]{0:T(128)S(1)} %pad_add_fusion.core_ref.place, ...), custom_call_target="tpu_custom_call" | custom-call | flops 5000000000 | bytes 15000000 | tf_op jit(solution)/shard_map/pallas_call | solution.py:884
  467.2 14.8 %shard_map.243 = (f32[49,16,512]{2,1,0:T(8,128)}, f32[16,8,384]{2,1,0:T(8,128)}, bf16[49,16,512]{2,1,0:T(8,128)(2,1)S(1)}, bf16[49,16,128]{2,1,0:T(8,128)(2,1)S(1)}) custom-call(s32[3]{0:T(128)S(1)} %pad_add_fusion.core_ref.place, bf16[49,16,512]{2,1,0:T(8,128)(2,1)} %get-tuple-element.209.d2, f32[49,16,512]{2,1,0:T(8,128)} %get-tuple-element.210.a_ref, ...), custom_call_target="tpu_custom_call" | custom-call | flops 5000000000 | bytes 15000000 | tf_op jit(solution)/shard_map/pallas_call | solution.py:884
  483.7 6.3 all-to-all-start.11
  502.1 6.0 shard_map.244
  510.5 8.6 %shard_map.245 = (bf16[4,2,2,16,2048]{4,3,2,1,0:T(8,128)(2,1)}, bf16[4,2,2,16,2048]{4,3,2,1,0:T(8,128)(2,1)}, bf16[49,16,512]{2,1,0:T(8,128)(2,1)S(1)}, f32[8,512]{1,0:T(8,128)S(1)}) custom-call(s32[3]{0:T(128)S(1)} %pad_add_fusion.core_ref.place, f32[49,16,512]{2,1,0:T(8,128)} %get-tuple-element.213.dn1, f32[49,16,512]{2,1,0:T(8,128)} %collective-permute-done.44.other, ...), custom_call_target="tpu_custom_call" | custom-call | flops 5000000000 | bytes 15000000 | tf_op jit(solution)/shard_map/pallas_call | solution.py:884
  530.0 4.2 collective-permute-start.51
  539.7 9.7 %all-to-all-start.12 = ((bf16[16,16,4480]{2,1,0:T(8,128)(2,1)}), bf16[16,16,4480]{2,1,0:T(8,128)(2,1)}, u32[]{:S(2)}, u32[]{:S(2)}) async-start(bf16[16,16,4480]{2,1,0:T(8,128)(2,1)} %pad_maximum_fusion), calls=%async_computation.12 | async-start | bytes 4587520 | tf_op jit(solution)/shard_map/all_to_all | solution.py:1048
  550.4 6.7 %shard_map.247.early_ref = bf16[49,16,2048]{2,1,0:T(8,128)(2,1)} custom-call(s32[3]{0:T(128)S(1)} %pad_add_fusion.core_ref.place, bf16[49,16,512]{2,1,0:T(8,128)(2,1)} %copy-done.18, bf16[49,16,2048]{2,1,0:T(8,128)(2,1)} %get-tuple-element.192.dz.dz_ref, bf16[4,2,16,1024]{3,2,1,0:T(8,128)(2,1)S(1)} %copy.116.rest_0_, ...), custom_call_target="tpu_custom_call" | custom-call | flops 5000000000 | bytes 15000000 | tf_op jit(solution)/shard_map/pallas_call | solution.py:884
  557.1 4.4 collective-permute-start.53
  564.3 9.8 %shard_map.246 = bf16[3,392,2048]{2,1,0:T(8,128)(2,1)} custom-call(s32[3]{0:T(128)S(1)} %pad_add_fusion.core_ref.place, bf16[49,16,2048]{2,1,0:T(8,128)(2,1)} %get-tuple-element.230.x_ref.early_ref, bf16[49,16,2048]{2,1,0:T(8,128)(2,1)} %get-tuple-element.231.late_ref, bf16[49,16,2048]{2,1,0:T(8,128)(2,1)} %collective-permute-done.51.early_in, ...), custom_call_target="tpu_custom_call" | custom-call | flops 5000000000 | bytes 15000000 | tf_op jit(solution)/shard_map/pallas_call | solution.py:884
  574.2 20.3 %collective-permute-done.64 = bf16[2,16,4608]{2,1,0:T(8,128)(2,1)S(1)} collective-permute-done((bf16[2,16,4608]{2,1,0:T(8,128)(2,1)S(1)}, bf16[2,16,4608]{2,1,0:T(8,128)(2,1)S(1)}, u32[]{:S(2)}, u32[]{:S(2)}) %collective-permute-start.64) | collective-permute-done | bytes 294944 | tf_op jit(solution)/shard_map/ppermute | solution.py:936
  598.6 21.6 %all-to-all-done.12 = bf16[16,16,4480]{2,1,0:T(8,128)(2,1)} async-done(((bf16[16,16,4480]{2,1,0:T(8,128)(2,1)}), bf16[16,16,4480]{2,1,0:T(8,128)(2,1)}, u32[]{:S(2)}, u32[]{:S(2)}) %all-to-all-start.12) | async-done | bytes 2293792 | tf_op jit(solution)/shard_map/all_to_all | solution.py:1048
  622.2 4.2 collective-permute-start.55
  626.4 9.8 %shard_map.248 = bf16[3,392,2048]{2,1,0:T(8,128)(2,1)} custom-call(s32[3]{0:T(128)S(1)} %pad_add_fusion.core_ref.place, bf16[49,16,2048]{2,1,0:T(8,128)(2,1)} %shard_map.247.early_ref, bf16[49,16,2048]{2,1,0:T(8,128)(2,1)} %get-tuple-element.236.late_ref, bf16[49,16,2048]{2,1,0:T(8,128)(2,1)} %collective-permute-done.53.early_in, ...), custom_call_target="tpu_custom_call" | custom-call | flops 5000000000 | bytes 15000000 | tf_op jit(solution)/shard_map/pallas_call | solution.py:884
  (352 shorter events, 152.9 us)
Async XLA Ops:
  7.2 94.2 %all-gather.5.cloned.1.call-start = ((), (), s32[]{:S(2)}) async-start(), calls=%async_computation.17 | async-start | bytes 3829760 | tf_op jit(solution)/shard_map/all_gather | solution.py:968
  21.5 13.0 %collective-permute-start.4 = (bf16[2,16,2176]{2,1,0:T(8,128)(2,1)S(1)}, bf16[2,16,2176]{2,1,0:T(8,128)(2,1)S(1)}, u32[]{:S(2)}, u32[]{:S(2)}) collective-permute-start(bf16[2,16,2176]{2,1,0:T(8,128)(2,1)S(1)} %maximum_select_fusion.10), channel_id=1, source_target_pairs={{0,4},{1,5},{2,6},{3,7},{4,0},{5,1},{6,2},{7,3},{8,12},{9,13},{10,... | collective-permute-start | bytes 417800 | tf_op jit(solution)/shard_map/ppermute | solution.py:936
  34.5 12.9 %collective-permute-start.5 = (bf16[16,4224]{1,0:T(8,128)(2,1)S(1)}, bf16[16,4224]{1,0:T(8,128)(2,1)S(1)}, u32[]{:S(2)}, u32[]{:S(2)}) collective-permute-start(bf16[16,4224]{1,0:T(8,128)(2,1)S(1)} %get-tuple-element.135), channel_id=1, source_target_pairs={{0,8},{1,9},{2,10},{3,11},{4,12},{5,13},{6,14},{7,15},{8,0},{9,1},... | collective-permute-start | bytes 405512 | tf_op jit(solution)/shard_map/ppermute | solution.py:936
  45.5 12.0 %collective-permute-start.8 = (bf16[4,2,16,1024]{3,2,0,1:T(8,128)(2,1)S(1)}, bf16[4,2,16,1024]{3,2,0,1:T(8,128)(2,1)S(1)}, u32[]{:S(2)}, u32[]{:S(2)}) collective-permute-start(bf16[4,2,16,1024]{3,2,0,1:T(8,128)(2,1)S(1)} %maximum_select_fusion.8), channel_id=1, source_target_pairs={{0,2},{1,3},{2,0},{3,1},{4,6},{5,7},{6,4},{7,5},{8,10},{9,11},{10,... | collective-permute-start | bytes 786440 | tf_op jit(solution)/shard_map/ppermute | solution.py:936
  45.8 13.6 %collective-permute-start.11 = (bf16[4,2,16,1024]{3,2,0,1:T(8,128)(2,1)S(1)}, bf16[4,2,16,1024]{3,2,0,1:T(8,128)(2,1)S(1)}, u32[]{:S(2)}, u32[]{:S(2)}) collective-permute-start(bf16[4,2,16,1024]{3,2,0,1:T(8,128)(2,1)S(1)} %maximum_select_fusion.8), channel_id=1, source_target_pairs={{0,16},{16,0},{1,17},{17,1},{2,18},{18,2},{3,19},{19,3},{4,20},{20... | collective-permute-start | bytes 786440 | tf_op jit(solution)/shard_map/ppermute | solution.py:933
  47.5 14.3 %collective-permute-start.6 = (bf16[2,16,4224]{2,1,0:T(8,128)(2,1)S(1)}, bf16[2,16,4224]{2,1,0:T(8,128)(2,1)S(1)}, u32[]{:S(2)}, u32[]{:S(2)}) collective-permute-start(bf16[2,16,4224]{2,1,0:T(8,128)(2,1)S(1)} %maximum_select_fusion.7), channel_id=1, source_target_pairs={{0,4},{1,5},{2,6},{3,7},{4,0},{5,1},{6,2},{7,3},{8,12},{9,13},{10,... | collective-permute-start | bytes 811016 | tf_op jit(solution)/shard_map/ppermute | solution.py:936
  48.6 13.2 %collective-permute-start.10 = (bf16[4,2,16,1152]{3,2,1,0:T(8,128)(2,1)S(1)}, bf16[4,2,16,1152]{3,2,1,0:T(8,128)(2,1)S(1)}, u32[]{:S(2)}, u32[]{:S(2)}) collective-permute-start(bf16[4,2,16,1152]{3,2,1,0:T(8,128)(2,1)S(1)} %maximum_select_fusion.4.rest_2_), channel_id=1, source_target_pairs={{0,1},{1,0},{2,3},{3,2},{4,5},{5,4},{6,7},{7,6},{8,9},{9,8},{10,11... | collective-permute-start | bytes 884744 | tf_op jit(solution)/shard_map/ppermute | solution.py:936
  72.2 23.3 %all-to-all-start = ((f32[16,8,384]{2,1,0:T(8,128)}), f32[16,8,384]{2,1,0:T(8,128)S(1)}, u32[]{:S(2)}, u32[]{:S(2)}) async-start(f32[16,8,384]{2,1,0:T(8,128)} %get-tuple-element.140), calls=%async_computation | async-start | bytes 393216 | tf_op jit(solution)/shard_map/all_to_all | solution.py:939
  79.6 124.6 %all-gather.7.cloned.1.call-start = ((), (), s32[]{:S(2)}) async-start(), calls=%async_computation.18 | async-start | bytes 4943872 | tf_op jit(solution)/shard_map/all_gather | solution.py:968
  79.7 13.7 %collective-permute-start.16 = (bf16[4,16,2048]{2,1,0:T(8,128)(2,1)S(1)}, bf16[4,16,2048]{2,1,0:T(8,128)(2,1)S(1)}, u32[]{:S(2)}, u32[]{:S(2)}) collective-permute-start(bf16[4,16,2048]{2,1,0:T(8,128)(2,1)S(1)} %get-tuple-element.287), channel_id=1, source_target_pairs={{0,1},{1,0},{2,3},{3,2},{4,5},{5,4},{6,7},{7,6},{8,9},{9,8},{10,11... | collective-permute-start | bytes 786440 | tf_op jit(solution)/shard_map/ppermute | solution.py:936
  80.1 14.5 %collective-permute-start.17 = (bf16[4,16,2176]{2,1,0:T(8,128)(2,1)S(1)}, bf16[4,16,2176]{2,1,0:T(8,128)(2,1)S(1)}, u32[]{:S(2)}, u32[]{:S(2)}) collective-permute-start(bf16[4,16,2176]{2,1,0:T(8,128)(2,1)S(1)} %get-tuple-element.285), channel_id=1, source_target_pairs={{0,2},{1,3},{2,0},{3,1},{4,6},{5,7},{6,4},{7,5},{8,10},{9,11},{10,... | collective-permute-start | bytes 835592 | tf_op jit(solution)/shard_map/ppermute | solution.py:936
  103.9 31.1 %collective-permute-start.21 = (bf16[4,2,16,2048]{3,2,0,1:T(8,128)(2,1)}, bf16[4,2,16,2048]{3,2,0,1:T(8,128)(2,1)}, u32[]{:S(2)}, u32[]{:S(2)}) collective-permute-start(bf16[4,2,16,2048]{3,2,0,1:T(8,128)(2,1)} %maximum_select_fusion.2), channel_id=1, source_target_pairs={{0,2},{1,3},{2,0},{3,1},{4,6},{5,7},{6,4},{7,5},{8,10},{9,11},{10,... | collective-permute-start | bytes 1572872 | tf_op jit(solution)/shard_map/ppermute | solution.py:936
  103.9 30.6 %collective-permute-start.22 = (bf16[4,2,16,2176]{3,2,1,0:T(8,128)(2,1)}, bf16[4,2,16,2176]{3,2,1,0:T(8,128)(2,1)}, u32[]{:S(2)}, u32[]{:S(2)}) collective-permute-start(bf16[4,2,16,2176]{3,2,1,0:T(8,128)(2,1)} %maximum_select_fusion.rest_2_.rest_10_), channel_id=1, source_target_pairs={{0,1},{1,0},{2,3},{3,2},{4,5},{5,4},{6,7},{7,6},{8,9},{9,8},{10,11... | collective-permute-start | bytes 1671176 | tf_op jit(solution)/shard_map/ppermute | solution.py:936
  128.5 15.9 %all-to-all-start.1 = ((f32[16,8,384]{2,1,0:T(8,128)}), f32[16,8,384]{2,1,0:T(8,128)S(1)}, u32[]{:S(2)}, u32[]{:S(2)}) async-start(f32[16,8,384]{2,1,0:T(8,128)} %get-tuple-element.146), calls=%async_computation.1 | async-start | bytes 393216 | tf_op jit(solution)/shard_map/all_to_all | solution.py:939
  133.5 18.9 %collective-permute-start.25 = (bf16[4,2,16,2176]{3,2,1,0:T(8,128)(2,1)}, bf16[4,2,16,2176]{3,2,1,0:T(8,128)(2,1)}, u32[]{:S(2)}, u32[]{:S(2)}) collective-permute-start(bf16[4,2,16,2176]{3,2,1,0:T(8,128)(2,1)} %maximum_select_fusion.rest_2_.rest_10_), channel_id=1, source_target_pairs={{0,16},{16,0},{1,17},{17,1},{2,18},{18,2},{3,19},{19,3},{4,20},{20... | collective-permute-start | bytes 1671176 | tf_op jit(solution)/shard_map/ppermute | solution.py:933
  134.5 17.9 %collective-permute-start.26 = (bf16[4,2,16,2176]{3,2,1,0:T(8,128)(2,1)}, bf16[4,2,16,2176]{3,2,1,0:T(8,128)(2,1)}, u32[]{:S(2)}, u32[]{:S(2)}) collective-permute-start(bf16[4,2,16,2176]{3,2,1,0:T(8,128)(2,1)} %collective-permute-done.22.rest_3_.rest_11_), channel_id=1, source_target_pairs={{0,16},{16,0},{1,17},{17,1},{2,18},{18,2},{3,19},{19,3},{4,20},{20... | collective-permute-start | bytes 1671176 | tf_op jit(solution)/shard_map/ppermute | solution.py:933
  134.6 13.8 %collective-permute-start.23 = (bf16[4,2,16,2048]{3,2,0,1:T(8,128)(2,1)}, bf16[4,2,16,2048]{3,2,0,1:T(8,128)(2,1)}, u32[]{:S(2)}, u32[]{:S(2)}) collective-permute-start(bf16[4,2,16,2048]{3,2,0,1:T(8,128)(2,1)} %maximum_select_fusion.2), channel_id=1, source_target_pairs={{0,16},{16,0},{1,17},{17,1},{2,18},{18,2},{3,19},{19,3},{4,20},{20... | collective-permute-start | bytes 1572872 | tf_op jit(solution)/shard_map/ppermute | solution.py:933
  135.1 15.5 %collective-permute-start.24 = (bf16[4,2,16,2048]{3,2,0,1:T(8,128)(2,1)}, bf16[4,2,16,2048]{3,2,0,1:T(8,128)(2,1)}, u32[]{:S(2)}, u32[]{:S(2)}) collective-permute-start(bf16[4,2,16,2048]{3,2,0,1:T(8,128)(2,1)} %collective-permute-done.21), channel_id=1, source_target_pairs={{0,16},{16,0},{1,17},{17,1},{2,18},{18,2},{3,19},{19,3},{4,20},{20... | collective-permute-start | bytes 1572872 | tf_op jit(solution)/shard_map/ppermute | solution.py:933
  204.2 14.6 %collective-permute-start.31 = (bf16[4,2,2,16,9088]{4,3,2,1,0:T(8,128)(2,1)}, bf16[4,2,2,16,9088]{4,3,2,1,0:T(8,128)(2,1)}, u32[]{:S(2)}, u32[]{:S(2)}) collective-permute-start(bf16[4,2,2,16,9088]{4,3,2,1,0:T(8,128)(2,1)} %bitcast.196), channel_id=1, source_target_pairs={{0,16},{16,0},{1,17},{17,1},{2,18},{18,2},{3,19},{19,3},{4,20},{20... | collective-permute-start | bytes 13959176 | tf_op jit(solution)/shard_map/ppermute | solution.py:933
  204.5 14.2 %collective-permute-start.29 = (f32[49,16,512]{2,1,0:T(8,128)}, f32[49,16,512]{2,1,0:T(8,128)}, u32[]{:S(2)}, u32[]{:S(2)}) collective-permute-start(f32[49,16,512]{2,1,0:T(8,128)} %get-tuple-element.152.a_in), channel_id=1, source_target_pairs={{0,16},{16,0},{1,17},{17,1},{2,18},{18,2},{3,19},{19,3},{4,20},{20... | collective-permute-start | bytes 4816904 | tf_op jit(solution)/shard_map/ppermute | solution.py:933
  204.7 12.2 %all-to-all-start.3 = ((f32[16,8,384]{2,1,0:T(8,128)}), f32[16,8,384]{2,1,0:T(8,128)S(1)}, u32[]{:S(2)}, u32[]{:S(2)}) async-start(f32[16,8,384]{2,1,0:T(8,128)} %get-tuple-element.153), calls=%async_computation.3 | async-start | bytes 393216 | tf_op jit(solution)/shard_map/all_to_all | solution.py:939
  350.8 24.4 %collective-permute-start.38 = (f32[49,16,512]{2,1,0:T(8,128)}, f32[49,16,512]{2,1,0:T(8,128)}, u32[]{:S(2)}, u32[]{:S(2)}) collective-permute-start(f32[49,16,512]{2,1,0:T(8,128)} %get-tuple-element.178.dn1), channel_id=1, source_target_pairs={{0,16},{16,0},{1,17},{17,1},{2,18},{18,2},{3,19},{19,3},{4,20},{20... | collective-permute-start | bytes 4816904 | tf_op jit(solution)/shard_map/ppermute | solution.py:933
  351.2 22.4 %all-to-all-start.8 = ((f32[16,8,384]{2,1,0:T(8,128)}), f32[16,8,384]{2,1,0:T(8,128)S(1)}, u32[]{:S(2)}, u32[]{:S(2)}) async-start(f32[16,8,384]{2,1,0:T(8,128)} %get-tuple-element.179), calls=%async_computation.8 | async-start | bytes 393216 | tf_op jit(solution)/shard_map/all_to_all | solution.py:939
  357.0 237.7 %reduce-scatter.5.cloned.1.call-start = ((), (), s32[]{:S(2)}) async-start(), calls=%async_computation.16 | async-start | bytes 4943872 | tf_op jit(solution)/shard_map/reduce_scatter | solution.py:1045
  375.2 14.9 %collective-permute-start.40 = (bf16[4,2,2,16,9088]{4,3,2,1,0:T(8,128)(2,1)}, bf16[4,2,2,16,9088]{4,3,2,1,0:T(8,128)(2,1)}, u32[]{:S(2)}, u32[]{:S(2)}) collective-permute-start(bf16[4,2,2,16,9088]{4,3,2,1,0:T(8,128)(2,1)} %get-tuple-element.195), channel_id=1, source_target_pairs={{0,16},{16,0},{1,17},{17,1},{2,18},{18,2},{3,19},{19,3},{4,20},{20... | collective-permute-start | bytes 13959176 | tf_op jit(solution)/shard_map/ppermute | solution.py:933
  430.4 19.1 %all-to-all-start.10 = ((f32[16,8,384]{2,1,0:T(8,128)}), f32[16,8,384]{2,1,0:T(8,128)S(1)}, u32[]{:S(2)}, u32[]{:S(2)}) async-start(f32[16,8,384]{2,1,0:T(8,128)} %get-tuple-element.202), calls=%async_computation.10 | async-start | bytes 393216 | tf_op jit(solution)/shard_map/all_to_all | solution.py:939
  451.6 44.7 %collective-permute-start.45 = (bf16[4,2,2,16,4096]{4,3,2,1,0:T(8,128)(2,1)}, bf16[4,2,2,16,4096]{4,3,2,1,0:T(8,128)(2,1)}, u32[]{:S(2)}, u32[]{:S(2)}) collective-permute-start(bf16[4,2,2,16,4096]{4,3,2,1,0:T(8,128)(2,1)} %get-tuple-element.216), channel_id=1, source_target_pairs={{0,16},{16,0},{1,17},{17,1},{2,18},{18,2},{3,19},{19,3},{4,20},{20... | collective-permute-start | bytes 6291464 | tf_op jit(solution)/shard_map/ppermute | solution.py:933
  466.1 25.8 %collective-permute-start.46 = (bf16[4,2,16,2048]{3,2,0,1:T(8,128)(2,1)}, bf16[4,2,16,2048]{3,2,0,1:T(8,128)(2,1)}, u32[]{:S(2)}, u32[]{:S(2)}) collective-permute-start(bf16[4,2,16,2048]{3,2,0,1:T(8,128)(2,1)} %copy.149), channel_id=1, source_target_pairs={{0,16},{16,0},{1,17},{17,1},{2,18},{18,2},{3,19},{19,3},{4,20},{20... | collective-permute-start | bytes 1572872 | tf_op jit(solution)/shard_map/ppermute | solution.py:933
  466.8 27.1 %collective-permute-start.47 = (bf16[4,2,16,2560]{3,2,1,0:T(8,128)(2,1)}, bf16[4,2,16,2560]{3,2,1,0:T(8,128)(2,1)}, u32[]{:S(2)}, u32[]{:S(2)}) collective-permute-start(bf16[4,2,16,2560]{3,2,1,0:T(8,128)(2,1)} %get-tuple-element.220), channel_id=1, source_target_pairs={{0,16},{16,0},{1,17},{17,1},{2,18},{18,2},{3,19},{19,3},{4,20},{20... | collective-permute-start | bytes 1966088 | tf_op jit(solution)/shard_map/ppermute | solution.py:933
  483.5 25.4 %collective-permute-start.44 = (f32[49,16,512]{2,1,0:T(8,128)}, f32[49,16,512]{2,1,0:T(8,128)}, u32[]{:S(2)}, u32[]{:S(2)}) collective-permute-start(f32[49,16,512]{2,1,0:T(8,128)} %get-tuple-element.213.dn1), channel_id=1, source_target_pairs={{0,16},{16,0},{1,17},{17,1},{2,18},{18,2},{3,19},{19,3},{4,20},{20... | collective-permute-start | bytes 4816904 | tf_op jit(solution)/shard_map/ppermute | solution.py:933
  483.7 24.4 %all-to-all-start.11 = ((f32[16,8,384]{2,1,0:T(8,128)}), f32[16,8,384]{2,1,0:T(8,128)S(1)}, u32[]{:S(2)}, u32[]{:S(2)}) async-start(f32[16,8,384]{2,1,0:T(8,128)} %get-tuple-element.214), calls=%async_computation.11 | async-start | bytes 393216 | tf_op jit(solution)/shard_map/all_to_all | solution.py:939
  490.0 146.2 %reduce-scatter.3.cloned.1.call-start = ((), (), s32[]{:S(2)}) async-start(), calls=%async_computation.15 | async-start | bytes 2228224 | tf_op jit(solution)/shard_map/reduce_scatter | solution.py:1045
  490.1 31.4 %collective-permute-start.61 = (bf16[4,2,16,2560]{3,2,1,0:T(8,128)(2,1)}, bf16[4,2,16,2560]{3,2,1,0:T(8,128)(2,1)}, u32[]{:S(2)}, u32[]{:S(2)}) collective-permute-start(bf16[4,2,16,2560]{3,2,1,0:T(8,128)(2,1)} %get-tuple-element.242), channel_id=1, source_target_pairs={{0,16},{16,0},{1,17},{17,1},{2,18},{18,2},{3,19},{19,3},{4,20},{20... | collective-permute-start | bytes 1966088 | tf_op jit(solution)/shard_map/ppermute | solution.py:933
  491.9 33.6 %collective-permute-start.58 = (bf16[4,2,16,2048]{3,2,0,1:T(8,128)(2,1)}, bf16[4,2,16,2048]{3,2,0,1:T(8,128)(2,1)}, u32[]{:S(2)}, u32[]{:S(2)}) collective-permute-start(bf16[4,2,16,2048]{3,2,0,1:T(8,128)(2,1)} %copy.155), channel_id=1, source_target_pairs={{0,16},{16,0},{1,17},{17,1},{2,18},{18,2},{3,19},{19,3},{4,20},{20... | collective-permute-start | bytes 1572872 | tf_op jit(solution)/shard_map/ppermute | solution.py:933
  496.0 25.0 %collective-permute-start.62 = (bf16[4,2,16,2560]{3,2,1,0:T(8,128)(2,1)}, bf16[4,2,16,2560]{3,2,1,0:T(8,128)(2,1)}, u32[]{:S(2)}, u32[]{:S(2)}) collective-permute-start(bf16[4,2,16,2560]{3,2,1,0:T(8,128)(2,1)} %add_convert_fusion.6), channel_id=1, source_target_pairs={{0,1},{1,0},{2,3},{3,2},{4,5},{5,4},{6,7},{7,6},{8,9},{9,8},{10,11... | collective-permute-start | bytes 1966088 | tf_op jit(solution)/shard_map/ppermute | solution.py:936
  509.0 16.5 %collective-permute-start.59 = (bf16[4,2,16,2048]{3,2,0,1:T(8,128)(2,1)}, bf16[4,2,16,2048]{3,2,0,1:T(8,128)(2,1)S(1)}, u32[]{:S(2)}, u32[]{:S(2)}) collective-permute-start(bf16[4,2,16,2048]{3,2,0,1:T(8,128)(2,1)} %add_convert_fusion.9), channel_id=1, source_target_pairs={{0,2},{1,3},{2,0},{3,1},{4,6},{5,7},{6,4},{7,5},{8,10},{9,11},{10,... | collective-permute-start | bytes 1572872 | tf_op jit(solution)/shard_map/ppermute | solution.py:936
  510.2 17.4 %collective-permute-start.50 = (bf16[4,2,2,16,2432]{4,3,2,1,0:T(8,128)(2,1)}, bf16[4,2,2,16,2432]{4,3,2,1,0:T(8,128)(2,1)S(1)}, u32[]{:S(2)}, u32[]{:S(2)}) collective-permute-start(bf16[4,2,2,16,2432]{4,3,2,1,0:T(8,128)(2,1)} %get-tuple-element.226), channel_id=1, source_target_pairs={{0,16},{16,0},{1,17},{17,1},{2,18},{18,2},{3,19},{19,3},{4,20},{20... | collective-permute-start | bytes 3735560 | tf_op jit(solution)/shard_map/ppermute | solution.py:933
  523.8 25.6 %collective-permute-start.63 = (bf16[4,16,2560]{2,1,0:T(8,128)(2,1)}, bf16[4,16,2560]{2,1,0:T(8,128)(2,1)}, u32[]{:S(2)}, u32[]{:S(2)}) collective-permute-start(bf16[4,16,2560]{2,1,0:T(8,128)(2,1)} %dynamic-slice_bitcast_fusion), channel_id=1, source_target_pairs={{0,2},{1,3},{2,0},{3,1},{4,6},{5,7},{6,4},{7,5},{8,10},{9,11},{10,... | collective-permute-start | bytes 983048 | tf_op jit(solution)/shard_map/ppermute | solution.py:936
  526.9 12.7 %collective-permute-start.60 = (bf16[4,16,2048]{2,1,0:T(8,128)(2,1)S(1)}, bf16[4,16,2048]{2,1,0:T(8,128)(2,1)S(1)}, u32[]{:S(2)}, u32[]{:S(2)}) collective-permute-start(bf16[4,16,2048]{2,1,0:T(8,128)(2,1)S(1)} %dynamic-slice_bitcast_fusion.2), channel_id=1, source_target_pairs={{0,1},{1,0},{2,3},{3,2},{4,5},{5,4},{6,7},{7,6},{8,9},{9,8},{10,11... | collective-permute-start | bytes 786440 | tf_op jit(solution)/shard_map/ppermute | solution.py:936
  530.0 34.3 %collective-permute-start.51 = (bf16[49,16,2048]{2,1,0:T(8,128)(2,1)}, bf16[49,16,2048]{2,1,0:T(8,128)(2,1)}, u32[]{:S(2)}, u32[]{:S(2)}) collective-permute-start(bf16[49,16,2048]{2,1,0:T(8,128)(2,1)} %get-tuple-element.230.x_ref.early_ref), channel_id=1, source_target_pairs={{16,0},{17,1},{18,2},{19,3},{20,4},{21,5},{22,6},{23,7},{24,8},{25... | collective-permute-start | bytes 9633800 | tf_op jit(solution)/shard_map/ppermute | solution.py:1285
  534.2 30.1 %collective-permute-start.52 = (bf16[49,16,2048]{2,1,0:T(8,128)(2,1)}, bf16[49,16,2048]{2,1,0:T(8,128)(2,1)}, u32[]{:S(2)}, u32[]{:S(2)}) collective-permute-start(bf16[49,16,2048]{2,1,0:T(8,128)(2,1)} %get-tuple-element.231.late_ref), channel_id=1, source_target_pairs={{0,16},{1,17},{2,18},{3,19},{4,20},{5,21},{6,22},{7,23},{8,24},{9,... | collective-permute-start | bytes 9633800 | tf_op jit(solution)/shard_map/ppermute | solution.py:1285
  539.7 80.5 %all-to-all-start.12 = ((bf16[16,16,4480]{2,1,0:T(8,128)(2,1)}), bf16[16,16,4480]{2,1,0:T(8,128)(2,1)}, u32[]{:S(2)}, u32[]{:S(2)}) async-start(bf16[16,16,4480]{2,1,0:T(8,128)(2,1)} %pad_maximum_fusion), calls=%async_computation.12 | async-start | bytes 4587520 | tf_op jit(solution)/shard_map/all_to_all | solution.py:1048
  557.1 69.3 %collective-permute-start.53 = (bf16[49,16,2048]{2,1,0:T(8,128)(2,1)}, bf16[49,16,2048]{2,1,0:T(8,128)(2,1)}, u32[]{:S(2)}, u32[]{:S(2)}) collective-permute-start(bf16[49,16,2048]{2,1,0:T(8,128)(2,1)} %shard_map.247.early_ref), channel_id=1, source_target_pairs={{16,0},{17,1},{18,2},{19,3},{20,4},{21,5},{22,6},{23,7},{24,8},{25... | collective-permute-start | bytes 9633800 | tf_op jit(solution)/shard_map/ppermute | solution.py:1285
  561.5 64.9 %collective-permute-start.54 = (bf16[49,16,2048]{2,1,0:T(8,128)(2,1)}, bf16[49,16,2048]{2,1,0:T(8,128)(2,1)}, u32[]{:S(2)}, u32[]{:S(2)}) collective-permute-start(bf16[49,16,2048]{2,1,0:T(8,128)(2,1)} %get-tuple-element.236.late_ref), channel_id=1, source_target_pairs={{0,16},{1,17},{2,18},{3,19},{4,20},{5,21},{6,22},{7,23},{8,24},{9,... | collective-permute-start | bytes 9633800 | tf_op jit(solution)/shard_map/ppermute | solution.py:1285
  563.1 31.4 %collective-permute-start.64 = (bf16[2,16,4608]{2,1,0:T(8,128)(2,1)S(1)}, bf16[2,16,4608]{2,1,0:T(8,128)(2,1)S(1)}, u32[]{:S(2)}, u32[]{:S(2)}) collective-permute-start(bf16[2,16,4608]{2,1,0:T(8,128)(2,1)S(1)} %dynamic-slice_bitcast_fusion.1), channel_id=1, source_target_pairs={{0,4},{1,5},{2,6},{3,7},{4,0},{5,1},{6,2},{7,3},{8,12},{9,13},{10,... | collective-permute-start | bytes 884744 | tf_op jit(solution)/shard_map/ppermute | solution.py:936
  594.6 41.7 %collective-permute-start.65 = (bf16[16,4608]{1,0:T(8,128)(2,1)S(1)}, bf16[16,4608]{1,0:T(8,128)(2,1)S(1)}, u32[]{:S(2)}, u32[]{:S(2)}) collective-permute-start(bf16[16,4608]{1,0:T(8,128)(2,1)S(1)} %dynamic-slice_bitcast_fusion.4), channel_id=1, source_target_pairs={{0,8},{1,9},{2,10},{3,11},{4,12},{5,13},{6,14},{7,15},{8,0},{9,1},... | collective-permute-start | bytes 442376 | tf_op jit(solution)/shard_map/ppermute | solution.py:936
  595.6 47.4 %collective-permute-start.57 = (bf16[16,9088]{1,0:T(8,128)(2,1)}, bf16[16,9088]{1,0:T(8,128)(2,1)S(1)}, u32[]{:S(2)}, u32[]{:S(2)}) collective-permute-start(bf16[16,9088]{1,0:T(8,128)(2,1)} %bitcast.177), channel_id=1, source_target_pairs={{0,16},{1,17},{2,18},{3,19},{4,20},{5,21},{6,22},{7,23},{8,24},{9,... | collective-permute-start | bytes 872456 | tf_op jit(solution)/shard_map/ppermute | solution.py:1054
  622.2 22.8 %collective-permute-start.55 = (f32[16,4480]{1,0:T(8,128)S(1)}, f32[16,4480]{1,0:T(8,128)S(1)}, u32[]{:S(2)}, u32[]{:S(2)}) collective-permute-start(f32[16,4480]{1,0:T(8,128)S(1)} %convert_reduce_fusion), channel_id=1, source_target_pairs={{16,0},{17,1},{18,2},{19,3},{20,4},{21,5},{22,6},{23,7},{24,8},{25... | collective-permute-start | bytes 860168 | tf_op jit(solution)/shard_map/ppermute | solution.py:1385
  (76 other events, 620.4 us)
Sparse Core Ops, SparseCore 0:
  17.4 83.9 all-gather.4
  104.2 87.1 all-gather.6
  395.9 120.3 reduce-scatter.4
  518.4 98.3 reduce-scatter.2
